TPU v7x, 32 devices: a whole 2x2x4 slice. The times are simulated.
32 devices in a mesh: groups: 2 (over x), ctx: 16 (over z, y, core).
Axes of the slice: x: 2, y: 2, z: 4, core: 2. Of those that a mesh axis runs over, the one named last changes fastest.
Arguments:
- queries: bfloat16 [2048, 12288], P(('groups', 'ctx')), parts along dimension 0, may hold values from -460 to 460
- latent_kv: bfloat16 [2048, 576], P(('groups', 'ctx')), parts along dimension 0, may hold values from -4 to 4
- key_proj: bfloat16 [64, 128, 512], P('ctx'), may hold values from -0.25 to 0.25
- value_proj: bfloat16 [64, 512, 128], P('ctx'), may hold values from -0.25 to 0.25
- moe_input: bfloat16 [2048, 3584], P(('groups', 'ctx')), parts along dimension 0, may hold values from -6 to 6
- routes: int32 [2048, 2], P(('groups', 'ctx')), parts along dimension 0, may hold values from 0 to 7, all different within a row; in each aligned block of 64 rows (0 to 63, 64 to 127, ...) at most 22 rows name the same one
- gates: float32 [2048, 2], P(('groups', 'ctx')), parts along dimension 0, may hold values from 0.1 to 0.6
- expert_gate: bfloat16 [16, 3584, 512], P('ctx'), may hold values from -0.09375 to 0.09375
- expert_up: bfloat16 [16, 3584, 512], P('ctx'), may hold values from -0.09375 to 0.09375
- expert_down: bfloat16 [16, 512, 3584], P('ctx'), may hold values from -0.1875 to 0.1875
Outputs:
- attention_out: bfloat16 [2048, 8192], P(('groups', 'ctx')), parts along dimension 0
- moe_out: bfloat16 [2048, 3584], P(('groups', 'ctx')), parts along dimension 0
There are 2 independent parts, one for each index of `groups`. A program takes and returns all parts, laid end to end along the dimension named above; an argument that names none is the same for every part. Nothing has to cross between parts.
Inputs may be any that keep to these rules, and one draw needn't show every extreme that they name: Within the 64 rows of one device at most 22 routes name the same expert; the routes of one row differ.
All inputs are finite; a program needn't handle non-finite values.
Results may differ from a plain program's by a relative error of at most 0.0059.
Values may be sent and summed in bfloat16 or wider, within the bound.
No kernel may reach another device: no remote copies, remote signals or barrier semaphores. Data moves between devices by JAX's collectives and lax.ppermute only.
A program may use at most 128 MiB of HBM per device.

v0:
```python
import math

import jax
import jax.numpy as jnp
from jax import lax
from jax.sharding import PartitionSpec as P

D = 3584
HEADS = 64
NOPE = 128
ROPE = 64
LATENT = 512
VDIM = 128
TOP = 2


def project_heads(row_data, weight):
    return jnp.einsum(
        "thi,hio->tho",
        row_data,
        lax.all_gather(weight, "ctx", axis=0, tiled=True),
        preferred_element_type=jnp.float32,
    ).astype(jnp.bfloat16)


def on_device(
    queries,
    latent_kv,
    key_proj,
    value_proj,
    moe_input,
    routes,
    gates,
    expert_gate,
    expert_up,
    expert_down,
):
    rank_index = lax.axis_index("ctx")
    tok_rows = queries.shape[0]
    first_pos = rank_index * tok_rows
    held_pos = first_pos + jnp.arange(tok_rows, dtype=jnp.int32)
    last_pos = first_pos + tok_rows - 1
    score_scale = 1.0 / math.sqrt(NOPE + ROPE)
    shaped = queries.reshape(tok_rows, HEADS, NOPE + ROPE)
    query_lat = project_heads(shaped[:, :, :NOPE], key_proj)
    query_all = jnp.concatenate([query_lat, shaped[:, :, NOPE:]], axis=2)
    row_count = tok_rows * HEADS
    block_rows = math.gcd(row_count, 512)
    block_count = row_count // block_rows
    query_blocks = query_all.reshape(block_count, block_rows, LATENT + ROPE)
    query_pos = (held_pos[:, None] + jnp.zeros((1, HEADS), jnp.int32)).reshape(
        block_count, block_rows
    )
    initial = (
        jnp.full((block_count, block_rows), -1e30, jnp.float32),
        jnp.zeros((block_count, block_rows), jnp.float32),
        jnp.zeros((block_count, block_rows, LATENT), jnp.float32),
    )
    shard_keys = lax.all_gather(latent_kv, "ctx", axis=0, tiled=True)

    def compute(carried_in):
        key_pos = jnp.arange(shard_keys.shape[0], dtype=jnp.int32)

        def per_block(inputs):
            query_rows, positions, row_max, running_sum, weighted = inputs
            scores = (
                jnp.dot(query_rows, shard_keys.T, preferred_element_type=jnp.float32) * score_scale
            )
            visible = key_pos[None, :] <= positions[:, None]
            scores = jnp.where(visible, scores, -1e30)
            new_max = jnp.maximum(row_max, jnp.max(scores, axis=1))
            weights = jnp.where(visible, jnp.exp(scores - new_max[:, None]), 0.0)
            rescale = jnp.exp(row_max - new_max)
            new_sum = running_sum * rescale + jnp.sum(weights, axis=1)
            new_weighted = weighted * rescale[:, None] + jnp.dot(
                weights.astype(jnp.bfloat16),
                shard_keys[:, :LATENT],
                preferred_element_type=jnp.float32,
            )
            return (new_max, new_sum, new_weighted)

        return lax.map(
            per_block, (query_blocks, query_pos, carried_in[0], carried_in[1], carried_in[2])
        )

    row_max, running_sum, weighted = lax.cond(
        jnp.int32(0) <= last_pos, compute, lambda carried_in: carried_in, initial
    )
    output_lat = (
        (weighted / running_sum[:, :, None]).astype(jnp.bfloat16).reshape(tok_rows, HEADS, LATENT)
    )
    attention_out = project_heads(output_lat, value_proj).reshape(tok_rows, HEADS * VDIM)
    experts = lax.axis_size("ctx") // 2
    capacity = 2 * ((4 * tok_rows * TOP + 6 * experts - 1) // (6 * experts))
    flat_ids = routes.reshape(-1)
    onehot = (flat_ids[:, None] == jnp.arange(experts, dtype=jnp.int32)[None, :]).astype(jnp.int32)
    slot_index = jnp.sum((jnp.cumsum(onehot, axis=0) - 1) * onehot, axis=1)
    target = flat_ids * capacity + slot_index
    token_row = jnp.arange(tok_rows * TOP, dtype=jnp.int32) // TOP
    bucket_rows = jnp.full((experts * capacity,), tok_rows, jnp.int32).at[target].set(token_row)
    padded = jnp.concatenate([moe_input, jnp.zeros((1, D), jnp.bfloat16)], axis=0)
    bucket = padded[bucket_rows].reshape(experts, capacity, D)
    outgoing = jnp.repeat(bucket, 2, axis=0)
    arrived = lax.all_to_all(outgoing, "ctx", split_axis=0, concat_axis=0, tiled=True)
    sources = arrived.shape[0]
    items = arrived.shape[1]
    row_data = arrived.reshape(sources * items, D)
    gate_pre = jnp.dot(row_data, expert_gate[0], preferred_element_type=jnp.float32)
    up_pre = jnp.dot(row_data, expert_up[0], preferred_element_type=jnp.float32)
    hidden = (jax.nn.silu(gate_pre) * up_pre).astype(jnp.bfloat16)
    result = jnp.dot(hidden, expert_down[0], preferred_element_type=jnp.float32).astype(
        jnp.bfloat16
    )
    returned = lax.all_to_all(
        result.reshape(sources, items, D), "ctx", split_axis=0, concat_axis=0, tiled=True
    )
    summed = jnp.sum(returned.reshape(experts, 2, capacity, D).astype(jnp.float32), axis=1).reshape(
        experts * capacity, D
    )
    picked = summed[target].reshape(tok_rows, TOP, D)
    moe_out = jnp.sum(picked * gates[:, :, None], axis=1).astype(jnp.bfloat16)
    return (attention_out, moe_out)


def solution(mesh):
    return jax.shard_map(
        on_device,
        mesh=mesh,
        in_specs=(
            P(("groups", "ctx"), None),
            P(("groups", "ctx"), None),
            P("ctx", None, None),
            P("ctx", None, None),
            P(("groups", "ctx"), None),
            P(("groups", "ctx"), None),
            P(("groups", "ctx"), None),
            P("ctx", None, None),
            P("ctx", None, None),
            P("ctx", None, None),
        ),
        out_specs=(P(("groups", "ctx"), None), P(("groups", "ctx"), None)),
        check_vma=False,
    )
```

profile of v0, /device:TPU:15, one launch (start us, length us, event | category | flops | bytes accessed | tf_op | source)
XLA Modules:
  0.0 341.0 jit_solution(9609944660586007285)
XLA Ops:
  7.2 0.7 all-gather.4.cloned.1.call-update
  7.9 0.7 all-gather.6.cloned.1.call-update
  8.7 0.7 all-gather.8.cloned.1.call-update
  9.4 0.8 copy.31
  10.3 0.7 broadcast_multiply_fusion
  11.5 1.1 concatenate.7
  12.7 1.0 scatter_custom_fusion
  13.7 1.3 gather_fusion
  15.7 116.6 %all_to_all.10 = bf16[16,22,3584]{2,1,0:T(8,128)(2,1)S(1)} all-to-all(bf16[16,22,3584]{2,1,0:T(8,128)(2,1)S(1)} %bitcast.62), channel_id=1, replica_groups=mesh['groups'=2,'ctx'=16] {'ctx'}, dimensions={0} | all-to-all | bytes 5046272 | tf_op jit(solution)/shard_map/all_to_all | solution.py:104
  132.4 2.2 reshape.122
  134.6 4.4 %fusion.29 = f32[352,512]{1,0:T(8,128)S(1)} fusion(bf16[352,3584]{1,0:T(8,128)(2,1)} %reshape.122, bf16[1,3584,512]{2,1,0:T(8,128)(2,1)} %param.21), kind=kOutput, calls=%fused_computation.41 | convolution fusion | flops 1291845632 | bytes 6914048 | tf_op jit(solution)/shard_map/dot_general | solution.py:108
  139.0 7.6 %convolution_convert_fusion = bf16[352,3584]{1,0:T(8,128)(2,1)} fusion(bf16[1,512,3584]{2,1,0:T(8,128)(2,1)} %param.23, bf16[352,3584]{1,0:T(8,128)(2,1)S(1)} %copy-done.2, bf16[1,3584,512]{2,1,0:T(8,128)(2,1)} %param.22, f32[352,512]{1,0:T(8,128)S(1)} %fusion.29), kind=kOutput, calls=%fused_computation.33 | convolution fusion | flops 2586034176 | bytes 13107200 | tf_op jit(solution)/shard_map/dot_general | solution.py:111
  146.6 4.3 %reshape.123 = bf16[16,22,3584]{2,1,0:T(8,128)(2,1)} reshape(bf16[352,3584]{1,0:T(8,128)(2,1)} %convolution_convert_fusion) | data formatting | bytes 5046272 | tf_op jit(solution)/shard_map/reshape | solution.py:115
  150.9 5.4 %all-to-all-start.1 = ((bf16[16,22,3584]{2,1,0:T(8,128)(2,1)}), bf16[16,22,3584]{2,1,0:T(8,128)(2,1)S(1)}, u32[]{:S(2)}, u32[]{:S(2)}) async-start(bf16[16,22,3584]{2,1,0:T(8,128)(2,1)} %reshape.123), calls=%async_computation.1 | async-start | bytes 5505024 | tf_op jit(solution)/shard_map/all_to_all | solution.py:114
  156.3 4.6 %reshape.117 = bf16[64,64,192]{2,1,0:T(8,128)(2,1)} reshape(bf16[64,12288]{1,0:T(8,128)(2,1)} %param.14) | data formatting | bytes 3145728 | tf_op jit(solution)/shard_map/reshape | solution.py:44
  161.0 1.6 copy-done
  162.6 1.2 slice.17
  163.8 2.9 copy.34
  166.8 73.1 %all-to-all-done.1 = bf16[16,22,3584]{2,1,0:T(8,128)(2,1)S(1)} async-done(((bf16[16,22,3584]{2,1,0:T(8,128)(2,1)}), bf16[16,22,3584]{2,1,0:T(8,128)(2,1)S(1)}, u32[]{:S(2)}, u32[]{:S(2)}) %all-to-all-start.1) | async-done | bytes 2523168 | tf_op jit(solution)/shard_map/all_to_all | solution.py:114
  239.9 2.1 convert_reduce_fusion
  242.0 1.9 reshape.124
  243.9 2.5 gather_fusion.1
  246.3 2.7 reshape.125
  249.1 3.3 multiply_reduce_fusion
  252.3 5.2 %convert_bitcast_fusion = bf16[64,64,512]{2,0,1:T(8,128)(2,1)S(1)} fusion(bf16[64,128,512]{2,1,0:T(8,128)(2,1)} %all-gather.4.cloned.1.call-done, bf16[64,64,128]{2,1,0:T(8,128)(2,1)S(1)} %slice-done), kind=kOutput, calls=%fused_computation.37 | convolution fusion | flops 538968064 | bytes 13631488 | tf_op jit(solution)/shard_map/thi,hio->tho/dot_general | solution.py:18
  257.5 3.1 pad_maximum_fusion
  260.7 57.8 %conditional.1 = (f32[8,512]{1,0:T(8,128)}, f32[8,512,512]{2,1,0:T(8,128)}) conditional(s32[]{:T(128)} %convert_element_type.39, () %tuple.20, (bf16[64,64,576]{2,0,1:T(8,128)(2,1)}, s32[]{:T(128)}, s32[64,1]{0,1:T(1,128)S(1)}, bf16[1024,576]{1,0:T(8,128)(2,1)}) %tuple.21), branch_computations={%region_0.0_spmd, %region_1.6_spmd} | conditional | flops 1149502976 | bytes 24467924 | solution.py:86
  260.7 7.9 %copy.27 = bf16[64,64,576]{2,1,0:T(8,128)(2,1)} copy(bf16[64,64,576]{2,0,1:T(8,128)(2,1)} %get-tuple-element.84) | data formatting | bytes 9437184 | tf_op jit(solution)/shard_map
  268.9 49.6 %while.12 = (s32[]{:T(128)}, f32[8,512]{1,0:T(8,128)}, f32[8,512,512]{2,1,0:T(8,128)}, s32[8,512]{1,0:T(8,128)S(1)}, bf16[8,512,576]{2,1,0:T(8,128)(2,1)}, /*ind...) while((s32[]{:T(128)}, f32[8,512]{1,0:T(8,128)}, f32[8,512,512]{2,1,0:T(8,128)}, ...), condition=%wide.region_5.5_spmd.clone, body=%wide.region_2.4_spmd.clone.sunk | while | flops 1149502976 | bytes 10261597 | solution.py:82
  268.9 2.3 fusion.66
  271.2 0.8 fusion.67
  271.9 1.9 fusion.68
  273.8 1.3 dynamic_update_slice.14
  275.2 2.3 fusion.66
  277.5 0.8 fusion.67
  278.2 1.8 fusion.68
  280.0 1.3 dynamic_update_slice.14
  281.4 2.3 fusion.66
  283.6 0.8 fusion.67
  284.4 1.8 fusion.68
  286.2 1.3 dynamic_update_slice.14
  287.5 2.3 fusion.66
  289.8 0.8 fusion.67
  290.6 1.8 fusion.68
  292.4 1.3 dynamic_update_slice.14
  293.7 2.3 fusion.66
  296.0 0.8 fusion.67
  296.8 1.8 fusion.68
  298.6 1.3 dynamic_update_slice.14
  300.0 2.3 fusion.66
  302.2 0.8 fusion.67
  303.0 1.8 fusion.68
  304.8 1.3 dynamic_update_slice.14
  306.1 2.3 fusion.66
  308.4 0.8 fusion.67
  309.2 1.8 fusion.68
  311.0 1.3 dynamic_update_slice.14
  312.3 2.3 fusion.66
  314.6 0.8 fusion.67
  315.4 1.8 fusion.68
  317.2 1.3 dynamic_update_slice.14
  318.5 5.2 %divide_convert_fusion = bf16[8,512,512]{2,1,0:T(8,128)(2,1)} fusion(f32[8,512,512]{2,1,0:T(8,128)} %get-tuple-element.60, f32[8,512]{1,0:T(8,128)} %get-tuple-element.61), kind=kLoop, calls=%fused_computation.31 | loop fusion | flops 4194304 | bytes 12599296 | tf_op jit(solution)/shard_map/convert_element_type | solution.py:90
  323.7 9.6 %fusion.34 = bf16[64,8,8,128]{3,2,1,0:T(8,128)(2,1)S(1)} fusion(bf16[64,512,128]{2,1,0:T(8,128)(2,1)} %all-gather.8.cloned.1.call-done, bf16[64,64,512]{2,1,0:T(8,128)(2,1)} %bitcast.61), kind=kOutput, calls=%fused_computation.45 | convolution fusion | flops 537395200 | bytes 13631488 | tf_op jit(solution)/shard_map/thi,hio->tho/dot_general | solution.py:18
  333.3 1.2 copy.45
  (62 shorter events, 2.1 us)
Async XLA Ops:
  7.2 245.1 %all-gather.4.cloned.1.call-start = ((), (), s32[]{:S(2)}) async-start(), calls=%async_computation.2 | async-start | bytes 8912896 | tf_op jit(solution)/shard_map/all_gather | solution.py:21
  7.9 252.8 %all-gather.6.cloned.1.call-start = ((), (), s32[]{:S(2)}) async-start(), calls=%async_computation.3 | async-start | bytes 1392640 | tf_op jit(solution)/shard_map/all_gather | solution.py:59
  8.6 315.1 %all-gather.8.cloned.1.call-start = ((), (), s32[]{:S(2)}) async-start(), calls=%async_computation.4 | async-start | bytes 8912896 | tf_op jit(solution)/shard_map/all_gather | solution.py:21
  134.6 4.4 %copy-start.2 = (bf16[352,3584]{1,0:T(8,128)(2,1)S(1)}, bf16[352,3584]{1,0:T(8,128)(2,1)}, u32[]{:S(2)}) copy-start(bf16[352,3584]{1,0:T(8,128)(2,1)} %reshape.122) | copy-start | bytes 7569412
  150.9 89.0 %all-to-all-start.1 = ((bf16[16,22,3584]{2,1,0:T(8,128)(2,1)}), bf16[16,22,3584]{2,1,0:T(8,128)(2,1)S(1)}, u32[]{:S(2)}, u32[]{:S(2)}) async-start(bf16[16,22,3584]{2,1,0:T(8,128)(2,1)} %reshape.123), calls=%async_computation.1 | async-start | bytes 5505024 | tf_op jit(solution)/shard_map/all_to_all | solution.py:114
  160.9 1.6 copy-start
  160.9 2.8 copy-start.3
  246.3 6.0 %slice-start = ((bf16[64,64,192]{2,1,0:T(8,128)(2,1)}), bf16[64,64,128]{2,1,0:T(8,128)(2,1)S(1)}, s32[]{:S(2)}) async-start(bf16[64,64,192]{2,1,0:T(8,128)(2,1)} %reshape.117), calls=%async_computation.5 | async-start | bytes 2097152 | tf_op jit(solution)/shard_map/slice | solution.py:45
  252.3 5.2 %copy-start.1 = (bf16[64,64,64]{2,0,1:T(8,128)(2,1)S(1)}, bf16[64,64,64]{2,0,1:T(8,128)(2,1)}, u32[]{:S(2)}) copy-start(bf16[64,64,64]{2,0,1:T(8,128)(2,1)} %copy.34) | copy-start | bytes 1572868
  260.7 8.2 %copy-start.4 = (bf16[1024,576]{1,0:T(8,128)(2,1)S(1)}, bf16[1024,576]{1,0:T(8,128)(2,1)}, u32[]{:S(2)}) copy-start(bf16[1024,576]{1,0:T(8,128)(2,1)} %get-tuple-element.154) | copy-start | bytes 3538948 | tf_op jit(solution)/shard_map/cond
Sparse Core Ops, SparseCore 0:
  10.2 117.4 all-gather.3
  129.9 56.3 all-gather.5
  188.4 89.9 all-gather.7
where the time goes:
time: 342 us; the launch traced here: 341 us
  blocking collectives  117 us (34%)
  waiting for transfers between devices  75.2 us (22%)
  matrix products  59.4 us (17%)
  local copies, waits for them, and re-layouts  49.3 us (14%)
  other arithmetic  21 us (6%)
  between operations  13.9 us (4%)
  starting transfers between devices  5.53 us (2%)
    all_to_all x1, blocking collectives, on_device(): lax.all_to_all(outgoing, 'ctx', split_axis=0, concat_axis=0, tiled=True)  117 us
    all_to_all x1, waiting for transfers between devices, on_device(): lax.all_to_all(result.reshape(sources, items, D), 'ctx', split_axis=0, co...  73.1 us
    dot_general x8, matrix products, per_block(): jnp.dot(query_rows, shard_keys.T, preferred_element_type=jnp.float32)  18.2 us
    dot_general x2, matrix products, project_heads(): jnp.einsum('thi,hio->tho', row_data, lax.all_gather(weight, 'ctx', axis=0...  14.8 us
    dot_general x8, matrix products, per_block(): jnp.dot(weights.astype(jnp.bfloat16), shard_keys[:, :LATENT], preferred_e...  14.4 us
    dynamic_update_slice x8, local copies, waits for them, and re-layouts, compute(): lax.map(per_block, (query_blocks, query_pos, carried_in[0], carried_in[1]...  10.7 us
    another operation x1, local copies, waits for them, and re-layouts  7.95 us
    dot_general x1, matrix products, on_device(): jnp.dot(hidden, expert_down[0], preferred_element_type=jnp.float32)  7.57 us
  transfers between devices with their start and end apart: 4, of which 1 were waited for; matrix products, arithmetic and copies ran while one was open for 34% of the time, Pallas kernels for 0%

commit v1 on v0

v1 whole, which is shorter than its diff:
```python
import functools
import math

import jax
import jax.numpy as jnp
from jax import lax
from jax.experimental import pallas as pl
from jax.experimental.pallas import tpu as pltpu
from jax.sharding import PartitionSpec as P

D = 3584
HEADS = 64
NOPE = 128
ROPE = 64
LATENT = 512
VDIM = 128
TOP = 2
HALF = 512
HALF_D = D // 2
VMEM_LIMIT = 50 * 1024 * 1024
F32 = jnp.float32
BF16 = jnp.bfloat16


def params(limit=VMEM_LIMIT):
    return pltpu.CompilerParams(vmem_limit_bytes=limit)


def slot_targets(routes, experts, rows):
    tok = routes.shape[0]
    lane = lax.broadcasted_iota(jnp.int32, (tok, 128), 1)
    first = routes[:, 0:1]
    second = routes[:, 1:2]
    hot0 = jnp.where(lane == first, 1.0, 0.0)
    hot1 = jnp.where(lane == second, 1.0, 0.0)
    earlier = jnp.where(
        lax.broadcasted_iota(jnp.int32, (tok, tok), 1) < lax.broadcasted_iota(jnp.int32, (tok, tok), 0),
        1.0,
        0.0,
    )
    counts = jnp.dot(earlier.astype(BF16), (hot0 + hot1).astype(BF16), preferred_element_type=F32)
    slot0 = jnp.sum(counts * hot0, axis=1, keepdims=True).astype(jnp.int32)
    slot1 = jnp.sum(counts * hot1, axis=1, keepdims=True).astype(jnp.int32)
    return first * rows + slot0, second * rows + slot1


def bucket_kernel(experts, rows, routes_ref, x_ref, out_ref):
    tok = x_ref.shape[0]
    target0, target1 = slot_targets(routes_ref[...], experts, rows)
    column = lax.broadcasted_iota(jnp.int32, (tok, experts * rows), 1)
    chosen = jnp.where((column == target0) | (column == target1), 1.0, 0.0).astype(BF16)
    for half in range(2):
        picked = lax.dot_general(
            chosen,
            x_ref[:, half * HALF_D : (half + 1) * HALF_D],
            (((0,), (0,)), ((), ())),
            preferred_element_type=F32,
        ).astype(BF16)
        for expert in range(experts):
            out_ref[2 * expert + half] = picked[expert * rows : (expert + 1) * rows]


def build_buckets(routes, moe_input, experts, rows):
    return pl.pallas_call(
        functools.partial(bucket_kernel, experts, rows),
        out_shape=jax.ShapeDtypeStruct((2 * experts, rows, HALF_D), BF16),
        compiler_params=params(),
        name="bucket_rows",
    )(routes, moe_input)


def combine_kernel(experts, rows, routes_ref, gates_ref, back_ref, out_ref):
    tok = routes_ref.shape[0]
    target0, target1 = slot_targets(routes_ref[...], experts, rows)
    targets = jnp.concatenate([target0, target1], axis=0)
    for half in range(2):
        total = jnp.zeros((2 * tok, HALF_D), F32)
        for expert in range(experts):
            column = lax.broadcasted_iota(jnp.int32, (2 * tok, rows), 1) + expert * rows
            chosen = jnp.where(column == targets, 1.0, 0.0).astype(BF16)
            total = total + jnp.dot(chosen, back_ref[2 * expert + half], preferred_element_type=F32)
        out_ref[:, half * HALF_D : (half + 1) * HALF_D] = (
            total[:tok] * gates_ref[:, 0:1] + total[tok:] * gates_ref[:, 1:2]
        ).astype(BF16)


def combine(routes, gates, back, experts, rows):
    return pl.pallas_call(
        functools.partial(combine_kernel, experts, rows),
        out_shape=jax.ShapeDtypeStruct((routes.shape[0], D), BF16),
        compiler_params=params(),
        name="combine_routes",
    )(routes, gates, back)


STEP = 896
STEPS = HALF_D // STEP


def first_half_kernel(core_ref, x_ref, gate_ref, up_ref, gate_sum, up_sum):
    step = pl.program_id(0)
    gate = jnp.dot(x_ref[...], gate_ref[0], preferred_element_type=F32)
    up = jnp.dot(x_ref[...], up_ref[0], preferred_element_type=F32)

    @pl.when(step == 0)
    def _():
        gate_sum[...] = gate
        up_sum[...] = up

    @pl.when(step > 0)
    def _():
        gate_sum[...] += gate
        up_sum[...] += up


def first_half(core, x, gate, up):
    count = x.shape[0]
    weights = pl.BlockSpec((1, STEP, HALF), lambda k, core: (0, core[0] * STEPS + k, 0))
    sums = pl.BlockSpec((count, HALF), lambda k, core: (0, 0))
    return pl.pallas_call(
        first_half_kernel,
        grid_spec=pltpu.PrefetchScalarGridSpec(
            num_scalar_prefetch=1,
            grid=(STEPS,),
            in_specs=[pl.BlockSpec((count, STEP), lambda k, core: (0, k)), weights, weights],
            out_specs=[sums, sums],
        ),
        out_shape=[jax.ShapeDtypeStruct((count, HALF), F32)] * 2,
        compiler_params=params(),
        cost_estimate=pl.CostEstimate(
            flops=4 * count * HALF_D * HALF, bytes_accessed=4 * HALF_D * HALF + 2 * count * HALF_D, transcendentals=0
        ),
        name="hidden_own_columns",
    )(core, x, gate, up)


def second_half_kernel(core_ref, x_ref, gate_ref, up_ref, gate_in, up_in, down_ref, hidden_ref, out_ref, gate_sum, up_sum):
    step = pl.program_id(0)
    gate = jnp.dot(x_ref[...], gate_ref[0], preferred_element_type=F32)
    up = jnp.dot(x_ref[...], up_ref[0], preferred_element_type=F32)

    @pl.when(step == 0)
    def _():
        gate_sum[...] = gate_in[...] + gate
        up_sum[...] = up_in[...] + up

    @pl.when(step > 0)
    def _():
        gate_sum[...] += gate
        up_sum[...] += up

    @pl.when(step == STEPS - 1)
    def _():
        value = gate_sum[...]
        hidden = (value / (1.0 + jnp.exp(-value)) * up_sum[...]).astype(BF16)
        hidden_ref[...] = hidden
        out_ref[...] = jnp.dot(hidden, down_ref[0], preferred_element_type=F32).astype(BF16)


def second_half(core, x, gate, up, gate_sum, up_sum, down):
    count = x.shape[0]
    weights = pl.BlockSpec((1, STEP, HALF), lambda k, core: (0, (1 - core[0]) * STEPS + k, 0))
    sums = pl.BlockSpec((count, HALF), lambda k, core: (0, 0))
    return pl.pallas_call(
        second_half_kernel,
        grid_spec=pltpu.PrefetchScalarGridSpec(
            num_scalar_prefetch=1,
            grid=(STEPS,),
            in_specs=[
                pl.BlockSpec((count, STEP), lambda k, core: (0, k)),
                weights,
                weights,
                sums,
                sums,
                pl.BlockSpec((1, HALF, HALF_D), lambda k, core: (0, 0, 1 - core[0])),
            ],
            out_specs=[sums, pl.BlockSpec((count, HALF_D), lambda k, core: (0, 0))],
            scratch_shapes=[pltpu.VMEM((count, HALF), F32)] * 2,
        ),
        out_shape=[jax.ShapeDtypeStruct((count, HALF), BF16), jax.ShapeDtypeStruct((count, HALF_D), BF16)],
        compiler_params=params(),
        cost_estimate=pl.CostEstimate(
            flops=6 * count * HALF_D * HALF, bytes_accessed=6 * HALF_D * HALF + 4 * count * HALF_D, transcendentals=count * HALF
        ),
        name="hidden_other_columns",
    )(core, x, gate, up, gate_sum, up_sum, down)


def down_kernel(core_ref, hidden_ref, down_ref, other_ref, out_ref):
    own = jnp.dot(hidden_ref[...], down_ref[0], preferred_element_type=F32).astype(BF16)
    out_ref[...] = (own.astype(F32) + other_ref[...].astype(F32)).astype(BF16)


def down_own(core, hidden, down, other):
    count = hidden.shape[0]
    whole = pl.BlockSpec((count, HALF_D), lambda k, core: (0, 0))
    return pl.pallas_call(
        down_kernel,
        grid_spec=pltpu.PrefetchScalarGridSpec(
            num_scalar_prefetch=1,
            grid=(1,),
            in_specs=[
                pl.BlockSpec((count, HALF), lambda k, core: (0, 0)),
                pl.BlockSpec((1, HALF, HALF_D), lambda k, core: (0, 0, core[0])),
                whole,
            ],
            out_specs=whole,
        ),
        out_shape=jax.ShapeDtypeStruct((count, HALF_D), BF16),
        compiler_params=params(),
        cost_estimate=pl.CostEstimate(
            flops=2 * count * HALF_D * HALF, bytes_accessed=2 * HALF_D * HALF + 4 * count * HALF_D, transcendentals=0
        ),
        name="down_own_columns",
    )(core, hidden, down, other)


def split_kernel(per_device, x_ref, out_ref):
    pieces = [x_ref[:, head * (NOPE + ROPE) : head * (NOPE + ROPE) + NOPE] for head in range(per_device)]
    pieces += [x_ref[:, head * (NOPE + ROPE) + NOPE : (head + 1) * (NOPE + ROPE)] for head in range(per_device)]
    out_ref[0] = jnp.concatenate(pieces, axis=1)


def split_queries(queries, shards):
    tok = queries.shape[0]
    width = queries.shape[1] // shards
    return pl.pallas_call(
        functools.partial(split_kernel, HEADS // shards),
        grid=(shards,),
        in_specs=[pl.BlockSpec((tok, width), lambda d: (0, d))],
        out_specs=pl.BlockSpec((1, tok, width), lambda d: (d, 0, 0)),
        out_shape=jax.ShapeDtypeStruct((shards, tok, width), BF16),
        compiler_params=params(),
        name="split_queries",
    )(queries)


BLOCK = 256
EXP_SCALE = math.log2(math.e) / math.sqrt(NOPE + ROPE)


def attention_kernel(nope_ref, rope_ref, kv_ref, key_ref, value_ref, out_ref, keys):
    head = pl.program_id(0)

    @pl.when(head == 0)
    def _():
        keys[:, : LATENT + ROPE] = kv_ref[...]
        keys[:, LATENT + ROPE :] = kv_ref[:, LATENT:]

    side = lax.broadcasted_iota(jnp.int32, (1, 2 * ROPE), 1) // ROPE == head % 2
    below = lax.broadcasted_iota(jnp.int32, (BLOCK, BLOCK), 1) <= lax.broadcasted_iota(
        jnp.int32, (BLOCK, BLOCK), 0
    )
    contract = (((1,), (1,)), ((), ()))
    for block in range(nope_ref.shape[0] // BLOCK):
        start = block * BLOCK
        rows = pl.ds(start, BLOCK)
        latent = jnp.dot(nope_ref[rows, :], key_ref[0], preferred_element_type=F32).astype(BF16)
        rope = jnp.where(side, rope_ref[rows, :], jnp.zeros((), BF16))
        query = jnp.concatenate([latent, rope], axis=1)
        diagonal = lax.dot_general(query, keys[rows, :], contract, preferred_element_type=F32)
        diagonal = jnp.where(below, diagonal, -1e30)
        top = jnp.max(diagonal, axis=1, keepdims=True)
        if block:
            past = lax.dot_general(query, keys[:start, :], contract, preferred_element_type=F32)
            top = jnp.maximum(top, jnp.max(past, axis=1, keepdims=True))
        weights = jnp.exp2((diagonal - top) * EXP_SCALE)
        total = jnp.sum(weights, axis=1, keepdims=True)
        mixed = jnp.dot(weights.astype(BF16), keys[rows, :LATENT], preferred_element_type=F32)
        if block:
            weights = jnp.exp2((past - top) * EXP_SCALE)
            total = total + jnp.sum(weights, axis=1, keepdims=True)
            mixed = mixed + jnp.dot(weights.astype(BF16), keys[:start, :LATENT], preferred_element_type=F32)
        mixed = (mixed / total).astype(BF16)
        out_ref[rows, :] = jnp.dot(mixed, value_ref[0], preferred_element_type=F32).astype(BF16)


def attention(queries, keys, key_proj, value_proj):
    length = queries.shape[0]
    heads = key_proj.shape[0]
    return pl.pallas_call(
        attention_kernel,
        grid=(heads,),
        in_specs=[
            pl.BlockSpec((length, NOPE), lambda h: (0, h)),
            pl.BlockSpec((length, 2 * ROPE), lambda h: (0, heads + h // 2)),
            pl.BlockSpec((length, LATENT + ROPE), lambda h: (0, 0)),
            pl.BlockSpec((1, NOPE, LATENT), lambda h: (h, 0, 0)),
            pl.BlockSpec((1, LATENT, VDIM), lambda h: (h, 0, 0)),
        ],
        out_specs=pl.BlockSpec((length, VDIM), lambda h: (0, h)),
        out_shape=jax.ShapeDtypeStruct((length, heads * VDIM), BF16),
        scratch_shapes=[pltpu.VMEM((length, LATENT + 2 * ROPE), BF16)],
        compiler_params=params(),
        cost_estimate=pl.CostEstimate(
            flops=2 * heads * length * length * (LATENT + ROPE),
            bytes_accessed=8 * length * LATENT,
            transcendentals=heads * length * length // 2,
        ),
        name="causal_attention",
    )(queries, queries, keys, key_proj, value_proj)


def on_device(
    queries,
    latent_kv,
    key_proj,
    value_proj,
    moe_input,
    routes,
    gates,
    expert_gate,
    expert_up,
    expert_down,
):
    shards = lax.axis_size("ctx")
    tok = queries.shape[0]
    experts = shards // 2
    capacity = 2 * ((4 * tok * TOP + 6 * experts - 1) // (6 * experts))
    rows = -(-capacity // 8) * 8
    core = (lax.axis_index("ctx") % 2).astype(jnp.int32).reshape(1)
    swap = [(i, i ^ 1) for i in range(shards)]

    keys = lax.all_gather(latent_kv, "ctx", axis=0, tiled=True)

    buckets = build_buckets(routes, moe_input, experts, rows)
    arrived = lax.all_to_all(buckets, "ctx", split_axis=0, concat_axis=0, tiled=True)
    own = arrived.reshape(shards * rows, HALF_D)
    other = lax.ppermute(own, "ctx", swap)

    sent = split_queries(queries, shards)
    held = lax.all_to_all(sent, "ctx", split_axis=0, concat_axis=0, tiled=True)

    gate_sum, up_sum = first_half(core, own, expert_gate, expert_up)
    hidden, for_other = second_half(core, other, expert_gate, expert_up, gate_sum, up_sum, expert_down)
    from_other = lax.ppermute(for_other, "ctx", swap)
    result = down_own(core, hidden, expert_down, from_other).reshape(shards, rows, HALF_D)
    back = lax.all_to_all(result, "ctx", split_axis=0, concat_axis=0, tiled=True)

    held = held.reshape(shards * tok, held.shape[2])
    values = attention(held, keys, key_proj, value_proj)
    values = lax.all_to_all(
        values.reshape(shards, tok, values.shape[1]), "ctx", split_axis=0, concat_axis=0, tiled=True
    )
    attention_out = values.transpose(1, 0, 2).reshape(tok, HEADS * VDIM)

    moe_out = combine(routes, gates, back, experts, rows)
    return (attention_out, moe_out)


def solution(mesh):
    return jax.shard_map(
        on_device,
        mesh=mesh,
        in_specs=(
            P(("groups", "ctx"), None),
            P(("groups", "ctx"), None),
            P("ctx", None, None),
            P("ctx", None, None),
            P(("groups", "ctx"), None),
            P(("groups", "ctx"), None),
            P(("groups", "ctx"), None),
            P("ctx", None, None),
            P("ctx", None, None),
            P("ctx", None, None),
        ),
        out_specs=(P(("groups", "ctx"), None), P(("groups", "ctx"), None)),
        check_vma=False,
    )
```

time: 342 us -> 202 us (0.59)
  the two profiles are of different devices: /device:TPU:15 before, /device:TPU:0 now
where the time goes in v1:
time: 202 us; the launch traced here: 199 us
  waiting for transfers between devices  111 us (55%)
  Pallas kernels  42.5 us (21%)
  starting transfers between devices  27.4 us (14%)
  between operations  14.1 us (7%)
  local copies, waits for them, and re-layouts  4.28 us (2%)
    all_gather x1, waiting for transfers between devices, on_device(): keys = lax.all_gather(latent_kv, 'ctx', axis=0, tiled=True)  50.9 us
    all_to_all x1, waiting for transfers between devices, on_device(): lax.all_to_all(result, 'ctx', split_axis=0, concat_axis=0, tiled=True)  27.4 us
    all_to_all x1, waiting for transfers between devices, on_device(): lax.all_to_all(buckets, 'ctx', split_axis=0, concat_axis=0, tiled=True)  22.6 us
    pallas_call x1, Pallas kernels, attention(): pl.pallas_call(attention_kernel, grid=(heads,), in_specs=[pl.BlockSpec((l...  18.1 us
    all_to_all x1, starting transfers between devices, on_device(): held = lax.all_to_all(sent, 'ctx', split_axis=0, concat_axis=0, tiled=True)  8.32 us
    all_to_all x1, starting transfers between devices, on_device(): lax.all_to_all(buckets, 'ctx', split_axis=0, concat_axis=0, tiled=True)  7.51 us
    all_to_all x1, starting transfers between devices, on_device(): lax.all_to_all(result, 'ctx', split_axis=0, concat_axis=0, tiled=True)  7 us
    all_to_all x1, waiting for transfers between devices, on_device(): lax.all_to_all(values.reshape(shards, tok, values.shape[1]), 'ctx', split...  6.5 us
  transfers between devices with their start and end apart: 7, of which 5 were waited for; matrix products, arithmetic and copies ran while one was open for 1% of the time, Pallas kernels for 19%

profile of v1, /device:TPU:0, one launch (start us, length us, event | category | flops | bytes accessed | tf_op | source)
XLA Modules:
  0.0 199.1 jit_solution(17312514625425412435)
XLA Ops:
  7.2 0.8 copy.14.routes_ref
  7.9 0.0 copy-start.1
  7.9 1.0 copy-done.1
  9.0 2.0 %bucket_rows.1 = bf16[16,24,1792]{2,1,0:T(8,128)(2,1)} custom-call(s32[64,2]{1,0:T(8,128)S(1)} %copy.14.routes_ref, bf16[64,3584]{1,0:T(8,128)(2,1)S(1)} %copy-done.1), custom_call_target="tpu_custom_call" | custom-call | tf_op jit(solution)/shard_map/bucket_rows/pallas_call | solution.py:64
  11.0 0.0 copy-start
  11.0 7.5 %all-to-all-start.2 = ((bf16[16,24,1792]{2,1,0:T(8,128)(2,1)}), bf16[16,24,1792]{2,1,0:T(8,128)(2,1)S(1)}, u32[]{:S(2)}, u32[]{:S(2)}) async-start(bf16[16,24,1792]{2,1,0:T(8,128)(2,1)} %bucket_rows.1), calls=%async_computation.2 | async-start | bytes 2752512 | tf_op jit(solution)/shard_map/all_to_all | solution.py:327
  18.5 0.0 copy-done
  18.5 6.0 %split_queries.1 = bf16[16,64,768]{2,1,0:T(8,128)(2,1)} custom-call(bf16[64,12288]{1,0:T(8,128)(2,1)S(1)} %copy-done), custom_call_target="tpu_custom_call" | custom-call | tf_op jit(solution)/shard_map/split_queries/pallas_call | solution.py:227
  24.5 0.0 copy-start.3
  24.5 0.0 copy-start.4
  24.5 22.6 %all-to-all-done.2 = bf16[16,24,1792]{2,1,0:T(8,128)(2,1)S(1)} async-done(((bf16[16,24,1792]{2,1,0:T(8,128)(2,1)}), bf16[16,24,1792]{2,1,0:T(8,128)(2,1)S(1)}, u32[]{:S(2)}, u32[]{:S(2)}) %all-to-all-start.2) | async-done | bytes 1376288 | tf_op jit(solution)/shard_map/all_to_all | solution.py:327
  47.0 8.3 %all-to-all-start = ((bf16[16,64,768]{2,1,0:T(8,128)(2,1)}), bf16[16,64,768]{2,1,0:T(8,128)(2,1)}, u32[]{:S(2)}, u32[]{:S(2)}) async-start(bf16[16,64,768]{2,1,0:T(8,128)(2,1)} %split_queries.1), calls=%async_computation | async-start | bytes 3145728 | tf_op jit(solution)/shard_map/all_to_all | solution.py:332
  55.4 0.0 all-gather.2.cloned.1.call-start
  55.4 0.7 all-gather.2.cloned.1.call-update
  56.1 0.4 collective-permute-start
  56.5 50.9 %all-gather.2.cloned.1.call-done.kv_ref = bf16[1024,576]{1,0:T(8,128)(2,1)} async-done(((bf16[64,576]{1,0:T(8,128)(2,1)}), bf16[1024,576]{1,0:T(8,128)(2,1)}) %all-gather.2.cloned.1.call-update) | async-done | bytes 1179664 | tf_op jit(solution)/shard_map/all_gather | solution.py:324
  107.4 0.0 all-to-all-done
  107.4 0.0 copy-done.3
  107.4 0.0 copy-done.4
  107.4 0.0 copy-start.2
  107.4 1.3 copy-done.2
  108.7 18.1 %causal_attention.1 = bf16[1024,512]{1,0:T(8,128)(2,1)} custom-call(bf16[1024,768]{1,0:T(8,128)(2,1)} %bitcast.nope_ref.rope_ref, bf16[1024,768]{1,0:T(8,128)(2,1)} %bitcast.nope_ref.rope_ref, bf16[1024,576]{1,0:T(8,128)(2,1)S(1)} %copy-done.2, bf16[4,128,512]{2,1,0:T(8,128)(2,1)S(1)} %copy-done.3, bf16[4,512,128]{2,1,0:T(8,128)(2,1)S(1)} %copy-done.4), custom_call_target="tpu_custom_call" | custom-call | flops 4831838208 | bytes 4194304 | tf_op jit(solution)/shard_map/causal_attention/pallas_call | solution.py:281
  126.9 3.7 %all-to-all-start.1 = ((bf16[16,64,512]{2,1,0:T(8,128)(2,1)}), bf16[16,64,512]{2,1,0:T(8,128)(2,1)S(1)}, u32[]{:S(2)}, u32[]{:S(2)}) async-start(bf16[16,64,512]{2,1,0:T(8,128)(2,1)} %bitcast.1), calls=%async_computation.1 | async-start | bytes 2097152 | tf_op jit(solution)/shard_map/all_to_all | solution.py:342
  130.5 3.8 %hidden_own_columns.1 = (f32[384,512]{1,0:T(8,128)S(1)}, f32[384,512]{1,0:T(8,128)S(1)}) custom-call(s32[1]{0:T(128)} %bitcast.3.core_ref, bf16[384,1792]{1,0:T(8,128)(2,1)S(1)} %bitcast.9, bf16[1,3584,512]{2,1,0:T(8,128)(2,1)} %gate_ref.3, bf16[1,3584,512]{2,1,0:T(8,128)(2,1)} %up_ref.3), custom_call_target="tpu_custom_call" | custom-call | flops 1409286144 | bytes 5046272 | tf_op jit(solution)/shard_map/hidden_own_columns/pallas_call | solution.py:120
  134.3 0.0 collective-permute-done.x_ref
  134.3 5.9 %hidden_other_columns.1 = (bf16[384,512]{1,0:T(8,128)(2,1)S(1)}, bf16[384,1792]{1,0:T(8,128)(2,1)S(1)}) custom-call(s32[1]{0:T(128)} %bitcast.3.core_ref, bf16[384,1792]{1,0:T(8,128)(2,1)} %collective-permute-done.x_ref, bf16[1,3584,512]{2,1,0:T(8,128)(2,1)} %gate_ref.3, bf16[1,3584,512]{2,1,0:T(8,128)(2,1)} %up_ref.3, ...), custom_call_target="tpu_custom_call" | custom-call | flops 2113929216 | bytes 8257536 | tf_op jit(solution)/shard_map/hidden_other_columns/pallas_call | solution.py:164
  140.3 0.4 collective-permute-start.1
  140.7 2.8 %collective-permute-done.1.other_ref = bf16[384,1792]{1,0:T(8,128)(2,1)S(1)} collective-permute-done((bf16[384,1792]{1,0:T(8,128)(2,1)S(1)}, bf16[384,1792]{1,0:T(8,128)(2,1)S(1)}, u32[]{:S(2)}, u32[]{:S(2)}) %collective-permute-start.1) | collective-permute-done | bytes 1376288 | tf_op jit(solution)/shard_map/ppermute | solution.py:336
  143.5 3.5 %down_own_columns.1 = bf16[384,1792]{1,0:T(8,128)(2,1)} custom-call(s32[1]{0:T(128)} %bitcast.3.core_ref, bf16[384,512]{1,0:T(8,128)(2,1)S(1)} %get-tuple-element.8.hidden_ref, bf16[1,512,3584]{2,1,0:T(8,128)(2,1)} %down_ref.3, bf16[384,1792]{1,0:T(8,128)(2,1)S(1)} %collective-permute-done.1.other_ref), custom_call_target="tpu_custom_call" | custom-call | flops 704643072 | bytes 4587520 | tf_op jit(solution)/shard_map/down_own_columns/pallas_call | solution.py:197
  147.0 6.5 %all-to-all-done.1 = bf16[16,64,512]{2,1,0:T(8,128)(2,1)S(1)} async-done(((bf16[16,64,512]{2,1,0:T(8,128)(2,1)}), bf16[16,64,512]{2,1,0:T(8,128)(2,1)S(1)}, u32[]{:S(2)}, u32[]{:S(2)}) %all-to-all-start.1) | async-done | bytes 1048608 | tf_op jit(solution)/shard_map/all_to_all | solution.py:342
  153.5 0.0 copy-start.5
  153.5 7.0 %all-to-all-start.3 = ((bf16[16,24,1792]{2,1,0:T(8,128)(2,1)}), bf16[16,24,1792]{2,1,0:T(8,128)(2,1)S(1)}, u32[]{:S(2)}, u32[]{:S(2)}) async-start(bf16[16,24,1792]{2,1,0:T(8,128)(2,1)} %bitcast.5), calls=%async_computation.3 | async-start | bytes 2752512 | tf_op jit(solution)/shard_map/all_to_all | solution.py:338
  160.5 0.0 copy-done.5
  160.5 0.1 copy.15.gates_ref
  160.6 1.1 copy.16
  161.6 27.4 %all-to-all-done.3.back_ref = bf16[16,24,1792]{2,1,0:T(8,128)(2,1)S(1)} async-done(((bf16[16,24,1792]{2,1,0:T(8,128)(2,1)}), bf16[16,24,1792]{2,1,0:T(8,128)(2,1)S(1)}, u32[]{:S(2)}, u32[]{:S(2)}) %all-to-all-start.3) | async-done | bytes 1376288 | tf_op jit(solution)/shard_map/all_to_all | solution.py:338
  189.0 3.2 %combine_routes.1 = bf16[64,3584]{1,0:T(8,128)(2,1)} custom-call(s32[64,2]{1,0:T(8,128)S(1)} %copy.14.routes_ref, f32[64,2]{1,0:T(8,128)S(1)} %copy.15.gates_ref, bf16[16,24,1792]{2,1,0:T(8,128)(2,1)S(1)} %all-to-all-done.3.back_ref), custom_call_target="tpu_custom_call" | custom-call | tf_op jit(solution)/shard_map/combine_routes/pallas_call | solution.py:88
Async XLA Ops:
  7.9 1.0 copy-start.1
  11.0 7.5 %copy-start = (bf16[64,12288]{1,0:T(8,128)(2,1)S(1)}, bf16[64,12288]{1,0:T(8,128)(2,1)}, u32[]{:S(2)}) copy-start(bf16[64,12288]{1,0:T(8,128)(2,1)} %x_ref.2) | copy-start | bytes 4718596
  11.0 36.1 %all-to-all-start.2 = ((bf16[16,24,1792]{2,1,0:T(8,128)(2,1)}), bf16[16,24,1792]{2,1,0:T(8,128)(2,1)S(1)}, u32[]{:S(2)}, u32[]{:S(2)}) async-start(bf16[16,24,1792]{2,1,0:T(8,128)(2,1)} %bucket_rows.1), calls=%async_computation.2 | async-start | bytes 2752512 | tf_op jit(solution)/shard_map/all_to_all | solution.py:327
  24.5 82.9 %copy-start.3 = (bf16[4,128,512]{2,1,0:T(8,128)(2,1)S(1)}, bf16[4,128,512]{2,1,0:T(8,128)(2,1)}, u32[]{:S(2)}) copy-start(bf16[4,128,512]{2,1,0:T(8,128)(2,1)} %key_ref.1) | copy-start | bytes 1572868
  24.5 82.9 %copy-start.4 = (bf16[4,512,128]{2,1,0:T(8,128)(2,1)S(1)}, bf16[4,512,128]{2,1,0:T(8,128)(2,1)}, u32[]{:S(2)}) copy-start(bf16[4,512,128]{2,1,0:T(8,128)(2,1)} %value_ref.1) | copy-start | bytes 1572868
  47.0 60.4 %all-to-all-start = ((bf16[16,64,768]{2,1,0:T(8,128)(2,1)}), bf16[16,64,768]{2,1,0:T(8,128)(2,1)}, u32[]{:S(2)}, u32[]{:S(2)}) async-start(bf16[16,64,768]{2,1,0:T(8,128)(2,1)} %split_queries.1), calls=%async_computation | async-start | bytes 3145728 | tf_op jit(solution)/shard_map/all_to_all | solution.py:332
  55.4 52.0 %all-gather.2.cloned.1.call-start = ((), (), s32[]{:S(2)}) async-start(), calls=%async_computation.4 | async-start | bytes 1392640 | tf_op jit(solution)/shard_map/all_gather | solution.py:324
  56.1 78.2 %collective-permute-start = (bf16[384,1792]{1,0:T(8,128)(2,1)S(1)}, bf16[384,1792]{1,0:T(8,128)(2,1)}, u32[]{:S(2)}, u32[]{:S(2)}) collective-permute-start(bf16[384,1792]{1,0:T(8,128)(2,1)S(1)} %bitcast.8), channel_id=1, source_target_pairs={{0,1},{1,0},{2,3},{3,2},{4,5},{5,4},{6,7},{7,6},{8,9},{9,8},{10,11... | collective-permute-start | bytes 4128776 | tf_op jit(solution)/shard_map/ppermute | solution.py:329
  107.4 1.3 copy-start.2
  126.9 26.6 %all-to-all-start.1 = ((bf16[16,64,512]{2,1,0:T(8,128)(2,1)}), bf16[16,64,512]{2,1,0:T(8,128)(2,1)S(1)}, u32[]{:S(2)}, u32[]{:S(2)}) async-start(bf16[16,64,512]{2,1,0:T(8,128)(2,1)} %bitcast.1), calls=%async_computation.1 | async-start | bytes 2097152 | tf_op jit(solution)/shard_map/all_to_all | solution.py:342
  140.3 3.2 %collective-permute-start.1 = (bf16[384,1792]{1,0:T(8,128)(2,1)S(1)}, bf16[384,1792]{1,0:T(8,128)(2,1)S(1)}, u32[]{:S(2)}, u32[]{:S(2)}) collective-permute-start(bf16[384,1792]{1,0:T(8,128)(2,1)S(1)} %get-tuple-element.9), channel_id=1, source_target_pairs={{0,1},{1,0},{2,3},{3,2},{4,5},{5,4},{6,7},{7,6},{8,9},{9,8},{10,11... | collective-permute-start | bytes 4128776 | tf_op jit(solution)/shard_map/ppermute | solution.py:336
  153.5 7.0 %copy-start.5 = (f32[64,2]{0,1:T(2,128)S(1)}, f32[64,2]{0,1:T(2,128)}, u32[]{:S(2)}) copy-start(f32[64,2]{0,1:T(2,128)} %param.16) | copy-start | bytes 1540
  153.5 35.6 %all-to-all-start.3 = ((bf16[16,24,1792]{2,1,0:T(8,128)(2,1)}), bf16[16,24,1792]{2,1,0:T(8,128)(2,1)S(1)}, u32[]{:S(2)}, u32[]{:S(2)}) async-start(bf16[16,24,1792]{2,1,0:T(8,128)(2,1)} %bitcast.5), calls=%async_computation.3 | async-start | bytes 2752512 | tf_op jit(solution)/shard_map/all_to_all | solution.py:338
Sparse Core Ops, SparseCore 0:
  58.5 48.8 all-gather.1

commit v2 on v1

--- a/solution.py
+++ b/solution.py
@@ -239,13 +239,16 @@
 EXP_SCALE = math.log2(math.e) / math.sqrt(NOPE + ROPE)
 
 
-def attention_kernel(nope_ref, rope_ref, kv_ref, key_ref, value_ref, out_ref, keys):
+def attention_kernel(rank_ref, nope_ref, rope_ref, kv_ref, key_ref, value_ref, out_ref, keys):
     head = pl.program_id(0)
+    shards, tok = kv_ref.shape[:2]
 
     @pl.when(head == 0)
     def _():
-        keys[:, : LATENT + ROPE] = kv_ref[...]
-        keys[:, LATENT + ROPE :] = kv_ref[:, LATENT:]
+        for place, offset in enumerate(doubling_masks(shards)[1]):
+            rows = pl.ds(pl.multiple_of((rank_ref[0] ^ offset) * tok, tok), tok)
+            keys[rows, : LATENT + ROPE] = kv_ref[place]
+            keys[rows, LATENT + ROPE :] = kv_ref[place, :, LATENT:]
 
     side = lax.broadcasted_iota(jnp.int32, (1, 2 * ROPE), 1) // ROPE == head % 2
     below = lax.broadcasted_iota(jnp.int32, (BLOCK, BLOCK), 1) <= lax.broadcasted_iota(
@@ -275,22 +278,25 @@
         out_ref[rows, :] = jnp.dot(mixed, value_ref[0], preferred_element_type=F32).astype(BF16)
 
 
-def attention(queries, keys, key_proj, value_proj):
+def attention(rank, queries, keys, key_proj, value_proj):
     length = queries.shape[0]
     heads = key_proj.shape[0]
     return pl.pallas_call(
         attention_kernel,
-        grid=(heads,),
-        in_specs=[
-            pl.BlockSpec((length, NOPE), lambda h: (0, h)),
-            pl.BlockSpec((length, 2 * ROPE), lambda h: (0, heads + h // 2)),
-            pl.BlockSpec((length, LATENT + ROPE), lambda h: (0, 0)),
-            pl.BlockSpec((1, NOPE, LATENT), lambda h: (h, 0, 0)),
-            pl.BlockSpec((1, LATENT, VDIM), lambda h: (h, 0, 0)),
-        ],
-        out_specs=pl.BlockSpec((length, VDIM), lambda h: (0, h)),
+        grid_spec=pltpu.PrefetchScalarGridSpec(
+            num_scalar_prefetch=1,
+            grid=(heads,),
+            in_specs=[
+                pl.BlockSpec((length, NOPE), lambda h, rank: (0, h)),
+                pl.BlockSpec((length, 2 * ROPE), lambda h, rank: (0, heads + h // 2)),
+                pl.BlockSpec(keys.shape, lambda h, rank: (0, 0, 0)),
+                pl.BlockSpec((1, NOPE, LATENT), lambda h, rank: (h, 0, 0)),
+                pl.BlockSpec((1, LATENT, VDIM), lambda h, rank: (h, 0, 0)),
+            ],
+            out_specs=pl.BlockSpec((length, VDIM), lambda h, rank: (0, h)),
+            scratch_shapes=[pltpu.VMEM((length, LATENT + 2 * ROPE), BF16)],
+        ),
         out_shape=jax.ShapeDtypeStruct((length, heads * VDIM), BF16),
-        scratch_shapes=[pltpu.VMEM((length, LATENT + 2 * ROPE), BF16)],
         compiler_params=params(),
         cost_estimate=pl.CostEstimate(
             flops=2 * heads * length * length * (LATENT + ROPE),
@@ -298,7 +304,20 @@
             transcendentals=heads * length * length // 2,
         ),
         name="causal_attention",
-    )(queries, queries, keys, key_proj, value_proj)
+    )(rank, queries, queries, keys, key_proj, value_proj)
+
+
+def exchange(blocks, mask):
+    met = lax.ppermute(blocks, "ctx", [(i, i ^ mask) for i in range(lax.axis_size("ctx"))])
+    return jnp.concatenate([blocks, met], axis=0)
+
+
+def doubling_masks(shards):
+    steps = [1 << bit for bit in reversed(range(shards.bit_length() - 1))]
+    order = [0]
+    for mask in steps:
+        order = order + [offset ^ mask for offset in order]
+    return steps, order
 
 
 def on_device(
@@ -318,10 +337,13 @@
     experts = shards // 2
     capacity = 2 * ((4 * tok * TOP + 6 * experts - 1) // (6 * experts))
     rows = -(-capacity // 8) * 8
-    core = (lax.axis_index("ctx") % 2).astype(jnp.int32).reshape(1)
+    rank = lax.axis_index("ctx").astype(jnp.int32).reshape(1)
+    core = rank % 2
     swap = [(i, i ^ 1) for i in range(shards)]
 
-    keys = lax.all_gather(latent_kv, "ctx", axis=0, tiled=True)
+    keys = latent_kv[None]
+    for mask in doubling_masks(shards)[0]:
+        keys = exchange(keys, mask)
 
     buckets = build_buckets(routes, moe_input, experts, rows)
     arrived = lax.all_to_all(buckets, "ctx", split_axis=0, concat_axis=0, tiled=True)
@@ -335,10 +357,11 @@
     hidden, for_other = second_half(core, other, expert_gate, expert_up, gate_sum, up_sum, expert_down)
     from_other = lax.ppermute(for_other, "ctx", swap)
     result = down_own(core, hidden, expert_down, from_other).reshape(shards, rows, HALF_D)
+
+    held = held.reshape(shards * tok, held.shape[2])
+    result, held = lax.optimization_barrier((result, held))
     back = lax.all_to_all(result, "ctx", split_axis=0, concat_axis=0, tiled=True)
-
-    held = held.reshape(shards * tok, held.shape[2])
-    values = attention(held, keys, key_proj, value_proj)
+    values = attention(rank, held, keys, key_proj, value_proj)
     values = lax.all_to_all(
         values.reshape(shards, tok, values.shape[1]), "ctx", split_axis=0, concat_axis=0, tiled=True
     )

time: 202 us -> 210 us (1.040)
  blocking collectives: 0 us -> 69 us
  waiting for transfers between devices: 111 us -> 76.4 us
  between operations: 14.1 us -> 0.83 us
  starting transfers between devices: 27.4 us -> 15 us
    all_to_all x0 -> x2, blocking collectives: none -> 69 us  [the longest x1 40 us: on_device(): lax.all_to_all(buckets, 'ctx', split_axis=0, concat_axis=0, tiled=True)]
    all_gather x1 -> x0, waiting for transfers between devices: 50.9 us -> none  [on_device(): keys = lax.all_gather(latent_kv, 'ctx', axis=0, tiled=True)]
    ppermute x0 -> x4, waiting for transfers between devices: none -> 49 us  [exchange(): lax.ppermute(blocks, 'ctx', [(i, i ^ mask) for i in range(lax.axis_size('...]
    all_to_all x2 -> x0, waiting for transfers between devices: 29.1 us -> none  [the longest x1 22.6 us: on_device(): lax.all_to_all(buckets, 'ctx', split_axis=0, concat_axis=0, tiled=True)]
    all_to_all x2 -> x0, starting transfers between devices: 11.2 us -> none  [the longest x1 7.51 us: on_device(): lax.all_to_all(buckets, 'ctx', split_axis=0, concat_axis=0, tiled=True)]
    ppermute x0 -> x4, starting transfers between devices: none -> 4.49 us  [exchange(): lax.ppermute(blocks, 'ctx', [(i, i ^ mask) for i in range(lax.axis_size('...]
    all_to_all x1, starting transfers between devices: 8.32 us -> 4.54 us  [on_device(): held = lax.all_to_all(sent, 'ctx', split_axis=0, concat_axis=0, tiled=True)]
    ppermute x1, waiting for transfers between devices: 2.76 us -> 0.01 us  [on_device(): from_other = lax.ppermute(for_other, 'ctx', swap)]
  transfers between devices with their start and end apart: 7 -> 8, of which waited for: 5 -> 4; matrix products, arithmetic and copies ran while one was open for 1% -> 1% of each run, Pallas kernels for 19% -> 9%
where the time goes in v2:
time: 210 us; the launch traced here: 207 us
  waiting for transfers between devices  76.4 us (36%)
  blocking collectives  69 us (33%)
  Pallas kernels  41 us (20%)
  starting transfers between devices  15 us (7%)
  local copies, waits for them, and re-layouts  4.25 us (2%)
    ppermute x4, waiting for transfers between devices, exchange(): lax.ppermute(blocks, 'ctx', [(i, i ^ mask) for i in range(lax.axis_size('...  49 us
    all_to_all x1, blocking collectives, on_device(): lax.all_to_all(buckets, 'ctx', split_axis=0, concat_axis=0, tiled=True)  40 us
    all_to_all x1, blocking collectives, on_device(): lax.all_to_all(values.reshape(shards, tok, values.shape[1]), 'ctx', split...  29 us
    all_to_all x1, waiting for transfers between devices, on_device(): lax.all_to_all(result, 'ctx', split_axis=0, concat_axis=0, tiled=True)  27.4 us
    pallas_call x1, Pallas kernels, attention(): pl.pallas_call(attention_kernel, grid_spec=pltpu.PrefetchScalarGridSpec(n...  17.6 us
    pallas_call x1, Pallas kernels, split_queries(): pl.pallas_call(functools.partial(split_kernel, HEADS // shards), grid=(sh...  5.96 us
    pallas_call x1, Pallas kernels, second_half(): pl.pallas_call(second_half_kernel, grid_spec=pltpu.PrefetchScalarGridSpec...  5.91 us
    all_to_all x1, starting transfers between devices, on_device(): lax.all_to_all(result, 'ctx', split_axis=0, concat_axis=0, tiled=True)  5.12 us
  transfers between devices with their start and end apart: 8, of which 4 were waited for; matrix products, arithmetic and copies ran while one was open for 1% of the time, Pallas kernels for 9%

profile of v2, /device:TPU:0, one launch (start us, length us, event | category | flops | bytes accessed | tf_op | source)
XLA Modules:
  0.0 206.6 jit_solution(11076404167549373525)
XLA Ops:
  0.6 0.8 copy.12.routes_ref
  1.4 0.0 copy-start.1
  1.4 1.0 copy-done.1
  2.4 0.9 bucket_rows.1
  3.3 0.0 copy-start
  3.4 40.0 %all_to_all.20 = bf16[16,24,1792]{2,1,0:T(8,128)(2,1)S(1)} all-to-all(bf16[16,24,1792]{2,1,0:T(8,128)(2,1)S(1)} %bucket_rows.1), channel_id=1, replica_groups=mesh['groups'=2,'ctx'=16] {'ctx'}, dimensions={0} | all-to-all | bytes 2752512 | tf_op jit(solution)/shard_map/all_to_all | solution.py:349
  43.3 0.8 collective-permute-start
  44.1 0.0 copy-done
  44.1 6.0 %split_queries.1 = bf16[16,64,768]{2,1,0:T(8,128)(2,1)} custom-call(bf16[64,12288]{1,0:T(8,128)(2,1)S(1)} %copy-done), custom_call_target="tpu_custom_call" | custom-call | tf_op jit(solution)/shard_map/split_queries/pallas_call | solution.py:227
  50.1 0.0 copy-start.5
  50.1 4.5 %all-to-all-start.1 = ((bf16[16,64,768]{2,1,0:T(8,128)(2,1)}), bf16[16,64,768]{2,1,0:T(8,128)(2,1)}, u32[]{:S(2)}, u32[]{:S(2)}) async-start(bf16[16,64,768]{2,1,0:T(8,128)(2,1)} %split_queries.1), calls=%async_computation.1 | async-start | bytes 3145728 | tf_op jit(solution)/shard_map/all_to_all | solution.py:354
  54.6 0.0 copy-done.5
  54.6 2.8 %collective-permute-start.2 = (bf16[1,64,576]{2,1,0:T(8,128)(2,1)S(1)}, bf16[1,64,576]{2,1,0:T(8,128)(2,1)S(1)}, u32[]{:S(2)}, u32[]{:S(2)}) collective-permute-start(bf16[1,64,576]{2,1,0:T(8,128)(2,1)S(1)} %bitcast.14), channel_id=1, source_target_pairs={{0,8},{1,9},{2,10},{3,11},{4,12},{5,13},{6,14},{7,15},{8,0},{9,1},... | collective-permute-start | bytes 221192 | tf_op jit(solution)/shard_map/ppermute | solution.py:311
  57.4 38.4 %collective-permute-done.2 = bf16[1,64,576]{2,1,0:T(8,128)(2,1)S(1)} collective-permute-done((bf16[1,64,576]{2,1,0:T(8,128)(2,1)S(1)}, bf16[1,64,576]{2,1,0:T(8,128)(2,1)S(1)}, u32[]{:S(2)}, u32[]{:S(2)}) %collective-permute-start.2) | collective-permute-done | bytes 73760 | tf_op jit(solution)/shard_map/ppermute | solution.py:311
  95.9 0.1 collective-permute-start.3
  95.9 3.8 %hidden_own_columns.1 = (f32[384,512]{1,0:T(8,128)S(1)}, f32[384,512]{1,0:T(8,128)S(1)}) custom-call(s32[1]{0:T(128)S(6)} %select_n.7.core_ref, bf16[384,1792]{1,0:T(8,128)(2,1)S(1)} %bitcast.11, bf16[1,3584,512]{2,1,0:T(8,128)(2,1)} %gate_ref.3, bf16[1,3584,512]{2,1,0:T(8,128)(2,1)} %up_ref.3), custom_call_target="tpu_custom_call" | custom-call | flops 1409286144 | bytes 5046272 | tf_op jit(solution)/shard_map/hidden_own_columns/pallas_call | solution.py:120
  99.7 0.0 collective-permute-done.x_ref
  99.7 0.0 copy-start.4
  99.7 1.1 copy-done.4
  100.8 5.9 %hidden_other_columns.1 = (bf16[384,512]{1,0:T(8,128)(2,1)S(1)}, bf16[384,1792]{1,0:T(8,128)(2,1)S(1)}) custom-call(s32[1]{0:T(128)S(6)} %select_n.7.core_ref, bf16[384,1792]{1,0:T(8,128)(2,1)} %copy-done.4, bf16[1,3584,512]{2,1,0:T(8,128)(2,1)} %gate_ref.3, bf16[1,3584,512]{2,1,0:T(8,128)(2,1)} %up_ref.3, f32[384,512]{1,0:T(8,128)S(1)} %get-tuple-element.8.gate_in, ...), custom_call_target="tpu_custom_call" | custom-call | flops 2113929216 | bytes 8257536 | tf_op jit(solution)/shard_map/hidden_other_columns/pallas_call | solution.py:164
  106.7 0.1 collective-permute-start.1
  106.8 0.0 collective-permute-done.3
  106.8 0.1 pad_maximum_fusion.1
  106.9 1.6 collective-permute-start.4
  108.5 8.6 %collective-permute-done.4 = bf16[4,64,576]{2,1,0:T(8,128)(2,1)S(1)} collective-permute-done((bf16[4,64,576]{2,1,0:T(8,128)(2,1)S(1)}, bf16[4,64,576]{2,1,0:T(8,128)(2,1)S(1)}, u32[]{:S(2)}, u32[]{:S(2)}) %collective-permute-start.4) | collective-permute-done | bytes 294944 | tf_op jit(solution)/shard_map/ppermute | solution.py:311
  117.1 0.1 pad_maximum_fusion
  117.2 0.1 collective-permute-start.5
  117.4 2.0 collective-permute-done.5
  119.3 0.1 constant_dynamic-update-slice_fusion.kv_ref
  119.4 0.0 collective-permute-done.1.other_ref
  119.5 0.0 copy-start.2
  119.5 0.0 copy-start.3
  119.5 3.6 %down_own_columns.1 = bf16[384,1792]{1,0:T(8,128)(2,1)} custom-call(s32[1]{0:T(128)S(6)} %select_n.7.core_ref, bf16[384,512]{1,0:T(8,128)(2,1)S(1)} %get-tuple-element.10.hidden_ref, bf16[1,512,3584]{2,1,0:T(8,128)(2,1)} %down_ref.3, bf16[384,1792]{1,0:T(8,128)(2,1)S(1)} %collective-permute-done.1.other_ref), custom_call_target="tpu_custom_call" | custom-call | flops 704643072 | bytes 4587520 | tf_op jit(solution)/shard_map/down_own_columns/pallas_call | solution.py:197
  123.0 0.0 all-to-all-done.1
  123.0 0.0 copy-done.2
  123.1 0.0 copy-done.3
  123.1 17.6 %causal_attention.1 = bf16[1024,512]{1,0:T(8,128)(2,1)S(1)} custom-call(s32[1]{0:T(128)} %bitcast.rank_ref, bf16[1024,768]{1,0:T(8,128)(2,1)} %bitcast.3.nope_ref.rope_ref, bf16[1024,768]{1,0:T(8,128)(2,1)} %bitcast.3.nope_ref.rope_ref, bf16[16,64,576]{2,1,0:T(8,128)(2,1)S(1)} %constant_dynamic-update-slice_fusion.kv_ref, ...), custom_call_target="tpu_custom_call" | custom-call | flops 4831838208 | bytes 4194304 | tf_op jit(solution)/shard_map/causal_attention/pallas_call | solution.py:284
  140.7 29.0 %all_to_all.21 = bf16[16,64,512]{2,1,0:T(8,128)(2,1)S(1)} all-to-all(bf16[16,64,512]{2,1,0:T(8,128)(2,1)S(1)} %bitcast.12), channel_id=1, replica_groups=mesh['groups'=2,'ctx'=16] {'ctx'}, dimensions={0} | all-to-all | bytes 2097152 | tf_op jit(solution)/shard_map/all_to_all | solution.py:365
  169.7 0.0 copy-start.6
  169.7 5.1 %all-to-all-start.3 = ((bf16[16,24,1792]{2,1,0:T(8,128)(2,1)}), bf16[16,24,1792]{2,1,0:T(8,128)(2,1)S(1)}, u32[]{:S(2)}, u32[]{:S(2)}) async-start(bf16[16,24,1792]{2,1,0:T(8,128)(2,1)} %bitcast.2), calls=%async_computation.3 | async-start | bytes 2752512 | tf_op jit(solution)/shard_map/all_to_all | solution.py:363
  174.8 0.0 copy-done.6
  174.8 0.1 copy.15.gates_ref
  174.9 1.1 copy.16
  176.0 27.4 %all-to-all-done.3.back_ref = bf16[16,24,1792]{2,1,0:T(8,128)(2,1)S(1)} async-done(((bf16[16,24,1792]{2,1,0:T(8,128)(2,1)}), bf16[16,24,1792]{2,1,0:T(8,128)(2,1)S(1)}, u32[]{:S(2)}, u32[]{:S(2)}) %all-to-all-start.3) | async-done | bytes 1376288 | tf_op jit(solution)/shard_map/all_to_all | solution.py:363
  203.4 3.2 %combine_routes.1 = bf16[64,3584]{1,0:T(8,128)(2,1)} custom-call(s32[64,2]{1,0:T(8,128)S(1)} %copy.12.routes_ref, f32[64,2]{1,0:T(8,128)S(1)} %copy.15.gates_ref, bf16[16,24,1792]{2,1,0:T(8,128)(2,1)S(1)} %all-to-all-done.3.back_ref), custom_call_target="tpu_custom_call" | custom-call | tf_op jit(solution)/shard_map/combine_routes/pallas_call | solution.py:88
  (5 shorter events, 0.1 us)
Async XLA Ops:
  1.4 1.0 copy-start.1
  3.3 40.8 %copy-start = (bf16[64,12288]{1,0:T(8,128)(2,1)S(1)}, bf16[64,12288]{1,0:T(8,128)(2,1)}, u32[]{:S(2)}) copy-start(bf16[64,12288]{1,0:T(8,128)(2,1)} %x_ref.3) | copy-start | bytes 4718596
  43.3 56.4 %collective-permute-start = (bf16[384,1792]{1,0:T(8,128)(2,1)S(1)}, bf16[384,1792]{1,0:T(8,128)(2,1)S(1)}, u32[]{:S(2)}, u32[]{:S(2)}) collective-permute-start(bf16[384,1792]{1,0:T(8,128)(2,1)S(1)} %bitcast.10), channel_id=1, source_target_pairs={{0,1},{1,0},{2,3},{3,2},{4,5},{5,4},{6,7},{7,6},{8,9},{9,8},{10,11... | collective-permute-start | bytes 4128776 | tf_op jit(solution)/shard_map/ppermute | solution.py:351
  50.1 4.6 %copy-start.5 = (bf16[64,576]{1,0:T(8,128)(2,1)S(1)}, bf16[64,576]{1,0:T(8,128)(2,1)}, u32[]{:S(2)}) copy-start(bf16[64,576]{1,0:T(8,128)(2,1)} %param.11) | copy-start | bytes 221188
  50.1 73.0 %all-to-all-start.1 = ((bf16[16,64,768]{2,1,0:T(8,128)(2,1)}), bf16[16,64,768]{2,1,0:T(8,128)(2,1)}, u32[]{:S(2)}, u32[]{:S(2)}) async-start(bf16[16,64,768]{2,1,0:T(8,128)(2,1)} %split_queries.1), calls=%async_computation.1 | async-start | bytes 3145728 | tf_op jit(solution)/shard_map/all_to_all | solution.py:354
  54.6 41.2 %collective-permute-start.2 = (bf16[1,64,576]{2,1,0:T(8,128)(2,1)S(1)}, bf16[1,64,576]{2,1,0:T(8,128)(2,1)S(1)}, u32[]{:S(2)}, u32[]{:S(2)}) collective-permute-start(bf16[1,64,576]{2,1,0:T(8,128)(2,1)S(1)} %bitcast.14), channel_id=1, source_target_pairs={{0,8},{1,9},{2,10},{3,11},{4,12},{5,13},{6,14},{7,15},{8,0},{9,1},... | collective-permute-start | bytes 221192 | tf_op jit(solution)/shard_map/ppermute | solution.py:311
  95.9 11.0 %collective-permute-start.3 = (bf16[2,64,576]{2,1,0:T(8,128)(2,1)S(1)}, bf16[2,64,576]{2,1,0:T(8,128)(2,1)S(1)}, u32[]{:S(2)}, u32[]{:S(2)}) collective-permute-start(bf16[2,64,576]{2,1,0:T(8,128)(2,1)S(1)} %pad_maximum_fusion.2), channel_id=1, source_target_pairs={{0,4},{1,5},{2,6},{3,7},{4,0},{5,1},{6,2},{7,3},{8,12},{9,13},{10,... | collective-permute-start | bytes 442376 | tf_op jit(solution)/shard_map/ppermute | solution.py:311
  99.7 1.1 copy-start.4
  106.7 12.7 %collective-permute-start.1 = (bf16[384,1792]{1,0:T(8,128)(2,1)S(1)}, bf16[384,1792]{1,0:T(8,128)(2,1)S(1)}, u32[]{:S(2)}, u32[]{:S(2)}) collective-permute-start(bf16[384,1792]{1,0:T(8,128)(2,1)S(1)} %get-tuple-element.11), channel_id=1, source_target_pairs={{0,1},{1,0},{2,3},{3,2},{4,5},{5,4},{6,7},{7,6},{8,9},{9,8},{10,11... | collective-permute-start | bytes 4128776 | tf_op jit(solution)/shard_map/ppermute | solution.py:358
  106.9 10.2 %collective-permute-start.4 = (bf16[4,64,576]{2,1,0:T(8,128)(2,1)S(1)}, bf16[4,64,576]{2,1,0:T(8,128)(2,1)S(1)}, u32[]{:S(2)}, u32[]{:S(2)}) collective-permute-start(bf16[4,64,576]{2,1,0:T(8,128)(2,1)S(1)} %pad_maximum_fusion.1), channel_id=1, source_target_pairs={{0,2},{1,3},{2,0},{3,1},{4,6},{5,7},{6,4},{7,5},{8,10},{9,11},{10,... | collective-permute-start | bytes 884744 | tf_op jit(solution)/shard_map/ppermute | solution.py:311
  117.2 2.2 %collective-permute-start.5 = (bf16[8,64,576]{2,1,0:T(8,128)(2,1)S(1)}, bf16[8,64,576]{2,1,0:T(8,128)(2,1)S(1)}, u32[]{:S(2)}, u32[]{:S(2)}) collective-permute-start(bf16[8,64,576]{2,1,0:T(8,128)(2,1)S(1)} %pad_maximum_fusion), channel_id=1, source_target_pairs={{0,1},{1,0},{2,3},{3,2},{4,5},{5,4},{6,7},{7,6},{8,9},{9,8},{10,11... | collective-permute-start | bytes 1769480 | tf_op jit(solution)/shard_map/ppermute | solution.py:311
  119.5 3.6 %copy-start.2 = (bf16[4,128,512]{2,1,0:T(8,128)(2,1)S(1)}, bf16[4,128,512]{2,1,0:T(8,128)(2,1)}, u32[]{:S(2)}) copy-start(bf16[4,128,512]{2,1,0:T(8,128)(2,1)} %key_ref.1) | copy-start | bytes 1572868
  119.5 3.6 %copy-start.3 = (bf16[4,512,128]{2,1,0:T(8,128)(2,1)S(1)}, bf16[4,512,128]{2,1,0:T(8,128)(2,1)}, u32[]{:S(2)}) copy-start(bf16[4,512,128]{2,1,0:T(8,128)(2,1)} %value_ref.1) | copy-start | bytes 1572868
  169.7 5.1 %copy-start.6 = (f32[64,2]{0,1:T(2,128)S(1)}, f32[64,2]{0,1:T(2,128)}, u32[]{:S(2)}) copy-start(f32[64,2]{0,1:T(2,128)} %param.16) | copy-start | bytes 1540
  169.7 33.7 %all-to-all-start.3 = ((bf16[16,24,1792]{2,1,0:T(8,128)(2,1)}), bf16[16,24,1792]{2,1,0:T(8,128)(2,1)S(1)}, u32[]{:S(2)}, u32[]{:S(2)}) async-start(bf16[16,24,1792]{2,1,0:T(8,128)(2,1)} %bitcast.2), calls=%async_computation.3 | async-start | bytes 2752512 | tf_op jit(solution)/shard_map/all_to_all | solution.py:363

commit v3 on v0

v3 whole, which is shorter than its diff:
```python
import functools
import math

import jax
import jax.numpy as jnp
from jax import lax
from jax.experimental import pallas as pl
from jax.experimental.pallas import tpu as pltpu
from jax.sharding import PartitionSpec as P

D = 3584
HEADS = 64
NOPE = 128
ROPE = 64
LATENT = 512
VDIM = 128
TOP = 2
HALF = 512
VMEM_LIMIT = 50 * 1024 * 1024
F32 = jnp.float32
BF16 = jnp.bfloat16


SMEM = pl.BlockSpec(memory_space=pltpu.SMEM)
VMEM = pl.BlockSpec(memory_space=pltpu.VMEM)
SMALL = pl.CostEstimate(flops=1, bytes_accessed=1, transcendentals=0)


def call(kernel, name, **options):
    return pl.pallas_call(
        kernel,
        name=name,
        cost_estimate=SMALL,
        compiler_params=pltpu.CompilerParams(vmem_limit_bytes=VMEM_LIMIT),
        **options,
    )


def slot_targets(routes, rows):
    tok = routes.shape[0]
    lane = lax.broadcasted_iota(jnp.int32, (tok, 128), 1)
    first = routes[:, 0:1]
    second = routes[:, 1:2]
    hot0 = jnp.where(lane == first, 1.0, 0.0)
    hot1 = jnp.where(lane == second, 1.0, 0.0)
    earlier = jnp.where(
        lax.broadcasted_iota(jnp.int32, (tok, tok), 1) < lax.broadcasted_iota(jnp.int32, (tok, tok), 0),
        1.0,
        0.0,
    )
    counts = jnp.dot(earlier.astype(BF16), (hot0 + hot1).astype(BF16), preferred_element_type=F32)
    slot0 = jnp.sum(counts * hot0, axis=1, keepdims=True).astype(jnp.int32)
    slot1 = jnp.sum(counts * hot1, axis=1, keepdims=True).astype(jnp.int32)
    return first * rows + slot0, second * rows + slot1


def bucket_kernel(rows, routes_ref, x_ref, out_ref):
    target0, target1 = slot_targets(routes_ref[...], rows)
    column = lax.broadcasted_iota(jnp.int32, (x_ref.shape[0], out_ref.shape[0]), 1)
    chosen = jnp.where((column == target0) | (column == target1), 1.0, 0.0).astype(BF16)
    out_ref[...] = lax.dot_general(
        chosen, x_ref[...], (((0,), (0,)), ((), ())), preferred_element_type=F32
    ).astype(BF16)


def build_buckets(routes, moe_input, experts, rows):
    return call(
        functools.partial(bucket_kernel, rows),
        "bucket_rows",
        out_shape=jax.ShapeDtypeStruct((experts * rows, D), BF16),
    )(routes, moe_input)


def combine_kernel(rows, routes_ref, gates_ref, back_ref, out_ref):
    tok = routes_ref.shape[0]
    target0, target1 = slot_targets(routes_ref[...], rows)
    targets = jnp.concatenate([target0, target1], axis=0)
    column = lax.broadcasted_iota(jnp.int32, (2 * tok, back_ref.shape[0]), 1)
    chosen = jnp.where(column == targets, 1.0, 0.0).astype(BF16)
    picked = jnp.dot(chosen, back_ref[...], preferred_element_type=F32)
    out_ref[...] = (picked[:tok] * gates_ref[:, 0:1] + picked[tok:] * gates_ref[:, 1:2]).astype(BF16)


def combine(routes, gates, back, rows):
    return call(
        functools.partial(combine_kernel, rows),
        "combine_routes",
        out_shape=jax.ShapeDtypeStruct((routes.shape[0], D), BF16),
    )(routes, gates, back)


STEP = 896
STEPS = D // STEP


def hidden_kernel(own_ref, other_ref, gate_ref, up_ref, down_ref, hidden_ref, out_ref, gate_sum, up_sum):
    step = pl.program_id(0)
    count = own_ref.shape[0]
    x = jnp.concatenate([own_ref[...], other_ref[...]], axis=0)
    gate = jnp.dot(x, gate_ref[0], preferred_element_type=F32)
    up = jnp.dot(x, up_ref[0], preferred_element_type=F32)

    @pl.when(step == 0)
    def _():
        gate_sum[...] = gate
        up_sum[...] = up

    @pl.when(step > 0)
    def _():
        gate_sum[...] += gate
        up_sum[...] += up

    @pl.when(step == STEPS - 1)
    def _():
        value = gate_sum[...]
        hidden = (value / (1.0 + jnp.exp(-value)) * up_sum[...]).astype(BF16)
        hidden_ref[...] = hidden[:count]
        out_ref[...] = jnp.dot(hidden[count:], down_ref[0], preferred_element_type=F32).astype(BF16)


def hidden_rows(own, other, gate, up, down):
    count = own.shape[0]
    part = pl.BlockSpec((count, STEP), lambda k: (0, k))
    weights = pl.BlockSpec((1, STEP, HALF), lambda k: (0, k, 0))
    return call(
        hidden_kernel,
        "expert_hidden",
        grid=(STEPS,),
        in_specs=[part, part, weights, weights, pl.BlockSpec((1, HALF, D), lambda k: (0, 0, 0))],
        out_specs=[
            pl.BlockSpec((count, HALF), lambda k: (0, 0)),
            pl.BlockSpec((count, D), lambda k: (0, 0)),
        ],
        scratch_shapes=[pltpu.VMEM((2 * count, HALF), F32)] * 2,
        out_shape=[jax.ShapeDtypeStruct((count, HALF), BF16), jax.ShapeDtypeStruct((count, D), BF16)],
    )(own, other, gate, up, down)


def down_kernel(hidden_ref, down_ref, other_ref, out_ref):
    own = jnp.dot(hidden_ref[...], down_ref[0], preferred_element_type=F32).astype(BF16)
    out_ref[...] = (own.astype(F32) + other_ref[...].astype(F32)).astype(BF16)


def down_own(hidden, down, other):
    return call(down_kernel, "down_own_rows", out_shape=jax.ShapeDtypeStruct(other.shape, BF16))(
        hidden, down, other
    )


def split_kernel(x_ref, out_ref):
    each = NOPE + ROPE
    heads = range(x_ref.shape[1] // each)
    pieces = [x_ref[:, head * each : head * each + NOPE] for head in heads]
    pieces += [x_ref[:, head * each + NOPE : (head + 1) * each] for head in heads]
    out_ref[0] = jnp.concatenate(pieces, axis=1)


def split_queries(queries, chips):
    tok = queries.shape[0]
    width = queries.shape[1] // chips
    return call(
        split_kernel,
        "split_queries",
        grid=(chips,),
        in_specs=[pl.BlockSpec((tok, width), lambda d: (0, d))],
        out_specs=pl.BlockSpec((1, tok, width), lambda d: (d, 0, 0)),
        out_shape=jax.ShapeDtypeStruct((chips, tok, width), BF16),
    )(queries)


BLOCK = 128
SPAN = 2 * BLOCK
EXP_SCALE = math.log2(math.e) / math.sqrt(NOPE + ROPE)


def attention_kernel(
    per_core,
    rank_ref,
    plain_ref,
    rope_ref,
    kv_ref,
    own_key_ref,
    other_key_ref,
    own_value_ref,
    other_value_ref,
    out_ref,
    keys,
    queries,
    mixed,
):
    pair = pl.program_id(0)
    shards, tok = kv_ref.shape[:2]
    count = plain_ref.shape[0]
    core = rank_ref[0] & 1
    mine = pair // per_core == core

    @pl.when(pair == 0)
    def _():
        for index, offset in enumerate(gather_order(shards)):
            place = pl.ds(pl.multiple_of((rank_ref[0] ^ offset) * tok, tok), tok)
            keys[place, : LATENT + ROPE] = kv_ref[index]
            keys[place, LATENT + ROPE :] = kv_ref[index, :, LATENT:]

    side = lax.broadcasted_iota(jnp.int32, (1, 2 * ROPE), 1) // ROPE
    for one in range(2):
        key = jnp.where(mine, own_key_ref[one], other_key_ref[one])
        latent = jnp.dot(plain_ref[:, one * NOPE : (one + 1) * NOPE], key, preferred_element_type=F32)
        queries[one, :, :LATENT] = latent.astype(BF16)
        queries[one, :, LATENT:] = jnp.where(side == one, rope_ref[...], jnp.zeros((), BF16))

    row = lax.broadcasted_iota(jnp.int32, (2 * BLOCK, SPAN), 0) % BLOCK
    position = (2 * (row // tok) + core) * tok + row % tok
    visible = lax.broadcasted_iota(jnp.int32, (2 * BLOCK, SPAN), 1) <= position
    contract = (((1,), (1,)), ((), ()))
    for block in range(count // BLOCK):
        start = block * SPAN
        rows = pl.ds(block * BLOCK, BLOCK)
        last = pl.ds(start, SPAN)
        query = jnp.concatenate([queries[0, rows, :], queries[1, rows, :]], axis=0)
        near = lax.dot_general(query, keys[last, :], contract, preferred_element_type=F32)
        near = jnp.where(visible, near, -1e30)
        top = jnp.max(near, axis=1, keepdims=True)
        if block:
            past = lax.dot_general(query, keys[:start, :], contract, preferred_element_type=F32)
            top = jnp.maximum(top, jnp.max(past, axis=1, keepdims=True))
        weights = jnp.exp2((near - top) * EXP_SCALE)
        total = jnp.sum(weights, axis=1, keepdims=True)
        summed = jnp.dot(weights.astype(BF16), keys[last, :LATENT], preferred_element_type=F32)
        if block:
            weights = jnp.exp2((past - top) * EXP_SCALE)
            total = total + jnp.sum(weights, axis=1, keepdims=True)
            summed = summed + jnp.dot(weights.astype(BF16), keys[:start, :LATENT], preferred_element_type=F32)
        result = (summed / total).astype(BF16)
        mixed[0, rows, :] = result[:BLOCK]
        mixed[1, rows, :] = result[BLOCK:]

    for one in range(2):
        value = jnp.where(mine, own_value_ref[one], other_value_ref[one])
        out_ref[:, one * VDIM : (one + 1) * VDIM] = jnp.dot(
            mixed[one], value, preferred_element_type=F32
        ).astype(BF16)


def attention(rank, queries, keys, key_proj, other_key, value_proj, other_value):
    count = queries.shape[0]
    pairs = key_proj.shape[0]
    per_core = pairs // 2
    key_spec = pl.BlockSpec((2, NOPE, LATENT), lambda p, rank: (p % per_core, 0, 0))
    value_spec = pl.BlockSpec((2, LATENT, VDIM), lambda p, rank: (p % per_core, 0, 0))
    return call(
        functools.partial(attention_kernel, per_core),
        "causal_attention",
        grid_spec=pltpu.PrefetchScalarGridSpec(
            num_scalar_prefetch=1,
            grid=(pairs,),
            in_specs=[
                pl.BlockSpec((count, 2 * NOPE), lambda p, rank: (0, p)),
                pl.BlockSpec((count, 2 * ROPE), lambda p, rank: (0, 2 * pairs + p)),
                pl.BlockSpec(keys.shape, lambda p, rank: (0, 0, 0)),
                key_spec,
                key_spec,
                value_spec,
                value_spec,
            ],
            out_specs=pl.BlockSpec((count, 2 * VDIM), lambda p, rank: (0, p)),
            scratch_shapes=[
                pltpu.VMEM((keys.shape[0] * keys.shape[1], LATENT + 2 * ROPE), BF16),
                pltpu.VMEM((2, count, LATENT + 2 * ROPE), BF16),
                pltpu.VMEM((2, count, LATENT), BF16),
            ],
        ),
        out_shape=jax.ShapeDtypeStruct((count, 2 * pairs * VDIM), BF16),
    )(rank, queries, queries, keys, key_proj, other_key, value_proj, other_value)


def send(array, mask):
    return lax.ppermute(array, "ctx", [(i, i ^ mask) for i in range(lax.axis_size("ctx"))])


def swap_chips(array):
    shards = lax.axis_size("ctx")
    return lax.all_to_all(
        array,
        "ctx",
        split_axis=0,
        concat_axis=0,
        axis_index_groups=[list(range(core, shards, 2)) for core in range(2)],
        tiled=True,
    )


def after(array, *others):
    return lax.optimization_barrier((array, *others))[0]


def gather_order(shards):
    top, below = shards // 2, shards // 4
    order = [0, top, below, top ^ below]
    mask = below // 2
    while mask:
        order = order + [offset ^ mask for offset in order]
        mask //= 2
    return order


def on_device(
    queries,
    latent_kv,
    key_proj,
    value_proj,
    moe_input,
    routes,
    gates,
    expert_gate,
    expert_up,
    expert_down,
):
    shards = lax.axis_size("ctx")
    tok = queries.shape[0]
    experts = shards // 2
    capacity = 2 * ((4 * tok * TOP + 6 * experts - 1) // (6 * experts))
    rows = -(-capacity // 8) * 8
    rank = lax.axis_index("ctx").astype(jnp.int32).reshape(1)

    keys = jnp.stack([latent_kv] + [send(latent_kv, offset) for offset in gather_order(shards)[1:4]])
    other_key = send(key_proj, 1)
    other_value = send(value_proj, 1)

    buckets = after(build_buckets(routes, moe_input, experts, rows), keys)
    own = swap_chips(buckets.reshape(experts, rows, D))
    sent = after(split_queries(queries, experts), own)
    held = swap_chips(sent)

    own = own.reshape(experts * rows, D)
    mask = shards // 8
    while mask:
        keys = jnp.concatenate([keys, send(keys, mask)], axis=0)
        mask //= 2
    other = send(own, 1)
    own = after(own, keys, other_key, other_value)
    hidden, for_other = hidden_rows(own, other, expert_gate, expert_up, expert_down)
    result = down_own(hidden, expert_down, send(for_other, 1))

    result, held = lax.optimization_barrier((result, held))
    back = swap_chips(result.reshape(experts, rows, D))
    values = attention(
        rank, held.reshape(experts * tok, held.shape[2]), keys, key_proj, other_key, value_proj, other_value
    )
    values, back = lax.optimization_barrier((values, back))
    values = swap_chips(values.reshape(experts, tok, values.shape[1]))
    moe_out = combine(routes, gates, back.reshape(experts * rows, D), rows)
    attention_out = values.transpose(1, 0, 2).reshape(tok, HEADS * VDIM)
    return (attention_out, moe_out)


def solution(mesh):
    return jax.shard_map(
        on_device,
        mesh=mesh,
        in_specs=(
            P(("groups", "ctx"), None),
            P(("groups", "ctx"), None),
            P("ctx", None, None),
            P("ctx", None, None),
            P(("groups", "ctx"), None),
            P(("groups", "ctx"), None),
            P(("groups", "ctx"), None),
            P("ctx", None, None),
            P("ctx", None, None),
            P("ctx", None, None),
        ),
        out_specs=(P(("groups", "ctx"), None), P(("groups", "ctx"), None)),
        check_vma=False,
    )
```

time: 342 us -> 161 us (0.47)
  the two profiles are of different devices: /device:TPU:15 before, /device:TPU:0 now
where the time goes in v3:
time: 161 us; the launch traced here: 160 us
  waiting for transfers between devices  90.1 us (56%)
  Pallas kernels  36.1 us (22%)
  starting transfers between devices  25.6 us (16%)
  local copies, waits for them, and re-layouts  7.52 us (5%)
    all_to_all x4, waiting for transfers between devices, swap_chips(): lax.all_to_all(array, 'ctx', split_axis=0, concat_axis=0, axis_index_grou...  82.9 us
    all_to_all x4, starting transfers between devices, swap_chips(): lax.all_to_all(array, 'ctx', split_axis=0, concat_axis=0, axis_index_grou...  16.6 us
    pallas_call x1, Pallas kernels, attention(): call(functools.partial(attention_kernel, per_core), 'causal_attention', g...  16.4 us
    ppermute x9, starting transfers between devices, send(): lax.ppermute(array, 'ctx', [(i, i ^ mask) for i in range(lax.axis_size('c...  9 us
    pallas_call x1, Pallas kernels, hidden_rows(): call(hidden_kernel, 'expert_hidden', grid=(STEPS,), in_specs=[part, part,...  8.82 us
    ppermute x9, waiting for transfers between devices, send(): lax.ppermute(array, 'ctx', [(i, i ^ mask) for i in range(lax.axis_size('c...  7.2 us
    unnamed x26, local copies, waits for them, and re-layouts  4.64 us
    pallas_call x1, Pallas kernels, down_own(): call(down_kernel, 'down_own_rows', out_shape=jax.ShapeDtypeStruct(other.s...  4.01 us
  transfers between devices with their start and end apart: 13, of which 8 were waited for; matrix products, arithmetic and copies ran while one was open for 3% of the time, Pallas kernels for 23%

profile of v3, /device:TPU:0, one launch (start us, length us, event | category | flops | bytes accessed | tf_op | source)
XLA Modules:
  0.0 160.1 jit_solution(6628520468934778634)
XLA Ops:
  0.6 4.1 %collective-permute-start = (bf16[64,576]{1,0:T(8,128)(2,1)}, bf16[64,576]{1,0:T(8,128)(2,1)S(1)}, u32[]{:S(2)}, u32[]{:S(2)}) collective-permute-start(bf16[64,576]{1,0:T(8,128)(2,1)} %param.11), channel_id=1, source_target_pairs={{0,8},{1,9},{2,10},{3,11},{4,12},{5,13},{6,14},{7,15},{8,0},{9,1},... | collective-permute-start | bytes 221192 | tf_op jit(solution)/shard_map/ppermute | solution.py:277
  4.7 1.6 collective-permute-start.1
  6.3 0.0 collective-permute-start.2
  6.3 0.8 copy.12.routes_ref
  7.1 0.0 copy-start.3
  7.1 1.0 copy-done.3
  8.1 0.0 copy-start.4
  8.1 2.0 %bucket_rows.1 = bf16[192,3584]{1,0:T(8,128)(2,1)} custom-call(s32[64,2]{1,0:T(8,128)S(1)} %copy.12.routes_ref, bf16[64,3584]{1,0:T(8,128)(2,1)S(1)} %copy-done.3), custom_call_target="tpu_custom_call" | custom-call | flops 1 | bytes 1 | tf_op jit(solution)/shard_map/bucket_rows/pallas_call | solution.py:67
  10.1 0.0 collective-permute-done
  10.1 0.0 copy-start.7
  10.1 0.0 collective-permute-done.1
  10.1 0.0 copy-start.5
  10.1 2.6 %collective-permute-done.2 = bf16[64,576]{1,0:T(8,128)(2,1)S(1)} collective-permute-done((bf16[64,576]{1,0:T(8,128)(2,1)}, bf16[64,576]{1,0:T(8,128)(2,1)S(1)}, u32[]{:S(2)}, u32[]{:S(2)}) %collective-permute-start.2) | collective-permute-done | bytes 73760 | tf_op jit(solution)/shard_map/ppermute | solution.py:277
  12.8 0.0 copy-done.4
  12.8 0.1 pad_maximum_fusion
  12.8 0.0 copy-start
  12.8 0.0 copy-done.7
  12.9 0.0 copy-done.5
  12.9 4.9 %all-to-all-start = ((bf16[8,24,3584]{2,1,0:T(8,128)(2,1)}), bf16[8,24,3584]{2,1,0:T(8,128)(2,1)S(1)}, u32[]{:S(2)}, u32[]{:S(2)}) async-start(bf16[8,24,3584]{2,1,0:T(8,128)(2,1)} %bitcast.5), calls=%async_computation | async-start | bytes 2752512 | tf_op jit(solution)/shard_map/all_to_all | solution.py:282
  17.8 0.0 copy-done
  17.8 3.4 %split_queries.1 = bf16[8,64,1536]{2,1,0:T(8,128)(2,1)} custom-call(bf16[64,12288]{1,0:T(8,128)(2,1)S(1)} %copy-done), custom_call_target="tpu_custom_call" | custom-call | flops 1 | bytes 1 | tf_op jit(solution)/shard_map/split_queries/pallas_call | solution.py:161
  21.1 0.7 constant_dynamic-update-slice_fusion.4
  21.8 2.0 %collective-permute-start.3 = (bf16[4,64,576]{2,1,0:T(8,128)(2,1)S(1)}, bf16[4,64,576]{2,1,0:T(8,128)(2,1)S(1)}, u32[]{:S(2)}, u32[]{:S(2)}) collective-permute-start(bf16[4,64,576]{2,1,0:T(8,128)(2,1)S(1)} %pad_maximum_fusion), channel_id=1, source_target_pairs={{0,2},{1,3},{2,0},{3,1},{4,6},{5,7},{6,4},{7,5},{8,10},{9,11},{10,... | collective-permute-start | bytes 884744 | tf_op jit(solution)/shard_map/ppermute | solution.py:277
  23.8 26.8 %all-to-all-done = bf16[8,24,3584]{2,1,0:T(8,128)(2,1)S(1)} async-done(((bf16[8,24,3584]{2,1,0:T(8,128)(2,1)}), bf16[8,24,3584]{2,1,0:T(8,128)(2,1)S(1)}, u32[]{:S(2)}, u32[]{:S(2)}) %all-to-all-start) | async-done | bytes 1376288 | tf_op jit(solution)/shard_map/all_to_all | solution.py:282
  50.6 0.0 copy-start.8
  50.6 0.0 copy-start.6
  50.6 0.0 collective-permute-start.7
  50.6 4.5 %all-to-all-start.1 = ((bf16[8,64,1536]{2,1,0:T(8,128)(2,1)}), bf16[8,64,1536]{2,1,0:T(8,128)(2,1)}, u32[]{:S(2)}, u32[]{:S(2)}) async-start(bf16[8,64,1536]{2,1,0:T(8,128)(2,1)} %split_queries.1), calls=%async_computation.1 | async-start | bytes 3145728 | tf_op jit(solution)/shard_map/all_to_all | solution.py:282
  55.1 0.0 copy-start.1
  55.1 0.0 copy-start.2
  55.1 0.0 copy-done.8
  55.1 0.7 constant_dynamic-update-slice_fusion.3
  55.8 0.0 copy-done.6
  55.8 0.7 constant_dynamic-update-slice_fusion.2
  56.5 0.7 constant_dynamic-update-slice_fusion.1
  57.1 0.0 collective-permute-done.3
  57.1 0.9 constant_dynamic-update-slice_fusion
  58.0 0.4 collective-permute-start.4
  58.4 0.0 copy-done.1
  58.4 0.1 collective-permute-start.5
  58.6 0.0 copy-done.2
  58.6 0.4 collective-permute-start.6
  58.9 1.4 collective-permute-done.4
  60.4 0.9 constant_dynamic-update-slice_fusion.5.kv_ref
  61.3 0.0 collective-permute-done.5.other_key_ref
  61.3 0.4 collective-permute-done.6.other_value_ref
  61.6 0.0 collective-permute-done.7.other_ref
  61.6 8.8 %expert_hidden.1 = (bf16[192,512]{1,0:T(8,128)(2,1)S(1)}, bf16[192,3584]{1,0:T(8,128)(2,1)S(1)}) custom-call(bf16[192,3584]{1,0:T(8,128)(2,1)S(1)} %bitcast.24, bf16[192,3584]{1,0:T(8,128)(2,1)} %collective-permute-done.7.other_ref, bf16[1,3584,512]{2,1,0:T(8,128)(2,1)} %gate_ref.1, bf16[1,3584,512]{2,1,0:T(8,128)(2,1)} %up_ref.1, bf16[1,512,3584]{2,1,0:T(8,128)(2,1)} %down_ref.3), custom_call_target="tpu_custom_call" | custom-call | flops 1 | bytes 1 | tf_op jit(solution)/shard_map/expert_hidden/pallas_call | solution.py:125
  70.5 0.4 collective-permute-start.8
  70.9 2.8 %collective-permute-done.8.other_ref = bf16[192,3584]{1,0:T(8,128)(2,1)S(1)} collective-permute-done((bf16[192,3584]{1,0:T(8,128)(2,1)S(1)}, bf16[192,3584]{1,0:T(8,128)(2,1)S(1)}, u32[]{:S(2)}, u32[]{:S(2)}) %collective-permute-start.8) | collective-permute-done | bytes 1376288 | tf_op jit(solution)/shard_map/ppermute | solution.py:277
  73.7 4.0 %down_own_rows.1 = bf16[192,3584]{1,0:T(8,128)(2,1)} custom-call(bf16[192,512]{1,0:T(8,128)(2,1)S(1)} %get-tuple-element.13.hidden_ref, bf16[1,512,3584]{2,1,0:T(8,128)(2,1)} %down_ref.3, bf16[192,3584]{1,0:T(8,128)(2,1)S(1)} %collective-permute-done.8.other_ref), custom_call_target="tpu_custom_call" | custom-call | flops 1 | bytes 1 | tf_op jit(solution)/shard_map/down_own_rows/pallas_call | solution.py:145
  77.7 15.2 %all-to-all-done.1 = bf16[8,64,1536]{2,1,0:T(8,128)(2,1)} async-done(((bf16[8,64,1536]{2,1,0:T(8,128)(2,1)}), bf16[8,64,1536]{2,1,0:T(8,128)(2,1)}, u32[]{:S(2)}, u32[]{:S(2)}) %all-to-all-start.1) | async-done | bytes 1572896 | tf_op jit(solution)/shard_map/all_to_all | solution.py:282
  92.9 3.6 %all-to-all-start.2 = ((bf16[8,24,3584]{2,1,0:T(8,128)(2,1)}), bf16[8,24,3584]{2,1,0:T(8,128)(2,1)S(1)}, u32[]{:S(2)}, u32[]{:S(2)}) async-start(bf16[8,24,3584]{2,1,0:T(8,128)(2,1)} %bitcast.8), calls=%async_computation.2 | async-start | bytes 2752512 | tf_op jit(solution)/shard_map/all_to_all | solution.py:282
  96.5 16.4 %causal_attention.1 = bf16[512,1024]{1,0:T(8,128)(2,1)} custom-call(s32[1]{0:T(128)} %bitcast.rank_ref, bf16[512,1536]{1,0:T(8,128)(2,1)} %bitcast.7.plain_ref.rope_ref, bf16[512,1536]{1,0:T(8,128)(2,1)} %bitcast.7.plain_ref.rope_ref, bf16[16,64,576]{2,1,0:T(8,128)(2,1)} %constant_dynamic-update-slice_fusion.5.kv_ref, bf16[4,128,512]{2,1,0:T(8,128)(2,1)S(1)} %copy-done.1, ...), custom_call_target="tpu_custom_call" | custom-call | flops 1 | bytes 1 | tf_op jit(solution)/shard_map/causal_attention/pallas_call | solution.py:250
  112.9 0.0 copy-start.9
  112.9 16.6 %all-to-all-done.2 = bf16[8,24,3584]{2,1,0:T(8,128)(2,1)S(1)} async-done(((bf16[8,24,3584]{2,1,0:T(8,128)(2,1)}), bf16[8,24,3584]{2,1,0:T(8,128)(2,1)S(1)}, u32[]{:S(2)}, u32[]{:S(2)}) %all-to-all-start.2) | async-done | bytes 1376288 | tf_op jit(solution)/shard_map/all_to_all | solution.py:282
  129.5 3.6 %all-to-all-start.3 = ((bf16[8,64,1024]{2,1,0:T(8,128)(2,1)}), bf16[8,64,1024]{2,1,0:T(8,128)(2,1)S(1)}, u32[]{:S(2)}, u32[]{:S(2)}) async-start(bf16[8,64,1024]{2,1,0:T(8,128)(2,1)} %bitcast.9), calls=%async_computation.3 | async-start | bytes 2097152 | tf_op jit(solution)/shard_map/all_to_all | solution.py:282
  133.1 0.0 copy-done.9
  133.1 0.1 copy.15.gates_ref
  133.2 1.6 combine_routes.1
  134.8 24.3 %all-to-all-done.3 = bf16[8,64,1024]{2,1,0:T(8,128)(2,1)S(1)} async-done(((bf16[8,64,1024]{2,1,0:T(8,128)(2,1)}), bf16[8,64,1024]{2,1,0:T(8,128)(2,1)S(1)}, u32[]{:S(2)}, u32[]{:S(2)}) %all-to-all-start.3) | async-done | bytes 1048608 | tf_op jit(solution)/shard_map/all_to_all | solution.py:282
  159.1 1.1 copy.16
Async XLA Ops:
  0.6 9.5 %collective-permute-start = (bf16[64,576]{1,0:T(8,128)(2,1)}, bf16[64,576]{1,0:T(8,128)(2,1)S(1)}, u32[]{:S(2)}, u32[]{:S(2)}) collective-permute-start(bf16[64,576]{1,0:T(8,128)(2,1)} %param.11), channel_id=1, source_target_pairs={{0,8},{1,9},{2,10},{3,11},{4,12},{5,13},{6,14},{7,15},{8,0},{9,1},... | collective-permute-start | bytes 221192 | tf_op jit(solution)/shard_map/ppermute | solution.py:277
  4.7 5.4 %collective-permute-start.1 = (bf16[64,576]{1,0:T(8,128)(2,1)}, bf16[64,576]{1,0:T(8,128)(2,1)S(1)}, u32[]{:S(2)}, u32[]{:S(2)}) collective-permute-start(bf16[64,576]{1,0:T(8,128)(2,1)} %param.11), channel_id=1, source_target_pairs={{0,4},{1,5},{2,6},{3,7},{4,0},{5,1},{6,2},{7,3},{8,12},{9,13},{10,... | collective-permute-start | bytes 221192 | tf_op jit(solution)/shard_map/ppermute | solution.py:277
  6.3 6.4 %collective-permute-start.2 = (bf16[64,576]{1,0:T(8,128)(2,1)}, bf16[64,576]{1,0:T(8,128)(2,1)S(1)}, u32[]{:S(2)}, u32[]{:S(2)}) collective-permute-start(bf16[64,576]{1,0:T(8,128)(2,1)} %param.11), channel_id=1, source_target_pairs={{0,12},{1,13},{2,14},{3,15},{4,8},{5,9},{6,10},{7,11},{8,4},{9,5},... | collective-permute-start | bytes 221192 | tf_op jit(solution)/shard_map/ppermute | solution.py:277
  7.1 1.0 copy-start.3
  8.1 4.7 %copy-start.4 = (bf16[64,576]{1,0:T(8,128)(2,1)S(1)}, bf16[64,576]{1,0:T(8,128)(2,1)}, u32[]{:S(2)}) copy-start(bf16[64,576]{1,0:T(8,128)(2,1)} %param.11) | copy-start | bytes 221188
  10.1 2.7 %copy-start.7 = (bf16[64,576]{1,0:T(8,128)(2,1)}, bf16[64,576]{1,0:T(8,128)(2,1)S(1)}, u32[]{:S(2)}) copy-start(bf16[64,576]{1,0:T(8,128)(2,1)S(1)} %collective-permute-done) | copy-start | bytes 221188
  10.1 2.7 %copy-start.5 = (bf16[64,576]{1,0:T(8,128)(2,1)}, bf16[64,576]{1,0:T(8,128)(2,1)S(1)}, u32[]{:S(2)}) copy-start(bf16[64,576]{1,0:T(8,128)(2,1)S(1)} %collective-permute-done.1) | copy-start | bytes 221188
  12.8 4.9 %copy-start = (bf16[64,12288]{1,0:T(8,128)(2,1)S(1)}, bf16[64,12288]{1,0:T(8,128)(2,1)}, u32[]{:S(2)}) copy-start(bf16[64,12288]{1,0:T(8,128)(2,1)} %x_ref.3) | copy-start | bytes 4718596
  12.9 37.7 %all-to-all-start = ((bf16[8,24,3584]{2,1,0:T(8,128)(2,1)}), bf16[8,24,3584]{2,1,0:T(8,128)(2,1)S(1)}, u32[]{:S(2)}, u32[]{:S(2)}) async-start(bf16[8,24,3584]{2,1,0:T(8,128)(2,1)} %bitcast.5), calls=%async_computation | async-start | bytes 2752512 | tf_op jit(solution)/shard_map/all_to_all | solution.py:282
  21.8 35.3 %collective-permute-start.3 = (bf16[4,64,576]{2,1,0:T(8,128)(2,1)S(1)}, bf16[4,64,576]{2,1,0:T(8,128)(2,1)S(1)}, u32[]{:S(2)}, u32[]{:S(2)}) collective-permute-start(bf16[4,64,576]{2,1,0:T(8,128)(2,1)S(1)} %pad_maximum_fusion), channel_id=1, source_target_pairs={{0,2},{1,3},{2,0},{3,1},{4,6},{5,7},{6,4},{7,5},{8,10},{9,11},{10,... | collective-permute-start | bytes 884744 | tf_op jit(solution)/shard_map/ppermute | solution.py:277
  50.6 4.5 %copy-start.8 = (bf16[64,576]{1,0:T(8,128)(2,1)S(1)}, bf16[64,576]{1,0:T(8,128)(2,1)}, u32[]{:S(2)}) copy-start(bf16[64,576]{1,0:T(8,128)(2,1)} %copy-done.7) | copy-start | bytes 221188
  50.6 5.2 %copy-start.6 = (bf16[64,576]{1,0:T(8,128)(2,1)S(1)}, bf16[64,576]{1,0:T(8,128)(2,1)}, u32[]{:S(2)}) copy-start(bf16[64,576]{1,0:T(8,128)(2,1)} %copy-done.5) | copy-start | bytes 221188
  50.6 11.1 %collective-permute-start.7 = (bf16[192,3584]{1,0:T(8,128)(2,1)S(1)}, bf16[192,3584]{1,0:T(8,128)(2,1)}, u32[]{:S(2)}, u32[]{:S(2)}) collective-permute-start(bf16[192,3584]{1,0:T(8,128)(2,1)S(1)} %bitcast.23), channel_id=1, source_target_pairs={{0,1},{1,0},{2,3},{3,2},{4,5},{5,4},{6,7},{7,6},{8,9},{9,8},{10,11... | collective-permute-start | bytes 4128776 | tf_op jit(solution)/shard_map/ppermute | solution.py:277
  50.6 42.3 %all-to-all-start.1 = ((bf16[8,64,1536]{2,1,0:T(8,128)(2,1)}), bf16[8,64,1536]{2,1,0:T(8,128)(2,1)}, u32[]{:S(2)}, u32[]{:S(2)}) async-start(bf16[8,64,1536]{2,1,0:T(8,128)(2,1)} %split_queries.1), calls=%async_computation.1 | async-start | bytes 3145728 | tf_op jit(solution)/shard_map/all_to_all | solution.py:282
  55.1 3.4 %copy-start.1 = (bf16[4,128,512]{2,1,0:T(8,128)(2,1)S(1)}, bf16[4,128,512]{2,1,0:T(8,128)(2,1)}, u32[]{:S(2)}) copy-start(bf16[4,128,512]{2,1,0:T(8,128)(2,1)} %own_key_ref.1) | copy-start | bytes 1572868
  55.1 3.5 %copy-start.2 = (bf16[4,512,128]{2,1,0:T(8,128)(2,1)S(1)}, bf16[4,512,128]{2,1,0:T(8,128)(2,1)}, u32[]{:S(2)}) copy-start(bf16[4,512,128]{2,1,0:T(8,128)(2,1)} %own_value_ref.1) | copy-start | bytes 1572868
  58.0 2.3 %collective-permute-start.4 = (bf16[8,64,576]{2,1,0:T(8,128)(2,1)}, bf16[8,64,576]{2,1,0:T(8,128)(2,1)S(1)}, u32[]{:S(2)}, u32[]{:S(2)}) collective-permute-start(bf16[8,64,576]{2,1,0:T(8,128)(2,1)} %get-tuple-element.20), channel_id=1, source_target_pairs={{0,1},{1,0},{2,3},{3,2},{4,5},{5,4},{6,7},{7,6},{8,9},{9,8},{10,11... | collective-permute-start | bytes 1769480 | tf_op jit(solution)/shard_map/ppermute | solution.py:277
  58.4 2.9 %collective-permute-start.5 = (bf16[4,128,512]{2,1,0:T(8,128)(2,1)S(1)}, bf16[4,128,512]{2,1,0:T(8,128)(2,1)S(1)}, u32[]{:S(2)}, u32[]{:S(2)}) collective-permute-start(bf16[4,128,512]{2,1,0:T(8,128)(2,1)S(1)} %copy-done.1), channel_id=1, source_target_pairs={{0,1},{1,0},{2,3},{3,2},{4,5},{5,4},{6,7},{7,6},{8,9},{9,8},{10,11... | collective-permute-start | bytes 1572872 | tf_op jit(solution)/shard_map/ppermute | solution.py:277
  58.6 3.1 %collective-permute-start.6 = (bf16[4,512,128]{2,1,0:T(8,128)(2,1)S(1)}, bf16[4,512,128]{2,1,0:T(8,128)(2,1)S(1)}, u32[]{:S(2)}, u32[]{:S(2)}) collective-permute-start(bf16[4,512,128]{2,1,0:T(8,128)(2,1)S(1)} %copy-done.2), channel_id=1, source_target_pairs={{0,1},{1,0},{2,3},{3,2},{4,5},{5,4},{6,7},{7,6},{8,9},{9,8},{10,11... | collective-permute-start | bytes 1572872 | tf_op jit(solution)/shard_map/ppermute | solution.py:277
  70.5 3.2 %collective-permute-start.8 = (bf16[192,3584]{1,0:T(8,128)(2,1)S(1)}, bf16[192,3584]{1,0:T(8,128)(2,1)S(1)}, u32[]{:S(2)}, u32[]{:S(2)}) collective-permute-start(bf16[192,3584]{1,0:T(8,128)(2,1)S(1)} %get-tuple-element.14), channel_id=1, source_target_pairs={{0,1},{1,0},{2,3},{3,2},{4,5},{5,4},{6,7},{7,6},{8,9},{9,8},{10,11... | collective-permute-start | bytes 4128776 | tf_op jit(solution)/shard_map/ppermute | solution.py:277
  92.9 36.6 %all-to-all-start.2 = ((bf16[8,24,3584]{2,1,0:T(8,128)(2,1)}), bf16[8,24,3584]{2,1,0:T(8,128)(2,1)S(1)}, u32[]{:S(2)}, u32[]{:S(2)}) async-start(bf16[8,24,3584]{2,1,0:T(8,128)(2,1)} %bitcast.8), calls=%async_computation.2 | async-start | bytes 2752512 | tf_op jit(solution)/shard_map/all_to_all | solution.py:282
  112.9 20.3 %copy-start.9 = (f32[64,2]{0,1:T(2,128)S(1)}, f32[64,2]{0,1:T(2,128)}, u32[]{:S(2)}) copy-start(f32[64,2]{0,1:T(2,128)} %param.16) | copy-start | bytes 1540
  129.5 29.6 %all-to-all-start.3 = ((bf16[8,64,1024]{2,1,0:T(8,128)(2,1)}), bf16[8,64,1024]{2,1,0:T(8,128)(2,1)S(1)}, u32[]{:S(2)}, u32[]{:S(2)}) async-start(bf16[8,64,1024]{2,1,0:T(8,128)(2,1)} %bitcast.9), calls=%async_computation.3 | async-start | bytes 2097152 | tf_op jit(solution)/shard_map/all_to_all | solution.py:282

commit v4 on v3

--- a/solution.py
+++ b/solution.py
@@ -54,30 +54,38 @@
     return first * rows + slot0, second * rows + slot1
 
 
-def bucket_kernel(rows, routes_ref, x_ref, out_ref):
+def bucket_kernel(rows, routes_ref, x_ref, *out_refs):
     target0, target1 = slot_targets(routes_ref[...], rows)
-    column = lax.broadcasted_iota(jnp.int32, (x_ref.shape[0], out_ref.shape[0]), 1)
+    column = lax.broadcasted_iota(jnp.int32, (x_ref.shape[0], len(out_refs) * rows), 1)
     chosen = jnp.where((column == target0) | (column == target1), 1.0, 0.0).astype(BF16)
-    out_ref[...] = lax.dot_general(
+    found = lax.dot_general(
         chosen, x_ref[...], (((0,), (0,)), ((), ())), preferred_element_type=F32
     ).astype(BF16)
+    for place, out_ref in enumerate(out_refs):
+        out_ref[...] = found[place * rows : (place + 1) * rows]
 
 
 def build_buckets(routes, moe_input, experts, rows):
     return call(
         functools.partial(bucket_kernel, rows),
         "bucket_rows",
-        out_shape=jax.ShapeDtypeStruct((experts * rows, D), BF16),
+        out_shape=[jax.ShapeDtypeStruct((rows, D), BF16)] * experts,
     )(routes, moe_input)
 
 
-def combine_kernel(rows, routes_ref, gates_ref, back_ref, out_ref):
+def stack(refs):
+    return jnp.concatenate([ref[...] for ref in refs], axis=0)
+
+
+def combine_kernel(rows, routes_ref, gates_ref, *refs):
+    out_ref = refs[-1]
+    back = stack(refs[:-1])
     tok = routes_ref.shape[0]
     target0, target1 = slot_targets(routes_ref[...], rows)
     targets = jnp.concatenate([target0, target1], axis=0)
-    column = lax.broadcasted_iota(jnp.int32, (2 * tok, back_ref.shape[0]), 1)
+    column = lax.broadcasted_iota(jnp.int32, (2 * tok, back.shape[0]), 1)
     chosen = jnp.where(column == targets, 1.0, 0.0).astype(BF16)
-    picked = jnp.dot(chosen, back_ref[...], preferred_element_type=F32)
+    picked = jnp.dot(chosen, back, preferred_element_type=F32)
     out_ref[...] = (picked[:tok] * gates_ref[:, 0:1] + picked[tok:] * gates_ref[:, 1:2]).astype(BF16)
 
 
@@ -86,17 +94,18 @@
         functools.partial(combine_kernel, rows),
         "combine_routes",
         out_shape=jax.ShapeDtypeStruct((routes.shape[0], D), BF16),
-    )(routes, gates, back)
+    )(routes, gates, *back)
 
 
 STEP = 896
 STEPS = D // STEP
 
 
-def hidden_kernel(own_ref, other_ref, gate_ref, up_ref, down_ref, hidden_ref, out_ref, gate_sum, up_sum):
+def hidden_kernel(*refs):
+    gate_ref, up_ref, down_ref, hidden_ref, out_ref, gate_sum, up_sum = refs[-7:]
     step = pl.program_id(0)
-    count = own_ref.shape[0]
-    x = jnp.concatenate([own_ref[...], other_ref[...]], axis=0)
+    count = hidden_ref.shape[0]
+    x = stack(refs[:-7])
     gate = jnp.dot(x, gate_ref[0], preferred_element_type=F32)
     up = jnp.dot(x, up_ref[0], preferred_element_type=F32)
 
@@ -119,32 +128,39 @@
 
 
 def hidden_rows(own, other, gate, up, down):
-    count = own.shape[0]
-    part = pl.BlockSpec((count, STEP), lambda k: (0, k))
+    rows = own[0].shape[0]
+    count = len(own) * rows
+    part = pl.BlockSpec((rows, STEP), lambda k: (0, k))
     weights = pl.BlockSpec((1, STEP, HALF), lambda k: (0, k, 0))
     return call(
         hidden_kernel,
         "expert_hidden",
         grid=(STEPS,),
-        in_specs=[part, part, weights, weights, pl.BlockSpec((1, HALF, D), lambda k: (0, 0, 0))],
+        in_specs=[part] * (2 * len(own))
+        + [weights, weights, pl.BlockSpec((1, HALF, D), lambda k: (0, 0, 0))],
         out_specs=[
             pl.BlockSpec((count, HALF), lambda k: (0, 0)),
             pl.BlockSpec((count, D), lambda k: (0, 0)),
         ],
         scratch_shapes=[pltpu.VMEM((2 * count, HALF), F32)] * 2,
         out_shape=[jax.ShapeDtypeStruct((count, HALF), BF16), jax.ShapeDtypeStruct((count, D), BF16)],
-    )(own, other, gate, up, down)
-
-
-def down_kernel(hidden_ref, down_ref, other_ref, out_ref):
+    )(*own, *other, gate, up, down)
+
+
+def down_kernel(hidden_ref, down_ref, other_ref, *out_refs):
     own = jnp.dot(hidden_ref[...], down_ref[0], preferred_element_type=F32).astype(BF16)
-    out_ref[...] = (own.astype(F32) + other_ref[...].astype(F32)).astype(BF16)
-
-
-def down_own(hidden, down, other):
-    return call(down_kernel, "down_own_rows", out_shape=jax.ShapeDtypeStruct(other.shape, BF16))(
-        hidden, down, other
-    )
+    both = (own.astype(F32) + other_ref[...].astype(F32)).astype(BF16)
+    rows = out_refs[0].shape[0]
+    for place, out_ref in enumerate(out_refs):
+        out_ref[...] = both[place * rows : (place + 1) * rows]
+
+
+def down_own(hidden, down, other, experts):
+    return call(
+        down_kernel,
+        "down_own_rows",
+        out_shape=[jax.ShapeDtypeStruct((other.shape[0] // experts, D), BF16)] * experts,
+    )(hidden, down, other)
 
 
 def split_kernel(x_ref, out_ref):
@@ -322,33 +338,35 @@
     rows = -(-capacity // 8) * 8
     rank = lax.axis_index("ctx").astype(jnp.int32).reshape(1)
 
+    named = routes ^ (rank // 2)
+    chips = range(1, experts)
+
     keys = jnp.stack([latent_kv] + [send(latent_kv, offset) for offset in gather_order(shards)[1:4]])
     other_key = send(key_proj, 1)
     other_value = send(value_proj, 1)
 
-    buckets = after(build_buckets(routes, moe_input, experts, rows), keys)
-    own = swap_chips(buckets.reshape(experts, rows, D))
-    sent = after(split_queries(queries, experts), own)
+    buckets = build_buckets(named, moe_input, experts, rows)
+    own = [buckets[0]] + [send(buckets[m], 2 * m) for m in chips]
+    sent = after(split_queries(queries, experts), keys, *own)
     held = swap_chips(sent)
 
-    own = own.reshape(experts * rows, D)
     mask = shards // 8
     while mask:
         keys = jnp.concatenate([keys, send(keys, mask)], axis=0)
         mask //= 2
-    other = send(own, 1)
-    own = after(own, keys, other_key, other_value)
+    other = [send(piece, 1) for piece in own]
+    own[0] = after(own[0], keys, other_key, other_value)
     hidden, for_other = hidden_rows(own, other, expert_gate, expert_up, expert_down)
-    result = down_own(hidden, expert_down, send(for_other, 1))
-
-    result, held = lax.optimization_barrier((result, held))
-    back = swap_chips(result.reshape(experts, rows, D))
+    result = down_own(hidden, expert_down, send(for_other, 1), experts)
+    back = [result[0]] + [send(result[m], 2 * m) for m in chips]
+
+    held = after(held, *result)
     values = attention(
         rank, held.reshape(experts * tok, held.shape[2]), keys, key_proj, other_key, value_proj, other_value
     )
-    values, back = lax.optimization_barrier((values, back))
+    values, *back = lax.optimization_barrier((values, *back))
     values = swap_chips(values.reshape(experts, tok, values.shape[1]))
-    moe_out = combine(routes, gates, back.reshape(experts * rows, D), rows)
+    moe_out = combine(named, gates, back, rows)
     attention_out = values.transpose(1, 0, 2).reshape(tok, HEADS * VDIM)
     return (attention_out, moe_out)
 

time: 161 us -> 151 us (0.938)
  waiting for transfers between devices: 90.1 us -> 54.2 us
  starting transfers between devices: 25.6 us -> 49.6 us
  local copies, waits for them, and re-layouts: 7.52 us -> 9.76 us
    all_to_all x4 -> x2, waiting for transfers between devices: 82.9 us -> 22.8 us  [swap_chips(): lax.all_to_all(array, 'ctx', split_axis=0, concat_axis=0, axis_index_grou...]
    ppermute x9 -> x30, waiting for transfers between devices: 7.2 us -> 31.4 us  [send(): lax.ppermute(array, 'ctx', [(i, i ^ mask) for i in range(lax.axis_size('c...]
    ppermute x9 -> x30, starting transfers between devices: 9 us -> 33.2 us  [send(): lax.ppermute(array, 'ctx', [(i, i ^ mask) for i in range(lax.axis_size('c...]
    unnamed x26 -> x18, local copies, waits for them, and re-layouts: 4.64 us -> 6.89 us
    all_to_all x4 -> x2, starting transfers between devices: 16.6 us -> 16.4 us  [swap_chips(): lax.all_to_all(array, 'ctx', split_axis=0, concat_axis=0, axis_index_grou...]
  transfers between devices with their start and end apart: 13 -> 32, of which waited for: 8 -> 10; matrix products, arithmetic and copies ran while one was open for 3% -> 4% of each run, Pallas kernels for 23% -> 24%
where the time goes in v4:
time: 151 us; the launch traced here: 150 us
  waiting for transfers between devices  54.2 us (36%)
  starting transfers between devices  49.6 us (33%)
  Pallas kernels  36.1 us (24%)
  local copies, waits for them, and re-layouts  9.76 us (6%)
    ppermute x30, starting transfers between devices, send(): lax.ppermute(array, 'ctx', [(i, i ^ mask) for i in range(lax.axis_size('c...  33.2 us
    ppermute x30, waiting for transfers between devices, send(): lax.ppermute(array, 'ctx', [(i, i ^ mask) for i in range(lax.axis_size('c...  31.4 us
    all_to_all x2, waiting for transfers between devices, swap_chips(): lax.all_to_all(array, 'ctx', split_axis=0, concat_axis=0, axis_index_grou...  22.8 us
    pallas_call x1, Pallas kernels, attention(): call(functools.partial(attention_kernel, per_core), 'causal_attention', g...  16.5 us
    all_to_all x2, starting transfers between devices, swap_chips(): lax.all_to_all(array, 'ctx', split_axis=0, concat_axis=0, axis_index_grou...  16.4 us
    pallas_call x1, Pallas kernels, hidden_rows(): call(hidden_kernel, 'expert_hidden', grid=(STEPS,), in_specs=[part] * (2...  9.98 us
    unnamed x18, local copies, waits for them, and re-layouts  6.89 us
    pallas_call x1, Pallas kernels, down_own(): call(down_kernel, 'down_own_rows', out_shape=[jax.ShapeDtypeStruct((other...  3.81 us
  transfers between devices with their start and end apart: 32, of which 10 were waited for; matrix products, arithmetic and copies ran while one was open for 4% of the time, Pallas kernels for 24%

profile of v4, /device:TPU:0, one launch (start us, length us, event | category | flops | bytes accessed | tf_op | source)
XLA Modules:
  0.0 150.5 jit_solution(544852913154790759)
XLA Ops:
  0.6 4.1 %collective-permute-start = (bf16[64,576]{1,0:T(8,128)(2,1)}, bf16[64,576]{1,0:T(8,128)(2,1)S(1)}, u32[]{:S(2)}, u32[]{:S(2)}) collective-permute-start(bf16[64,576]{1,0:T(8,128)(2,1)} %param.11), channel_id=1, source_target_pairs={{0,8},{1,9},{2,10},{3,11},{4,12},{5,13},{6,14},{7,15},{8,0},{9,1},... | collective-permute-start | bytes 221192 | tf_op jit(solution)/shard_map/ppermute | solution.py:293
  4.7 1.6 %collective-permute-start.1 = (bf16[64,576]{1,0:T(8,128)(2,1)}, bf16[64,576]{1,0:T(8,128)(2,1)S(1)}, u32[]{:S(2)}, u32[]{:S(2)}) collective-permute-start(bf16[64,576]{1,0:T(8,128)(2,1)} %param.11), channel_id=1, source_target_pairs={{0,4},{1,5},{2,6},{3,7},{4,0},{5,1},{6,2},{7,3},{8,12},{9,13},{10,... | collective-permute-start | bytes 221192 | tf_op jit(solution)/shard_map/ppermute | solution.py:293
  6.3 0.0 collective-permute-start.2
  6.3 0.8 copy.12
  7.1 1.0 copy-done.3
  8.1 0.9 bucket_rows.1
  9.0 1.8 %collective-permute-start.3 = (bf16[24,3584]{1,0:T(8,128)(2,1)S(1)}, bf16[24,3584]{1,0:T(8,128)(2,1)S(1)}, u32[]{:S(2)}, u32[]{:S(2)}) collective-permute-start(bf16[24,3584]{1,0:T(8,128)(2,1)S(1)} %get-tuple-element.33), channel_id=1, source_target_pairs={{0,2},{1,3},{2,0},{3,1},{4,6},{5,7},{6,4},{7,5},{8,10},{9,11},{10,... | collective-permute-start | bytes 516104 | tf_op jit(solution)/shard_map/ppermute | solution.py:293
  10.8 0.7 collective-permute-start.4
  11.5 1.6 %constant_dynamic-update-slice_fusion.4 = (bf16[8,64,576]{2,1,0:T(8,128)(2,1)}, bf16[16,64,576]{2,1,0:T(8,128)(2,1)}) fusion(bf16[64,576]{1,0:T(8,128)(2,1)} %param.11), kind=kLoop, calls=%fused_computation.5 | loop fusion | bytes 237568
  13.1 1.4 copy-done
  14.5 3.3 %split_queries.1 = bf16[8,64,1536]{2,1,0:T(8,128)(2,1)} custom-call(bf16[64,12288]{1,0:T(8,128)(2,1)S(1)} %copy-done), custom_call_target="tpu_custom_call" | custom-call | flops 1 | bytes 1 | tf_op jit(solution)/shard_map/split_queries/pallas_call | solution.py:177
  17.8 1.1 collective-permute-start.5
  18.9 0.7 constant_dynamic-update-slice_fusion.3
  19.5 0.0 collective-permute-done.1
  19.5 2.4 %collective-permute-start.6 = (bf16[24,3584]{1,0:T(8,128)(2,1)S(1)}, bf16[24,3584]{1,0:T(8,128)(2,1)S(1)}, u32[]{:S(2)}, u32[]{:S(2)}) collective-permute-start(bf16[24,3584]{1,0:T(8,128)(2,1)S(1)} %get-tuple-element.36), channel_id=1, source_target_pairs={{0,8},{1,9},{2,10},{3,11},{4,12},{5,13},{6,14},{7,15},{8,0},{9,1},... | collective-permute-start | bytes 516104 | tf_op jit(solution)/shard_map/ppermute | solution.py:293
  22.0 0.0 collective-permute-done.2
  22.0 1.7 %collective-permute-start.7 = (bf16[24,3584]{1,0:T(8,128)(2,1)S(1)}, bf16[24,3584]{1,0:T(8,128)(2,1)S(1)}, u32[]{:S(2)}, u32[]{:S(2)}) collective-permute-start(bf16[24,3584]{1,0:T(8,128)(2,1)S(1)} %get-tuple-element.37), channel_id=1, source_target_pairs={{0,10},{1,11},{2,8},{3,9},{4,14},{5,15},{6,12},{7,13},{8,2},{9,3},... | collective-permute-start | bytes 516104 | tf_op jit(solution)/shard_map/ppermute | solution.py:293
  23.7 0.1 pad_maximum_fusion
  23.7 0.0 collective-permute-done.3.refs_1_
  23.7 3.7 %collective-permute-start.8 = (bf16[24,3584]{1,0:T(8,128)(2,1)S(1)}, bf16[24,3584]{1,0:T(8,128)(2,1)S(1)}, u32[]{:S(2)}, u32[]{:S(2)}) collective-permute-start(bf16[24,3584]{1,0:T(8,128)(2,1)S(1)} %get-tuple-element.38), channel_id=1, source_target_pairs={{0,12},{1,13},{2,14},{3,15},{4,8},{5,9},{6,10},{7,11},{8,4},{9,5},... | collective-permute-start | bytes 516104 | tf_op jit(solution)/shard_map/ppermute | solution.py:293
  27.4 0.0 collective-permute-done.4.refs_2_
  27.4 0.0 collective-permute-start.9
  27.4 1.7 %collective-permute-start.10 = (bf16[4,64,576]{2,1,0:T(8,128)(2,1)S(1)}, bf16[4,64,576]{2,1,0:T(8,128)(2,1)S(1)}, u32[]{:S(2)}, u32[]{:S(2)}) collective-permute-start(bf16[4,64,576]{2,1,0:T(8,128)(2,1)S(1)} %pad_maximum_fusion), channel_id=1, source_target_pairs={{0,2},{1,3},{2,0},{3,1},{4,6},{5,7},{6,4},{7,5},{8,10},{9,11},{10,... | collective-permute-start | bytes 884744 | tf_op jit(solution)/shard_map/ppermute | solution.py:293
  29.1 0.7 constant_dynamic-update-slice_fusion.2
  29.8 12.1 %collective-permute-done.6.refs_4_ = bf16[24,3584]{1,0:T(8,128)(2,1)S(1)} collective-permute-done((bf16[24,3584]{1,0:T(8,128)(2,1)S(1)}, bf16[24,3584]{1,0:T(8,128)(2,1)S(1)}, u32[]{:S(2)}, u32[]{:S(2)}) %collective-permute-start.6) | collective-permute-done | bytes 172064 | tf_op jit(solution)/shard_map/ppermute | solution.py:293
  41.9 4.8 %collective-permute-done.7.refs_5_ = bf16[24,3584]{1,0:T(8,128)(2,1)S(1)} collective-permute-done((bf16[24,3584]{1,0:T(8,128)(2,1)S(1)}, bf16[24,3584]{1,0:T(8,128)(2,1)S(1)}, u32[]{:S(2)}, u32[]{:S(2)}) %collective-permute-start.7) | collective-permute-done | bytes 172064 | tf_op jit(solution)/shard_map/ppermute | solution.py:293
  46.7 0.0 copy-start.2
  46.7 9.1 %all-to-all-start = ((bf16[8,64,1536]{2,1,0:T(8,128)(2,1)}), bf16[8,64,1536]{2,1,0:T(8,128)(2,1)}, u32[]{:S(2)}, u32[]{:S(2)}) async-start(bf16[8,64,1536]{2,1,0:T(8,128)(2,1)} %split_queries.1), calls=%async_computation | async-start | bytes 3145728 | tf_op jit(solution)/shard_map/all_to_all | solution.py:298
  55.8 0.7 constant_dynamic-update-slice_fusion.1
  56.5 0.9 constant_dynamic-update-slice_fusion
  57.4 0.5 collective-permute-start.12
  58.0 0.1 collective-permute-start.13
  58.0 0.4 collective-permute-start.14
  58.5 0.1 collective-permute-start.15
  58.5 2.7 %collective-permute-done.14.refs_8_ = bf16[24,3584]{1,0:T(8,128)(2,1)S(1)} collective-permute-done((bf16[24,3584]{1,0:T(8,128)(2,1)S(1)}, bf16[24,3584]{1,0:T(8,128)(2,1)S(1)}, u32[]{:S(2)}, u32[]{:S(2)}) %collective-permute-start.14) | collective-permute-done | bytes 172064 | tf_op jit(solution)/shard_map/ppermute | solution.py:293
  61.3 0.1 collective-permute-start.16
  61.4 0.1 collective-permute-done.15.refs_9_
  61.5 0.3 collective-permute-start.17
  61.8 0.9 collective-permute-done.16.refs_10_
  62.7 0.1 collective-permute-start.18
  62.8 0.4 collective-permute-start.19
  63.2 0.1 collective-permute-start.20
  63.4 0.4 collective-permute-start.21
  63.7 0.9 constant_dynamic-update-slice_fusion.5.kv_ref
  64.7 0.2 collective-permute-done.21.refs_15_
  64.9 10.0 %expert_hidden.1 = (bf16[192,512]{1,0:T(8,128)(2,1)S(1)}, bf16[192,3584]{1,0:T(8,128)(2,1)}) custom-call(bf16[24,3584]{1,0:T(8,128)(2,1)S(1)} %get-tuple-element.41.refs_0_, bf16[24,3584]{1,0:T(8,128)(2,1)S(1)} %collective-permute-done.3.refs_1_, bf16[24,3584]{1,0:T(8,128)(2,1)S(1)} %collective-permute-done.4.refs_2_, ...), custom_call_target="tpu_custom_call" | custom-call | flops 1 | bytes 1 | tf_op jit(solution)/shard_map/expert_hidden/pallas_call | solution.py:135
  74.8 0.3 collective-permute-start.22
  75.1 3.1 %collective-permute-done.22.other_ref = bf16[192,3584]{1,0:T(8,128)(2,1)S(1)} collective-permute-done((bf16[192,3584]{1,0:T(8,128)(2,1)}, bf16[192,3584]{1,0:T(8,128)(2,1)S(1)}, u32[]{:S(2)}, u32[]{:S(2)}) %collective-permute-start.22) | collective-permute-done | bytes 1376288 | tf_op jit(solution)/shard_map/ppermute | solution.py:293
  78.2 3.8 %down_own_rows.1 = (bf16[24,3584]{1,0:T(8,128)(2,1)S(1)}, bf16[24,3584]{1,0:T(8,128)(2,1)S(1)}, bf16[24,3584]{1,0:T(8,128)(2,1)S(1)}, bf16[24,3584]{1,0:T(8,128)...) custom-call(bf16[192,512]{1,0:T(8,128)(2,1)S(1)} %get-tuple-element., ...), custom_call_target="tpu_custom_call" | custom-call | flops 1 | bytes 1 | tf_op jit(solution)/shard_map/down_own_rows/pallas_call | solution.py:159
  82.0 2.0 %collective-permute-start.23 = (bf16[24,3584]{1,0:T(8,128)(2,1)S(1)}, bf16[24,3584]{1,0:T(8,128)(2,1)S(1)}, u32[]{:S(2)}, u32[]{:S(2)}) collective-permute-start(bf16[24,3584]{1,0:T(8,128)(2,1)S(1)} %get-tuple-element.45), channel_id=1, source_target_pairs={{0,2},{1,3},{2,0},{3,1},{4,6},{5,7},{6,4},{7,5},{8,10},{9,11},{10,... | collective-permute-start | bytes 516104 | tf_op jit(solution)/shard_map/ppermute | solution.py:293
  84.0 1.5 collective-permute-start.24
  85.5 0.0 collective-permute-start.25
  85.5 3.0 %collective-permute-start.26 = (bf16[24,3584]{1,0:T(8,128)(2,1)}, bf16[24,3584]{1,0:T(8,128)(2,1)S(1)}, u32[]{:S(2)}, u32[]{:S(2)}) collective-permute-start(bf16[24,3584]{1,0:T(8,128)(2,1)} %get-tuple-element.48), channel_id=1, source_target_pairs={{0,8},{1,9},{2,10},{3,11},{4,12},{5,13},{6,14},{7,15},{8,0},{9,1},... | collective-permute-start | bytes 516104 | tf_op jit(solution)/shard_map/ppermute | solution.py:293
  88.5 1.4 collective-permute-start.27
  89.8 1.0 collective-permute-done.23.refs_1_
  90.8 2.3 %collective-permute-start.28 = (bf16[24,3584]{1,0:T(8,128)(2,1)}, bf16[24,3584]{1,0:T(8,128)(2,1)S(1)}, u32[]{:S(2)}, u32[]{:S(2)}) collective-permute-start(bf16[24,3584]{1,0:T(8,128)(2,1)} %get-tuple-element.50), channel_id=1, source_target_pairs={{0,12},{1,13},{2,14},{3,15},{4,8},{5,9},{6,10},{7,11},{8,4},{9,5},... | collective-permute-start | bytes 516104 | tf_op jit(solution)/shard_map/ppermute | solution.py:293
  93.1 6.5 %collective-permute-done.24.refs_2_ = bf16[24,3584]{1,0:T(8,128)(2,1)S(1)} collective-permute-done((bf16[24,3584]{1,0:T(8,128)(2,1)S(1)}, bf16[24,3584]{1,0:T(8,128)(2,1)S(1)}, u32[]{:S(2)}, u32[]{:S(2)}) %collective-permute-start.24) | collective-permute-done | bytes 172064 | tf_op jit(solution)/shard_map/ppermute | solution.py:293
  99.6 1.5 %collective-permute-start.29 = (bf16[24,3584]{1,0:T(8,128)(2,1)}, bf16[24,3584]{1,0:T(8,128)(2,1)S(1)}, u32[]{:S(2)}, u32[]{:S(2)}) collective-permute-start(bf16[24,3584]{1,0:T(8,128)(2,1)} %get-tuple-element.51), channel_id=1, source_target_pairs={{0,14},{1,15},{2,12},{3,13},{4,10},{5,11},{6,8},{7,9},{8,6},{9,7},... | collective-permute-start | bytes 516104 | tf_op jit(solution)/shard_map/ppermute | solution.py:293
  101.1 16.5 %causal_attention.1 = bf16[512,1024]{1,0:T(8,128)(2,1)} custom-call(s32[1]{0:T(128)} %bitcast.rank_ref, bf16[512,1536]{1,0:T(8,128)(2,1)} %bitcast.6.plain_ref.rope_ref, bf16[512,1536]{1,0:T(8,128)(2,1)} %bitcast.6.plain_ref.rope_ref, bf16[16,64,576]{2,1,0:T(8,128)(2,1)} %constant_dynamic-update-slice_fusion.5.kv_ref, bf16[4,128,512]{2,1,0:T(8,128)(2,1)S(1)} %copy-done.1, ...), custom_call_target="tpu_custom_call" | custom-call | flops 1 | bytes 1 | tf_op jit(solution)/shard_map/causal_attention/pallas_call | solution.py:266
  117.7 7.3 %all-to-all-start.1 = ((bf16[8,64,1024]{2,1,0:T(8,128)(2,1)}), bf16[8,64,1024]{2,1,0:T(8,128)(2,1)S(1)}, u32[]{:S(2)}, u32[]{:S(2)}) async-start(bf16[8,64,1024]{2,1,0:T(8,128)(2,1)} %bitcast.7), calls=%async_computation.1 | async-start | bytes 2097152 | tf_op jit(solution)/shard_map/all_to_all | solution.py:298
  125.0 0.1 copy.14.gates_ref
  125.1 1.5 %combine_routes.1 = bf16[64,3584]{1,0:T(8,128)(2,1)} custom-call(s32[64,2]{1,0:T(8,128)S(1)} %broadcast_xor_fusion.routes_ref, f32[64,2]{1,0:T(8,128)S(1)} %copy.14.gates_ref, bf16[24,3584]{1,0:T(8,128)(2,1)S(1)} %get-tuple-element.54.refs_0_, bf16[24,3584]{1,0:T(8,128)(2,1)S(1)} %collective-permute-done.23.refs_1_, ...), custom_call_target="tpu_custom_call" | custom-call | flops 1 | bytes 1 | tf_op jit(solution)/shard_map/combine_routes/pallas_call | solution.py:93
  126.6 22.8 %all-to-all-done.1 = bf16[8,64,1024]{2,1,0:T(8,128)(2,1)S(1)} async-done(((bf16[8,64,1024]{2,1,0:T(8,128)(2,1)}), bf16[8,64,1024]{2,1,0:T(8,128)(2,1)S(1)}, u32[]{:S(2)}, u32[]{:S(2)}) %all-to-all-start.1) | async-done | bytes 1048608 | tf_op jit(solution)/shard_map/all_to_all | solution.py:298
  149.4 1.1 copy.15
  (29 shorter events, 0.1 us)
Async XLA Ops:
  0.6 17.2 %collective-permute-start = (bf16[64,576]{1,0:T(8,128)(2,1)}, bf16[64,576]{1,0:T(8,128)(2,1)S(1)}, u32[]{:S(2)}, u32[]{:S(2)}) collective-permute-start(bf16[64,576]{1,0:T(8,128)(2,1)} %param.11), channel_id=1, source_target_pairs={{0,8},{1,9},{2,10},{3,11},{4,12},{5,13},{6,14},{7,15},{8,0},{9,1},... | collective-permute-start | bytes 221192 | tf_op jit(solution)/shard_map/ppermute | solution.py:293
  4.7 14.8 %collective-permute-start.1 = (bf16[64,576]{1,0:T(8,128)(2,1)}, bf16[64,576]{1,0:T(8,128)(2,1)S(1)}, u32[]{:S(2)}, u32[]{:S(2)}) collective-permute-start(bf16[64,576]{1,0:T(8,128)(2,1)} %param.11), channel_id=1, source_target_pairs={{0,4},{1,5},{2,6},{3,7},{4,0},{5,1},{6,2},{7,3},{8,12},{9,13},{10,... | collective-permute-start | bytes 221192 | tf_op jit(solution)/shard_map/ppermute | solution.py:293
  6.3 15.7 %collective-permute-start.2 = (bf16[64,576]{1,0:T(8,128)(2,1)}, bf16[64,576]{1,0:T(8,128)(2,1)S(1)}, u32[]{:S(2)}, u32[]{:S(2)}) collective-permute-start(bf16[64,576]{1,0:T(8,128)(2,1)} %param.11), channel_id=1, source_target_pairs={{0,12},{1,13},{2,14},{3,15},{4,8},{5,9},{6,10},{7,11},{8,4},{9,5},... | collective-permute-start | bytes 221192 | tf_op jit(solution)/shard_map/ppermute | solution.py:293
  7.1 1.0 copy-start.3
  9.0 14.7 %collective-permute-start.3 = (bf16[24,3584]{1,0:T(8,128)(2,1)S(1)}, bf16[24,3584]{1,0:T(8,128)(2,1)S(1)}, u32[]{:S(2)}, u32[]{:S(2)}) collective-permute-start(bf16[24,3584]{1,0:T(8,128)(2,1)S(1)} %get-tuple-element.33), channel_id=1, source_target_pairs={{0,2},{1,3},{2,0},{3,1},{4,6},{5,7},{6,4},{7,5},{8,10},{9,11},{10,... | collective-permute-start | bytes 516104 | tf_op jit(solution)/shard_map/ppermute | solution.py:293
  10.8 16.6 %collective-permute-start.4 = (bf16[24,3584]{1,0:T(8,128)(2,1)S(1)}, bf16[24,3584]{1,0:T(8,128)(2,1)S(1)}, u32[]{:S(2)}, u32[]{:S(2)}) collective-permute-start(bf16[24,3584]{1,0:T(8,128)(2,1)S(1)} %get-tuple-element.34), channel_id=1, source_target_pairs={{0,4},{1,5},{2,6},{3,7},{4,0},{5,1},{6,2},{7,3},{8,12},{9,13},{10,... | collective-permute-start | bytes 516104 | tf_op jit(solution)/shard_map/ppermute | solution.py:293
  13.1 1.4 copy-start
  14.5 9.2 %copy-start.4 = (bf16[64,576]{1,0:T(8,128)(2,1)S(1)}, bf16[64,576]{1,0:T(8,128)(2,1)}, u32[]{:S(2)}) copy-start(bf16[64,576]{1,0:T(8,128)(2,1)} %param.11) | copy-start | bytes 221188
  17.8 9.6 %collective-permute-start.5 = (bf16[24,3584]{1,0:T(8,128)(2,1)S(1)}, bf16[24,3584]{1,0:T(8,128)(2,1)S(1)}, u32[]{:S(2)}, u32[]{:S(2)}) collective-permute-start(bf16[24,3584]{1,0:T(8,128)(2,1)S(1)} %get-tuple-element.35), channel_id=1, source_target_pairs={{0,6},{1,7},{2,4},{3,5},{4,2},{5,3},{6,0},{7,1},{8,14},{9,15},{10,... | collective-permute-start | bytes 516104 | tf_op jit(solution)/shard_map/ppermute | solution.py:293
  19.5 22.3 %collective-permute-start.6 = (bf16[24,3584]{1,0:T(8,128)(2,1)S(1)}, bf16[24,3584]{1,0:T(8,128)(2,1)S(1)}, u32[]{:S(2)}, u32[]{:S(2)}) collective-permute-start(bf16[24,3584]{1,0:T(8,128)(2,1)S(1)} %get-tuple-element.36), channel_id=1, source_target_pairs={{0,8},{1,9},{2,10},{3,11},{4,12},{5,13},{6,14},{7,15},{8,0},{9,1},... | collective-permute-start | bytes 516104 | tf_op jit(solution)/shard_map/ppermute | solution.py:293
  22.0 24.7 %collective-permute-start.7 = (bf16[24,3584]{1,0:T(8,128)(2,1)S(1)}, bf16[24,3584]{1,0:T(8,128)(2,1)S(1)}, u32[]{:S(2)}, u32[]{:S(2)}) collective-permute-start(bf16[24,3584]{1,0:T(8,128)(2,1)S(1)} %get-tuple-element.37), channel_id=1, source_target_pairs={{0,10},{1,11},{2,8},{3,9},{4,14},{5,15},{6,12},{7,13},{8,2},{9,3},... | collective-permute-start | bytes 516104 | tf_op jit(solution)/shard_map/ppermute | solution.py:293
  23.7 22.9 %collective-permute-start.8 = (bf16[24,3584]{1,0:T(8,128)(2,1)S(1)}, bf16[24,3584]{1,0:T(8,128)(2,1)S(1)}, u32[]{:S(2)}, u32[]{:S(2)}) collective-permute-start(bf16[24,3584]{1,0:T(8,128)(2,1)S(1)} %get-tuple-element.38), channel_id=1, source_target_pairs={{0,12},{1,13},{2,14},{3,15},{4,8},{5,9},{6,10},{7,11},{8,4},{9,5},... | collective-permute-start | bytes 516104 | tf_op jit(solution)/shard_map/ppermute | solution.py:293
  27.4 19.3 %collective-permute-start.9 = (bf16[24,3584]{1,0:T(8,128)(2,1)S(1)}, bf16[24,3584]{1,0:T(8,128)(2,1)S(1)}, u32[]{:S(2)}, u32[]{:S(2)}) collective-permute-start(bf16[24,3584]{1,0:T(8,128)(2,1)S(1)} %get-tuple-element.39), channel_id=1, source_target_pairs={{0,14},{1,15},{2,12},{3,13},{4,10},{5,11},{6,8},{7,9},{8,6},{9,7},... | collective-permute-start | bytes 516104 | tf_op jit(solution)/shard_map/ppermute | solution.py:293
  27.4 29.1 %collective-permute-start.10 = (bf16[4,64,576]{2,1,0:T(8,128)(2,1)S(1)}, bf16[4,64,576]{2,1,0:T(8,128)(2,1)S(1)}, u32[]{:S(2)}, u32[]{:S(2)}) collective-permute-start(bf16[4,64,576]{2,1,0:T(8,128)(2,1)S(1)} %pad_maximum_fusion), channel_id=1, source_target_pairs={{0,2},{1,3},{2,0},{3,1},{4,6},{5,7},{6,4},{7,5},{8,10},{9,11},{10,... | collective-permute-start | bytes 884744 | tf_op jit(solution)/shard_map/ppermute | solution.py:293
  46.7 10.8 %copy-start.1 = (bf16[4,128,512]{2,1,0:T(8,128)(2,1)S(1)}, bf16[4,128,512]{2,1,0:T(8,128)(2,1)}, u32[]{:S(2)}) copy-start(bf16[4,128,512]{2,1,0:T(8,128)(2,1)} %own_key_ref.1) | copy-start | bytes 1572868
  46.7 11.3 %copy-start.2 = (bf16[4,512,128]{2,1,0:T(8,128)(2,1)S(1)}, bf16[4,512,128]{2,1,0:T(8,128)(2,1)}, u32[]{:S(2)}) copy-start(bf16[4,512,128]{2,1,0:T(8,128)(2,1)} %own_value_ref.1) | copy-start | bytes 1572868
  46.7 54.4 %all-to-all-start = ((bf16[8,64,1536]{2,1,0:T(8,128)(2,1)}), bf16[8,64,1536]{2,1,0:T(8,128)(2,1)}, u32[]{:S(2)}, u32[]{:S(2)}) async-start(bf16[8,64,1536]{2,1,0:T(8,128)(2,1)} %split_queries.1), calls=%async_computation | async-start | bytes 3145728 | tf_op jit(solution)/shard_map/all_to_all | solution.py:298
  57.4 5.9 %collective-permute-start.11 = (bf16[8,64,576]{2,1,0:T(8,128)(2,1)}, bf16[8,64,576]{2,1,0:T(8,128)(2,1)S(1)}, u32[]{:S(2)}, u32[]{:S(2)}) collective-permute-start(bf16[8,64,576]{2,1,0:T(8,128)(2,1)} %get-tuple-element.62), channel_id=1, source_target_pairs={{0,1},{1,0},{2,3},{3,2},{4,5},{5,4},{6,7},{7,6},{8,9},{9,8},{10,11... | collective-permute-start | bytes 1769480 | tf_op jit(solution)/shard_map/ppermute | solution.py:293
  57.4 5.4 %collective-permute-start.12 = (bf16[4,128,512]{2,1,0:T(8,128)(2,1)S(1)}, bf16[4,128,512]{2,1,0:T(8,128)(2,1)S(1)}, u32[]{:S(2)}, u32[]{:S(2)}) collective-permute-start(bf16[4,128,512]{2,1,0:T(8,128)(2,1)S(1)} %copy-done.1), channel_id=1, source_target_pairs={{0,1},{1,0},{2,3},{3,2},{4,5},{5,4},{6,7},{7,6},{8,9},{9,8},{10,11... | collective-permute-start | bytes 1572872 | tf_op jit(solution)/shard_map/ppermute | solution.py:293
  58.0 5.3 %collective-permute-start.13 = (bf16[4,512,128]{2,1,0:T(8,128)(2,1)S(1)}, bf16[4,512,128]{2,1,0:T(8,128)(2,1)S(1)}, u32[]{:S(2)}, u32[]{:S(2)}) collective-permute-start(bf16[4,512,128]{2,1,0:T(8,128)(2,1)S(1)} %copy-done.2), channel_id=1, source_target_pairs={{0,1},{1,0},{2,3},{3,2},{4,5},{5,4},{6,7},{7,6},{8,9},{9,8},{10,11... | collective-permute-start | bytes 1572872 | tf_op jit(solution)/shard_map/ppermute | solution.py:293
  58.0 3.3 %collective-permute-start.14 = (bf16[24,3584]{1,0:T(8,128)(2,1)S(1)}, bf16[24,3584]{1,0:T(8,128)(2,1)S(1)}, u32[]{:S(2)}, u32[]{:S(2)}) collective-permute-start(bf16[24,3584]{1,0:T(8,128)(2,1)S(1)} %get-tuple-element.41.refs_0_), channel_id=1, source_target_pairs={{0,1},{1,0},{2,3},{3,2},{4,5},{5,4},{6,7},{7,6},{8,9},{9,8},{10,11... | collective-permute-start | bytes 516104 | tf_op jit(solution)/shard_map/ppermute | solution.py:293
  58.5 3.1 %collective-permute-start.15 = (bf16[24,3584]{1,0:T(8,128)(2,1)S(1)}, bf16[24,3584]{1,0:T(8,128)(2,1)S(1)}, u32[]{:S(2)}, u32[]{:S(2)}) collective-permute-start(bf16[24,3584]{1,0:T(8,128)(2,1)S(1)} %collective-permute-done.3.refs_1_), channel_id=1, source_target_pairs={{0,1},{1,0},{2,3},{3,2},{4,5},{5,4},{6,7},{7,6},{8,9},{9,8},{10,11... | collective-permute-start | bytes 516104 | tf_op jit(solution)/shard_map/ppermute | solution.py:293
  61.3 1.4 collective-permute-start.16
  61.5 3.1 %collective-permute-start.17 = (bf16[24,3584]{1,0:T(8,128)(2,1)S(1)}, bf16[24,3584]{1,0:T(8,128)(2,1)S(1)}, u32[]{:S(2)}, u32[]{:S(2)}) collective-permute-start(bf16[24,3584]{1,0:T(8,128)(2,1)S(1)} %collective-permute-done.5.refs_3_), channel_id=1, source_target_pairs={{0,1},{1,0},{2,3},{3,2},{4,5},{5,4},{6,7},{7,6},{8,9},{9,8},{10,11... | collective-permute-start | bytes 516104 | tf_op jit(solution)/shard_map/ppermute | solution.py:293
  62.7 2.0 %collective-permute-start.18 = (bf16[24,3584]{1,0:T(8,128)(2,1)S(1)}, bf16[24,3584]{1,0:T(8,128)(2,1)S(1)}, u32[]{:S(2)}, u32[]{:S(2)}) collective-permute-start(bf16[24,3584]{1,0:T(8,128)(2,1)S(1)} %collective-permute-done.6.refs_4_), channel_id=1, source_target_pairs={{0,1},{1,0},{2,3},{3,2},{4,5},{5,4},{6,7},{7,6},{8,9},{9,8},{10,11... | collective-permute-start | bytes 516104 | tf_op jit(solution)/shard_map/ppermute | solution.py:293
  62.8 1.8 %collective-permute-start.19 = (bf16[24,3584]{1,0:T(8,128)(2,1)S(1)}, bf16[24,3584]{1,0:T(8,128)(2,1)S(1)}, u32[]{:S(2)}, u32[]{:S(2)}) collective-permute-start(bf16[24,3584]{1,0:T(8,128)(2,1)S(1)} %collective-permute-done.7.refs_5_), channel_id=1, source_target_pairs={{0,1},{1,0},{2,3},{3,2},{4,5},{5,4},{6,7},{7,6},{8,9},{9,8},{10,11... | collective-permute-start | bytes 516104 | tf_op jit(solution)/shard_map/ppermute | solution.py:293
  63.2 1.4 collective-permute-start.20
  63.4 1.5 %collective-permute-start.21 = (bf16[24,3584]{1,0:T(8,128)(2,1)S(1)}, bf16[24,3584]{1,0:T(8,128)(2,1)S(1)}, u32[]{:S(2)}, u32[]{:S(2)}) collective-permute-start(bf16[24,3584]{1,0:T(8,128)(2,1)S(1)} %collective-permute-done.9.refs_7_), channel_id=1, source_target_pairs={{0,1},{1,0},{2,3},{3,2},{4,5},{5,4},{6,7},{7,6},{8,9},{9,8},{10,11... | collective-permute-start | bytes 516104 | tf_op jit(solution)/shard_map/ppermute | solution.py:293
  74.8 3.3 %collective-permute-start.22 = (bf16[192,3584]{1,0:T(8,128)(2,1)}, bf16[192,3584]{1,0:T(8,128)(2,1)S(1)}, u32[]{:S(2)}, u32[]{:S(2)}) collective-permute-start(bf16[192,3584]{1,0:T(8,128)(2,1)} %get-tuple-element.43), channel_id=1, source_target_pairs={{0,1},{1,0},{2,3},{3,2},{4,5},{5,4},{6,7},{7,6},{8,9},{9,8},{10,11... | collective-permute-start | bytes 4128776 | tf_op jit(solution)/shard_map/ppermute | solution.py:293
  82.0 8.8 %collective-permute-start.23 = (bf16[24,3584]{1,0:T(8,128)(2,1)S(1)}, bf16[24,3584]{1,0:T(8,128)(2,1)S(1)}, u32[]{:S(2)}, u32[]{:S(2)}) collective-permute-start(bf16[24,3584]{1,0:T(8,128)(2,1)S(1)} %get-tuple-element.45), channel_id=1, source_target_pairs={{0,2},{1,3},{2,0},{3,1},{4,6},{5,7},{6,4},{7,5},{8,10},{9,11},{10,... | collective-permute-start | bytes 516104 | tf_op jit(solution)/shard_map/ppermute | solution.py:293
  84.0 15.6 %collective-permute-start.24 = (bf16[24,3584]{1,0:T(8,128)(2,1)S(1)}, bf16[24,3584]{1,0:T(8,128)(2,1)S(1)}, u32[]{:S(2)}, u32[]{:S(2)}) collective-permute-start(bf16[24,3584]{1,0:T(8,128)(2,1)S(1)} %get-tuple-element.46), channel_id=1, source_target_pairs={{0,4},{1,5},{2,6},{3,7},{4,0},{5,1},{6,2},{7,3},{8,12},{9,13},{10,... | collective-permute-start | bytes 516104 | tf_op jit(solution)/shard_map/ppermute | solution.py:293
  85.5 32.2 %collective-permute-start.25 = (bf16[24,3584]{1,0:T(8,128)(2,1)}, bf16[24,3584]{1,0:T(8,128)(2,1)S(1)}, u32[]{:S(2)}, u32[]{:S(2)}) collective-permute-start(bf16[24,3584]{1,0:T(8,128)(2,1)} %get-tuple-element.47), channel_id=1, source_target_pairs={{0,6},{1,7},{2,4},{3,5},{4,2},{5,3},{6,0},{7,1},{8,14},{9,15},{10,... | collective-permute-start | bytes 516104 | tf_op jit(solution)/shard_map/ppermute | solution.py:293
  85.5 32.2 %collective-permute-start.26 = (bf16[24,3584]{1,0:T(8,128)(2,1)}, bf16[24,3584]{1,0:T(8,128)(2,1)S(1)}, u32[]{:S(2)}, u32[]{:S(2)}) collective-permute-start(bf16[24,3584]{1,0:T(8,128)(2,1)} %get-tuple-element.48), channel_id=1, source_target_pairs={{0,8},{1,9},{2,10},{3,11},{4,12},{5,13},{6,14},{7,15},{8,0},{9,1},... | collective-permute-start | bytes 516104 | tf_op jit(solution)/shard_map/ppermute | solution.py:293
  88.5 29.2 %collective-permute-start.27 = (bf16[24,3584]{1,0:T(8,128)(2,1)}, bf16[24,3584]{1,0:T(8,128)(2,1)S(1)}, u32[]{:S(2)}, u32[]{:S(2)}) collective-permute-start(bf16[24,3584]{1,0:T(8,128)(2,1)} %get-tuple-element.49), channel_id=1, source_target_pairs={{0,10},{1,11},{2,8},{3,9},{4,14},{5,15},{6,12},{7,13},{8,2},{9,3},... | collective-permute-start | bytes 516104 | tf_op jit(solution)/shard_map/ppermute | solution.py:293
  90.8 26.9 %collective-permute-start.28 = (bf16[24,3584]{1,0:T(8,128)(2,1)}, bf16[24,3584]{1,0:T(8,128)(2,1)S(1)}, u32[]{:S(2)}, u32[]{:S(2)}) collective-permute-start(bf16[24,3584]{1,0:T(8,128)(2,1)} %get-tuple-element.50), channel_id=1, source_target_pairs={{0,12},{1,13},{2,14},{3,15},{4,8},{5,9},{6,10},{7,11},{8,4},{9,5},... | collective-permute-start | bytes 516104 | tf_op jit(solution)/shard_map/ppermute | solution.py:293
  99.6 18.1 %collective-permute-start.29 = (bf16[24,3584]{1,0:T(8,128)(2,1)}, bf16[24,3584]{1,0:T(8,128)(2,1)S(1)}, u32[]{:S(2)}, u32[]{:S(2)}) collective-permute-start(bf16[24,3584]{1,0:T(8,128)(2,1)} %get-tuple-element.51), channel_id=1, source_target_pairs={{0,14},{1,15},{2,12},{3,13},{4,10},{5,11},{6,8},{7,9},{8,6},{9,7},... | collective-permute-start | bytes 516104 | tf_op jit(solution)/shard_map/ppermute | solution.py:293
  117.6 7.3 %copy-start.5 = (f32[64,2]{0,1:T(2,128)S(1)}, f32[64,2]{0,1:T(2,128)}, u32[]{:S(2)}) copy-start(f32[64,2]{0,1:T(2,128)} %param.16) | copy-start | bytes 1540
  117.7 31.7 %all-to-all-start.1 = ((bf16[8,64,1024]{2,1,0:T(8,128)(2,1)}), bf16[8,64,1024]{2,1,0:T(8,128)(2,1)S(1)}, u32[]{:S(2)}, u32[]{:S(2)}) async-start(bf16[8,64,1024]{2,1,0:T(8,128)(2,1)} %bitcast.7), calls=%async_computation.1 | async-start | bytes 2097152 | tf_op jit(solution)/shard_map/all_to_all | solution.py:298

commit v5 on v4

v5 whole, which is shorter than its diff:
```python
import functools
import math

import jax
import jax.numpy as jnp
from jax import lax
from jax.experimental import pallas as pl
from jax.experimental.pallas import tpu as pltpu
from jax.sharding import PartitionSpec as P

D = 3584
HEADS = 64
NOPE = 128
ROPE = 64
LATENT = 512
VDIM = 128
TOP = 2
HALF = 512
VMEM_LIMIT = 50 * 1024 * 1024
F32 = jnp.float32
BF16 = jnp.bfloat16


SMEM = pl.BlockSpec(memory_space=pltpu.SMEM)
VMEM = pl.BlockSpec(memory_space=pltpu.VMEM)
SMALL = pl.CostEstimate(flops=1, bytes_accessed=1, transcendentals=0)


def call(kernel, name, **options):
    return pl.pallas_call(
        kernel,
        name=name,
        cost_estimate=SMALL,
        compiler_params=pltpu.CompilerParams(vmem_limit_bytes=VMEM_LIMIT),
        **options,
    )


def slot_targets(routes, rows):
    tok = routes.shape[0]
    lane = lax.broadcasted_iota(jnp.int32, (tok, 128), 1)
    first = routes[:, 0:1]
    second = routes[:, 1:2]
    hot0 = jnp.where(lane == first, 1.0, 0.0)
    hot1 = jnp.where(lane == second, 1.0, 0.0)
    earlier = jnp.where(
        lax.broadcasted_iota(jnp.int32, (tok, tok), 1) < lax.broadcasted_iota(jnp.int32, (tok, tok), 0),
        1.0,
        0.0,
    )
    counts = jnp.dot(earlier.astype(BF16), (hot0 + hot1).astype(BF16), preferred_element_type=F32)
    slot0 = jnp.sum(counts * hot0, axis=1, keepdims=True).astype(jnp.int32)
    slot1 = jnp.sum(counts * hot1, axis=1, keepdims=True).astype(jnp.int32)
    return first * rows + slot0, second * rows + slot1


def bucket_kernel(rows, routes_ref, x_ref, *out_refs):
    target0, target1 = slot_targets(routes_ref[...], rows)
    column = lax.broadcasted_iota(jnp.int32, (x_ref.shape[0], len(out_refs) * rows), 1)
    chosen = jnp.where((column == target0) | (column == target1), 1.0, 0.0).astype(BF16)
    found = lax.dot_general(
        chosen, x_ref[...], (((0,), (0,)), ((), ())), preferred_element_type=F32
    ).astype(BF16)
    for place, out_ref in enumerate(out_refs):
        out_ref[...] = found[place * rows : (place + 1) * rows]


def build_buckets(routes, moe_input, experts, rows):
    return call(
        functools.partial(bucket_kernel, rows),
        "bucket_rows",
        out_shape=[jax.ShapeDtypeStruct((rows, D), BF16)] * experts,
    )(routes, moe_input)


def stack(refs):
    return jnp.concatenate([ref[...] for ref in refs], axis=0)


def combine_kernel(rows, routes_ref, gates_ref, back_ref, out_ref):
    back = back_ref[...]
    tok = routes_ref.shape[0]
    target0, target1 = slot_targets(routes_ref[...], rows)
    targets = jnp.concatenate([target0, target1], axis=0)
    column = lax.broadcasted_iota(jnp.int32, (2 * tok, back.shape[0]), 1)
    chosen = jnp.where(column == targets, 1.0, 0.0).astype(BF16)
    picked = jnp.dot(chosen, back, preferred_element_type=F32)
    out_ref[...] = (picked[:tok] * gates_ref[:, 0:1] + picked[tok:] * gates_ref[:, 1:2]).astype(BF16)


def combine(routes, gates, back, rows):
    return call(
        functools.partial(combine_kernel, rows),
        "combine_routes",
        out_shape=jax.ShapeDtypeStruct((routes.shape[0], D), BF16),
    )(routes, gates, back)


STEP = 896
STEPS = D // STEP


def hidden_kernel(*refs):
    gate_ref, up_ref, down_ref, hidden_ref, out_ref, gate_sum, up_sum = refs[-7:]
    step = pl.program_id(0)
    count = hidden_ref.shape[0]
    x = stack(refs[:-7])
    gate = jnp.dot(x, gate_ref[0], preferred_element_type=F32)
    up = jnp.dot(x, up_ref[0], preferred_element_type=F32)

    @pl.when(step == 0)
    def _():
        gate_sum[...] = gate
        up_sum[...] = up

    @pl.when(step > 0)
    def _():
        gate_sum[...] += gate
        up_sum[...] += up

    @pl.when(step == STEPS - 1)
    def _():
        value = gate_sum[...]
        hidden = (value / (1.0 + jnp.exp(-value)) * up_sum[...]).astype(BF16)
        hidden_ref[...] = hidden[:count]
        out_ref[...] = jnp.dot(hidden[count:], down_ref[0], preferred_element_type=F32).astype(BF16)


def hidden_rows(own, other, gate, up, down):
    rows = own[0].shape[0]
    count = len(own) * rows
    part = pl.BlockSpec((rows, STEP), lambda k: (0, k))
    weights = pl.BlockSpec((1, STEP, HALF), lambda k: (0, k, 0))
    return call(
        hidden_kernel,
        "expert_hidden",
        grid=(STEPS,),
        in_specs=[part] * (2 * len(own))
        + [weights, weights, pl.BlockSpec((1, HALF, D), lambda k: (0, 0, 0))],
        out_specs=[
            pl.BlockSpec((count, HALF), lambda k: (0, 0)),
            pl.BlockSpec((count, D), lambda k: (0, 0)),
        ],
        scratch_shapes=[pltpu.VMEM((2 * count, HALF), F32)] * 2,
        out_shape=[jax.ShapeDtypeStruct((count, HALF), BF16), jax.ShapeDtypeStruct((count, D), BF16)],
    )(*own, *other, gate, up, down)


def down_kernel(rank_ref, hidden_ref, down_ref, other_ref, out_ref):
    own = jnp.dot(hidden_ref[...], down_ref[0], preferred_element_type=F32).astype(BF16)
    both = (own.astype(F32) + other_ref[...].astype(F32)).astype(BF16)
    rows = out_ref.shape[1]
    for offset in range(out_ref.shape[0]):
        out_ref[(rank_ref[0] // 2) ^ offset] = both[offset * rows : (offset + 1) * rows]


def down_own(rank, hidden, down, other, experts):
    return call(
        down_kernel,
        "down_own_rows",
        in_specs=[SMEM, VMEM, VMEM, VMEM],
        out_specs=VMEM,
        out_shape=jax.ShapeDtypeStruct((experts, other.shape[0] // experts, D), BF16),
    )(rank, hidden, down, other)


class Split:
    def __init__(self, groups, shards, heads):
        self.groups, self.shards = groups, shards
        self.each = heads // shards
        self.wide = groups == 2 and self.each % (2 * groups) == 0
        self.chips = shards // 2
        self.own_pairs = self.each // 2 // (groups if self.wide else 1)
        self.holders = 2 if self.wide else 1
        self.pairs = 2 * self.holders * self.own_pairs
        self.parts = groups if self.wide else 1

    def first_head(self, rank, chip, pair):
        core, rest = divmod(pair, self.holders * self.own_pairs)
        holder, own = divmod(rest, self.own_pairs)
        if not self.wide:
            return (2 * chip + ((rank & 1) ^ core)) * self.each + 2 * own
        group, low = divmod(chip, self.shards // 4)
        top = (rank & (self.shards // 2)) ^ (holder * (self.shards // 2))
        return (top + 2 * low + ((rank & 1) ^ core)) * self.each + 2 * (group * self.own_pairs + own)

    def exchange(self, array):
        half = self.shards // 2
        if self.wide:
            tops, steps = (0, half), [g * self.shards + c for g in range(self.groups) for c in range(0, half, 2)]
            sets = [[start + core + step for step in steps] for start in tops for core in range(2)]
        else:
            starts = range(0, self.groups * self.shards, self.shards)
            sets = [[start + core + c for c in range(0, self.shards, 2)] for start in starts for core in range(2)]
        return lax.all_to_all(
            array, ("groups", "ctx"), split_axis=0, concat_axis=0, axis_index_groups=sets, tiled=True
        )


def split_kernel(split, rank_ref, x_ref, out_ref):
    each = NOPE + ROPE
    for chip in range(split.chips):
        for pair in range(split.pairs):
            start = pl.multiple_of(split.first_head(rank_ref[0], chip, pair) * each, 128)
            part = x_ref[:, pl.ds(start, 2 * each)]
            out_ref[chip, :, pair * 2 * each : (pair + 1) * 2 * each] = jnp.concatenate(
                [part[:, :NOPE], part[:, each : each + NOPE], part[:, NOPE:each], part[:, each + NOPE :]], axis=1
            )


def split_queries(split, rank, queries):
    tok = queries.shape[0]
    return call(
        functools.partial(split_kernel, split),
        "split_queries",
        in_specs=[SMEM, VMEM],
        out_specs=VMEM,
        out_shape=jax.ShapeDtypeStruct((split.chips, tok, 2 * split.pairs * (NOPE + ROPE)), BF16),
    )(rank, queries)


def join_kernel(split, rank_ref, x_ref, out_ref):
    for chip in range(split.chips):
        for pair in range(split.pairs):
            start = pl.multiple_of(split.first_head(rank_ref[0], chip, pair) * VDIM, 128)
            out_ref[:, pl.ds(start, 2 * VDIM)] = x_ref[chip, :, pair * 2 * VDIM : (pair + 1) * 2 * VDIM]


def join_values(split, rank, values):
    return call(
        functools.partial(join_kernel, split),
        "join_values",
        in_specs=[SMEM, VMEM],
        out_specs=VMEM,
        out_shape=jax.ShapeDtypeStruct((values.shape[1], HEADS * VDIM), BF16),
    )(rank, values)


BLOCK = 128
SPAN = 2 * BLOCK
EXP_SCALE = math.log2(math.e) / math.sqrt(NOPE + ROPE)


def attention_kernel(split, rank_ref, query_ref, kv_ref, weight_ref, out_ref, keys, queries, mixed):
    tok = kv_ref.shape[1]
    part_rows = query_ref.shape[0] // split.parts
    core = rank_ref[0] & 1

    @pl.when(pl.program_id(0) == 0)
    def _():
        for index, offset in enumerate(gather_order(split)):
            group, ctx = divmod(offset, split.shards)
            group = rank_ref[1] ^ group if split.wide else 0
            place = pl.ds(pl.multiple_of((rank_ref[0] ^ ctx) * tok, tok), tok)
            keys[group, place, : LATENT + ROPE] = kv_ref[index]
            keys[group, place, LATENT + ROPE :] = kv_ref[index, :, LATENT:]

    contract = (((1,), (1,)), ((), ()))
    side = lax.broadcasted_iota(jnp.int32, (1, 2 * ROPE), 1) // ROPE
    for one in range(2):
        latent = lax.dot_general(
            query_ref[:, one * NOPE : (one + 1) * NOPE], weight_ref[0, one], contract, preferred_element_type=F32
        )
        queries[one, :, :LATENT] = latent.astype(BF16)
        queries[one, :, LATENT:] = jnp.where(side == one, query_ref[:, 2 * NOPE :], jnp.zeros((), BF16))

    row = lax.broadcasted_iota(jnp.int32, (2 * BLOCK, SPAN), 0) % BLOCK
    position = (2 * (row // tok) + core) * tok + row % tok
    visible = lax.broadcasted_iota(jnp.int32, (2 * BLOCK, SPAN), 1) <= position

    def attend(part, block, before):
        start = before * SPAN
        first = part * part_rows + block * BLOCK
        rows = pl.ds(first, BLOCK)
        last = pl.ds(start, SPAN)
        query = jnp.concatenate([queries[0, rows, :], queries[1, rows, :]], axis=0)
        near = lax.dot_general(query, keys[part, last, :], contract, preferred_element_type=F32)
        near = jnp.where(visible, near, -1e30)
        top = jnp.max(near, axis=1, keepdims=True)
        if before:
            past = lax.dot_general(query, keys[part, :start, :], contract, preferred_element_type=F32)
            top = jnp.maximum(top, jnp.max(past, axis=1, keepdims=True))
        weights = jnp.exp2((near - top) * EXP_SCALE)
        total = jnp.sum(weights, axis=1, keepdims=True)
        summed = jnp.dot(weights.astype(BF16), keys[part, last, :LATENT], preferred_element_type=F32)
        if before:
            weights = jnp.exp2((past - top) * EXP_SCALE)
            total = total + jnp.sum(weights, axis=1, keepdims=True)
            summed = summed + jnp.dot(
                weights.astype(BF16), keys[part, :start, :LATENT], preferred_element_type=F32
            )
        result = (summed / total).astype(BF16)
        mixed[0, rows, :] = result[:BLOCK]
        mixed[1, rows, :] = result[BLOCK:]

    blocks = part_rows // BLOCK
    if split.wide:
        for half in range(2):

            @pl.when(rank_ref[0] // (split.shards // 2) == half)
            def _():
                for part in range(split.parts):
                    for block in range(blocks):
                        attend(part, block, half * blocks + block)

    else:
        for block in range(blocks):
            attend(0, block, block)

    for one in range(2):
        out_ref[:, one * VDIM : (one + 1) * VDIM] = jnp.dot(
            mixed[one], weight_ref[0, 2 + one], preferred_element_type=F32
        ).astype(BF16)


def attention(split, place, queries, keys, weights):
    count = queries.shape[0]
    length = keys.shape[0] * keys.shape[1] // split.parts
    return call(
        functools.partial(attention_kernel, split),
        "causal_attention",
        grid_spec=pltpu.PrefetchScalarGridSpec(
            num_scalar_prefetch=1,
            grid=(split.pairs,),
            in_specs=[
                pl.BlockSpec((count, 2 * (NOPE + ROPE)), lambda p, place: (0, p)),
                pl.BlockSpec(keys.shape, lambda p, place: (0, 0, 0)),
                pl.BlockSpec((1, 4, LATENT, VDIM), lambda p, place: (p, 0, 0, 0)),
            ],
            out_specs=pl.BlockSpec((count, 2 * VDIM), lambda p, place: (0, p)),
            scratch_shapes=[
                pltpu.VMEM((split.parts, length, LATENT + 2 * ROPE), BF16),
                pltpu.VMEM((2, count, LATENT + 2 * ROPE), BF16),
                pltpu.VMEM((2, count, LATENT), BF16),
            ],
        ),
        out_shape=jax.ShapeDtypeStruct((count, 2 * split.pairs * VDIM), BF16),
    )(place, queries, keys, weights)


def send(array, mask):
    count = lax.axis_size("groups") * lax.axis_size("ctx")
    return lax.ppermute(array, ("groups", "ctx"), [(i, i ^ mask) for i in range(count)])


def swap_chips(array):
    shards = lax.axis_size("ctx")
    return lax.all_to_all(
        array,
        "ctx",
        split_axis=0,
        concat_axis=0,
        axis_index_groups=[list(range(core, shards, 2)) for core in range(2)],
        tiled=True,
    )


def after(array, *others):
    return lax.optimization_barrier((array, *others))[0]


def gather_masks(split):
    top, below = split.shards // 2, split.shards // 4
    later = [1 << bit for bit in reversed(range(1, below.bit_length() - 1))]
    return [top, below, top ^ below], later + ([split.shards] if split.wide else []) + [1]


def gather_order(split):
    direct, later = gather_masks(split)
    order = [0] + direct
    for mask in later:
        order = order + [offset ^ mask for offset in order]
    return order


def on_device(
    queries,
    latent_kv,
    key_proj,
    value_proj,
    moe_input,
    routes,
    gates,
    expert_gate,
    expert_up,
    expert_down,
):
    shards = lax.axis_size("ctx")
    split = Split(lax.axis_size("groups"), shards, HEADS)
    tok = queries.shape[0]
    experts = shards // 2
    capacity = 2 * ((4 * tok * TOP + 6 * experts - 1) // (6 * experts))
    rows = -(-capacity // 8) * 8
    rank = lax.axis_index("ctx").astype(jnp.int32).reshape(1)
    group = lax.axis_index("groups").astype(jnp.int32).reshape(1)
    place = jnp.concatenate([rank, group])

    named = routes ^ (rank // 2)
    chips = range(1, experts)

    direct, later = gather_masks(split)
    keys = jnp.stack([latent_kv] + [send(latent_kv, offset) for offset in direct])
    for mask in later[:-1]:
        keys = jnp.concatenate([keys, send(keys, mask)], axis=0)

    buckets = build_buckets(named, moe_input, experts, rows)
    own = [buckets[0]] + [send(buckets[m], 2 * m) for m in chips]
    sent = after(split_queries(split, rank, queries), keys, *own)
    held = split.exchange(sent)

    weights = jnp.concatenate(
        [
            key_proj.swapaxes(1, 2).reshape(-1, 2, LATENT, NOPE),
            value_proj.reshape(-1, 2, LATENT, VDIM),
        ],
        axis=1,
    )
    if split.wide:
        weights = lax.dynamic_slice_in_dim(weights, group[0] * split.own_pairs, split.own_pairs, axis=0)
        weights = after(weights, *own)
        weights = jnp.concatenate([weights, send(weights, shards // 2)], axis=0)

    keys = jnp.concatenate([keys, send(keys, later[-1])], axis=0)
    other = [send(piece, 1) for piece in own]
    own[0] = after(own[0], keys)
    hidden, for_other = hidden_rows(own, other, expert_gate, expert_up, expert_down)
    result = down_own(rank, hidden, expert_down, send(for_other, 1), experts)
    weights = jnp.concatenate([weights, send(weights, 1)], axis=0)

    result, held, weights = lax.optimization_barrier((result, held, weights))
    back = swap_chips(result)
    values = attention(split, place, held.reshape(experts * tok, held.shape[2]), keys, weights)
    values, back = lax.optimization_barrier((values, back))
    values = split.exchange(values.reshape(experts, tok, values.shape[1]))
    moe_out = combine(routes, gates, back.reshape(experts * rows, D), rows)
    return (join_values(split, rank, values), moe_out)


def solution(mesh):
    return jax.shard_map(
        on_device,
        mesh=mesh,
        in_specs=(
            P(("groups", "ctx"), None),
            P(("groups", "ctx"), None),
            P("ctx", None, None),
            P("ctx", None, None),
            P(("groups", "ctx"), None),
            P(("groups", "ctx"), None),
            P(("groups", "ctx"), None),
            P("ctx", None, None),
            P("ctx", None, None),
            P("ctx", None, None),
        ),
        out_specs=(P(("groups", "ctx"), None), P(("groups", "ctx"), None)),
        check_vma=False,
    )
```

time: 151 us -> 163 us (1.079)
  waiting for transfers between devices: 54.2 us -> 62.4 us
  local copies, waits for them, and re-layouts: 9.76 us -> 14.4 us
  other arithmetic: 0.07 us -> 3.77 us
  Pallas kernels: 36.1 us -> 32.5 us
    all_to_all x0 -> x2, waiting for transfers between devices: none -> 13.1 us  [exchange(): lax.all_to_all(array, ('groups', 'ctx'), split_axis=0, concat_axis=0, axi...]
    all_to_all x0 -> x2, starting transfers between devices: none -> 11 us  [exchange(): lax.all_to_all(array, ('groups', 'ctx'), split_axis=0, concat_axis=0, axi...]
    all_to_all x2 -> x1, starting transfers between devices: 16.4 us -> 8.36 us  [swap_chips(): lax.all_to_all(array, 'ctx', split_axis=0, concat_axis=0, axis_index_grou...]
    all_to_all x2 -> x1, waiting for transfers between devices: 22.8 us -> 17.7 us  [swap_chips(): lax.all_to_all(array, 'ctx', split_axis=0, concat_axis=0, axis_index_grou...]
    ppermute x30 -> x24, starting transfers between devices: 33.2 us -> 29.4 us  [send(): lax.ppermute(array, ('groups', 'ctx'), [(i, i ^ mask) for i in range(coun...]
    pallas_call x3 -> x4, Pallas kernels: 23.7 us -> 20 us  [the longest x1 14.3 us: attention(): call(functools.partial(attention_kernel, split), 'causal_attention', grid...]
    concatenate x0 -> x4, other arithmetic: none -> 2.81 us  [the longest x1 1.56 us: on_device(): weights = jnp.concatenate([weights, send(weights, 1)], axis=0)]
    concatenate x0 -> x1, local copies, waits for them, and re-layouts: none -> 2.5 us  [on_device(): keys = jnp.concatenate([keys, send(keys, later[-1])], axis=0)]
  transfers between devices with their start and end apart: 32 -> 27, of which waited for: 10 -> 12; matrix products, arithmetic and copies ran while one was open for 4% -> 8% of each run, Pallas kernels for 24% -> 19%
where the time goes in v5:
time: 163 us
  waiting for transfers between devices  62.4 us (38%)
  starting transfers between devices  48.8 us (30%)
  Pallas kernels  32.5 us (20%)
  local copies, waits for them, and re-layouts  14.4 us (9%)
  other arithmetic  3.77 us (2%)
    ppermute x24, waiting for transfers between devices, send(): lax.ppermute(array, ('groups', 'ctx'), [(i, i ^ mask) for i in range(coun...  31.5 us
    ppermute x24, starting transfers between devices, send(): lax.ppermute(array, ('groups', 'ctx'), [(i, i ^ mask) for i in range(coun...  29.4 us
    all_to_all x1, waiting for transfers between devices, swap_chips(): lax.all_to_all(array, 'ctx', split_axis=0, concat_axis=0, axis_index_grou...  17.7 us
    pallas_call x1, Pallas kernels, attention(): call(functools.partial(attention_kernel, split), 'causal_attention', grid...  14.3 us
    all_to_all x2, waiting for transfers between devices, exchange(): lax.all_to_all(array, ('groups', 'ctx'), split_axis=0, concat_axis=0, axi...  13.1 us
    all_to_all x2, starting transfers between devices, exchange(): lax.all_to_all(array, ('groups', 'ctx'), split_axis=0, concat_axis=0, axi...  11 us
    pallas_call x1, Pallas kernels, hidden_rows(): call(hidden_kernel, 'expert_hidden', grid=(STEPS,), in_specs=[part] * (2...  10 us
    unnamed x29, local copies, waits for them, and re-layouts  8.81 us
  transfers between devices with their start and end apart: 27, of which 12 were waited for; matrix products, arithmetic and copies ran while one was open for 8% of the time, Pallas kernels for 19%

profile of v5, /device:TPU:0, one launch (start us, length us, event | category | flops | bytes accessed | tf_op | source)
XLA Modules:
  0.0 162.5 jit_solution(7705326646682617718)
XLA Ops:
  0.7 4.1 %collective-permute-start = (bf16[64,576]{1,0:T(8,128)(2,1)}, bf16[64,576]{1,0:T(8,128)(2,1)S(1)}, u32[]{:S(2)}, u32[]{:S(2)}) collective-permute-start(bf16[64,576]{1,0:T(8,128)(2,1)} %param.11), channel_id=1, source_target_pairs={{0,8},{1,9},{2,10},{3,11},{4,12},{5,13},{6,14},{7,15},{8,0},{9,1},... | collective-permute-start | bytes 221192 | tf_op jit(solution)/shard_map/ppermute | solution.py:343
  4.8 1.6 collective-permute-start.1
  6.3 1.6 %constant_dynamic-update-slice_fusion.10 = (bf16[16,64,576]{2,1,0:T(8,128)(2,1)S(1)}, bf16[8,64,576]{2,1,0:T(8,128)(2,1)}, bf16[32,64,576]{2,1,0:T(8,128)(2,1)}) fusion(bf16[64,576]{1,0:T(8,128)(2,1)} %param.11), kind=kLoop, calls=%fused_computation.16 | loop fusion | bytes 319488
  8.0 1.0 collective-permute-done
  9.0 0.5 collective-permute-done.1
  9.5 3.3 %collective-permute-done.2 = bf16[64,576]{1,0:T(8,128)(2,1)S(1)} collective-permute-done((bf16[64,576]{1,0:T(8,128)(2,1)}, bf16[64,576]{1,0:T(8,128)(2,1)S(1)}, u32[]{:S(2)}, u32[]{:S(2)}) %collective-permute-start.2) | collective-permute-done | bytes 73760 | tf_op jit(solution)/shard_map/ppermute | solution.py:343
  12.8 1.0 pad_maximum_fusion.2
  13.7 1.7 %collective-permute-start.3 = (bf16[4,64,576]{2,1,0:T(8,128)(2,1)S(1)}, bf16[4,64,576]{2,1,0:T(8,128)(2,1)S(1)}, u32[]{:S(2)}, u32[]{:S(2)}) collective-permute-start(bf16[4,64,576]{2,1,0:T(8,128)(2,1)S(1)} %pad_maximum_fusion.2), channel_id=1, source_target_pairs={{0,2},{1,3},{2,0},{3,1},{4,6},{5,7},{6,4},{7,5},{8,10},{9,11},{10,... | collective-permute-start | bytes 884744 | tf_op jit(solution)/shard_map/ppermute | solution.py:343
  15.4 0.7 constant_dynamic-update-slice_fusion.9
  16.1 0.7 constant_dynamic-update-slice_fusion.8
  16.8 0.7 constant_dynamic-update-slice_fusion.7
  17.5 4.2 %collective-permute-done.3 = bf16[4,64,576]{2,1,0:T(8,128)(2,1)S(1)} collective-permute-done((bf16[4,64,576]{2,1,0:T(8,128)(2,1)S(1)}, bf16[4,64,576]{2,1,0:T(8,128)(2,1)S(1)}, u32[]{:S(2)}, u32[]{:S(2)}) %collective-permute-start.3) | collective-permute-done | bytes 294944 | tf_op jit(solution)/shard_map/ppermute | solution.py:343
  21.7 0.9 constant_dynamic-update-slice_fusion.6
  22.6 1.1 copy-done.6
  23.7 1.5 collective-permute-start.4
  25.2 0.1 copy.16.routes_ref
  25.3 0.9 bucket_rows.1
  26.2 1.6 collective-permute-start.6
  27.8 2.3 %collective-permute-start.7 = (bf16[24,3584]{1,0:T(8,128)(2,1)S(1)}, bf16[24,3584]{1,0:T(8,128)(2,1)S(1)}, u32[]{:S(2)}, u32[]{:S(2)}) collective-permute-start(bf16[24,3584]{1,0:T(8,128)(2,1)S(1)} %get-tuple-element.23), channel_id=1, source_target_pairs={{0,4},{1,5},{2,6},{3,7},{4,0},{5,1},{6,2},{7,3},{8,12},{9,13},{10,... | collective-permute-start | bytes 516104 | tf_op jit(solution)/shard_map/ppermute | solution.py:343
  30.2 0.0 collective-permute-start.8
  30.2 3.8 %collective-permute-start.9 = (bf16[24,3584]{1,0:T(8,128)(2,1)S(1)}, bf16[24,3584]{1,0:T(8,128)(2,1)S(1)}, u32[]{:S(2)}, u32[]{:S(2)}) collective-permute-start(bf16[24,3584]{1,0:T(8,128)(2,1)S(1)} %get-tuple-element.25), channel_id=1, source_target_pairs={{0,8},{1,9},{2,10},{3,11},{4,12},{5,13},{6,14},{7,15},{8,0},{9,1},... | collective-permute-start | bytes 516104 | tf_op jit(solution)/shard_map/ppermute | solution.py:343
  33.9 4.7 %collective-permute-start.10 = (bf16[24,3584]{1,0:T(8,128)(2,1)S(1)}, bf16[24,3584]{1,0:T(8,128)(2,1)S(1)}, u32[]{:S(2)}, u32[]{:S(2)}) collective-permute-start(bf16[24,3584]{1,0:T(8,128)(2,1)S(1)} %get-tuple-element.26), channel_id=1, source_target_pairs={{0,10},{1,11},{2,8},{3,9},{4,14},{5,15},{6,12},{7,13},{8,2},{9,3},... | collective-permute-start | bytes 516104 | tf_op jit(solution)/shard_map/ppermute | solution.py:343
  38.7 1.1 collective-permute-done.7.refs_2_
  39.7 3.5 %collective-permute-start.11 = (bf16[24,3584]{1,0:T(8,128)(2,1)S(1)}, bf16[24,3584]{1,0:T(8,128)(2,1)S(1)}, u32[]{:S(2)}, u32[]{:S(2)}) collective-permute-start(bf16[24,3584]{1,0:T(8,128)(2,1)S(1)} %get-tuple-element.27), channel_id=1, source_target_pairs={{0,12},{1,13},{2,14},{3,15},{4,8},{5,9},{6,10},{7,11},{8,4},{9,5},... | collective-permute-start | bytes 516104 | tf_op jit(solution)/shard_map/ppermute | solution.py:343
  43.2 0.0 collective-permute-done.4
  43.2 0.8 copy-done.4
  44.1 1.5 split_queries.1
  45.6 1.0 constant_dynamic-update-slice_fusion.5
  46.6 0.0 collective-permute-done.8.refs_3_
  46.6 11.9 %collective-permute-done.10.refs_5_ = bf16[24,3584]{1,0:T(8,128)(2,1)S(1)} collective-permute-done((bf16[24,3584]{1,0:T(8,128)(2,1)S(1)}, bf16[24,3584]{1,0:T(8,128)(2,1)S(1)}, u32[]{:S(2)}, u32[]{:S(2)}) %collective-permute-start.10) | collective-permute-done | bytes 172064 | tf_op jit(solution)/shard_map/ppermute | solution.py:343
  58.5 7.4 %all-to-all-start = ((bf16[8,64,1536]{2,1,0:T(8,128)(2,1)}), bf16[8,64,1536]{2,1,0:T(8,128)(2,1)S(1)}, u32[]{:S(2)}, u32[]{:S(2)}) async-start(bf16[8,64,1536]{2,1,0:T(8,128)(2,1)} %split_queries.1), calls=%async_computation | async-start | bytes 3145728 | tf_op jit(solution)/shard_map/all_to_all | solution.py:195
  65.9 0.5 collective-permute-start.13
  66.4 2.0 %copy.18 = bf16[4,512,128]{2,1,0:T(8,128)(2,1)} copy(bf16[4,512,128]{1,2,0:T(8,128)(2,1)} %bitcast.29) | data formatting | bytes 1048576 | tf_op jit(solution)/shard_map/transpose | solution.py:413
  68.5 1.1 fusion
  69.5 2.4 %collective-permute-start.22 = (bf16[1,4,512,128]{3,2,1,0:T(8,128)(2,1)S(1)}, bf16[1,4,512,128]{3,2,1,0:T(8,128)(2,1)S(1)}, u32[]{:S(2)}, u32[]{:S(2)}) collective-permute-start(bf16[1,4,512,128]{3,2,1,0:T(8,128)(2,1)S(1)} %fusion), channel_id=1, source_target_pairs={{0,8},{1,9},{2,10},{3,11},{4,12},{5,13},{6,14},{7,15},{8,0},{9,1},... | collective-permute-start | bytes 1572872 | tf_op jit(solution)/shard_map/ppermute | solution.py:343
  72.0 0.5 collective-permute-start.15
  72.5 0.0 collective-permute-start.16
  72.5 0.9 collective-permute-done.14.refs_9_
  73.4 0.1 collective-permute-start.17
  73.5 0.1 collective-permute-done.15.refs_10_
  73.6 0.3 collective-permute-start.18
  73.9 0.2 collective-permute-start.19
  74.1 0.3 collective-permute-start.20
  74.4 2.5 %constant_dynamic-update-slice_fusion.11.kv_ref = bf16[32,64,576]{2,1,0:T(8,128)(2,1)} fusion(bf16[32,64,576]{2,1,0:T(8,128)(2,1)} %get-tuple-element.39, bf16[16,64,576]{2,1,0:T(8,128)(2,1)} %collective-permute-done.5), kind=kLoop, calls=%fused_computation.17 | loop fusion | bytes 2621440 | tf_op jit(solution)/shard_map/concatenate | solution.py:423
  76.9 10.0 %expert_hidden.1 = (bf16[192,512]{1,0:T(8,128)(2,1)S(1)}, bf16[192,3584]{1,0:T(8,128)(2,1)}) custom-call(bf16[24,3584]{1,0:T(8,128)(2,1)S(1)} %get-tuple-element.21.refs_0_, bf16[24,3584]{1,0:T(8,128)(2,1)S(1)} %collective-permute-done.6.refs_1_, bf16[24,3584]{1,0:T(8,128)(2,1)S(1)} %collective-permute-done.7.refs_2_, ...), custom_call_target="tpu_custom_call" | custom-call | flops 1 | bytes 1 | tf_op jit(solution)/shard_map/expert_hidden/pallas_call | solution.py:134
  87.0 0.2 collective-permute-start.21
  87.2 5.9 %collective-permute-done.22 = bf16[1,4,512,128]{3,2,1,0:T(8,128)(2,1)S(1)} collective-permute-done((bf16[1,4,512,128]{3,2,1,0:T(8,128)(2,1)S(1)}, bf16[1,4,512,128]{3,2,1,0:T(8,128)(2,1)S(1)}, u32[]{:S(2)}, u32[]{:S(2)}) %collective-permute-start.22) | collective-permute-done | bytes 524320 | tf_op jit(solution)/shard_map/ppermute | solution.py:343
  93.1 0.1 pad_maximum_fusion.1
  93.2 0.1 collective-permute-start.23
  93.3 2.6 %collective-permute-done.23 = bf16[2,4,512,128]{3,2,1,0:T(8,128)(2,1)S(1)} collective-permute-done((bf16[2,4,512,128]{3,2,1,0:T(8,128)(2,1)S(1)}, bf16[2,4,512,128]{3,2,1,0:T(8,128)(2,1)S(1)}, u32[]{:S(2)}, u32[]{:S(2)}) %collective-permute-start.23) | collective-permute-done | bytes 1048608 | tf_op jit(solution)/shard_map/ppermute | solution.py:343
  95.9 1.6 pad_maximum_fusion.weight_ref
  97.5 3.0 %down_own_rows.1 = bf16[8,24,3584]{2,1,0:T(8,128)(2,1)S(1)} custom-call(s32[1]{0:T(128)} %bitcast.rank_ref, bf16[192,512]{1,0:T(8,128)(2,1)S(1)} %get-tuple-element.29.hidden_ref, bf16[1,512,3584]{2,1,0:T(8,128)(2,1)} %down_ref.1, bf16[192,3584]{1,0:T(8,128)(2,1)S(1)} %collective-permute-done.21.other_ref), custom_call_target="tpu_custom_call" | custom-call | flops 1 | bytes 1 | tf_op jit(solution)/shard_map/down_own_rows/pallas_call | solution.py:158
  100.5 1.1 copy-done
  101.6 8.4 %all-to-all-start.1 = ((bf16[8,24,3584]{2,1,0:T(8,128)(2,1)}), bf16[8,24,3584]{2,1,0:T(8,128)(2,1)S(1)}, u32[]{:S(2)}, u32[]{:S(2)}) async-start(bf16[8,24,3584]{2,1,0:T(8,128)(2,1)} %copy-done), calls=%async_computation.1 | async-start | bytes 2752512 | tf_op jit(solution)/shard_map/all_to_all | solution.py:348
  110.0 0.1 pad_add_fusion.rank_ref
  110.0 14.3 %causal_attention.1 = bf16[512,1024]{1,0:T(8,128)(2,1)S(1)} custom-call(s32[2]{0:T(128)S(1)} %pad_add_fusion.rank_ref, bf16[512,1536]{1,0:T(8,128)(2,1)S(1)} %bitcast.25, bf16[32,64,576]{2,1,0:T(8,128)(2,1)} %constant_dynamic-update-slice_fusion.11.kv_ref, bf16[4,4,512,128]{3,2,1,0:T(8,128)(2,1)} %pad_maximum_fusion.weight_ref), custom_call_target="tpu_custom_call" | custom-call | flops 1 | bytes 1 | tf_op jit(solution)/shard_map/causal_attention/pallas_call | solution.py:319
  124.4 0.0 copy-start.1
  124.4 1.0 copy-done.1
  125.4 17.7 %all-to-all-done.1 = bf16[8,24,3584]{2,1,0:T(8,128)(2,1)S(1)} async-done(((bf16[8,24,3584]{2,1,0:T(8,128)(2,1)}), bf16[8,24,3584]{2,1,0:T(8,128)(2,1)S(1)}, u32[]{:S(2)}, u32[]{:S(2)}) %all-to-all-start.1) | async-done | bytes 1376288 | tf_op jit(solution)/shard_map/all_to_all | solution.py:348
  143.1 3.6 %all-to-all-start.2 = ((bf16[8,64,1024]{2,1,0:T(8,128)(2,1)}), bf16[8,64,1024]{2,1,0:T(8,128)(2,1)S(1)}, u32[]{:S(2)}, u32[]{:S(2)}) async-start(bf16[8,64,1024]{2,1,0:T(8,128)(2,1)} %bitcast.27), calls=%async_computation.2 | async-start | bytes 2097152 | tf_op jit(solution)/shard_map/all_to_all | solution.py:195
  146.7 0.1 copy.20.gates_ref
  146.8 1.6 combine_routes.1
  148.3 13.1 %all-to-all-done.2.x_ref = bf16[8,64,1024]{2,1,0:T(8,128)(2,1)S(1)} async-done(((bf16[8,64,1024]{2,1,0:T(8,128)(2,1)}), bf16[8,64,1024]{2,1,0:T(8,128)(2,1)S(1)}, u32[]{:S(2)}, u32[]{:S(2)}) %all-to-all-start.2) | async-done | bytes 1048608 | tf_op jit(solution)/shard_map/all_to_all | solution.py:195
  161.5 1.1 join_values.1
  (35 shorter events, 0.1 us)
Async XLA Ops:
  0.6 24.6 %copy-start.9 = (s32[64,2]{0,1:T(2,128)S(1)}, s32[64,2]{0,1:T(2,128)}, u32[]{:S(2)}) copy-start(s32[64,2]{0,1:T(2,128)} %param.15) | copy-start | bytes 1540
  0.6 24.7 %copy-start.3 = (bf16[64,3584]{1,0:T(8,128)(2,1)S(1)}, bf16[64,3584]{1,0:T(8,128)(2,1)}, u32[]{:S(2)}) copy-start(bf16[64,3584]{1,0:T(8,128)(2,1)} %x_ref.2) | copy-start | bytes 1376260
  0.6 43.4 %copy-start.2 = (bf16[64,12288]{1,0:T(8,128)(2,1)S(1)}, bf16[64,12288]{1,0:T(8,128)(2,1)}, u32[]{:S(2)}) copy-start(bf16[64,12288]{1,0:T(8,128)(2,1)} %x_ref.3) | copy-start | bytes 4718596
  0.7 8.3 %collective-permute-start = (bf16[64,576]{1,0:T(8,128)(2,1)}, bf16[64,576]{1,0:T(8,128)(2,1)S(1)}, u32[]{:S(2)}, u32[]{:S(2)}) collective-permute-start(bf16[64,576]{1,0:T(8,128)(2,1)} %param.11), channel_id=1, source_target_pairs={{0,8},{1,9},{2,10},{3,11},{4,12},{5,13},{6,14},{7,15},{8,0},{9,1},... | collective-permute-start | bytes 221192 | tf_op jit(solution)/shard_map/ppermute | solution.py:343
  4.8 4.8 %collective-permute-start.1 = (bf16[64,576]{1,0:T(8,128)(2,1)}, bf16[64,576]{1,0:T(8,128)(2,1)S(1)}, u32[]{:S(2)}, u32[]{:S(2)}) collective-permute-start(bf16[64,576]{1,0:T(8,128)(2,1)} %param.11), channel_id=1, source_target_pairs={{0,4},{1,5},{2,6},{3,7},{4,0},{5,1},{6,2},{7,3},{8,12},{9,13},{10,... | collective-permute-start | bytes 221192 | tf_op jit(solution)/shard_map/ppermute | solution.py:343
  6.3 6.4 %collective-permute-start.2 = (bf16[64,576]{1,0:T(8,128)(2,1)}, bf16[64,576]{1,0:T(8,128)(2,1)S(1)}, u32[]{:S(2)}, u32[]{:S(2)}) collective-permute-start(bf16[64,576]{1,0:T(8,128)(2,1)} %param.11), channel_id=1, source_target_pairs={{0,12},{1,13},{2,14},{3,15},{4,8},{5,9},{6,10},{7,11},{8,4},{9,5},... | collective-permute-start | bytes 221192 | tf_op jit(solution)/shard_map/ppermute | solution.py:343
  13.7 7.9 %collective-permute-start.3 = (bf16[4,64,576]{2,1,0:T(8,128)(2,1)S(1)}, bf16[4,64,576]{2,1,0:T(8,128)(2,1)S(1)}, u32[]{:S(2)}, u32[]{:S(2)}) collective-permute-start(bf16[4,64,576]{2,1,0:T(8,128)(2,1)S(1)} %pad_maximum_fusion.2), channel_id=1, source_target_pairs={{0,2},{1,3},{2,0},{3,1},{4,6},{5,7},{6,4},{7,5},{8,10},{9,11},{10,... | collective-permute-start | bytes 884744 | tf_op jit(solution)/shard_map/ppermute | solution.py:343
  22.6 1.1 copy-start.6
  23.7 19.5 %collective-permute-start.4 = (bf16[8,64,576]{2,1,0:T(8,128)(2,1)}, bf16[8,64,576]{2,1,0:T(8,128)(2,1)S(1)}, u32[]{:S(2)}, u32[]{:S(2)}) collective-permute-start(bf16[8,64,576]{2,1,0:T(8,128)(2,1)} %get-tuple-element.42), channel_id=1, source_target_pairs={{0,16},{1,17},{2,18},{3,19},{4,20},{5,21},{6,22},{7,23},{8,24},{9,... | collective-permute-start | bytes 1769480 | tf_op jit(solution)/shard_map/ppermute | solution.py:343
  25.3 20.3 %copy-start.7 = (bf16[16,64,576]{2,1,0:T(8,128)(2,1)S(1)}, bf16[16,64,576]{2,1,0:T(8,128)(2,1)}, u32[]{:S(2)}) copy-start(bf16[16,64,576]{2,1,0:T(8,128)(2,1)} %copy-done.6) | copy-start | bytes 3538948
  26.2 7.7 %collective-permute-start.6 = (bf16[24,3584]{1,0:T(8,128)(2,1)S(1)}, bf16[24,3584]{1,0:T(8,128)(2,1)S(1)}, u32[]{:S(2)}, u32[]{:S(2)}) collective-permute-start(bf16[24,3584]{1,0:T(8,128)(2,1)S(1)} %get-tuple-element.22), channel_id=1, source_target_pairs={{0,2},{1,3},{2,0},{3,1},{4,6},{5,7},{6,4},{7,5},{8,10},{9,11},{10,... | collective-permute-start | bytes 516104 | tf_op jit(solution)/shard_map/ppermute | solution.py:343
  27.8 11.9 %collective-permute-start.7 = (bf16[24,3584]{1,0:T(8,128)(2,1)S(1)}, bf16[24,3584]{1,0:T(8,128)(2,1)S(1)}, u32[]{:S(2)}, u32[]{:S(2)}) collective-permute-start(bf16[24,3584]{1,0:T(8,128)(2,1)S(1)} %get-tuple-element.23), channel_id=1, source_target_pairs={{0,4},{1,5},{2,6},{3,7},{4,0},{5,1},{6,2},{7,3},{8,12},{9,13},{10,... | collective-permute-start | bytes 516104 | tf_op jit(solution)/shard_map/ppermute | solution.py:343
  30.2 16.5 %collective-permute-start.8 = (bf16[24,3584]{1,0:T(8,128)(2,1)S(1)}, bf16[24,3584]{1,0:T(8,128)(2,1)S(1)}, u32[]{:S(2)}, u32[]{:S(2)}) collective-permute-start(bf16[24,3584]{1,0:T(8,128)(2,1)S(1)} %get-tuple-element.24), channel_id=1, source_target_pairs={{0,6},{1,7},{2,4},{3,5},{4,2},{5,3},{6,0},{7,1},{8,14},{9,15},{10,... | collective-permute-start | bytes 516104 | tf_op jit(solution)/shard_map/ppermute | solution.py:343
  30.2 16.5 %collective-permute-start.9 = (bf16[24,3584]{1,0:T(8,128)(2,1)S(1)}, bf16[24,3584]{1,0:T(8,128)(2,1)S(1)}, u32[]{:S(2)}, u32[]{:S(2)}) collective-permute-start(bf16[24,3584]{1,0:T(8,128)(2,1)S(1)} %get-tuple-element.25), channel_id=1, source_target_pairs={{0,8},{1,9},{2,10},{3,11},{4,12},{5,13},{6,14},{7,15},{8,0},{9,1},... | collective-permute-start | bytes 516104 | tf_op jit(solution)/shard_map/ppermute | solution.py:343
  33.9 24.5 %collective-permute-start.10 = (bf16[24,3584]{1,0:T(8,128)(2,1)S(1)}, bf16[24,3584]{1,0:T(8,128)(2,1)S(1)}, u32[]{:S(2)}, u32[]{:S(2)}) collective-permute-start(bf16[24,3584]{1,0:T(8,128)(2,1)S(1)} %get-tuple-element.26), channel_id=1, source_target_pairs={{0,10},{1,11},{2,8},{3,9},{4,14},{5,15},{6,12},{7,13},{8,2},{9,3},... | collective-permute-start | bytes 516104 | tf_op jit(solution)/shard_map/ppermute | solution.py:343
  39.7 18.7 %collective-permute-start.11 = (bf16[24,3584]{1,0:T(8,128)(2,1)S(1)}, bf16[24,3584]{1,0:T(8,128)(2,1)S(1)}, u32[]{:S(2)}, u32[]{:S(2)}) collective-permute-start(bf16[24,3584]{1,0:T(8,128)(2,1)S(1)} %get-tuple-element.27), channel_id=1, source_target_pairs={{0,12},{1,13},{2,14},{3,15},{4,8},{5,9},{6,10},{7,11},{8,4},{9,5},... | collective-permute-start | bytes 516104 | tf_op jit(solution)/shard_map/ppermute | solution.py:343
  43.2 0.8 copy-start.4
  44.0 1.6 copy-start.5
  44.1 14.4 %collective-permute-start.12 = (bf16[24,3584]{1,0:T(8,128)(2,1)S(1)}, bf16[24,3584]{1,0:T(8,128)(2,1)S(1)}, u32[]{:S(2)}, u32[]{:S(2)}) collective-permute-start(bf16[24,3584]{1,0:T(8,128)(2,1)S(1)} %get-tuple-element.28), channel_id=1, source_target_pairs={{0,14},{1,15},{2,12},{3,13},{4,10},{5,11},{6,8},{7,9},{8,6},{9,7},... | collective-permute-start | bytes 516104 | tf_op jit(solution)/shard_map/ppermute | solution.py:343
  46.6 11.9 %copy-start.8 = (bf16[16,64,576]{2,1,0:T(8,128)(2,1)}, bf16[16,64,576]{2,1,0:T(8,128)(2,1)S(1)}, u32[]{:S(2)}) copy-start(bf16[16,64,576]{2,1,0:T(8,128)(2,1)S(1)} %get-tuple-element.38) | copy-start | bytes 3538948
  58.5 43.1 %all-to-all-start = ((bf16[8,64,1536]{2,1,0:T(8,128)(2,1)}), bf16[8,64,1536]{2,1,0:T(8,128)(2,1)S(1)}, u32[]{:S(2)}, u32[]{:S(2)}) async-start(bf16[8,64,1536]{2,1,0:T(8,128)(2,1)} %split_queries.1), calls=%async_computation | async-start | bytes 3145728 | tf_op jit(solution)/shard_map/all_to_all | solution.py:195
  65.9 8.2 %collective-permute-start.5 = (bf16[16,64,576]{2,1,0:T(8,128)(2,1)}, bf16[16,64,576]{2,1,0:T(8,128)(2,1)}, u32[]{:S(2)}, u32[]{:S(2)}) collective-permute-start(bf16[16,64,576]{2,1,0:T(8,128)(2,1)} %copy-done.8), channel_id=1, source_target_pairs={{0,1},{1,0},{2,3},{3,2},{4,5},{5,4},{6,7},{7,6},{8,9},{9,8},{10,11... | collective-permute-start | bytes 3538952 | tf_op jit(solution)/shard_map/ppermute | solution.py:343
  65.9 6.5 %collective-permute-start.13 = (bf16[24,3584]{1,0:T(8,128)(2,1)S(1)}, bf16[24,3584]{1,0:T(8,128)(2,1)S(1)}, u32[]{:S(2)}, u32[]{:S(2)}) collective-permute-start(bf16[24,3584]{1,0:T(8,128)(2,1)S(1)} %get-tuple-element.21.refs_0_), channel_id=1, source_target_pairs={{0,1},{1,0},{2,3},{3,2},{4,5},{5,4},{6,7},{7,6},{8,9},{9,8},{10,11... | collective-permute-start | bytes 516104 | tf_op jit(solution)/shard_map/ppermute | solution.py:343
  69.5 23.6 %collective-permute-start.22 = (bf16[1,4,512,128]{3,2,1,0:T(8,128)(2,1)S(1)}, bf16[1,4,512,128]{3,2,1,0:T(8,128)(2,1)S(1)}, u32[]{:S(2)}, u32[]{:S(2)}) collective-permute-start(bf16[1,4,512,128]{3,2,1,0:T(8,128)(2,1)S(1)} %fusion), channel_id=1, source_target_pairs={{0,8},{1,9},{2,10},{3,11},{4,12},{5,13},{6,14},{7,15},{8,0},{9,1},... | collective-permute-start | bytes 1572872 | tf_op jit(solution)/shard_map/ppermute | solution.py:343
  72.0 1.4 collective-permute-start.14
  72.0 1.6 %collective-permute-start.15 = (bf16[24,3584]{1,0:T(8,128)(2,1)S(1)}, bf16[24,3584]{1,0:T(8,128)(2,1)S(1)}, u32[]{:S(2)}, u32[]{:S(2)}) collective-permute-start(bf16[24,3584]{1,0:T(8,128)(2,1)S(1)} %collective-permute-done.7.refs_2_), channel_id=1, source_target_pairs={{0,1},{1,0},{2,3},{3,2},{4,5},{5,4},{6,7},{7,6},{8,9},{9,8},{10,11... | collective-permute-start | bytes 516104 | tf_op jit(solution)/shard_map/ppermute | solution.py:343
  72.5 1.4 collective-permute-start.16
  73.4 3.5 %collective-permute-start.17 = (bf16[24,3584]{1,0:T(8,128)(2,1)S(1)}, bf16[24,3584]{1,0:T(8,128)(2,1)S(1)}, u32[]{:S(2)}, u32[]{:S(2)}) collective-permute-start(bf16[24,3584]{1,0:T(8,128)(2,1)S(1)} %collective-permute-done.9.refs_4_), channel_id=1, source_target_pairs={{0,1},{1,0},{2,3},{3,2},{4,5},{5,4},{6,7},{7,6},{8,9},{9,8},{10,11... | collective-permute-start | bytes 516104 | tf_op jit(solution)/shard_map/ppermute | solution.py:343
  73.6 3.3 %collective-permute-start.18 = (bf16[24,3584]{1,0:T(8,128)(2,1)S(1)}, bf16[24,3584]{1,0:T(8,128)(2,1)S(1)}, u32[]{:S(2)}, u32[]{:S(2)}) collective-permute-start(bf16[24,3584]{1,0:T(8,128)(2,1)S(1)} %collective-permute-done.10.refs_5_), channel_id=1, source_target_pairs={{0,1},{1,0},{2,3},{3,2},{4,5},{5,4},{6,7},{7,6},{8,9},{9,8},{10,11... | collective-permute-start | bytes 516104 | tf_op jit(solution)/shard_map/ppermute | solution.py:343
  73.9 3.0 %collective-permute-start.19 = (bf16[24,3584]{1,0:T(8,128)(2,1)S(1)}, bf16[24,3584]{1,0:T(8,128)(2,1)S(1)}, u32[]{:S(2)}, u32[]{:S(2)}) collective-permute-start(bf16[24,3584]{1,0:T(8,128)(2,1)S(1)} %collective-permute-done.11.refs_6_), channel_id=1, source_target_pairs={{0,1},{1,0},{2,3},{3,2},{4,5},{5,4},{6,7},{7,6},{8,9},{9,8},{10,11... | collective-permute-start | bytes 516104 | tf_op jit(solution)/shard_map/ppermute | solution.py:343
  74.1 2.8 %collective-permute-start.20 = (bf16[24,3584]{1,0:T(8,128)(2,1)S(1)}, bf16[24,3584]{1,0:T(8,128)(2,1)S(1)}, u32[]{:S(2)}, u32[]{:S(2)}) collective-permute-start(bf16[24,3584]{1,0:T(8,128)(2,1)S(1)} %collective-permute-done.12.refs_7_), channel_id=1, source_target_pairs={{0,1},{1,0},{2,3},{3,2},{4,5},{5,4},{6,7},{7,6},{8,9},{9,8},{10,11... | collective-permute-start | bytes 516104 | tf_op jit(solution)/shard_map/ppermute | solution.py:343
  87.0 10.5 %collective-permute-start.21 = (bf16[192,3584]{1,0:T(8,128)(2,1)}, bf16[192,3584]{1,0:T(8,128)(2,1)S(1)}, u32[]{:S(2)}, u32[]{:S(2)}) collective-permute-start(bf16[192,3584]{1,0:T(8,128)(2,1)} %get-tuple-element.30), channel_id=1, source_target_pairs={{0,1},{1,0},{2,3},{3,2},{4,5},{5,4},{6,7},{7,6},{8,9},{9,8},{10,11... | collective-permute-start | bytes 4128776 | tf_op jit(solution)/shard_map/ppermute | solution.py:343
  93.2 2.7 %collective-permute-start.23 = (bf16[2,4,512,128]{3,2,1,0:T(8,128)(2,1)S(1)}, bf16[2,4,512,128]{3,2,1,0:T(8,128)(2,1)S(1)}, u32[]{:S(2)}, u32[]{:S(2)}) collective-permute-start(bf16[2,4,512,128]{3,2,1,0:T(8,128)(2,1)S(1)} %pad_maximum_fusion.1), channel_id=1, source_target_pairs={{0,1},{1,0},{2,3},{3,2},{4,5},{5,4},{6,7},{7,6},{8,9},{9,8},{10,11... | collective-permute-start | bytes 3145736 | tf_op jit(solution)/shard_map/ppermute | solution.py:343
  100.5 1.1 copy-start
  101.6 41.4 %all-to-all-start.1 = ((bf16[8,24,3584]{2,1,0:T(8,128)(2,1)}), bf16[8,24,3584]{2,1,0:T(8,128)(2,1)S(1)}, u32[]{:S(2)}, u32[]{:S(2)}) async-start(bf16[8,24,3584]{2,1,0:T(8,128)(2,1)} %copy-done), calls=%async_computation.1 | async-start | bytes 2752512 | tf_op jit(solution)/shard_map/all_to_all | solution.py:348
  124.4 1.0 copy-start.1
  125.4 21.3 %copy-start.10 = (f32[64,2]{0,1:T(2,128)S(1)}, f32[64,2]{0,1:T(2,128)}, u32[]{:S(2)}) copy-start(f32[64,2]{0,1:T(2,128)} %param.16) | copy-start | bytes 1540
  143.1 18.4 %all-to-all-start.2 = ((bf16[8,64,1024]{2,1,0:T(8,128)(2,1)}), bf16[8,64,1024]{2,1,0:T(8,128)(2,1)S(1)}, u32[]{:S(2)}, u32[]{:S(2)}) async-start(bf16[8,64,1024]{2,1,0:T(8,128)(2,1)} %bitcast.27), calls=%async_computation.2 | async-start | bytes 2097152 | tf_op jit(solution)/shard_map/all_to_all | solution.py:195

commit v6 on v5

--- a/solution.py
+++ b/solution.py
@@ -241,7 +241,9 @@
 EXP_SCALE = math.log2(math.e) / math.sqrt(NOPE + ROPE)
 
 
-def attention_kernel(split, rank_ref, query_ref, kv_ref, weight_ref, out_ref, keys, queries, mixed):
+def attention_kernel(
+    split, rank_ref, query_ref, kv_ref, other_kv_ref, weight_ref, other_weight_ref, out_ref, keys, queries, mixed
+):
     tok = kv_ref.shape[1]
     part_rows = query_ref.shape[0] // split.parts
     core = rank_ref[0] & 1
@@ -249,17 +251,23 @@
     @pl.when(pl.program_id(0) == 0)
     def _():
         for index, offset in enumerate(gather_order(split)):
-            group, ctx = divmod(offset, split.shards)
-            group = rank_ref[1] ^ group if split.wide else 0
-            place = pl.ds(pl.multiple_of((rank_ref[0] ^ ctx) * tok, tok), tok)
-            keys[group, place, : LATENT + ROPE] = kv_ref[index]
-            keys[group, place, LATENT + ROPE :] = kv_ref[index, :, LATENT:]
+            for from_ref, swapped in ((kv_ref, 0), (other_kv_ref, 1)):
+                group, ctx = divmod(offset ^ swapped, split.shards)
+                group = rank_ref[1] ^ group if split.wide else 0
+                place = pl.ds(pl.multiple_of((rank_ref[0] ^ ctx) * tok, tok), tok)
+                keys[group, place, : LATENT + ROPE] = from_ref[index]
+                keys[group, place, LATENT + ROPE :] = from_ref[index, :, LATENT:]
+
+    own_core = pl.program_id(0) < split.pairs // 2
+
+    def weight(index):
+        return jnp.where(own_core, weight_ref[0, index], other_weight_ref[0, index])
 
     contract = (((1,), (1,)), ((), ()))
     side = lax.broadcasted_iota(jnp.int32, (1, 2 * ROPE), 1) // ROPE
     for one in range(2):
         latent = lax.dot_general(
-            query_ref[:, one * NOPE : (one + 1) * NOPE], weight_ref[0, one], contract, preferred_element_type=F32
+            query_ref[:, one * NOPE : (one + 1) * NOPE], weight(one), contract, preferred_element_type=F32
         )
         queries[one, :, :LATENT] = latent.astype(BF16)
         queries[one, :, LATENT:] = jnp.where(side == one, query_ref[:, 2 * NOPE :], jnp.zeros((), BF16))
@@ -309,13 +317,15 @@
 
     for one in range(2):
         out_ref[:, one * VDIM : (one + 1) * VDIM] = jnp.dot(
-            mixed[one], weight_ref[0, 2 + one], preferred_element_type=F32
+            mixed[one], weight(2 + one), preferred_element_type=F32
         ).astype(BF16)
 
 
-def attention(split, place, queries, keys, weights):
+def attention(split, place, queries, keys, other_keys, weights, other_weights):
     count = queries.shape[0]
-    length = keys.shape[0] * keys.shape[1] // split.parts
+    length = 2 * keys.shape[0] * keys.shape[1] // split.parts
+    whole = pl.BlockSpec(keys.shape, lambda p, place: (0, 0, 0))
+    each = split.pairs // 2
     return call(
         functools.partial(attention_kernel, split),
         "causal_attention",
@@ -324,8 +334,10 @@
             grid=(split.pairs,),
             in_specs=[
                 pl.BlockSpec((count, 2 * (NOPE + ROPE)), lambda p, place: (0, p)),
-                pl.BlockSpec(keys.shape, lambda p, place: (0, 0, 0)),
-                pl.BlockSpec((1, 4, LATENT, VDIM), lambda p, place: (p, 0, 0, 0)),
+                whole,
+                whole,
+                pl.BlockSpec((1, 4, LATENT, VDIM), lambda p, place: (jnp.minimum(p, each - 1), 0, 0, 0)),
+                pl.BlockSpec((1, 4, LATENT, VDIM), lambda p, place: (jnp.maximum(p - each, 0), 0, 0, 0)),
             ],
             out_specs=pl.BlockSpec((count, 2 * VDIM), lambda p, place: (0, p)),
             scratch_shapes=[
@@ -335,7 +347,7 @@
             ],
         ),
         out_shape=jax.ShapeDtypeStruct((count, 2 * split.pairs * VDIM), BF16),
-    )(place, queries, keys, weights)
+    )(place, queries, keys, other_keys, weights, other_weights)
 
 
 def send(array, mask):
@@ -362,7 +374,7 @@
 def gather_masks(split):
     top, below = split.shards // 2, split.shards // 4
     later = [1 << bit for bit in reversed(range(1, below.bit_length() - 1))]
-    return [top, below, top ^ below], later + ([split.shards] if split.wide else []) + [1]
+    return [top, below, top ^ below], later + ([split.shards] if split.wide else [])
 
 
 def gather_order(split):
@@ -400,12 +412,13 @@
 
     direct, later = gather_masks(split)
     keys = jnp.stack([latent_kv] + [send(latent_kv, offset) for offset in direct])
-    for mask in later[:-1]:
-        keys = jnp.concatenate([keys, send(keys, mask)], axis=0)
 
     buckets = build_buckets(named, moe_input, experts, rows)
     own = [buckets[0]] + [send(buckets[m], 2 * m) for m in chips]
-    sent = after(split_queries(split, rank, queries), keys, *own)
+    keys = after(keys, own[1])
+    for mask in later:
+        keys = jnp.concatenate([keys, send(keys, mask)], axis=0)
+    sent = after(split_queries(split, rank, queries), keys, *own[1 : experts // 2])
     held = split.exchange(sent)
 
     weights = jnp.concatenate(
@@ -417,19 +430,17 @@
     )
     if split.wide:
         weights = lax.dynamic_slice_in_dim(weights, group[0] * split.own_pairs, split.own_pairs, axis=0)
-        weights = after(weights, *own)
+        weights = after(weights, *own[1 : experts // 2])
         weights = jnp.concatenate([weights, send(weights, shards // 2)], axis=0)
 
-    keys = jnp.concatenate([keys, send(keys, later[-1])], axis=0)
     other = [send(piece, 1) for piece in own]
-    own[0] = after(own[0], keys)
     hidden, for_other = hidden_rows(own, other, expert_gate, expert_up, expert_down)
     result = down_own(rank, hidden, expert_down, send(for_other, 1), experts)
-    weights = jnp.concatenate([weights, send(weights, 1)], axis=0)
 
     result, held, weights = lax.optimization_barrier((result, held, weights))
     back = swap_chips(result)
-    values = attention(split, place, held.reshape(experts * tok, held.shape[2]), keys, weights)
+    held = held.reshape(experts * tok, held.shape[2])
+    values = attention(split, place, held, keys, send(keys, 1), weights, send(weights, 1))
     values, back = lax.optimization_barrier((values, back))
     values = split.exchange(values.reshape(experts, tok, values.shape[1]))
     moe_out = combine(routes, gates, back.reshape(experts * rows, D), rows)

time: 163 us -> 177 us (1.086)
  waiting for transfers between devices: 62.4 us -> 95.7 us
  starting transfers between devices: 48.8 us -> 38.5 us
  local copies, waits for them, and re-layouts: 14.4 us -> 6.54 us
  other arithmetic: 3.77 us -> 1.28 us
    ppermute x24, waiting for transfers between devices: 31.5 us -> 70.4 us  [send(): lax.ppermute(array, ('groups', 'ctx'), [(i, i ^ mask) for i in range(coun...]
    all_to_all x1, waiting for transfers between devices: 17.7 us -> 12.4 us  [swap_chips(): lax.all_to_all(array, 'ctx', split_axis=0, concat_axis=0, axis_index_grou...]
    unnamed x29 -> x14, local copies, waits for them, and re-layouts: 8.81 us -> 4.32 us
    all_to_all x1, starting transfers between devices: 8.36 us -> 3.92 us  [swap_chips(): lax.all_to_all(array, 'ctx', split_axis=0, concat_axis=0, axis_index_grou...]
    ppermute x24, starting transfers between devices: 29.4 us -> 25.9 us  [send(): lax.ppermute(array, ('groups', 'ctx'), [(i, i ^ mask) for i in range(coun...]
    concatenate x1 -> x0, local copies, waits for them, and re-layouts: 2.5 us -> none  [on_device(): keys = jnp.concatenate([keys, send(keys, later[-1])], axis=0)]
    all_to_all x2, starting transfers between devices: 11 us -> 8.7 us  [exchange(): lax.all_to_all(array, ('groups', 'ctx'), split_axis=0, concat_axis=0, axi...]
  transfers between devices with their start and end apart: 27 -> 27, of which waited for: 12 -> 17; matrix products, arithmetic and copies ran while one was open for 8% -> 3% of each run, Pallas kernels for 19% -> 19%
where the time goes in v6:
time: 177 us
  waiting for transfers between devices  95.7 us (54%)
  starting transfers between devices  38.5 us (22%)
  Pallas kernels  34.2 us (19%)
  local copies, waits for them, and re-layouts  6.54 us (4%)
    ppermute x24, waiting for transfers between devices, send(): lax.ppermute(array, ('groups', 'ctx'), [(i, i ^ mask) for i in range(coun...  70.4 us
    ppermute x24, starting transfers between devices, send(): lax.ppermute(array, ('groups', 'ctx'), [(i, i ^ mask) for i in range(coun...  25.9 us
    pallas_call x1, Pallas kernels, attention(): call(functools.partial(attention_kernel, split), 'causal_attention', grid...  15 us
    all_to_all x2, waiting for transfers between devices, exchange(): lax.all_to_all(array, ('groups', 'ctx'), split_axis=0, concat_axis=0, axi...  12.9 us
    all_to_all x1, waiting for transfers between devices, swap_chips(): lax.all_to_all(array, 'ctx', split_axis=0, concat_axis=0, axis_index_grou...  12.4 us
    pallas_call x1, Pallas kernels, hidden_rows(): call(hidden_kernel, 'expert_hidden', grid=(STEPS,), in_specs=[part] * (2...  9.98 us
    all_to_all x2, starting transfers between devices, exchange(): lax.all_to_all(array, ('groups', 'ctx'), split_axis=0, concat_axis=0, axi...  8.7 us
    unnamed x14, local copies, waits for them, and re-layouts  4.32 us
  transfers between devices with their start and end apart: 27, of which 17 were waited for; matrix products, arithmetic and copies ran while one was open for 3% of the time, Pallas kernels for 19%

profile of v6, /device:TPU:0, one launch (start us, length us, event | category | flops | bytes accessed | tf_op | source)
XLA Modules:
  0.0 176.9 jit_solution(9161020924862054377)
XLA Ops:
  0.6 4.1 %collective-permute-start.16 = (bf16[64,576]{1,0:T(8,128)(2,1)}, bf16[64,576]{1,0:T(8,128)(2,1)S(1)}, u32[]{:S(2)}, u32[]{:S(2)}) collective-permute-start(bf16[64,576]{1,0:T(8,128)(2,1)} %param.11), channel_id=1, source_target_pairs={{0,8},{1,9},{2,10},{3,11},{4,12},{5,13},{6,14},{7,15},{8,0},{9,1},... | collective-permute-start | bytes 221192 | tf_op jit(solution)/shard_map/ppermute | solution.py:355
  4.7 1.6 collective-permute-start.17
  6.3 0.8 copy.16.routes_ref
  7.1 1.0 copy-done.1
  8.1 0.9 bucket_rows.1
  9.0 1.8 %collective-permute-start = (bf16[24,3584]{1,0:T(8,128)(2,1)S(1)}, bf16[24,3584]{1,0:T(8,128)(2,1)S(1)}, u32[]{:S(2)}, u32[]{:S(2)}) collective-permute-start(bf16[24,3584]{1,0:T(8,128)(2,1)S(1)} %get-tuple-element.21), channel_id=1, source_target_pairs={{0,2},{1,3},{2,0},{3,1},{4,6},{5,7},{6,4},{7,5},{8,10},{9,11},{10,... | collective-permute-start | bytes 516104 | tf_op jit(solution)/shard_map/ppermute | solution.py:355
  10.9 1.9 %collective-permute-done.18 = bf16[64,576]{1,0:T(8,128)(2,1)S(1)} collective-permute-done((bf16[64,576]{1,0:T(8,128)(2,1)}, bf16[64,576]{1,0:T(8,128)(2,1)S(1)}, u32[]{:S(2)}, u32[]{:S(2)}) %collective-permute-start.18) | collective-permute-done | bytes 73760 | tf_op jit(solution)/shard_map/ppermute | solution.py:355
  12.8 1.0 pad_maximum_fusion.2
  13.7 0.9 collective-permute-done.refs_1_
  14.7 1.6 collective-permute-start.19
  16.3 6.4 %collective-permute-done.19 = bf16[4,64,576]{2,1,0:T(8,128)(2,1)S(1)} collective-permute-done((bf16[4,64,576]{2,1,0:T(8,128)(2,1)S(1)}, bf16[4,64,576]{2,1,0:T(8,128)(2,1)S(1)}, u32[]{:S(2)}, u32[]{:S(2)}) %collective-permute-start.19) | collective-permute-done | bytes 294944 | tf_op jit(solution)/shard_map/ppermute | solution.py:355
  22.6 0.1 pad_maximum_fusion.1
  22.7 1.4 collective-permute-start.20
  24.2 1.5 collective-permute-start.1
  25.6 1.5 collective-permute-start.2
  27.1 1.5 split_queries.1
  28.7 0.7 constant_dynamic-update-slice_fusion.2
  29.4 0.8 constant_dynamic-update-slice_fusion.1
  30.2 6.7 %collective-permute-done.20 = bf16[8,64,576]{2,1,0:T(8,128)(2,1)S(1)} collective-permute-done((bf16[8,64,576]{2,1,0:T(8,128)(2,1)S(1)}, bf16[8,64,576]{2,1,0:T(8,128)(2,1)S(1)}, u32[]{:S(2)}, u32[]{:S(2)}) %collective-permute-start.20) | collective-permute-done | bytes 589856 | tf_op jit(solution)/shard_map/ppermute | solution.py:355
  36.9 0.9 constant_dynamic-update-slice_fusion.kv_ref
  37.8 0.0 collective-permute-done.1.refs_2_
  37.8 0.0 collective-permute-done.2.refs_3_
  37.8 5.1 %all-to-all-start = ((bf16[8,64,1536]{2,1,0:T(8,128)(2,1)}), bf16[8,64,1536]{2,1,0:T(8,128)(2,1)}, u32[]{:S(2)}, u32[]{:S(2)}) async-start(bf16[8,64,1536]{2,1,0:T(8,128)(2,1)} %split_queries.1), calls=%async_computation | async-start | bytes 3145728 | tf_op jit(solution)/shard_map/all_to_all | solution.py:195
  42.9 3.9 %collective-permute-start.3 = (bf16[24,3584]{1,0:T(8,128)(2,1)S(1)}, bf16[24,3584]{1,0:T(8,128)(2,1)S(1)}, u32[]{:S(2)}, u32[]{:S(2)}) collective-permute-start(bf16[24,3584]{1,0:T(8,128)(2,1)S(1)} %get-tuple-element.24), channel_id=1, source_target_pairs={{0,8},{1,9},{2,10},{3,11},{4,12},{5,13},{6,14},{7,15},{8,0},{9,1},... | collective-permute-start | bytes 516104 | tf_op jit(solution)/shard_map/ppermute | solution.py:355
  46.8 1.3 collective-permute-start.4
  48.1 3.8 %collective-permute-start.5 = (bf16[24,3584]{1,0:T(8,128)(2,1)S(1)}, bf16[24,3584]{1,0:T(8,128)(2,1)S(1)}, u32[]{:S(2)}, u32[]{:S(2)}) collective-permute-start(bf16[24,3584]{1,0:T(8,128)(2,1)S(1)} %get-tuple-element.26), channel_id=1, source_target_pairs={{0,12},{1,13},{2,14},{3,15},{4,8},{5,9},{6,10},{7,11},{8,4},{9,5},... | collective-permute-start | bytes 516104 | tf_op jit(solution)/shard_map/ppermute | solution.py:355
  51.9 0.0 collective-permute-start.6
  51.9 0.0 collective-permute-start.7
  51.9 13.2 %collective-permute-done.3.refs_4_ = bf16[24,3584]{1,0:T(8,128)(2,1)S(1)} collective-permute-done((bf16[24,3584]{1,0:T(8,128)(2,1)S(1)}, bf16[24,3584]{1,0:T(8,128)(2,1)S(1)}, u32[]{:S(2)}, u32[]{:S(2)}) %collective-permute-start.3) | collective-permute-done | bytes 172064 | tf_op jit(solution)/shard_map/ppermute | solution.py:355
  65.1 0.0 collective-permute-start.10
  65.1 3.7 %collective-permute-done.4.refs_5_ = bf16[24,3584]{1,0:T(8,128)(2,1)S(1)} collective-permute-done((bf16[24,3584]{1,0:T(8,128)(2,1)S(1)}, bf16[24,3584]{1,0:T(8,128)(2,1)S(1)}, u32[]{:S(2)}, u32[]{:S(2)}) %collective-permute-start.4) | collective-permute-done | bytes 172064 | tf_op jit(solution)/shard_map/ppermute | solution.py:355
  68.8 0.0 collective-permute-start.11
  68.8 9.1 %collective-permute-done.5.refs_6_ = bf16[24,3584]{1,0:T(8,128)(2,1)S(1)} collective-permute-done((bf16[24,3584]{1,0:T(8,128)(2,1)S(1)}, bf16[24,3584]{1,0:T(8,128)(2,1)S(1)}, u32[]{:S(2)}, u32[]{:S(2)}) %collective-permute-start.5) | collective-permute-done | bytes 172064 | tf_op jit(solution)/shard_map/ppermute | solution.py:355
  77.9 0.0 collective-permute-start.8
  77.9 1.5 collective-permute-done.6.refs_7_
  79.4 0.5 collective-permute-start.13
  79.9 0.1 collective-permute-start.14
  80.0 0.4 collective-permute-start.9
  80.4 0.4 collective-permute-done.12.refs_13_
  80.8 0.2 collective-permute-done.13.refs_14_
  81.1 0.3 collective-permute-done.14.refs_15_
  81.3 0.0 collective-permute-done.8.refs_9_
  81.3 0.2 collective-permute-done.9.refs_10_
  81.6 10.0 %expert_hidden.1 = (bf16[192,512]{1,0:T(8,128)(2,1)S(1)}, bf16[192,3584]{1,0:T(8,128)(2,1)}) custom-call(bf16[24,3584]{1,0:T(8,128)(2,1)S(1)} %get-tuple-element.20.refs_0_, bf16[24,3584]{1,0:T(8,128)(2,1)S(1)} %collective-permute-done.refs_1_, bf16[24,3584]{1,0:T(8,128)(2,1)S(1)} %collective-permute-done.1.refs_2_, ...), custom_call_target="tpu_custom_call" | custom-call | flops 1 | bytes 1 | tf_op jit(solution)/shard_map/expert_hidden/pallas_call | solution.py:134
  91.6 0.3 collective-permute-start.15
  91.8 1.3 copy.18
  93.2 0.1 fusion
  93.2 1.6 collective-permute-start.21
  94.8 21.9 %collective-permute-done.21 = bf16[1,4,512,128]{3,2,1,0:T(8,128)(2,1)S(1)} collective-permute-done((bf16[1,4,512,128]{3,2,1,0:T(8,128)(2,1)S(1)}, bf16[1,4,512,128]{3,2,1,0:T(8,128)(2,1)S(1)}, u32[]{:S(2)}, u32[]{:S(2)}) %collective-permute-start.21) | collective-permute-done | bytes 524320 | tf_op jit(solution)/shard_map/ppermute | solution.py:355
  116.7 0.1 pad_maximum_fusion.weight_ref
  116.8 4.1 %down_own_rows.1 = bf16[8,24,3584]{2,1,0:T(8,128)(2,1)} custom-call(s32[1]{0:T(128)} %bitcast.rank_ref, bf16[192,512]{1,0:T(8,128)(2,1)S(1)} %get-tuple-element.28.hidden_ref, bf16[1,512,3584]{2,1,0:T(8,128)(2,1)} %down_ref.1, bf16[192,3584]{1,0:T(8,128)(2,1)S(1)} %collective-permute-done.15.other_ref), custom_call_target="tpu_custom_call" | custom-call | flops 1 | bytes 1 | tf_op jit(solution)/shard_map/down_own_rows/pallas_call | solution.py:158
  120.9 3.9 %all-to-all-start.1 = ((bf16[8,24,3584]{2,1,0:T(8,128)(2,1)}), bf16[8,24,3584]{2,1,0:T(8,128)(2,1)S(1)}, u32[]{:S(2)}, u32[]{:S(2)}) async-start(bf16[8,24,3584]{2,1,0:T(8,128)(2,1)} %down_own_rows.1), calls=%async_computation.1 | async-start | bytes 2752512 | tf_op jit(solution)/shard_map/all_to_all | solution.py:360
  124.8 0.5 collective-permute-start.23
  125.3 0.1 pad_add_fusion.rank_ref
  125.4 3.8 %collective-permute-done.22.other_kv_ref = bf16[16,64,576]{2,1,0:T(8,128)(2,1)S(1)} collective-permute-done((bf16[16,64,576]{2,1,0:T(8,128)(2,1)}, bf16[16,64,576]{2,1,0:T(8,128)(2,1)S(1)}, u32[]{:S(2)}, u32[]{:S(2)}) %collective-permute-start.22) | collective-permute-done | bytes 1179680 | tf_op jit(solution)/shard_map/ppermute | solution.py:355
  129.2 0.1 collective-permute-done.23.other_weight_ref
  129.4 0.9 copy-done.2
  130.3 15.0 %causal_attention.1 = bf16[512,1024]{1,0:T(8,128)(2,1)} custom-call(s32[2]{0:T(128)S(1)} %pad_add_fusion.rank_ref, bf16[512,1536]{1,0:T(8,128)(2,1)} %bitcast.10.query_ref, bf16[16,64,576]{2,1,0:T(8,128)(2,1)} %constant_dynamic-update-slice_fusion.kv_ref, bf16[16,64,576]{2,1,0:T(8,128)(2,1)} %copy-done.2, ...), custom_call_target="tpu_custom_call" | custom-call | flops 1 | bytes 1 | tf_op jit(solution)/shard_map/causal_attention/pallas_call | solution.py:329
  145.3 12.4 %all-to-all-done.1 = bf16[8,24,3584]{2,1,0:T(8,128)(2,1)S(1)} async-done(((bf16[8,24,3584]{2,1,0:T(8,128)(2,1)}), bf16[8,24,3584]{2,1,0:T(8,128)(2,1)S(1)}, u32[]{:S(2)}, u32[]{:S(2)}) %all-to-all-start.1) | async-done | bytes 1376288 | tf_op jit(solution)/shard_map/all_to_all | solution.py:360
  157.7 3.6 %all-to-all-start.2 = ((bf16[8,64,1024]{2,1,0:T(8,128)(2,1)}), bf16[8,64,1024]{2,1,0:T(8,128)(2,1)S(1)}, u32[]{:S(2)}, u32[]{:S(2)}) async-start(bf16[8,64,1024]{2,1,0:T(8,128)(2,1)} %bitcast.11), calls=%async_computation.2 | async-start | bytes 2097152 | tf_op jit(solution)/shard_map/all_to_all | solution.py:195
  161.3 0.1 copy.20.gates_ref
  161.4 1.5 combine_routes.1
  162.9 12.9 %all-to-all-done.2.x_ref = bf16[8,64,1024]{2,1,0:T(8,128)(2,1)S(1)} async-done(((bf16[8,64,1024]{2,1,0:T(8,128)(2,1)}), bf16[8,64,1024]{2,1,0:T(8,128)(2,1)S(1)}, u32[]{:S(2)}, u32[]{:S(2)}) %all-to-all-start.2) | async-done | bytes 1048608 | tf_op jit(solution)/shard_map/all_to_all | solution.py:195
  175.8 1.1 join_values.1
  (19 shorter events, 0.0 us)
Async XLA Ops:
  0.6 26.5 %copy-start = (bf16[64,12288]{1,0:T(8,128)(2,1)S(1)}, bf16[64,12288]{1,0:T(8,128)(2,1)}, u32[]{:S(2)}) copy-start(bf16[64,12288]{1,0:T(8,128)(2,1)} %x_ref.3) | copy-start | bytes 4718596
  0.6 10.2 %collective-permute-start.16 = (bf16[64,576]{1,0:T(8,128)(2,1)}, bf16[64,576]{1,0:T(8,128)(2,1)S(1)}, u32[]{:S(2)}, u32[]{:S(2)}) collective-permute-start(bf16[64,576]{1,0:T(8,128)(2,1)} %param.11), channel_id=1, source_target_pairs={{0,8},{1,9},{2,10},{3,11},{4,12},{5,13},{6,14},{7,15},{8,0},{9,1},... | collective-permute-start | bytes 221192 | tf_op jit(solution)/shard_map/ppermute | solution.py:355
  4.7 6.1 %collective-permute-start.17 = (bf16[64,576]{1,0:T(8,128)(2,1)}, bf16[64,576]{1,0:T(8,128)(2,1)S(1)}, u32[]{:S(2)}, u32[]{:S(2)}) collective-permute-start(bf16[64,576]{1,0:T(8,128)(2,1)} %param.11), channel_id=1, source_target_pairs={{0,4},{1,5},{2,6},{3,7},{4,0},{5,1},{6,2},{7,3},{8,12},{9,13},{10,... | collective-permute-start | bytes 221192 | tf_op jit(solution)/shard_map/ppermute | solution.py:355
  6.3 6.4 %collective-permute-start.18 = (bf16[64,576]{1,0:T(8,128)(2,1)}, bf16[64,576]{1,0:T(8,128)(2,1)S(1)}, u32[]{:S(2)}, u32[]{:S(2)}) collective-permute-start(bf16[64,576]{1,0:T(8,128)(2,1)} %param.11), channel_id=1, source_target_pairs={{0,12},{1,13},{2,14},{3,15},{4,8},{5,9},{6,10},{7,11},{8,4},{9,5},... | collective-permute-start | bytes 221192 | tf_op jit(solution)/shard_map/ppermute | solution.py:355
  7.1 1.0 copy-start.1
  9.0 5.6 %collective-permute-start = (bf16[24,3584]{1,0:T(8,128)(2,1)S(1)}, bf16[24,3584]{1,0:T(8,128)(2,1)S(1)}, u32[]{:S(2)}, u32[]{:S(2)}) collective-permute-start(bf16[24,3584]{1,0:T(8,128)(2,1)S(1)} %get-tuple-element.21), channel_id=1, source_target_pairs={{0,2},{1,3},{2,0},{3,1},{4,6},{5,7},{6,4},{7,5},{8,10},{9,11},{10,... | collective-permute-start | bytes 516104 | tf_op jit(solution)/shard_map/ppermute | solution.py:355
  14.7 8.0 %collective-permute-start.19 = (bf16[4,64,576]{2,1,0:T(8,128)(2,1)S(1)}, bf16[4,64,576]{2,1,0:T(8,128)(2,1)S(1)}, u32[]{:S(2)}, u32[]{:S(2)}) collective-permute-start(bf16[4,64,576]{2,1,0:T(8,128)(2,1)S(1)} %pad_maximum_fusion.2), channel_id=1, source_target_pairs={{0,2},{1,3},{2,0},{3,1},{4,6},{5,7},{6,4},{7,5},{8,10},{9,11},{10,... | collective-permute-start | bytes 884744 | tf_op jit(solution)/shard_map/ppermute | solution.py:355
  22.7 14.1 %collective-permute-start.20 = (bf16[8,64,576]{2,1,0:T(8,128)(2,1)S(1)}, bf16[8,64,576]{2,1,0:T(8,128)(2,1)S(1)}, u32[]{:S(2)}, u32[]{:S(2)}) collective-permute-start(bf16[8,64,576]{2,1,0:T(8,128)(2,1)S(1)} %pad_maximum_fusion.1), channel_id=1, source_target_pairs={{0,16},{1,17},{2,18},{3,19},{4,20},{5,21},{6,22},{7,23},{8,24},{9,... | collective-permute-start | bytes 1769480 | tf_op jit(solution)/shard_map/ppermute | solution.py:355
  24.2 13.6 %collective-permute-start.1 = (bf16[24,3584]{1,0:T(8,128)(2,1)S(1)}, bf16[24,3584]{1,0:T(8,128)(2,1)S(1)}, u32[]{:S(2)}, u32[]{:S(2)}) collective-permute-start(bf16[24,3584]{1,0:T(8,128)(2,1)S(1)} %get-tuple-element.22), channel_id=1, source_target_pairs={{0,4},{1,5},{2,6},{3,7},{4,0},{5,1},{6,2},{7,3},{8,12},{9,13},{10,... | collective-permute-start | bytes 516104 | tf_op jit(solution)/shard_map/ppermute | solution.py:355
  25.6 12.1 %collective-permute-start.2 = (bf16[24,3584]{1,0:T(8,128)(2,1)S(1)}, bf16[24,3584]{1,0:T(8,128)(2,1)S(1)}, u32[]{:S(2)}, u32[]{:S(2)}) collective-permute-start(bf16[24,3584]{1,0:T(8,128)(2,1)S(1)} %get-tuple-element.23), channel_id=1, source_target_pairs={{0,6},{1,7},{2,4},{3,5},{4,2},{5,3},{6,0},{7,1},{8,14},{9,15},{10,... | collective-permute-start | bytes 516104 | tf_op jit(solution)/shard_map/ppermute | solution.py:355
  37.8 83.1 %all-to-all-start = ((bf16[8,64,1536]{2,1,0:T(8,128)(2,1)}), bf16[8,64,1536]{2,1,0:T(8,128)(2,1)}, u32[]{:S(2)}, u32[]{:S(2)}) async-start(bf16[8,64,1536]{2,1,0:T(8,128)(2,1)} %split_queries.1), calls=%async_computation | async-start | bytes 3145728 | tf_op jit(solution)/shard_map/all_to_all | solution.py:195
  42.9 22.2 %collective-permute-start.3 = (bf16[24,3584]{1,0:T(8,128)(2,1)S(1)}, bf16[24,3584]{1,0:T(8,128)(2,1)S(1)}, u32[]{:S(2)}, u32[]{:S(2)}) collective-permute-start(bf16[24,3584]{1,0:T(8,128)(2,1)S(1)} %get-tuple-element.24), channel_id=1, source_target_pairs={{0,8},{1,9},{2,10},{3,11},{4,12},{5,13},{6,14},{7,15},{8,0},{9,1},... | collective-permute-start | bytes 516104 | tf_op jit(solution)/shard_map/ppermute | solution.py:355
  46.8 22.0 %collective-permute-start.4 = (bf16[24,3584]{1,0:T(8,128)(2,1)S(1)}, bf16[24,3584]{1,0:T(8,128)(2,1)S(1)}, u32[]{:S(2)}, u32[]{:S(2)}) collective-permute-start(bf16[24,3584]{1,0:T(8,128)(2,1)S(1)} %get-tuple-element.25), channel_id=1, source_target_pairs={{0,10},{1,11},{2,8},{3,9},{4,14},{5,15},{6,12},{7,13},{8,2},{9,3},... | collective-permute-start | bytes 516104 | tf_op jit(solution)/shard_map/ppermute | solution.py:355
  48.1 29.8 %collective-permute-start.5 = (bf16[24,3584]{1,0:T(8,128)(2,1)S(1)}, bf16[24,3584]{1,0:T(8,128)(2,1)S(1)}, u32[]{:S(2)}, u32[]{:S(2)}) collective-permute-start(bf16[24,3584]{1,0:T(8,128)(2,1)S(1)} %get-tuple-element.26), channel_id=1, source_target_pairs={{0,12},{1,13},{2,14},{3,15},{4,8},{5,9},{6,10},{7,11},{8,4},{9,5},... | collective-permute-start | bytes 516104 | tf_op jit(solution)/shard_map/ppermute | solution.py:355
  51.9 27.5 %collective-permute-start.6 = (bf16[24,3584]{1,0:T(8,128)(2,1)S(1)}, bf16[24,3584]{1,0:T(8,128)(2,1)S(1)}, u32[]{:S(2)}, u32[]{:S(2)}) collective-permute-start(bf16[24,3584]{1,0:T(8,128)(2,1)S(1)} %get-tuple-element.27), channel_id=1, source_target_pairs={{0,14},{1,15},{2,12},{3,13},{4,10},{5,11},{6,8},{7,9},{8,6},{9,7},... | collective-permute-start | bytes 516104 | tf_op jit(solution)/shard_map/ppermute | solution.py:355
  51.9 27.5 %collective-permute-start.7 = (bf16[24,3584]{1,0:T(8,128)(2,1)S(1)}, bf16[24,3584]{1,0:T(8,128)(2,1)S(1)}, u32[]{:S(2)}, u32[]{:S(2)}) collective-permute-start(bf16[24,3584]{1,0:T(8,128)(2,1)S(1)} %get-tuple-element.20.refs_0_), channel_id=1, source_target_pairs={{0,1},{1,0},{2,3},{3,2},{4,5},{5,4},{6,7},{7,6},{8,9},{9,8},{10,11... | collective-permute-start | bytes 516104 | tf_op jit(solution)/shard_map/ppermute | solution.py:355
  65.1 14.8 %collective-permute-start.10 = (bf16[24,3584]{1,0:T(8,128)(2,1)S(1)}, bf16[24,3584]{1,0:T(8,128)(2,1)S(1)}, u32[]{:S(2)}, u32[]{:S(2)}) collective-permute-start(bf16[24,3584]{1,0:T(8,128)(2,1)S(1)} %collective-permute-done.2.refs_3_), channel_id=1, source_target_pairs={{0,1},{1,0},{2,3},{3,2},{4,5},{5,4},{6,7},{7,6},{8,9},{9,8},{10,11... | collective-permute-start | bytes 516104 | tf_op jit(solution)/shard_map/ppermute | solution.py:355
  68.8 11.2 %collective-permute-start.11 = (bf16[24,3584]{1,0:T(8,128)(2,1)S(1)}, bf16[24,3584]{1,0:T(8,128)(2,1)S(1)}, u32[]{:S(2)}, u32[]{:S(2)}) collective-permute-start(bf16[24,3584]{1,0:T(8,128)(2,1)S(1)} %collective-permute-done.3.refs_4_), channel_id=1, source_target_pairs={{0,1},{1,0},{2,3},{3,2},{4,5},{5,4},{6,7},{7,6},{8,9},{9,8},{10,11... | collective-permute-start | bytes 516104 | tf_op jit(solution)/shard_map/ppermute | solution.py:355
  77.9 3.5 %collective-permute-start.8 = (bf16[24,3584]{1,0:T(8,128)(2,1)S(1)}, bf16[24,3584]{1,0:T(8,128)(2,1)S(1)}, u32[]{:S(2)}, u32[]{:S(2)}) collective-permute-start(bf16[24,3584]{1,0:T(8,128)(2,1)S(1)} %collective-permute-done.refs_1_), channel_id=1, source_target_pairs={{0,1},{1,0},{2,3},{3,2},{4,5},{5,4},{6,7},{7,6},{8,9},{9,8},{10,11... | collective-permute-start | bytes 516104 | tf_op jit(solution)/shard_map/ppermute | solution.py:355
  79.4 1.4 collective-permute-start.12
  79.4 1.6 collective-permute-start.13
  79.9 1.4 collective-permute-start.14
  80.0 1.6 collective-permute-start.9
  91.6 1.6 copy-start.3
  91.6 25.2 %collective-permute-start.15 = (bf16[192,3584]{1,0:T(8,128)(2,1)}, bf16[192,3584]{1,0:T(8,128)(2,1)S(1)}, u32[]{:S(2)}, u32[]{:S(2)}) collective-permute-start(bf16[192,3584]{1,0:T(8,128)(2,1)} %get-tuple-element.29), channel_id=1, source_target_pairs={{0,1},{1,0},{2,3},{3,2},{4,5},{5,4},{6,7},{7,6},{8,9},{9,8},{10,11... | collective-permute-start | bytes 4128776 | tf_op jit(solution)/shard_map/ppermute | solution.py:355
  93.2 23.5 %collective-permute-start.21 = (bf16[1,4,512,128]{3,2,1,0:T(8,128)(2,1)S(1)}, bf16[1,4,512,128]{3,2,1,0:T(8,128)(2,1)S(1)}, u32[]{:S(2)}, u32[]{:S(2)}) collective-permute-start(bf16[1,4,512,128]{3,2,1,0:T(8,128)(2,1)S(1)} %fusion), channel_id=1, source_target_pairs={{0,8},{1,9},{2,10},{3,11},{4,12},{5,13},{6,14},{7,15},{8,0},{9,1},... | collective-permute-start | bytes 1572872 | tf_op jit(solution)/shard_map/ppermute | solution.py:355
  120.9 36.8 %all-to-all-start.1 = ((bf16[8,24,3584]{2,1,0:T(8,128)(2,1)}), bf16[8,24,3584]{2,1,0:T(8,128)(2,1)S(1)}, u32[]{:S(2)}, u32[]{:S(2)}) async-start(bf16[8,24,3584]{2,1,0:T(8,128)(2,1)} %down_own_rows.1), calls=%async_computation.1 | async-start | bytes 2752512 | tf_op jit(solution)/shard_map/all_to_all | solution.py:360
  124.8 4.4 %collective-permute-start.22 = (bf16[16,64,576]{2,1,0:T(8,128)(2,1)}, bf16[16,64,576]{2,1,0:T(8,128)(2,1)S(1)}, u32[]{:S(2)}, u32[]{:S(2)}) collective-permute-start(bf16[16,64,576]{2,1,0:T(8,128)(2,1)} %constant_dynamic-update-slice_fusion.kv_ref), channel_id=1, source_target_pairs={{0,1},{1,0},{2,3},{3,2},{4,5},{5,4},{6,7},{7,6},{8,9},{9,8},{10,11... | collective-permute-start | bytes 3538952 | tf_op jit(solution)/shard_map/ppermute | solution.py:355
  124.8 4.5 %collective-permute-start.23 = (bf16[2,4,512,128]{3,2,1,0:T(8,128)(2,1)S(1)}, bf16[2,4,512,128]{3,2,1,0:T(8,128)(2,1)S(1)}, u32[]{:S(2)}, u32[]{:S(2)}) collective-permute-start(bf16[2,4,512,128]{3,2,1,0:T(8,128)(2,1)S(1)} %pad_maximum_fusion.weight_ref), channel_id=1, source_target_pairs={{0,1},{1,0},{2,3},{3,2},{4,5},{5,4},{6,7},{7,6},{8,9},{9,8},{10,11... | collective-permute-start | bytes 3145736 | tf_op jit(solution)/shard_map/ppermute | solution.py:355
  129.2 1.1 copy-start.2
  145.3 16.0 %copy-start.4 = (f32[64,2]{0,1:T(2,128)S(1)}, f32[64,2]{0,1:T(2,128)}, u32[]{:S(2)}) copy-start(f32[64,2]{0,1:T(2,128)} %param.16) | copy-start | bytes 1540
  157.7 18.2 %all-to-all-start.2 = ((bf16[8,64,1024]{2,1,0:T(8,128)(2,1)}), bf16[8,64,1024]{2,1,0:T(8,128)(2,1)S(1)}, u32[]{:S(2)}, u32[]{:S(2)}) async-start(bf16[8,64,1024]{2,1,0:T(8,128)(2,1)} %bitcast.11), calls=%async_computation.2 | async-start | bytes 2097152 | tf_op jit(solution)/shard_map/all_to_all | solution.py:195

commit v7 on v6

--- a/solution.py
+++ b/solution.py
@@ -23,14 +23,13 @@
 
 SMEM = pl.BlockSpec(memory_space=pltpu.SMEM)
 VMEM = pl.BlockSpec(memory_space=pltpu.VMEM)
-SMALL = pl.CostEstimate(flops=1, bytes_accessed=1, transcendentals=0)
-
-
-def call(kernel, name, **options):
+
+
+def call(kernel, name, flops=0, moved=0, **options):
     return pl.pallas_call(
         kernel,
         name=name,
-        cost_estimate=SMALL,
+        cost_estimate=pl.CostEstimate(flops=flops, bytes_accessed=moved, transcendentals=0),
         compiler_params=pltpu.CompilerParams(vmem_limit_bytes=VMEM_LIMIT),
         **options,
     )
@@ -54,27 +53,22 @@
     return first * rows + slot0, second * rows + slot1
 
 
-def bucket_kernel(rows, routes_ref, x_ref, *out_refs):
+def bucket_kernel(rows, routes_ref, x_ref, out_ref):
     target0, target1 = slot_targets(routes_ref[...], rows)
-    column = lax.broadcasted_iota(jnp.int32, (x_ref.shape[0], len(out_refs) * rows), 1)
+    column = lax.broadcasted_iota(jnp.int32, (x_ref.shape[0], out_ref.shape[0]), 1)
     chosen = jnp.where((column == target0) | (column == target1), 1.0, 0.0).astype(BF16)
-    found = lax.dot_general(
+    out_ref[...] = lax.dot_general(
         chosen, x_ref[...], (((0,), (0,)), ((), ())), preferred_element_type=F32
     ).astype(BF16)
-    for place, out_ref in enumerate(out_refs):
-        out_ref[...] = found[place * rows : (place + 1) * rows]
 
 
 def build_buckets(routes, moe_input, experts, rows):
     return call(
         functools.partial(bucket_kernel, rows),
         "bucket_rows",
-        out_shape=[jax.ShapeDtypeStruct((rows, D), BF16)] * experts,
+        moved=2 * D * (moe_input.shape[0] + experts * rows),
+        out_shape=jax.ShapeDtypeStruct((experts * rows, D), BF16),
     )(routes, moe_input)
-
-
-def stack(refs):
-    return jnp.concatenate([ref[...] for ref in refs], axis=0)
 
 
 def combine_kernel(rows, routes_ref, gates_ref, back_ref, out_ref):
@@ -92,6 +86,7 @@
     return call(
         functools.partial(combine_kernel, rows),
         "combine_routes",
+        moved=2 * D * (routes.shape[0] + back.shape[0]),
         out_shape=jax.ShapeDtypeStruct((routes.shape[0], D), BF16),
     )(routes, gates, back)
 
@@ -100,68 +95,44 @@
 STEPS = D // STEP
 
 
-def hidden_kernel(*refs):
-    gate_ref, up_ref, down_ref, hidden_ref, out_ref, gate_sum, up_sum = refs[-7:]
+def expert_kernel(x_ref, gate0, up0, gate1, up1, down0, down1, out_ref, sums, hidden):
     step = pl.program_id(0)
-    count = hidden_ref.shape[0]
-    x = stack(refs[:-7])
-    gate = jnp.dot(x, gate_ref[0], preferred_element_type=F32)
-    up = jnp.dot(x, up_ref[0], preferred_element_type=F32)
-
-    @pl.when(step == 0)
+
+    @pl.when(step < STEPS)
     def _():
-        gate_sum[...] = gate
-        up_sum[...] = up
-
-    @pl.when(step > 0)
+        x = x_ref[...]
+        for index, weight_ref in enumerate((gate0, up0, gate1, up1)):
+            part = jnp.dot(x, weight_ref[0], preferred_element_type=F32)
+            sums[index] = jnp.where(step == 0, part, sums[index] + part)
+
+    @pl.when(step == STEPS)
     def _():
-        gate_sum[...] += gate
-        up_sum[...] += up
-
-    @pl.when(step == STEPS - 1)
+        for half in range(2):
+            value = sums[2 * half]
+            hidden[half] = (value / (1.0 + jnp.exp(-value)) * sums[2 * half + 1]).astype(BF16)
+
+    @pl.when(step >= STEPS)
     def _():
-        value = gate_sum[...]
-        hidden = (value / (1.0 + jnp.exp(-value)) * up_sum[...]).astype(BF16)
-        hidden_ref[...] = hidden[:count]
-        out_ref[...] = jnp.dot(hidden[count:], down_ref[0], preferred_element_type=F32).astype(BF16)
-
-
-def hidden_rows(own, other, gate, up, down):
-    rows = own[0].shape[0]
-    count = len(own) * rows
-    part = pl.BlockSpec((rows, STEP), lambda k: (0, k))
-    weights = pl.BlockSpec((1, STEP, HALF), lambda k: (0, k, 0))
-    return call(
-        hidden_kernel,
-        "expert_hidden",
-        grid=(STEPS,),
-        in_specs=[part] * (2 * len(own))
-        + [weights, weights, pl.BlockSpec((1, HALF, D), lambda k: (0, 0, 0))],
-        out_specs=[
-            pl.BlockSpec((count, HALF), lambda k: (0, 0)),
-            pl.BlockSpec((count, D), lambda k: (0, 0)),
-        ],
-        scratch_shapes=[pltpu.VMEM((2 * count, HALF), F32)] * 2,
-        out_shape=[jax.ShapeDtypeStruct((count, HALF), BF16), jax.ShapeDtypeStruct((count, D), BF16)],
-    )(*own, *other, gate, up, down)
-
-
-def down_kernel(rank_ref, hidden_ref, down_ref, other_ref, out_ref):
-    own = jnp.dot(hidden_ref[...], down_ref[0], preferred_element_type=F32).astype(BF16)
-    both = (own.astype(F32) + other_ref[...].astype(F32)).astype(BF16)
-    rows = out_ref.shape[1]
-    for offset in range(out_ref.shape[0]):
-        out_ref[(rank_ref[0] // 2) ^ offset] = both[offset * rows : (offset + 1) * rows]
-
-
-def down_own(rank, hidden, down, other, experts):
-    return call(
-        down_kernel,
-        "down_own_rows",
-        in_specs=[SMEM, VMEM, VMEM, VMEM],
-        out_specs=VMEM,
-        out_shape=jax.ShapeDtypeStruct((experts, other.shape[0] // experts, D), BF16),
-    )(rank, hidden, down, other)
+        first = jnp.dot(hidden[0], down0[0], preferred_element_type=F32).astype(BF16)
+        second = jnp.dot(hidden[1], down1[0], preferred_element_type=F32).astype(BF16)
+        out_ref[...] = (first.astype(F32) + second.astype(F32)).astype(BF16)
+
+
+def expert_rows(x, own, other):
+    count = x.shape[0]
+    weights = pl.BlockSpec((1, STEP, HALF), lambda k: (0, jnp.minimum(k, STEPS - 1), 0))
+    down = pl.BlockSpec((1, HALF, STEP), lambda k: (0, 0, jnp.maximum(k - STEPS, 0)))
+    return call(
+        expert_kernel,
+        "expert_rows",
+        flops=12 * count * D * HALF,
+        moved=12 * D * HALF + 4 * count * D,
+        grid=(2 * STEPS,),
+        in_specs=[pl.BlockSpec((count, STEP), lambda k: (0, jnp.minimum(k, STEPS - 1)))] + [weights] * 4 + [down] * 2,
+        out_specs=pl.BlockSpec((count, STEP), lambda k: (0, jnp.maximum(k - STEPS, 0))),
+        scratch_shapes=[pltpu.VMEM((4, count, HALF), F32), pltpu.VMEM((2, count, HALF), BF16)],
+        out_shape=jax.ShapeDtypeStruct((count, D), BF16),
+    )(x, own[0], own[1], other[0], other[1], own[2], other[2])
 
 
 class Split:
@@ -213,6 +184,7 @@
     return call(
         functools.partial(split_kernel, split),
         "split_queries",
+        moved=4 * queries.size,
         in_specs=[SMEM, VMEM],
         out_specs=VMEM,
         out_shape=jax.ShapeDtypeStruct((split.chips, tok, 2 * split.pairs * (NOPE + ROPE)), BF16),
@@ -230,6 +202,7 @@
     return call(
         functools.partial(join_kernel, split),
         "join_values",
+        moved=4 * values.size,
         in_specs=[SMEM, VMEM],
         out_specs=VMEM,
         out_shape=jax.ShapeDtypeStruct((values.shape[1], HEADS * VDIM), BF16),
@@ -329,6 +302,8 @@
     return call(
         functools.partial(attention_kernel, split),
         "causal_attention",
+        flops=4 * count * length * split.pairs * (2 * LATENT + ROPE),
+        moved=4 * (queries.size + keys.size + weights.size),
         grid_spec=pltpu.PrefetchScalarGridSpec(
             num_scalar_prefetch=1,
             grid=(split.pairs,),
@@ -407,19 +382,18 @@
     group = lax.axis_index("groups").astype(jnp.int32).reshape(1)
     place = jnp.concatenate([rank, group])
 
-    named = routes ^ (rank // 2)
-    chips = range(1, experts)
-
     direct, later = gather_masks(split)
     keys = jnp.stack([latent_kv] + [send(latent_kv, offset) for offset in direct])
 
-    buckets = build_buckets(named, moe_input, experts, rows)
-    own = [buckets[0]] + [send(buckets[m], 2 * m) for m in chips]
-    keys = after(keys, own[1])
+    buckets = after(build_buckets(routes, moe_input, experts, rows), keys)
+    arrived = swap_chips(buckets.reshape(experts, rows, D)).reshape(experts * rows, D)
+
     for mask in later:
         keys = jnp.concatenate([keys, send(keys, mask)], axis=0)
-    sent = after(split_queries(split, rank, queries), keys, *own[1 : experts // 2])
-    held = split.exchange(sent)
+    own_half = [expert_gate, expert_up, expert_down]
+    other_half = [send(part, 1) for part in own_half]
+    sent = after(split_queries(split, rank, queries), keys, arrived, *other_half)
+    held = split.exchange(sent).reshape(experts * tok, -1)
 
     weights = jnp.concatenate(
         [
@@ -430,16 +404,12 @@
     )
     if split.wide:
         weights = lax.dynamic_slice_in_dim(weights, group[0] * split.own_pairs, split.own_pairs, axis=0)
-        weights = after(weights, *own[1 : experts // 2])
+        weights = after(weights, arrived)
         weights = jnp.concatenate([weights, send(weights, shards // 2)], axis=0)
 
-    other = [send(piece, 1) for piece in own]
-    hidden, for_other = hidden_rows(own, other, expert_gate, expert_up, expert_down)
-    result = down_own(rank, hidden, expert_down, send(for_other, 1), experts)
-
+    result = expert_rows(arrived, own_half, other_half)
     result, held, weights = lax.optimization_barrier((result, held, weights))
-    back = swap_chips(result)
-    held = held.reshape(experts * tok, held.shape[2])
+    back = swap_chips(result.reshape(experts, rows, D))
     values = attention(split, place, held, keys, send(keys, 1), weights, send(weights, 1))
     values, back = lax.optimization_barrier((values, back))
     values = split.exchange(values.reshape(experts, tok, values.shape[1]))

time: 177 us -> 165 us (0.932)
  waiting for transfers between devices: 95.7 us -> 78.9 us
  local copies, waits for them, and re-layouts: 6.54 us -> 10.3 us
    ppermute x24 -> x11, waiting for transfers between devices: 70.4 us -> 55.9 us  [send(): lax.ppermute(array, ('groups', 'ctx'), [(i, i ^ mask) for i in range(coun...]
    all_to_all x1 -> x2, starting transfers between devices: 3.92 us -> 13.5 us  [swap_chips(): lax.all_to_all(array, 'ctx', split_axis=0, concat_axis=0, axis_index_grou...]
    ppermute x24 -> x11, starting transfers between devices: 25.9 us -> 17.2 us  [send(): lax.ppermute(array, ('groups', 'ctx'), [(i, i ^ mask) for i in range(coun...]
    unnamed x14 -> x22, local copies, waits for them, and re-layouts: 4.32 us -> 7.14 us
    concatenate x1 -> x2, local copies, waits for them, and re-layouts: 0.91 us -> 2.86 us  [on_device(): keys = jnp.concatenate([keys, send(keys, mask)], axis=0)]
    all_to_all x1 -> x2, waiting for transfers between devices: 12.4 us -> 10.9 us  [swap_chips(): lax.all_to_all(array, 'ctx', split_axis=0, concat_axis=0, axis_index_grou...]
    pallas_call x7 -> x6, Pallas kernels: 34.2 us -> 34.4 us  [the longest x1 14.9 us: attention(): call(functools.partial(attention_kernel, split), 'causal_attention', flop...]
  transfers between devices with their start and end apart: 27 -> 15, of which waited for: 17 -> 8; matrix products, arithmetic and copies ran while one was open for 3% -> 5% of each run, Pallas kernels for 19% -> 20%
where the time goes in v7:
time: 165 us
  waiting for transfers between devices  78.9 us (48%)
  starting transfers between devices  40 us (24%)
  Pallas kernels  34.4 us (21%)
  local copies, waits for them, and re-layouts  10.3 us (6%)
    ppermute x11, waiting for transfers between devices, send(): lax.ppermute(array, ('groups', 'ctx'), [(i, i ^ mask) for i in range(coun...  55.9 us
    ppermute x11, starting transfers between devices, send(): lax.ppermute(array, ('groups', 'ctx'), [(i, i ^ mask) for i in range(coun...  17.2 us
    pallas_call x1, Pallas kernels, attention(): call(functools.partial(attention_kernel, split), 'causal_attention', flop...  14.9 us
    all_to_all x2, starting transfers between devices, swap_chips(): lax.all_to_all(array, 'ctx', split_axis=0, concat_axis=0, axis_index_grou...  13.5 us
    pallas_call x1, Pallas kernels, expert_rows(): call(expert_kernel, 'expert_rows', flops=12 * count * D * HALF, moved=12...  13.3 us
    all_to_all x2, waiting for transfers between devices, exchange(): lax.all_to_all(array, ('groups', 'ctx'), split_axis=0, concat_axis=0, axi...  12.1 us
    all_to_all x2, waiting for transfers between devices, swap_chips(): lax.all_to_all(array, 'ctx', split_axis=0, concat_axis=0, axis_index_grou...  10.9 us
    all_to_all x2, starting transfers between devices, exchange(): lax.all_to_all(array, ('groups', 'ctx'), split_axis=0, concat_axis=0, axi...  9.32 us
  transfers between devices with their start and end apart: 15, of which 8 were waited for; matrix products, arithmetic and copies ran while one was open for 5% of the time, Pallas kernels for 20%

profile of v7, /device:TPU:0, one launch (start us, length us, event | category | flops | bytes accessed | tf_op | source)
XLA Modules:
  0.0 164.5 jit_solution(14371757066661195144)
XLA Ops:
  0.6 0.5 collective-permute-start.3
  1.1 0.1 collective-permute-start.4
  1.2 0.4 collective-permute-start.5
  1.7 3.7 %collective-permute-start = (bf16[64,576]{1,0:T(8,128)(2,1)}, bf16[64,576]{1,0:T(8,128)(2,1)S(1)}, u32[]{:S(2)}, u32[]{:S(2)}) collective-permute-start(bf16[64,576]{1,0:T(8,128)(2,1)} %param.11), channel_id=1, source_target_pairs={{0,8},{1,9},{2,10},{3,11},{4,12},{5,13},{6,14},{7,15},{8,0},{9,1},... | collective-permute-start | bytes 221192 | tf_op jit(solution)/shard_map/ppermute | solution.py:330
  5.3 1.6 collective-permute-start.1
  6.9 3.5 %collective-permute-done = bf16[64,576]{1,0:T(8,128)(2,1)S(1)} collective-permute-done((bf16[64,576]{1,0:T(8,128)(2,1)}, bf16[64,576]{1,0:T(8,128)(2,1)S(1)}, u32[]{:S(2)}, u32[]{:S(2)}) %collective-permute-start) | collective-permute-done | bytes 73760 | tf_op jit(solution)/shard_map/ppermute | solution.py:330
  10.4 0.0 copy-start.5
  10.4 3.4 %collective-permute-start.2 = (bf16[64,576]{1,0:T(8,128)(2,1)}, bf16[64,576]{1,0:T(8,128)(2,1)S(1)}, u32[]{:S(2)}, u32[]{:S(2)}) collective-permute-start(bf16[64,576]{1,0:T(8,128)(2,1)} %param.11), channel_id=1, source_target_pairs={{0,12},{1,13},{2,14},{3,15},{4,8},{5,9},{6,10},{7,11},{8,4},{9,5},... | collective-permute-start | bytes 221192 | tf_op jit(solution)/shard_map/ppermute | solution.py:330
  13.9 0.8 copy.12.routes_ref
  14.7 0.0 copy-start.1
  14.7 1.0 copy-done.1
  15.7 0.0 copy-start.4
  15.7 2.0 %bucket_rows.1 = bf16[192,3584]{1,0:T(8,128)(2,1)} custom-call(s32[64,2]{1,0:T(8,128)S(1)} %copy.12.routes_ref, bf16[64,3584]{1,0:T(8,128)(2,1)S(1)} %copy-done.1), custom_call_target="tpu_custom_call" | custom-call | bytes 1835008 | tf_op jit(solution)/shard_map/bucket_rows/pallas_call | solution.py:66
  17.7 0.0 collective-permute-done.1
  17.7 0.0 collective-permute-done.2
  17.7 0.0 copy-done.4
  17.7 0.1 pad_maximum_fusion.1
  17.8 0.0 copy-done.5
  17.8 4.9 %all-to-all-start = ((bf16[8,24,3584]{2,1,0:T(8,128)(2,1)}), bf16[8,24,3584]{2,1,0:T(8,128)(2,1)S(1)}, u32[]{:S(2)}, u32[]{:S(2)}) async-start(bf16[8,24,3584]{2,1,0:T(8,128)(2,1)} %bitcast.6), calls=%async_computation | async-start | bytes 2752512 | tf_op jit(solution)/shard_map/all_to_all | solution.py:335
  22.7 0.0 copy-start
  22.7 0.7 constant_dynamic-update-slice_fusion.4
  23.3 2.0 %collective-permute-start.6 = (bf16[4,64,576]{2,1,0:T(8,128)(2,1)S(1)}, bf16[4,64,576]{2,1,0:T(8,128)(2,1)S(1)}, u32[]{:S(2)}, u32[]{:S(2)}) collective-permute-start(bf16[4,64,576]{2,1,0:T(8,128)(2,1)S(1)} %pad_maximum_fusion.1), channel_id=1, source_target_pairs={{0,2},{1,3},{2,0},{3,1},{4,6},{5,7},{6,4},{7,5},{8,10},{9,11},{10,... | collective-permute-start | bytes 884744 | tf_op jit(solution)/shard_map/ppermute | solution.py:330
  25.4 1.5 constant_dynamic-update-slice_fusion.3
  26.9 0.7 constant_dynamic-update-slice_fusion.2
  27.6 0.7 constant_dynamic-update-slice_fusion.1
  28.2 15.8 %collective-permute-done.6 = bf16[4,64,576]{2,1,0:T(8,128)(2,1)S(1)} collective-permute-done((bf16[4,64,576]{2,1,0:T(8,128)(2,1)S(1)}, bf16[4,64,576]{2,1,0:T(8,128)(2,1)S(1)}, u32[]{:S(2)}, u32[]{:S(2)}) %collective-permute-start.6) | collective-permute-done | bytes 294944 | tf_op jit(solution)/shard_map/ppermute | solution.py:330
  44.0 0.9 constant_dynamic-update-slice_fusion
  44.9 1.5 collective-permute-start.7
  46.4 0.0 copy-done
  46.4 1.6 split_queries.1
  47.9 11.0 %collective-permute-done.7 = bf16[8,64,576]{2,1,0:T(8,128)(2,1)} collective-permute-done((bf16[8,64,576]{2,1,0:T(8,128)(2,1)}, bf16[8,64,576]{2,1,0:T(8,128)(2,1)}, u32[]{:S(2)}, u32[]{:S(2)}) %collective-permute-start.7) | collective-permute-done | bytes 589856 | tf_op jit(solution)/shard_map/ppermute | solution.py:330
  59.0 2.0 %constant_dynamic-update-slice_fusion.5.kv_ref = bf16[16,64,576]{2,1,0:T(8,128)(2,1)} fusion(bf16[16,64,576]{2,1,0:T(8,128)(2,1)} %get-tuple-element.19, bf16[8,64,576]{2,1,0:T(8,128)(2,1)} %collective-permute-done.7), kind=kLoop, calls=%fused_computation.10 | loop fusion | bytes 1310720 | tf_op jit(solution)/shard_map/concatenate | solution.py:392
  60.9 0.0 all-to-all-done
  60.9 0.0 collective-permute-done.3.gate1
  60.9 0.0 collective-permute-done.4.up1
  60.9 0.0 collective-permute-done.5.down1
  61.0 0.0 copy-start.2
  61.0 5.8 %all-to-all-start.1 = ((bf16[8,64,1536]{2,1,0:T(8,128)(2,1)}), bf16[8,64,1536]{2,1,0:T(8,128)(2,1)}, u32[]{:S(2)}, u32[]{:S(2)}) async-start(bf16[8,64,1536]{2,1,0:T(8,128)(2,1)} %split_queries.1), calls=%async_computation.1 | async-start | bytes 3145728 | tf_op jit(solution)/shard_map/all_to_all | solution.py:166
  66.7 0.0 copy-start.3
  66.7 0.0 copy-done.2
  66.7 0.3 copy.13
  67.0 0.7 copy-done.3
  67.8 3.5 %collective-permute-start.8 = (bf16[1,4,512,128]{3,2,1,0:T(8,128)(2,1)S(1)}, bf16[1,4,512,128]{3,2,1,0:T(8,128)(2,1)S(1)}, u32[]{:S(2)}, u32[]{:S(2)}) collective-permute-start(bf16[1,4,512,128]{3,2,1,0:T(8,128)(2,1)S(1)} %fusion), channel_id=1, source_target_pairs={{0,8},{1,9},{2,10},{3,11},{4,12},{5,13},{6,14},{7,15},{8,0},{9,1},... | collective-permute-start | bytes 1572872 | tf_op jit(solution)/shard_map/ppermute | solution.py:330
  71.3 21.7 %collective-permute-done.8 = bf16[1,4,512,128]{3,2,1,0:T(8,128)(2,1)S(1)} collective-permute-done((bf16[1,4,512,128]{3,2,1,0:T(8,128)(2,1)S(1)}, bf16[1,4,512,128]{3,2,1,0:T(8,128)(2,1)S(1)}, u32[]{:S(2)}, u32[]{:S(2)}) %collective-permute-start.8) | collective-permute-done | bytes 524320 | tf_op jit(solution)/shard_map/ppermute | solution.py:330
  92.9 0.1 pad_maximum_fusion.weight_ref
  93.0 13.3 %expert_rows.1 = bf16[192,3584]{1,0:T(8,128)(2,1)} custom-call(bf16[192,3584]{1,0:T(8,128)(2,1)S(1)} %bitcast.24, bf16[1,3584,512]{2,1,0:T(8,128)(2,1)} %gate0.1, bf16[1,3584,512]{2,1,0:T(8,128)(2,1)} %up0.1, bf16[1,3584,512]{2,1,0:T(8,128)(2,1)} %collective-permute-done.3.gate1, bf16[1,3584,512]{2,1,0:T(8,128)(2,1)} %collective-permute-done.4.up1, ...), custom_call_target="tpu_custom_call" | custom-call | flops 4227858432 | bytes 24772608 | tf_op jit(solution)/shard_map/expert_rows/pallas_call | solution.py:125
  106.3 0.0 all-to-all-done.1
  106.3 8.6 %all-to-all-start.2 = ((bf16[8,24,3584]{2,1,0:T(8,128)(2,1)}), bf16[8,24,3584]{2,1,0:T(8,128)(2,1)S(1)}, u32[]{:S(2)}, u32[]{:S(2)}) async-start(bf16[8,24,3584]{2,1,0:T(8,128)(2,1)} %bitcast.12), calls=%async_computation.2 | async-start | bytes 2752512 | tf_op jit(solution)/shard_map/all_to_all | solution.py:335
  114.9 0.0 collective-permute-start.9
  114.9 0.5 collective-permute-start.10
  115.4 0.1 pad_add_fusion.rank_ref
  115.5 3.8 %collective-permute-done.9.other_kv_ref = bf16[16,64,576]{2,1,0:T(8,128)(2,1)S(1)} collective-permute-done((bf16[16,64,576]{2,1,0:T(8,128)(2,1)}, bf16[16,64,576]{2,1,0:T(8,128)(2,1)S(1)}, u32[]{:S(2)}, u32[]{:S(2)}) %collective-permute-start.9) | collective-permute-done | bytes 1179680 | tf_op jit(solution)/shard_map/ppermute | solution.py:330
  119.3 0.0 copy-start.7
  119.3 0.1 collective-permute-done.10.other_weight_ref
  119.4 0.9 copy-done.7
  120.4 14.9 %causal_attention.1 = bf16[512,1024]{1,0:T(8,128)(2,1)} custom-call(s32[2]{0:T(128)S(1)} %pad_add_fusion.rank_ref, bf16[512,1536]{1,0:T(8,128)(2,1)} %bitcast.8.query_ref, bf16[16,64,576]{2,1,0:T(8,128)(2,1)} %constant_dynamic-update-slice_fusion.5.kv_ref, bf16[16,64,576]{2,1,0:T(8,128)(2,1)} %copy-done.7, ...), custom_call_target="tpu_custom_call" | custom-call | flops 9126805504 | bytes 7602176 | tf_op jit(solution)/shard_map/causal_attention/pallas_call | solution.py:302
  135.3 0.0 copy-start.6
  135.3 10.9 %all-to-all-done.2 = bf16[8,24,3584]{2,1,0:T(8,128)(2,1)S(1)} async-done(((bf16[8,24,3584]{2,1,0:T(8,128)(2,1)}), bf16[8,24,3584]{2,1,0:T(8,128)(2,1)S(1)}, u32[]{:S(2)}, u32[]{:S(2)}) %all-to-all-start.2) | async-done | bytes 1376288 | tf_op jit(solution)/shard_map/all_to_all | solution.py:335
  146.1 3.6 %all-to-all-start.3 = ((bf16[8,64,1024]{2,1,0:T(8,128)(2,1)}), bf16[8,64,1024]{2,1,0:T(8,128)(2,1)S(1)}, u32[]{:S(2)}, u32[]{:S(2)}) async-start(bf16[8,64,1024]{2,1,0:T(8,128)(2,1)} %bitcast.13), calls=%async_computation.3 | async-start | bytes 2097152 | tf_op jit(solution)/shard_map/all_to_all | solution.py:166
  149.7 0.0 copy-done.6
  149.7 0.1 copy.15.gates_ref
  149.8 1.5 combine_routes.1
  151.4 12.1 %all-to-all-done.3.x_ref = bf16[8,64,1024]{2,1,0:T(8,128)(2,1)S(1)} async-done(((bf16[8,64,1024]{2,1,0:T(8,128)(2,1)}), bf16[8,64,1024]{2,1,0:T(8,128)(2,1)S(1)}, u32[]{:S(2)}, u32[]{:S(2)}) %all-to-all-start.3) | async-done | bytes 1048608 | tf_op jit(solution)/shard_map/all_to_all | solution.py:166
  163.4 1.1 join_values.1
  (1 shorter events, 0.0 us)
Async XLA Ops:
  0.6 60.3 %collective-permute-start.3 = (bf16[1,3584,512]{2,1,0:T(8,128)(2,1)}, bf16[1,3584,512]{2,1,0:T(8,128)(2,1)}, u32[]{:S(2)}, u32[]{:S(2)}) collective-permute-start(bf16[1,3584,512]{2,1,0:T(8,128)(2,1)} %gate0.1), channel_id=1, source_target_pairs={{0,1},{1,0},{2,3},{3,2},{4,5},{5,4},{6,7},{7,6},{8,9},{9,8},{10,11... | collective-permute-start | bytes 11010056 | tf_op jit(solution)/shard_map/ppermute | solution.py:330
  1.1 59.8 %collective-permute-start.4 = (bf16[1,3584,512]{2,1,0:T(8,128)(2,1)}, bf16[1,3584,512]{2,1,0:T(8,128)(2,1)}, u32[]{:S(2)}, u32[]{:S(2)}) collective-permute-start(bf16[1,3584,512]{2,1,0:T(8,128)(2,1)} %up0.1), channel_id=1, source_target_pairs={{0,1},{1,0},{2,3},{3,2},{4,5},{5,4},{6,7},{7,6},{8,9},{9,8},{10,11... | collective-permute-start | bytes 11010056 | tf_op jit(solution)/shard_map/ppermute | solution.py:330
  1.2 59.7 %collective-permute-start.5 = (bf16[1,512,3584]{2,1,0:T(8,128)(2,1)}, bf16[1,512,3584]{2,1,0:T(8,128)(2,1)}, u32[]{:S(2)}, u32[]{:S(2)}) collective-permute-start(bf16[1,512,3584]{2,1,0:T(8,128)(2,1)} %down0.1), channel_id=1, source_target_pairs={{0,1},{1,0},{2,3},{3,2},{4,5},{5,4},{6,7},{7,6},{8,9},{9,8},{10,11... | collective-permute-start | bytes 11010056 | tf_op jit(solution)/shard_map/ppermute | solution.py:330
  1.7 8.8 %collective-permute-start = (bf16[64,576]{1,0:T(8,128)(2,1)}, bf16[64,576]{1,0:T(8,128)(2,1)S(1)}, u32[]{:S(2)}, u32[]{:S(2)}) collective-permute-start(bf16[64,576]{1,0:T(8,128)(2,1)} %param.11), channel_id=1, source_target_pairs={{0,8},{1,9},{2,10},{3,11},{4,12},{5,13},{6,14},{7,15},{8,0},{9,1},... | collective-permute-start | bytes 221192 | tf_op jit(solution)/shard_map/ppermute | solution.py:330
  5.3 12.4 %collective-permute-start.1 = (bf16[64,576]{1,0:T(8,128)(2,1)}, bf16[64,576]{1,0:T(8,128)(2,1)S(1)}, u32[]{:S(2)}, u32[]{:S(2)}) collective-permute-start(bf16[64,576]{1,0:T(8,128)(2,1)} %param.11), channel_id=1, source_target_pairs={{0,4},{1,5},{2,6},{3,7},{4,0},{5,1},{6,2},{7,3},{8,12},{9,13},{10,... | collective-permute-start | bytes 221192 | tf_op jit(solution)/shard_map/ppermute | solution.py:330
  10.4 7.4 %copy-start.5 = (bf16[64,576]{1,0:T(8,128)(2,1)}, bf16[64,576]{1,0:T(8,128)(2,1)S(1)}, u32[]{:S(2)}) copy-start(bf16[64,576]{1,0:T(8,128)(2,1)S(1)} %collective-permute-done) | copy-start | bytes 221188
  10.4 7.3 %collective-permute-start.2 = (bf16[64,576]{1,0:T(8,128)(2,1)}, bf16[64,576]{1,0:T(8,128)(2,1)S(1)}, u32[]{:S(2)}, u32[]{:S(2)}) collective-permute-start(bf16[64,576]{1,0:T(8,128)(2,1)} %param.11), channel_id=1, source_target_pairs={{0,12},{1,13},{2,14},{3,15},{4,8},{5,9},{6,10},{7,11},{8,4},{9,5},... | collective-permute-start | bytes 221192 | tf_op jit(solution)/shard_map/ppermute | solution.py:330
  14.7 1.0 copy-start.1
  15.7 2.0 %copy-start.4 = (bf16[64,576]{1,0:T(8,128)(2,1)S(1)}, bf16[64,576]{1,0:T(8,128)(2,1)}, u32[]{:S(2)}) copy-start(bf16[64,576]{1,0:T(8,128)(2,1)} %param.11) | copy-start | bytes 221188
  17.8 43.1 %all-to-all-start = ((bf16[8,24,3584]{2,1,0:T(8,128)(2,1)}), bf16[8,24,3584]{2,1,0:T(8,128)(2,1)S(1)}, u32[]{:S(2)}, u32[]{:S(2)}) async-start(bf16[8,24,3584]{2,1,0:T(8,128)(2,1)} %bitcast.6), calls=%async_computation | async-start | bytes 2752512 | tf_op jit(solution)/shard_map/all_to_all | solution.py:335
  22.7 23.7 %copy-start = (bf16[64,12288]{1,0:T(8,128)(2,1)S(1)}, bf16[64,12288]{1,0:T(8,128)(2,1)}, u32[]{:S(2)}) copy-start(bf16[64,12288]{1,0:T(8,128)(2,1)} %x_ref.3) | copy-start | bytes 4718596
  23.3 20.7 %collective-permute-start.6 = (bf16[4,64,576]{2,1,0:T(8,128)(2,1)S(1)}, bf16[4,64,576]{2,1,0:T(8,128)(2,1)S(1)}, u32[]{:S(2)}, u32[]{:S(2)}) collective-permute-start(bf16[4,64,576]{2,1,0:T(8,128)(2,1)S(1)} %pad_maximum_fusion.1), channel_id=1, source_target_pairs={{0,2},{1,3},{2,0},{3,1},{4,6},{5,7},{6,4},{7,5},{8,10},{9,11},{10,... | collective-permute-start | bytes 884744 | tf_op jit(solution)/shard_map/ppermute | solution.py:330
  44.9 14.1 %collective-permute-start.7 = (bf16[8,64,576]{2,1,0:T(8,128)(2,1)}, bf16[8,64,576]{2,1,0:T(8,128)(2,1)}, u32[]{:S(2)}, u32[]{:S(2)}) collective-permute-start(bf16[8,64,576]{2,1,0:T(8,128)(2,1)} %get-tuple-element.18), channel_id=1, source_target_pairs={{0,16},{1,17},{2,18},{3,19},{4,20},{5,21},{6,22},{7,23},{8,24},{9,... | collective-permute-start | bytes 1769480 | tf_op jit(solution)/shard_map/ppermute | solution.py:330
  61.0 5.8 %copy-start.2 = (bf16[4,128,512]{2,1,0:T(8,128)(2,1)S(1)}, bf16[4,128,512]{2,1,0:T(8,128)(2,1)}, u32[]{:S(2)}) copy-start(bf16[4,128,512]{2,1,0:T(8,128)(2,1)} %param.12) | copy-start | bytes 1572868
  61.0 45.4 %all-to-all-start.1 = ((bf16[8,64,1536]{2,1,0:T(8,128)(2,1)}), bf16[8,64,1536]{2,1,0:T(8,128)(2,1)}, u32[]{:S(2)}, u32[]{:S(2)}) async-start(bf16[8,64,1536]{2,1,0:T(8,128)(2,1)} %split_queries.1), calls=%async_computation.1 | async-start | bytes 3145728 | tf_op jit(solution)/shard_map/all_to_all | solution.py:166
  66.7 1.0 copy-start.3
  67.8 25.1 %collective-permute-start.8 = (bf16[1,4,512,128]{3,2,1,0:T(8,128)(2,1)S(1)}, bf16[1,4,512,128]{3,2,1,0:T(8,128)(2,1)S(1)}, u32[]{:S(2)}, u32[]{:S(2)}) collective-permute-start(bf16[1,4,512,128]{3,2,1,0:T(8,128)(2,1)S(1)} %fusion), channel_id=1, source_target_pairs={{0,8},{1,9},{2,10},{3,11},{4,12},{5,13},{6,14},{7,15},{8,0},{9,1},... | collective-permute-start | bytes 1572872 | tf_op jit(solution)/shard_map/ppermute | solution.py:330
  106.3 39.8 %all-to-all-start.2 = ((bf16[8,24,3584]{2,1,0:T(8,128)(2,1)}), bf16[8,24,3584]{2,1,0:T(8,128)(2,1)S(1)}, u32[]{:S(2)}, u32[]{:S(2)}) async-start(bf16[8,24,3584]{2,1,0:T(8,128)(2,1)} %bitcast.12), calls=%async_computation.2 | async-start | bytes 2752512 | tf_op jit(solution)/shard_map/all_to_all | solution.py:335
  114.9 4.4 %collective-permute-start.9 = (bf16[16,64,576]{2,1,0:T(8,128)(2,1)}, bf16[16,64,576]{2,1,0:T(8,128)(2,1)S(1)}, u32[]{:S(2)}, u32[]{:S(2)}) collective-permute-start(bf16[16,64,576]{2,1,0:T(8,128)(2,1)} %constant_dynamic-update-slice_fusion.5.kv_ref), channel_id=1, source_target_pairs={{0,1},{1,0},{2,3},{3,2},{4,5},{5,4},{6,7},{7,6},{8,9},{9,8},{10,11... | collective-permute-start | bytes 3538952 | tf_op jit(solution)/shard_map/ppermute | solution.py:330
  114.9 4.5 %collective-permute-start.10 = (bf16[2,4,512,128]{3,2,1,0:T(8,128)(2,1)S(1)}, bf16[2,4,512,128]{3,2,1,0:T(8,128)(2,1)S(1)}, u32[]{:S(2)}, u32[]{:S(2)}) collective-permute-start(bf16[2,4,512,128]{3,2,1,0:T(8,128)(2,1)S(1)} %pad_maximum_fusion.weight_ref), channel_id=1, source_target_pairs={{0,1},{1,0},{2,3},{3,2},{4,5},{5,4},{6,7},{7,6},{8,9},{9,8},{10,11... | collective-permute-start | bytes 3145736 | tf_op jit(solution)/shard_map/ppermute | solution.py:330
  119.3 1.1 copy-start.7
  135.3 14.4 %copy-start.6 = (f32[64,2]{0,1:T(2,128)S(1)}, f32[64,2]{0,1:T(2,128)}, u32[]{:S(2)}) copy-start(f32[64,2]{0,1:T(2,128)} %param.16) | copy-start | bytes 1540
  146.1 17.3 %all-to-all-start.3 = ((bf16[8,64,1024]{2,1,0:T(8,128)(2,1)}), bf16[8,64,1024]{2,1,0:T(8,128)(2,1)S(1)}, u32[]{:S(2)}, u32[]{:S(2)}) async-start(bf16[8,64,1024]{2,1,0:T(8,128)(2,1)} %bitcast.13), calls=%async_computation.3 | async-start | bytes 2097152 | tf_op jit(solution)/shard_map/all_to_all | solution.py:166

commit v8 on v7

--- a/solution.py
+++ b/solution.py
@@ -349,7 +349,7 @@
 def gather_masks(split):
     top, below = split.shards // 2, split.shards // 4
     later = [1 << bit for bit in reversed(range(1, below.bit_length() - 1))]
-    return [top, below, top ^ below], later + ([split.shards] if split.wide else [])
+    return [top, below, top ^ below], ([split.shards] if split.wide else []) + later
 
 
 def gather_order(split):
@@ -390,9 +390,10 @@
 
     for mask in later:
         keys = jnp.concatenate([keys, send(keys, mask)], axis=0)
+    other_keys = send(keys, 1)
     own_half = [expert_gate, expert_up, expert_down]
     other_half = [send(part, 1) for part in own_half]
-    sent = after(split_queries(split, rank, queries), keys, arrived, *other_half)
+    sent = after(split_queries(split, rank, queries), other_keys, arrived, *other_half)
     held = split.exchange(sent).reshape(experts * tok, -1)
 
     weights = jnp.concatenate(
@@ -408,9 +409,10 @@
         weights = jnp.concatenate([weights, send(weights, shards // 2)], axis=0)
 
     result = expert_rows(arrived, own_half, other_half)
-    result, held, weights = lax.optimization_barrier((result, held, weights))
+    other_weights = send(after(weights, result), 1)
+    result, held = lax.optimization_barrier((result, held))
     back = swap_chips(result.reshape(experts, rows, D))
-    values = attention(split, place, held, keys, send(keys, 1), weights, send(weights, 1))
+    values = attention(split, place, held, keys, other_keys, weights, other_weights)
     values, back = lax.optimization_barrier((values, back))
     values = split.exchange(values.reshape(experts, tok, values.shape[1]))
     moe_out = combine(routes, gates, back.reshape(experts * rows, D), rows)

time: 165 us -> 153 us (0.927)
  starting transfers between devices: 40 us -> 30.1 us
    ppermute x11, waiting for transfers between devices: 55.9 us -> 33.9 us  [send(): lax.ppermute(array, ('groups', 'ctx'), [(i, i ^ mask) for i in range(coun...]
    all_to_all x2, waiting for transfers between devices: 12.1 us -> 29.1 us  [exchange(): lax.all_to_all(array, ('groups', 'ctx'), split_axis=0, concat_axis=0, axi...]
    all_to_all x2, starting transfers between devices: 13.5 us -> 7.14 us  [swap_chips(): lax.all_to_all(array, 'ctx', split_axis=0, concat_axis=0, axis_index_grou...]
    all_to_all x2, waiting for transfers between devices: 10.9 us -> 14.6 us  [swap_chips(): lax.all_to_all(array, 'ctx', split_axis=0, concat_axis=0, axis_index_grou...]
    ppermute x11, starting transfers between devices: 17.2 us -> 15 us  [send(): lax.ppermute(array, ('groups', 'ctx'), [(i, i ^ mask) for i in range(coun...]
    unnamed x22 -> x19, local copies, waits for them, and re-layouts: 7.14 us -> 6.28 us
  transfers between devices with their start and end apart: 15 -> 15, of which waited for: 8 -> 8; matrix products, arithmetic and copies ran while one was open for 5% -> 5% of each run, Pallas kernels for 20% -> 22%
where the time goes in v8:
time: 153 us; the launch traced here: 152 us
  waiting for transfers between devices  77.6 us (51%)
  Pallas kernels  34.3 us (22%)
  starting transfers between devices  30.1 us (20%)
  local copies, waits for them, and re-layouts  9.41 us (6%)
    ppermute x11, waiting for transfers between devices, send(): lax.ppermute(array, ('groups', 'ctx'), [(i, i ^ mask) for i in range(coun...  33.9 us
    all_to_all x2, waiting for transfers between devices, exchange(): lax.all_to_all(array, ('groups', 'ctx'), split_axis=0, concat_axis=0, axi...  29.1 us
    ppermute x11, starting transfers between devices, send(): lax.ppermute(array, ('groups', 'ctx'), [(i, i ^ mask) for i in range(coun...  15 us
    pallas_call x1, Pallas kernels, attention(): call(functools.partial(attention_kernel, split), 'causal_attention', flop...  15 us
    all_to_all x2, waiting for transfers between devices, swap_chips(): lax.all_to_all(array, 'ctx', split_axis=0, concat_axis=0, axis_index_grou...  14.6 us
    pallas_call x1, Pallas kernels, expert_rows(): call(expert_kernel, 'expert_rows', flops=12 * count * D * HALF, moved=12...  13.2 us
    all_to_all x2, starting transfers between devices, exchange(): lax.all_to_all(array, ('groups', 'ctx'), split_axis=0, concat_axis=0, axi...  7.99 us
    all_to_all x2, starting transfers between devices, swap_chips(): lax.all_to_all(array, 'ctx', split_axis=0, concat_axis=0, axis_index_grou...  7.14 us
  transfers between devices with their start and end apart: 15, of which 8 were waited for; matrix products, arithmetic and copies ran while one was open for 5% of the time, Pallas kernels for 22%

profile of v8, /device:TPU:0, one launch (start us, length us, event | category | flops | bytes accessed | tf_op | source)
XLA Modules:
  0.0 152.4 jit_solution(3564099127610508295)
XLA Ops:
  0.6 0.0 copy-start.4
  0.6 0.5 collective-permute-start.3
  1.2 0.1 collective-permute-start.4
  1.2 0.4 collective-permute-start.5
  1.7 3.7 %collective-permute-start = (bf16[64,576]{1,0:T(8,128)(2,1)}, bf16[64,576]{1,0:T(8,128)(2,1)S(1)}, u32[]{:S(2)}, u32[]{:S(2)}) collective-permute-start(bf16[64,576]{1,0:T(8,128)(2,1)} %param.11), channel_id=1, source_target_pairs={{0,8},{1,9},{2,10},{3,11},{4,12},{5,13},{6,14},{7,15},{8,0},{9,1},... | collective-permute-start | bytes 221192 | tf_op jit(solution)/shard_map/ppermute | solution.py:330
  5.3 1.6 %collective-permute-start.1 = (bf16[64,576]{1,0:T(8,128)(2,1)}, bf16[64,576]{1,0:T(8,128)(2,1)S(1)}, u32[]{:S(2)}, u32[]{:S(2)}) collective-permute-start(bf16[64,576]{1,0:T(8,128)(2,1)} %param.11), channel_id=1, source_target_pairs={{0,4},{1,5},{2,6},{3,7},{4,0},{5,1},{6,2},{7,3},{8,12},{9,13},{10,... | collective-permute-start | bytes 221192 | tf_op jit(solution)/shard_map/ppermute | solution.py:330
  6.9 3.5 %collective-permute-done = bf16[64,576]{1,0:T(8,128)(2,1)S(1)} collective-permute-done((bf16[64,576]{1,0:T(8,128)(2,1)}, bf16[64,576]{1,0:T(8,128)(2,1)S(1)}, u32[]{:S(2)}, u32[]{:S(2)}) %collective-permute-start) | collective-permute-done | bytes 73760 | tf_op jit(solution)/shard_map/ppermute | solution.py:330
  10.4 3.4 %collective-permute-start.2 = (bf16[64,576]{1,0:T(8,128)(2,1)}, bf16[64,576]{1,0:T(8,128)(2,1)S(1)}, u32[]{:S(2)}, u32[]{:S(2)}) collective-permute-start(bf16[64,576]{1,0:T(8,128)(2,1)} %param.11), channel_id=1, source_target_pairs={{0,12},{1,13},{2,14},{3,15},{4,8},{5,9},{6,10},{7,11},{8,4},{9,5},... | collective-permute-start | bytes 221192 | tf_op jit(solution)/shard_map/ppermute | solution.py:330
  13.9 1.6 %constant_dynamic-update-slice_fusion.4 = (bf16[8,64,576]{2,1,0:T(8,128)(2,1)}, bf16[16,64,576]{2,1,0:T(8,128)(2,1)}) fusion(bf16[64,576]{1,0:T(8,128)(2,1)} %param.11), kind=kLoop, calls=%fused_computation.8 | loop fusion | bytes 237568
  15.5 0.8 copy.12.routes_ref
  16.3 0.0 copy-start.1
  16.3 1.0 copy-done.1
  17.3 2.0 %bucket_rows.1 = bf16[192,3584]{1,0:T(8,128)(2,1)} custom-call(s32[64,2]{1,0:T(8,128)S(1)} %copy.12.routes_ref, bf16[64,3584]{1,0:T(8,128)(2,1)S(1)} %copy-done.1), custom_call_target="tpu_custom_call" | custom-call | bytes 1835008 | tf_op jit(solution)/shard_map/bucket_rows/pallas_call | solution.py:66
  19.3 0.0 collective-permute-done.1
  19.3 0.0 collective-permute-done.2
  19.3 0.0 copy-done.4
  19.3 0.1 pad_maximum_fusion
  19.4 1.6 %collective-permute-start.6 = (bf16[4,64,576]{2,1,0:T(8,128)(2,1)S(1)}, bf16[4,64,576]{2,1,0:T(8,128)(2,1)}, u32[]{:S(2)}, u32[]{:S(2)}) collective-permute-start(bf16[4,64,576]{2,1,0:T(8,128)(2,1)S(1)} %pad_maximum_fusion), channel_id=1, source_target_pairs={{0,16},{1,17},{2,18},{3,19},{4,20},{5,21},{6,22},{7,23},{8,24},{9,... | collective-permute-start | bytes 884744 | tf_op jit(solution)/shard_map/ppermute | solution.py:330
  20.9 3.6 %all-to-all-start = ((bf16[8,24,3584]{2,1,0:T(8,128)(2,1)}), bf16[8,24,3584]{2,1,0:T(8,128)(2,1)S(1)}, u32[]{:S(2)}, u32[]{:S(2)}) async-start(bf16[8,24,3584]{2,1,0:T(8,128)(2,1)} %bitcast.6), calls=%async_computation | async-start | bytes 2752512 | tf_op jit(solution)/shard_map/all_to_all | solution.py:335
  24.5 0.7 constant_dynamic-update-slice_fusion.3
  25.2 0.7 constant_dynamic-update-slice_fusion.2
  25.9 0.0 copy-start
  25.9 0.7 constant_dynamic-update-slice_fusion.1
  26.5 2.4 %collective-permute-done.6 = bf16[4,64,576]{2,1,0:T(8,128)(2,1)} collective-permute-done((bf16[4,64,576]{2,1,0:T(8,128)(2,1)S(1)}, bf16[4,64,576]{2,1,0:T(8,128)(2,1)}, u32[]{:S(2)}, u32[]{:S(2)}) %collective-permute-start.6) | collective-permute-done | bytes 294944 | tf_op jit(solution)/shard_map/ppermute | solution.py:330
  29.0 1.9 %constant_dynamic-update-slice_fusion = (bf16[8,64,576]{2,1,0:T(8,128)(2,1)}, bf16[16,64,576]{2,1,0:T(8,128)(2,1)}) fusion(bf16[8,64,576]{2,1,0:T(8,128)(2,1)} %get-tuple-element.20, bf16[4,64,576]{2,1,0:T(8,128)(2,1)} %collective-permute-done.6, bf16[16,64,576]{2,1,0:T(8,128)(2,1)} %get-tuple-element.21), kind=kLoop, calls=%fused_computation.4 | loop fusion | bytes 983040 | tf_op jit(solution)/shard_map/concatenate | solution.py:392
  30.8 1.5 collective-permute-start.7
  32.3 23.5 %collective-permute-done.7 = bf16[8,64,576]{2,1,0:T(8,128)(2,1)S(1)} collective-permute-done((bf16[8,64,576]{2,1,0:T(8,128)(2,1)}, bf16[8,64,576]{2,1,0:T(8,128)(2,1)S(1)}, u32[]{:S(2)}, u32[]{:S(2)}) %collective-permute-start.7) | collective-permute-done | bytes 589856 | tf_op jit(solution)/shard_map/ppermute | solution.py:330
  55.8 0.9 constant_dynamic-update-slice_fusion.5.kv_ref
  56.7 0.0 collective-permute-start.8
  56.7 0.0 copy-done
  56.7 1.5 %split_queries.1 = bf16[8,64,1536]{2,1,0:T(8,128)(2,1)} custom-call(s32[1]{0:T(128)} %bitcast.rank_ref, bf16[64,12288]{1,0:T(8,128)(2,1)S(1)} %copy-done), custom_call_target="tpu_custom_call" | custom-call | bytes 3145728 | tf_op jit(solution)/shard_map/split_queries/pallas_call | solution.py:184
  58.3 1.8 %collective-permute-done.8.other_kv_ref = bf16[16,64,576]{2,1,0:T(8,128)(2,1)} collective-permute-done((bf16[16,64,576]{2,1,0:T(8,128)(2,1)}, bf16[16,64,576]{2,1,0:T(8,128)(2,1)}, u32[]{:S(2)}, u32[]{:S(2)}) %collective-permute-start.8) | collective-permute-done | bytes 1179680 | tf_op jit(solution)/shard_map/ppermute | solution.py:330
  60.1 0.0 all-to-all-done
  60.1 0.0 collective-permute-done.3.gate1
  60.1 0.0 collective-permute-done.4.up1
  60.1 0.0 collective-permute-done.5.down1
  60.1 0.0 copy-start.2
  60.2 4.4 %all-to-all-start.1 = ((bf16[8,64,1536]{2,1,0:T(8,128)(2,1)}), bf16[8,64,1536]{2,1,0:T(8,128)(2,1)}, u32[]{:S(2)}, u32[]{:S(2)}) async-start(bf16[8,64,1536]{2,1,0:T(8,128)(2,1)} %split_queries.1), calls=%async_computation.1 | async-start | bytes 3145728 | tf_op jit(solution)/shard_map/all_to_all | solution.py:166
  64.6 0.0 copy-start.3
  64.6 0.0 copy-done.2
  64.6 0.3 copy.13
  64.9 0.7 copy-done.3
  65.7 2.1 %collective-permute-start.9 = (bf16[1,4,512,128]{3,2,1,0:T(8,128)(2,1)S(1)}, bf16[1,4,512,128]{3,2,1,0:T(8,128)(2,1)S(1)}, u32[]{:S(2)}, u32[]{:S(2)}) collective-permute-start(bf16[1,4,512,128]{3,2,1,0:T(8,128)(2,1)S(1)} %fusion), channel_id=1, source_target_pairs={{0,8},{1,9},{2,10},{3,11},{4,12},{5,13},{6,14},{7,15},{8,0},{9,1},... | collective-permute-start | bytes 1572872 | tf_op jit(solution)/shard_map/ppermute | solution.py:330
  67.8 13.2 %expert_rows.1 = bf16[192,3584]{1,0:T(8,128)(2,1)} custom-call(bf16[192,3584]{1,0:T(8,128)(2,1)S(1)} %bitcast.24, bf16[1,3584,512]{2,1,0:T(8,128)(2,1)} %gate0.1, bf16[1,3584,512]{2,1,0:T(8,128)(2,1)} %up0.1, bf16[1,3584,512]{2,1,0:T(8,128)(2,1)} %collective-permute-done.3.gate1, bf16[1,3584,512]{2,1,0:T(8,128)(2,1)} %collective-permute-done.4.up1, ...), custom_call_target="tpu_custom_call" | custom-call | flops 4227858432 | bytes 24772608 | tf_op jit(solution)/shard_map/expert_rows/pallas_call | solution.py:125
  81.0 16.4 %all-to-all-done.1 = bf16[8,64,1536]{2,1,0:T(8,128)(2,1)} async-done(((bf16[8,64,1536]{2,1,0:T(8,128)(2,1)}), bf16[8,64,1536]{2,1,0:T(8,128)(2,1)}, u32[]{:S(2)}, u32[]{:S(2)}) %all-to-all-start.1) | async-done | bytes 1572896 | tf_op jit(solution)/shard_map/all_to_all | solution.py:166
  97.4 3.6 %all-to-all-start.2 = ((bf16[8,24,3584]{2,1,0:T(8,128)(2,1)}), bf16[8,24,3584]{2,1,0:T(8,128)(2,1)S(1)}, u32[]{:S(2)}, u32[]{:S(2)}) async-start(bf16[8,24,3584]{2,1,0:T(8,128)(2,1)} %bitcast.12), calls=%async_computation.2 | async-start | bytes 2752512 | tf_op jit(solution)/shard_map/all_to_all | solution.py:335
  101.1 0.0 collective-permute-done.9
  101.1 0.1 constant_dynamic-update-slice_fusion.11.weight_ref
  101.1 0.1 collective-permute-start.10
  101.2 0.1 pad_add_fusion.rank_ref
  101.3 2.6 %collective-permute-done.10.other_weight_ref = bf16[2,4,512,128]{3,2,1,0:T(8,128)(2,1)S(1)} collective-permute-done((bf16[2,4,512,128]{3,2,1,0:T(8,128)(2,1)S(1)}, bf16[2,4,512,128]{3,2,1,0:T(8,128)(2,1)S(1)}, u32[]{:S(2)}, u32[]{:S(2)}) %collective-permute-start.10) | collective-permute-done | bytes 1048608 | tf_op jit(solution)/shard_map/ppermute | solution.py:330
  103.9 15.0 %causal_attention.1 = bf16[512,1024]{1,0:T(8,128)(2,1)} custom-call(s32[2]{0:T(128)S(1)} %pad_add_fusion.rank_ref, bf16[512,1536]{1,0:T(8,128)(2,1)} %bitcast.8.query_ref, bf16[16,64,576]{2,1,0:T(8,128)(2,1)} %constant_dynamic-update-slice_fusion.5.kv_ref, bf16[16,64,576]{2,1,0:T(8,128)(2,1)} %collective-permute-done.8.other_kv_ref, ...), custom_call_target="tpu_custom_call" | custom-call | flops 9126805504 | bytes 7602176 | tf_op jit(solution)/shard_map/causal_attention/pallas_call | solution.py:302
  118.8 0.0 copy-start.5
  118.8 14.6 %all-to-all-done.2 = bf16[8,24,3584]{2,1,0:T(8,128)(2,1)S(1)} async-done(((bf16[8,24,3584]{2,1,0:T(8,128)(2,1)}), bf16[8,24,3584]{2,1,0:T(8,128)(2,1)S(1)}, u32[]{:S(2)}, u32[]{:S(2)}) %all-to-all-start.2) | async-done | bytes 1376288 | tf_op jit(solution)/shard_map/all_to_all | solution.py:335
  133.5 3.6 %all-to-all-start.3 = ((bf16[8,64,1024]{2,1,0:T(8,128)(2,1)}), bf16[8,64,1024]{2,1,0:T(8,128)(2,1)S(1)}, u32[]{:S(2)}, u32[]{:S(2)}) async-start(bf16[8,64,1024]{2,1,0:T(8,128)(2,1)} %bitcast.13), calls=%async_computation.3 | async-start | bytes 2097152 | tf_op jit(solution)/shard_map/all_to_all | solution.py:166
  137.0 0.0 copy-done.5
  137.0 0.1 copy.15.gates_ref
  137.1 1.5 %combine_routes.1 = bf16[64,3584]{1,0:T(8,128)(2,1)} custom-call(s32[64,2]{1,0:T(8,128)S(1)} %copy.12.routes_ref, f32[64,2]{1,0:T(8,128)S(1)} %copy.15.gates_ref, bf16[192,3584]{1,0:T(8,128)(2,1)S(1)} %bitcast.23), custom_call_target="tpu_custom_call" | custom-call | bytes 1835008 | tf_op jit(solution)/shard_map/combine_routes/pallas_call | solution.py:86
  138.7 12.6 %all-to-all-done.3.x_ref = bf16[8,64,1024]{2,1,0:T(8,128)(2,1)S(1)} async-done(((bf16[8,64,1024]{2,1,0:T(8,128)(2,1)}), bf16[8,64,1024]{2,1,0:T(8,128)(2,1)S(1)}, u32[]{:S(2)}, u32[]{:S(2)}) %all-to-all-start.3) | async-done | bytes 1048608 | tf_op jit(solution)/shard_map/all_to_all | solution.py:166
  151.3 1.1 join_values.1
  (2 shorter events, 0.1 us)
Async XLA Ops:
  0.6 18.7 %copy-start.4 = (bf16[64,576]{1,0:T(8,128)(2,1)S(1)}, bf16[64,576]{1,0:T(8,128)(2,1)}, u32[]{:S(2)}) copy-start(bf16[64,576]{1,0:T(8,128)(2,1)} %param.11) | copy-start | bytes 221188
  0.6 59.5 %collective-permute-start.3 = (bf16[1,3584,512]{2,1,0:T(8,128)(2,1)}, bf16[1,3584,512]{2,1,0:T(8,128)(2,1)}, u32[]{:S(2)}, u32[]{:S(2)}) collective-permute-start(bf16[1,3584,512]{2,1,0:T(8,128)(2,1)} %gate0.1), channel_id=1, source_target_pairs={{0,1},{1,0},{2,3},{3,2},{4,5},{5,4},{6,7},{7,6},{8,9},{9,8},{10,11... | collective-permute-start | bytes 11010056 | tf_op jit(solution)/shard_map/ppermute | solution.py:330
  1.2 59.0 %collective-permute-start.4 = (bf16[1,3584,512]{2,1,0:T(8,128)(2,1)}, bf16[1,3584,512]{2,1,0:T(8,128)(2,1)}, u32[]{:S(2)}, u32[]{:S(2)}) collective-permute-start(bf16[1,3584,512]{2,1,0:T(8,128)(2,1)} %up0.1), channel_id=1, source_target_pairs={{0,1},{1,0},{2,3},{3,2},{4,5},{5,4},{6,7},{7,6},{8,9},{9,8},{10,11... | collective-permute-start | bytes 11010056 | tf_op jit(solution)/shard_map/ppermute | solution.py:330
  1.2 58.9 %collective-permute-start.5 = (bf16[1,512,3584]{2,1,0:T(8,128)(2,1)}, bf16[1,512,3584]{2,1,0:T(8,128)(2,1)}, u32[]{:S(2)}, u32[]{:S(2)}) collective-permute-start(bf16[1,512,3584]{2,1,0:T(8,128)(2,1)} %down0.1), channel_id=1, source_target_pairs={{0,1},{1,0},{2,3},{3,2},{4,5},{5,4},{6,7},{7,6},{8,9},{9,8},{10,11... | collective-permute-start | bytes 11010056 | tf_op jit(solution)/shard_map/ppermute | solution.py:330
  1.7 8.8 %collective-permute-start = (bf16[64,576]{1,0:T(8,128)(2,1)}, bf16[64,576]{1,0:T(8,128)(2,1)S(1)}, u32[]{:S(2)}, u32[]{:S(2)}) collective-permute-start(bf16[64,576]{1,0:T(8,128)(2,1)} %param.11), channel_id=1, source_target_pairs={{0,8},{1,9},{2,10},{3,11},{4,12},{5,13},{6,14},{7,15},{8,0},{9,1},... | collective-permute-start | bytes 221192 | tf_op jit(solution)/shard_map/ppermute | solution.py:330
  5.3 14.0 %collective-permute-start.1 = (bf16[64,576]{1,0:T(8,128)(2,1)}, bf16[64,576]{1,0:T(8,128)(2,1)S(1)}, u32[]{:S(2)}, u32[]{:S(2)}) collective-permute-start(bf16[64,576]{1,0:T(8,128)(2,1)} %param.11), channel_id=1, source_target_pairs={{0,4},{1,5},{2,6},{3,7},{4,0},{5,1},{6,2},{7,3},{8,12},{9,13},{10,... | collective-permute-start | bytes 221192 | tf_op jit(solution)/shard_map/ppermute | solution.py:330
  10.4 8.9 %collective-permute-start.2 = (bf16[64,576]{1,0:T(8,128)(2,1)}, bf16[64,576]{1,0:T(8,128)(2,1)S(1)}, u32[]{:S(2)}, u32[]{:S(2)}) collective-permute-start(bf16[64,576]{1,0:T(8,128)(2,1)} %param.11), channel_id=1, source_target_pairs={{0,12},{1,13},{2,14},{3,15},{4,8},{5,9},{6,10},{7,11},{8,4},{9,5},... | collective-permute-start | bytes 221192 | tf_op jit(solution)/shard_map/ppermute | solution.py:330
  16.3 1.0 copy-start.1
  19.4 9.6 %collective-permute-start.6 = (bf16[4,64,576]{2,1,0:T(8,128)(2,1)S(1)}, bf16[4,64,576]{2,1,0:T(8,128)(2,1)}, u32[]{:S(2)}, u32[]{:S(2)}) collective-permute-start(bf16[4,64,576]{2,1,0:T(8,128)(2,1)S(1)} %pad_maximum_fusion), channel_id=1, source_target_pairs={{0,16},{1,17},{2,18},{3,19},{4,20},{5,21},{6,22},{7,23},{8,24},{9,... | collective-permute-start | bytes 884744 | tf_op jit(solution)/shard_map/ppermute | solution.py:330
  20.9 39.2 %all-to-all-start = ((bf16[8,24,3584]{2,1,0:T(8,128)(2,1)}), bf16[8,24,3584]{2,1,0:T(8,128)(2,1)S(1)}, u32[]{:S(2)}, u32[]{:S(2)}) async-start(bf16[8,24,3584]{2,1,0:T(8,128)(2,1)} %bitcast.6), calls=%async_computation | async-start | bytes 2752512 | tf_op jit(solution)/shard_map/all_to_all | solution.py:335
  25.9 30.9 %copy-start = (bf16[64,12288]{1,0:T(8,128)(2,1)S(1)}, bf16[64,12288]{1,0:T(8,128)(2,1)}, u32[]{:S(2)}) copy-start(bf16[64,12288]{1,0:T(8,128)(2,1)} %x_ref.3) | copy-start | bytes 4718596
  30.8 25.0 %collective-permute-start.7 = (bf16[8,64,576]{2,1,0:T(8,128)(2,1)}, bf16[8,64,576]{2,1,0:T(8,128)(2,1)S(1)}, u32[]{:S(2)}, u32[]{:S(2)}) collective-permute-start(bf16[8,64,576]{2,1,0:T(8,128)(2,1)} %get-tuple-element.18), channel_id=1, source_target_pairs={{0,2},{1,3},{2,0},{3,1},{4,6},{5,7},{6,4},{7,5},{8,10},{9,11},{10,... | collective-permute-start | bytes 1769480 | tf_op jit(solution)/shard_map/ppermute | solution.py:330
  56.7 3.4 %collective-permute-start.8 = (bf16[16,64,576]{2,1,0:T(8,128)(2,1)}, bf16[16,64,576]{2,1,0:T(8,128)(2,1)}, u32[]{:S(2)}, u32[]{:S(2)}) collective-permute-start(bf16[16,64,576]{2,1,0:T(8,128)(2,1)} %constant_dynamic-update-slice_fusion.5.kv_ref), channel_id=1, source_target_pairs={{0,1},{1,0},{2,3},{3,2},{4,5},{5,4},{6,7},{7,6},{8,9},{9,8},{10,11... | collective-permute-start | bytes 3538952 | tf_op jit(solution)/shard_map/ppermute | solution.py:330
  60.1 4.5 %copy-start.2 = (bf16[4,128,512]{2,1,0:T(8,128)(2,1)S(1)}, bf16[4,128,512]{2,1,0:T(8,128)(2,1)}, u32[]{:S(2)}) copy-start(bf16[4,128,512]{2,1,0:T(8,128)(2,1)} %param.12) | copy-start | bytes 1572868
  60.2 37.3 %all-to-all-start.1 = ((bf16[8,64,1536]{2,1,0:T(8,128)(2,1)}), bf16[8,64,1536]{2,1,0:T(8,128)(2,1)}, u32[]{:S(2)}, u32[]{:S(2)}) async-start(bf16[8,64,1536]{2,1,0:T(8,128)(2,1)} %split_queries.1), calls=%async_computation.1 | async-start | bytes 3145728 | tf_op jit(solution)/shard_map/all_to_all | solution.py:166
  64.6 1.0 copy-start.3
  65.7 35.4 %collective-permute-start.9 = (bf16[1,4,512,128]{3,2,1,0:T(8,128)(2,1)S(1)}, bf16[1,4,512,128]{3,2,1,0:T(8,128)(2,1)S(1)}, u32[]{:S(2)}, u32[]{:S(2)}) collective-permute-start(bf16[1,4,512,128]{3,2,1,0:T(8,128)(2,1)S(1)} %fusion), channel_id=1, source_target_pairs={{0,8},{1,9},{2,10},{3,11},{4,12},{5,13},{6,14},{7,15},{8,0},{9,1},... | collective-permute-start | bytes 1572872 | tf_op jit(solution)/shard_map/ppermute | solution.py:330
  97.4 36.0 %all-to-all-start.2 = ((bf16[8,24,3584]{2,1,0:T(8,128)(2,1)}), bf16[8,24,3584]{2,1,0:T(8,128)(2,1)S(1)}, u32[]{:S(2)}, u32[]{:S(2)}) async-start(bf16[8,24,3584]{2,1,0:T(8,128)(2,1)} %bitcast.12), calls=%async_computation.2 | async-start | bytes 2752512 | tf_op jit(solution)/shard_map/all_to_all | solution.py:335
  101.1 2.7 %collective-permute-start.10 = (bf16[2,4,512,128]{3,2,1,0:T(8,128)(2,1)S(1)}, bf16[2,4,512,128]{3,2,1,0:T(8,128)(2,1)S(1)}, u32[]{:S(2)}, u32[]{:S(2)}) collective-permute-start(bf16[2,4,512,128]{3,2,1,0:T(8,128)(2,1)S(1)} %constant_dynamic-update-slice_fusion.11.weight_ref), channel_id=1, source_target_pairs={{0,1},{1,0},{2,3},{3,2},{4,5},{5,4},{6,7},{7,6},{8,9},{9,8},{10,11... | collective-permute-start | bytes 3145736 | tf_op jit(solution)/shard_map/ppermute | solution.py:330
  118.8 18.2 %copy-start.5 = (f32[64,2]{0,1:T(2,128)S(1)}, f32[64,2]{0,1:T(2,128)}, u32[]{:S(2)}) copy-start(f32[64,2]{0,1:T(2,128)} %param.16) | copy-start | bytes 1540
  133.5 17.9 %all-to-all-start.3 = ((bf16[8,64,1024]{2,1,0:T(8,128)(2,1)}), bf16[8,64,1024]{2,1,0:T(8,128)(2,1)S(1)}, u32[]{:S(2)}, u32[]{:S(2)}) async-start(bf16[8,64,1024]{2,1,0:T(8,128)(2,1)} %bitcast.13), calls=%async_computation.3 | async-start | bytes 2097152 | tf_op jit(solution)/shard_map/all_to_all | solution.py:166

commit v9 on v8

--- a/solution.py
+++ b/solution.py
@@ -71,8 +71,9 @@
     )(routes, moe_input)
 
 
-def combine_kernel(rows, routes_ref, gates_ref, back_ref, out_ref):
-    back = back_ref[...]
+def combine_kernel(rows, routes_ref, gates_ref, *refs):
+    out_ref = refs[-1]
+    back = jnp.concatenate([ref[...] for ref in refs[:-1]], axis=0)
     tok = routes_ref.shape[0]
     target0, target1 = slot_targets(routes_ref[...], rows)
     targets = jnp.concatenate([target0, target1], axis=0)
@@ -86,16 +87,19 @@
     return call(
         functools.partial(combine_kernel, rows),
         "combine_routes",
-        moved=2 * D * (routes.shape[0] + back.shape[0]),
+        moved=2 * D * (routes.shape[0] + len(back) * rows),
         out_shape=jax.ShapeDtypeStruct((routes.shape[0], D), BF16),
-    )(routes, gates, back)
+    )(routes, gates, *back)
 
 
 STEP = 896
 STEPS = D // STEP
 
 
-def expert_kernel(x_ref, gate0, up0, gate1, up1, down0, down1, out_ref, sums, hidden):
+def expert_kernel(rank_ref, x_ref, gate0, up0, gate1, up1, down0, down1, *refs):
+    out_refs = refs[:-3]
+    sums, hidden, result = refs[-3:]
+    rows = result.shape[1]
     step = pl.program_id(0)
 
     @pl.when(step < STEPS)
@@ -115,24 +119,37 @@
     def _():
         first = jnp.dot(hidden[0], down0[0], preferred_element_type=F32).astype(BF16)
         second = jnp.dot(hidden[1], down1[0], preferred_element_type=F32).astype(BF16)
-        out_ref[...] = (first.astype(F32) + second.astype(F32)).astype(BF16)
-
-
-def expert_rows(x, own, other):
+        both = (first.astype(F32) + second.astype(F32)).astype(BF16)
+        for chip in range(len(out_refs)):
+            result[chip] = both[chip * rows : (chip + 1) * rows]
+        for offset, out_ref in enumerate(out_refs):
+            out_ref[...] = result[(rank_ref[0] // 2) ^ offset]
+
+
+def expert_rows(rank, x, own, other, experts):
     count = x.shape[0]
-    weights = pl.BlockSpec((1, STEP, HALF), lambda k: (0, jnp.minimum(k, STEPS - 1), 0))
-    down = pl.BlockSpec((1, HALF, STEP), lambda k: (0, 0, jnp.maximum(k - STEPS, 0)))
+    rows = count // experts
+    weights = pl.BlockSpec((1, STEP, HALF), lambda k, rank: (0, jnp.minimum(k, STEPS - 1), 0))
+    down = pl.BlockSpec((1, HALF, STEP), lambda k, rank: (0, 0, jnp.maximum(k - STEPS, 0)))
+    columns = pl.BlockSpec((count, STEP), lambda k, rank: (0, jnp.minimum(k, STEPS - 1)))
     return call(
         expert_kernel,
         "expert_rows",
         flops=12 * count * D * HALF,
         moved=12 * D * HALF + 4 * count * D,
-        grid=(2 * STEPS,),
-        in_specs=[pl.BlockSpec((count, STEP), lambda k: (0, jnp.minimum(k, STEPS - 1)))] + [weights] * 4 + [down] * 2,
-        out_specs=pl.BlockSpec((count, STEP), lambda k: (0, jnp.maximum(k - STEPS, 0))),
-        scratch_shapes=[pltpu.VMEM((4, count, HALF), F32), pltpu.VMEM((2, count, HALF), BF16)],
-        out_shape=jax.ShapeDtypeStruct((count, D), BF16),
-    )(x, own[0], own[1], other[0], other[1], own[2], other[2])
+        grid_spec=pltpu.PrefetchScalarGridSpec(
+            num_scalar_prefetch=1,
+            grid=(2 * STEPS,),
+            in_specs=[columns] + [weights] * 4 + [down] * 2,
+            out_specs=[pl.BlockSpec((rows, STEP), lambda k, rank: (0, jnp.maximum(k - STEPS, 0)))] * experts,
+            scratch_shapes=[
+                pltpu.VMEM((4, count, HALF), F32),
+                pltpu.VMEM((2, count, HALF), BF16),
+                pltpu.VMEM((experts, rows, STEP), BF16),
+            ],
+        ),
+        out_shape=[jax.ShapeDtypeStruct((rows, D), BF16)] * experts,
+    )(rank, x, own[0], own[1], other[0], other[1], own[2], other[2])
 
 
 class Split:
@@ -383,16 +400,17 @@
     place = jnp.concatenate([rank, group])
 
     direct, later = gather_masks(split)
-    keys = jnp.stack([latent_kv] + [send(latent_kv, offset) for offset in direct])
-
-    buckets = after(build_buckets(routes, moe_input, experts, rows), keys)
+    keys = [latent_kv] + [send(latent_kv, offset) for offset in direct]
+
+    buckets = after(build_buckets(routes, moe_input, experts, rows), *keys)
     arrived = swap_chips(buckets.reshape(experts, rows, D)).reshape(experts * rows, D)
 
+    keys = jnp.stack(keys)
     for mask in later:
         keys = jnp.concatenate([keys, send(keys, mask)], axis=0)
     other_keys = send(keys, 1)
     own_half = [expert_gate, expert_up, expert_down]
-    other_half = [send(part, 1) for part in own_half]
+    other_half = [send(after(part, buckets), 1) for part in own_half]
     sent = after(split_queries(split, rank, queries), other_keys, arrived, *other_half)
     held = split.exchange(sent).reshape(experts * tok, -1)
 
@@ -408,14 +426,14 @@
         weights = after(weights, arrived)
         weights = jnp.concatenate([weights, send(weights, shards // 2)], axis=0)
 
-    result = expert_rows(arrived, own_half, other_half)
-    other_weights = send(after(weights, result), 1)
-    result, held = lax.optimization_barrier((result, held))
-    back = swap_chips(result.reshape(experts, rows, D))
+    result = expert_rows(rank, arrived, own_half, other_half, experts)
+    back = [result[0]] + [send(result[m], 2 * m) for m in range(1, experts)]
+    other_weights = send(after(weights, result[0]), 1)
+    held = after(held, result[0])
     values = attention(split, place, held, keys, other_keys, weights, other_weights)
-    values, back = lax.optimization_barrier((values, back))
+    values, *back = lax.optimization_barrier((values, *back))
     values = split.exchange(values.reshape(experts, tok, values.shape[1]))
-    moe_out = combine(routes, gates, back.reshape(experts * rows, D), rows)
+    moe_out = combine(routes ^ (rank // 2), gates, back, rows)
     return (join_values(split, rank, values), moe_out)
 
 

time: 153 us -> 166 us (1.085)
  starting transfers between devices: 30.1 us -> 44.6 us
  waiting for transfers between devices: 77.6 us -> 75.7 us
    ppermute x11 -> x18, waiting for transfers between devices: 33.9 us -> 62.7 us  [send(): lax.ppermute(array, ('groups', 'ctx'), [(i, i ^ mask) for i in range(coun...]
    all_to_all x2, waiting for transfers between devices: 29.1 us -> 13 us  [exchange(): lax.all_to_all(array, ('groups', 'ctx'), split_axis=0, concat_axis=0, axi...]
    all_to_all x2 -> x1, waiting for transfers between devices: 14.6 us -> 0.01 us  [swap_chips(): lax.all_to_all(array, 'ctx', split_axis=0, concat_axis=0, axis_index_grou...]
    ppermute x11 -> x18, starting transfers between devices: 15 us -> 27.3 us  [send(): lax.ppermute(array, ('groups', 'ctx'), [(i, i ^ mask) for i in range(coun...]
    all_to_all x2, starting transfers between devices: 7.99 us -> 12.6 us  [exchange(): lax.all_to_all(array, ('groups', 'ctx'), split_axis=0, concat_axis=0, axi...]
    all_to_all x2 -> x1, starting transfers between devices: 7.14 us -> 4.69 us  [swap_chips(): lax.all_to_all(array, 'ctx', split_axis=0, concat_axis=0, axis_index_grou...]
    unnamed x19 -> x27, local copies, waits for them, and re-layouts: 6.28 us -> 6.51 us
  transfers between devices with their start and end apart: 15 -> 21, of which waited for: 8 -> 7; matrix products, arithmetic and copies ran while one was open for 5% -> 4% of each run, Pallas kernels for 22% -> 20%
where the time goes in v9:
time: 166 us; the launch traced here: 165 us
  waiting for transfers between devices  75.7 us (46%)
  starting transfers between devices  44.6 us (27%)
  Pallas kernels  34.2 us (21%)
  local copies, waits for them, and re-layouts  9.62 us (6%)
    ppermute x18, waiting for transfers between devices, send(): lax.ppermute(array, ('groups', 'ctx'), [(i, i ^ mask) for i in range(coun...  62.7 us
    ppermute x18, starting transfers between devices, send(): lax.ppermute(array, ('groups', 'ctx'), [(i, i ^ mask) for i in range(coun...  27.3 us
    pallas_call x1, Pallas kernels, attention(): call(functools.partial(attention_kernel, split), 'causal_attention', flop...  14.9 us
    pallas_call x1, Pallas kernels, expert_rows(): call(expert_kernel, 'expert_rows', flops=12 * count * D * HALF, moved=12...  13.2 us
    all_to_all x2, waiting for transfers between devices, exchange(): lax.all_to_all(array, ('groups', 'ctx'), split_axis=0, concat_axis=0, axi...  13 us
    all_to_all x2, starting transfers between devices, exchange(): lax.all_to_all(array, ('groups', 'ctx'), split_axis=0, concat_axis=0, axi...  12.6 us
    unnamed x27, local copies, waits for them, and re-layouts  6.51 us
    all_to_all x1, starting transfers between devices, swap_chips(): lax.all_to_all(array, 'ctx', split_axis=0, concat_axis=0, axis_index_grou...  4.69 us
  transfers between devices with their start and end apart: 21, of which 7 were waited for; matrix products, arithmetic and copies ran while one was open for 4% of the time, Pallas kernels for 20%

profile of v9, /device:TPU:0, one launch (start us, length us, event | category | flops | bytes accessed | tf_op | source)
XLA Modules:
  0.0 165.1 jit_solution(13207932895612530412)
XLA Ops:
  0.6 4.1 %collective-permute-start = (bf16[64,576]{1,0:T(8,128)(2,1)}, bf16[64,576]{1,0:T(8,128)(2,1)S(1)}, u32[]{:S(2)}, u32[]{:S(2)}) collective-permute-start(bf16[64,576]{1,0:T(8,128)(2,1)} %param.11), channel_id=1, source_target_pairs={{0,8},{1,9},{2,10},{3,11},{4,12},{5,13},{6,14},{7,15},{8,0},{9,1},... | collective-permute-start | bytes 221192 | tf_op jit(solution)/shard_map/ppermute | solution.py:347
  4.7 1.6 collective-permute-start.1
  6.3 0.0 collective-permute-start.2
  6.3 0.8 copy.16.routes_ref
  7.1 1.0 copy-done.1
  8.1 2.0 %bucket_rows.1 = bf16[192,3584]{1,0:T(8,128)(2,1)} custom-call(s32[64,2]{1,0:T(8,128)S(1)} %copy.16.routes_ref, bf16[64,3584]{1,0:T(8,128)(2,1)S(1)} %copy-done.1), custom_call_target="tpu_custom_call" | custom-call | bytes 1835008 | tf_op jit(solution)/shard_map/bucket_rows/pallas_call | solution.py:66
  10.1 0.0 collective-permute-done
  10.1 0.0 collective-permute-done.1
  10.1 2.6 %collective-permute-done.2 = bf16[64,576]{1,0:T(8,128)(2,1)S(1)} collective-permute-done((bf16[64,576]{1,0:T(8,128)(2,1)}, bf16[64,576]{1,0:T(8,128)(2,1)S(1)}, u32[]{:S(2)}, u32[]{:S(2)}) %collective-permute-start.2) | collective-permute-done | bytes 73760 | tf_op jit(solution)/shard_map/ppermute | solution.py:347
  12.8 0.0 collective-permute-start.6
  12.8 0.5 collective-permute-start.7
  13.3 0.0 collective-permute-start.8
  13.3 0.7 constant_dynamic-update-slice_fusion.4
  13.9 0.1 pad_maximum_fusion
  14.0 1.6 collective-permute-start.3
  15.6 4.7 %all-to-all-start = ((bf16[8,24,3584]{2,1,0:T(8,128)(2,1)}), bf16[8,24,3584]{2,1,0:T(8,128)(2,1)S(1)}, u32[]{:S(2)}, u32[]{:S(2)}) async-start(bf16[8,24,3584]{2,1,0:T(8,128)(2,1)} %bitcast.6), calls=%async_computation | async-start | bytes 2752512 | tf_op jit(solution)/shard_map/all_to_all | solution.py:352
  20.3 0.7 constant_dynamic-update-slice_fusion.3
  21.0 0.7 constant_dynamic-update-slice_fusion.2
  21.7 0.7 constant_dynamic-update-slice_fusion.1
  22.3 2.0 %collective-permute-done.3 = bf16[4,64,576]{2,1,0:T(8,128)(2,1)} collective-permute-done((bf16[4,64,576]{2,1,0:T(8,128)(2,1)S(1)}, bf16[4,64,576]{2,1,0:T(8,128)(2,1)}, u32[]{:S(2)}, u32[]{:S(2)}) %collective-permute-start.3) | collective-permute-done | bytes 294944 | tf_op jit(solution)/shard_map/ppermute | solution.py:347
  24.3 1.9 %constant_dynamic-update-slice_fusion = (bf16[8,64,576]{2,1,0:T(8,128)(2,1)}, bf16[16,64,576]{2,1,0:T(8,128)(2,1)}) fusion(bf16[8,64,576]{2,1,0:T(8,128)(2,1)} %get-tuple-element.54, bf16[4,64,576]{2,1,0:T(8,128)(2,1)} %collective-permute-done.3, bf16[16,64,576]{2,1,0:T(8,128)(2,1)} %get-tuple-element.55), kind=kLoop, calls=%fused_computation.4 | loop fusion | bytes 983040 | tf_op jit(solution)/shard_map/concatenate | solution.py:410
  26.2 1.6 collective-permute-start.4
  27.8 24.5 %collective-permute-done.4 = bf16[8,64,576]{2,1,0:T(8,128)(2,1)S(1)} collective-permute-done((bf16[8,64,576]{2,1,0:T(8,128)(2,1)}, bf16[8,64,576]{2,1,0:T(8,128)(2,1)S(1)}, u32[]{:S(2)}, u32[]{:S(2)}) %collective-permute-start.4) | collective-permute-done | bytes 589856 | tf_op jit(solution)/shard_map/ppermute | solution.py:347
  52.3 0.9 constant_dynamic-update-slice_fusion.5.kv_ref
  53.2 0.0 collective-permute-start.5
  53.2 1.5 split_queries.1
  54.7 1.9 %collective-permute-done.5.other_kv_ref = bf16[16,64,576]{2,1,0:T(8,128)(2,1)} collective-permute-done((bf16[16,64,576]{2,1,0:T(8,128)(2,1)}, bf16[16,64,576]{2,1,0:T(8,128)(2,1)}, u32[]{:S(2)}, u32[]{:S(2)}) %collective-permute-start.5) | collective-permute-done | bytes 1179680 | tf_op jit(solution)/shard_map/ppermute | solution.py:347
  56.5 0.0 all-to-all-done
  56.5 0.0 collective-permute-done.6.gate1
  56.6 0.0 collective-permute-done.7.up1
  56.6 0.0 collective-permute-done.8.down1
  56.6 0.0 copy-start.6
  56.6 4.4 %all-to-all-start.1 = ((bf16[8,64,1536]{2,1,0:T(8,128)(2,1)}), bf16[8,64,1536]{2,1,0:T(8,128)(2,1)}, u32[]{:S(2)}, u32[]{:S(2)}) async-start(bf16[8,64,1536]{2,1,0:T(8,128)(2,1)} %split_queries.1), calls=%async_computation.1 | async-start | bytes 3145728 | tf_op jit(solution)/shard_map/all_to_all | solution.py:183
  61.0 0.0 copy-start.7
  61.0 0.3 copy.17
  61.3 0.7 copy-done.7
  62.1 2.0 %collective-permute-start.9 = (bf16[1,4,512,128]{3,2,1,0:T(8,128)(2,1)S(1)}, bf16[1,4,512,128]{3,2,1,0:T(8,128)(2,1)S(1)}, u32[]{:S(2)}, u32[]{:S(2)}) collective-permute-start(bf16[1,4,512,128]{3,2,1,0:T(8,128)(2,1)S(1)} %fusion), channel_id=1, source_target_pairs={{0,8},{1,9},{2,10},{3,11},{4,12},{5,13},{6,14},{7,15},{8,0},{9,1},... | collective-permute-start | bytes 1572872 | tf_op jit(solution)/shard_map/ppermute | solution.py:347
  64.2 28.4 %collective-permute-done.9 = bf16[1,4,512,128]{3,2,1,0:T(8,128)(2,1)S(1)} collective-permute-done((bf16[1,4,512,128]{3,2,1,0:T(8,128)(2,1)S(1)}, bf16[1,4,512,128]{3,2,1,0:T(8,128)(2,1)S(1)}, u32[]{:S(2)}, u32[]{:S(2)}) %collective-permute-start.9) | collective-permute-done | bytes 524320 | tf_op jit(solution)/shard_map/ppermute | solution.py:347
  92.6 0.1 constant_dynamic-update-slice_fusion.11.weight_ref
  92.6 13.2 %expert_rows.1 = (bf16[24,3584]{1,0:T(8,128)(2,1)S(1)}, bf16[24,3584]{1,0:T(8,128)(2,1)S(1)}, bf16[24,3584]{1,0:T(8,128)(2,1)S(1)}, bf16[24,3584]{1,0:T(8,128)(2...) custom-call(s32[1]{0:T(128)} %bitcast.rank_ref, ...), custom_call_target="tpu_custom_call" | custom-call | flops 4227858432 | bytes 24772608 | tf_op jit(solution)/shard_map/expert_rows/pallas_call | solution.py:135
  105.8 0.1 collective-permute-start.10
  105.9 0.1 collective-permute-start.11
  106.0 0.5 copy-done.4
  106.5 4.4 %collective-permute-start.12 = (bf16[24,3584]{1,0:T(8,128)(2,1)S(1)}, bf16[24,3584]{1,0:T(8,128)(2,1)S(1)}, u32[]{:S(2)}, u32[]{:S(2)}) collective-permute-start(bf16[24,3584]{1,0:T(8,128)(2,1)S(1)} %get-tuple-element.37), channel_id=1, source_target_pairs={{0,4},{1,5},{2,6},{3,7},{4,0},{5,1},{6,2},{7,3},{8,12},{9,13},{10,... | collective-permute-start | bytes 516104 | tf_op jit(solution)/shard_map/ppermute | solution.py:347
  110.9 0.1 pad_add_fusion.rank_ref
  111.0 1.0 collective-permute-start.13
  111.9 1.0 collective-permute-start.14
  112.9 0.0 all-to-all-done.1
  112.9 0.0 collective-permute-done.11.refs_1_
  112.9 2.9 %collective-permute-start.15 = (bf16[24,3584]{1,0:T(8,128)(2,1)}, bf16[24,3584]{1,0:T(8,128)(2,1)S(1)}, u32[]{:S(2)}, u32[]{:S(2)}) collective-permute-start(bf16[24,3584]{1,0:T(8,128)(2,1)} %get-tuple-element.40), channel_id=1, source_target_pairs={{0,10},{1,11},{2,8},{3,9},{4,14},{5,15},{6,12},{7,13},{8,2},{9,3},... | collective-permute-start | bytes 516104 | tf_op jit(solution)/shard_map/ppermute | solution.py:347
  115.8 3.4 %collective-permute-done.12.refs_2_ = bf16[24,3584]{1,0:T(8,128)(2,1)S(1)} collective-permute-done((bf16[24,3584]{1,0:T(8,128)(2,1)S(1)}, bf16[24,3584]{1,0:T(8,128)(2,1)S(1)}, u32[]{:S(2)}, u32[]{:S(2)}) %collective-permute-start.12) | collective-permute-done | bytes 172064 | tf_op jit(solution)/shard_map/ppermute | solution.py:347
  119.1 2.6 %collective-permute-start.16 = (bf16[24,3584]{1,0:T(8,128)(2,1)}, bf16[24,3584]{1,0:T(8,128)(2,1)S(1)}, u32[]{:S(2)}, u32[]{:S(2)}) collective-permute-start(bf16[24,3584]{1,0:T(8,128)(2,1)} %copy-done.5), channel_id=1, source_target_pairs={{0,12},{1,13},{2,14},{3,15},{4,8},{5,9},{6,10},{7,11},{8,4},{9,5},... | collective-permute-start | bytes 516104 | tf_op jit(solution)/shard_map/ppermute | solution.py:347
  121.7 0.0 collective-permute-done.10.other_weight_ref
  121.8 3.9 %collective-permute-start.17 = (bf16[24,3584]{1,0:T(8,128)(2,1)}, bf16[24,3584]{1,0:T(8,128)(2,1)S(1)}, u32[]{:S(2)}, u32[]{:S(2)}) collective-permute-start(bf16[24,3584]{1,0:T(8,128)(2,1)} %copy-done.4), channel_id=1, source_target_pairs={{0,14},{1,15},{2,12},{3,13},{4,10},{5,11},{6,8},{7,9},{8,6},{9,7},... | collective-permute-start | bytes 516104 | tf_op jit(solution)/shard_map/ppermute | solution.py:347
  125.7 14.9 %causal_attention.1 = bf16[512,1024]{1,0:T(8,128)(2,1)} custom-call(s32[2]{0:T(128)S(1)} %pad_add_fusion.rank_ref, bf16[512,1536]{1,0:T(8,128)(2,1)} %bitcast.8.query_ref, bf16[16,64,576]{2,1,0:T(8,128)(2,1)} %constant_dynamic-update-slice_fusion.5.kv_ref, bf16[16,64,576]{2,1,0:T(8,128)(2,1)} %collective-permute-done.5.other_kv_ref, ...), custom_call_target="tpu_custom_call" | custom-call | flops 9126805504 | bytes 7602176 | tf_op jit(solution)/shard_map/causal_attention/pallas_call | solution.py:319
  140.6 0.0 collective-permute-done.13.refs_3_
  140.6 0.0 collective-permute-done.15.refs_5_
  140.6 0.0 copy-start.2
  140.6 0.7 copy-done.2
  141.3 8.1 %all-to-all-start.2 = ((bf16[8,64,1024]{2,1,0:T(8,128)(2,1)}), bf16[8,64,1024]{2,1,0:T(8,128)(2,1)S(1)}, u32[]{:S(2)}, u32[]{:S(2)}) async-start(bf16[8,64,1024]{2,1,0:T(8,128)(2,1)} %bitcast.12), calls=%async_computation.2 | async-start | bytes 2097152 | tf_op jit(solution)/shard_map/all_to_all | solution.py:183
  149.4 0.1 copy.20.gates_ref
  149.5 1.5 combine_routes.1
  151.1 13.0 %all-to-all-done.2.x_ref = bf16[8,64,1024]{2,1,0:T(8,128)(2,1)S(1)} async-done(((bf16[8,64,1024]{2,1,0:T(8,128)(2,1)}), bf16[8,64,1024]{2,1,0:T(8,128)(2,1)S(1)}, u32[]{:S(2)}, u32[]{:S(2)}) %all-to-all-start.2) | async-done | bytes 1048608 | tf_op jit(solution)/shard_map/all_to_all | solution.py:183
  164.1 1.1 join_values.1
  (19 shorter events, 0.1 us)
Async XLA Ops:
  0.6 9.5 %collective-permute-start = (bf16[64,576]{1,0:T(8,128)(2,1)}, bf16[64,576]{1,0:T(8,128)(2,1)S(1)}, u32[]{:S(2)}, u32[]{:S(2)}) collective-permute-start(bf16[64,576]{1,0:T(8,128)(2,1)} %param.11), channel_id=1, source_target_pairs={{0,8},{1,9},{2,10},{3,11},{4,12},{5,13},{6,14},{7,15},{8,0},{9,1},... | collective-permute-start | bytes 221192 | tf_op jit(solution)/shard_map/ppermute | solution.py:347
  4.7 5.4 %collective-permute-start.1 = (bf16[64,576]{1,0:T(8,128)(2,1)}, bf16[64,576]{1,0:T(8,128)(2,1)S(1)}, u32[]{:S(2)}, u32[]{:S(2)}) collective-permute-start(bf16[64,576]{1,0:T(8,128)(2,1)} %param.11), channel_id=1, source_target_pairs={{0,4},{1,5},{2,6},{3,7},{4,0},{5,1},{6,2},{7,3},{8,12},{9,13},{10,... | collective-permute-start | bytes 221192 | tf_op jit(solution)/shard_map/ppermute | solution.py:347
  6.3 6.4 %collective-permute-start.2 = (bf16[64,576]{1,0:T(8,128)(2,1)}, bf16[64,576]{1,0:T(8,128)(2,1)S(1)}, u32[]{:S(2)}, u32[]{:S(2)}) collective-permute-start(bf16[64,576]{1,0:T(8,128)(2,1)} %param.11), channel_id=1, source_target_pairs={{0,12},{1,13},{2,14},{3,15},{4,8},{5,9},{6,10},{7,11},{8,4},{9,5},... | collective-permute-start | bytes 221192 | tf_op jit(solution)/shard_map/ppermute | solution.py:347
  7.1 1.0 copy-start.1
  8.1 5.2 %copy-start.8 = (bf16[64,576]{1,0:T(8,128)(2,1)S(1)}, bf16[64,576]{1,0:T(8,128)(2,1)}, u32[]{:S(2)}) copy-start(bf16[64,576]{1,0:T(8,128)(2,1)} %param.11) | copy-start | bytes 221188
  12.8 43.8 %collective-permute-start.6 = (bf16[1,3584,512]{2,1,0:T(8,128)(2,1)}, bf16[1,3584,512]{2,1,0:T(8,128)(2,1)}, u32[]{:S(2)}, u32[]{:S(2)}) collective-permute-start(bf16[1,3584,512]{2,1,0:T(8,128)(2,1)} %gate0.1), channel_id=1, source_target_pairs={{0,1},{1,0},{2,3},{3,2},{4,5},{5,4},{6,7},{7,6},{8,9},{9,8},{10,11... | collective-permute-start | bytes 11010056 | tf_op jit(solution)/shard_map/ppermute | solution.py:347
  12.8 43.8 %collective-permute-start.7 = (bf16[1,3584,512]{2,1,0:T(8,128)(2,1)}, bf16[1,3584,512]{2,1,0:T(8,128)(2,1)}, u32[]{:S(2)}, u32[]{:S(2)}) collective-permute-start(bf16[1,3584,512]{2,1,0:T(8,128)(2,1)} %up0.1), channel_id=1, source_target_pairs={{0,1},{1,0},{2,3},{3,2},{4,5},{5,4},{6,7},{7,6},{8,9},{9,8},{10,11... | collective-permute-start | bytes 11010056 | tf_op jit(solution)/shard_map/ppermute | solution.py:347
  13.3 43.3 %collective-permute-start.8 = (bf16[1,512,3584]{2,1,0:T(8,128)(2,1)}, bf16[1,512,3584]{2,1,0:T(8,128)(2,1)}, u32[]{:S(2)}, u32[]{:S(2)}) collective-permute-start(bf16[1,512,3584]{2,1,0:T(8,128)(2,1)} %down0.1), channel_id=1, source_target_pairs={{0,1},{1,0},{2,3},{3,2},{4,5},{5,4},{6,7},{7,6},{8,9},{9,8},{10,11... | collective-permute-start | bytes 11010056 | tf_op jit(solution)/shard_map/ppermute | solution.py:347
  14.0 10.3 %collective-permute-start.3 = (bf16[4,64,576]{2,1,0:T(8,128)(2,1)S(1)}, bf16[4,64,576]{2,1,0:T(8,128)(2,1)}, u32[]{:S(2)}, u32[]{:S(2)}) collective-permute-start(bf16[4,64,576]{2,1,0:T(8,128)(2,1)S(1)} %pad_maximum_fusion), channel_id=1, source_target_pairs={{0,16},{1,17},{2,18},{3,19},{4,20},{5,21},{6,22},{7,23},{8,24},{9,... | collective-permute-start | bytes 884744 | tf_op jit(solution)/shard_map/ppermute | solution.py:347
  15.6 40.9 %all-to-all-start = ((bf16[8,24,3584]{2,1,0:T(8,128)(2,1)}), bf16[8,24,3584]{2,1,0:T(8,128)(2,1)S(1)}, u32[]{:S(2)}, u32[]{:S(2)}) async-start(bf16[8,24,3584]{2,1,0:T(8,128)(2,1)} %bitcast.6), calls=%async_computation | async-start | bytes 2752512 | tf_op jit(solution)/shard_map/all_to_all | solution.py:352
  21.7 31.5 %copy-start = (bf16[64,12288]{1,0:T(8,128)(2,1)S(1)}, bf16[64,12288]{1,0:T(8,128)(2,1)}, u32[]{:S(2)}) copy-start(bf16[64,12288]{1,0:T(8,128)(2,1)} %x_ref.2) | copy-start | bytes 4718596
  26.2 26.1 %collective-permute-start.4 = (bf16[8,64,576]{2,1,0:T(8,128)(2,1)}, bf16[8,64,576]{2,1,0:T(8,128)(2,1)S(1)}, u32[]{:S(2)}, u32[]{:S(2)}) collective-permute-start(bf16[8,64,576]{2,1,0:T(8,128)(2,1)} %get-tuple-element.52), channel_id=1, source_target_pairs={{0,2},{1,3},{2,0},{3,1},{4,6},{5,7},{6,4},{7,5},{8,10},{9,11},{10,... | collective-permute-start | bytes 1769480 | tf_op jit(solution)/shard_map/ppermute | solution.py:347
  53.2 3.4 %collective-permute-start.5 = (bf16[16,64,576]{2,1,0:T(8,128)(2,1)}, bf16[16,64,576]{2,1,0:T(8,128)(2,1)}, u32[]{:S(2)}, u32[]{:S(2)}) collective-permute-start(bf16[16,64,576]{2,1,0:T(8,128)(2,1)} %constant_dynamic-update-slice_fusion.5.kv_ref), channel_id=1, source_target_pairs={{0,1},{1,0},{2,3},{3,2},{4,5},{5,4},{6,7},{7,6},{8,9},{9,8},{10,11... | collective-permute-start | bytes 3538952 | tf_op jit(solution)/shard_map/ppermute | solution.py:347
  56.6 4.5 %copy-start.6 = (bf16[4,128,512]{2,1,0:T(8,128)(2,1)S(1)}, bf16[4,128,512]{2,1,0:T(8,128)(2,1)}, u32[]{:S(2)}) copy-start(bf16[4,128,512]{2,1,0:T(8,128)(2,1)} %param.12) | copy-start | bytes 1572868
  56.6 56.3 %all-to-all-start.1 = ((bf16[8,64,1536]{2,1,0:T(8,128)(2,1)}), bf16[8,64,1536]{2,1,0:T(8,128)(2,1)}, u32[]{:S(2)}, u32[]{:S(2)}) async-start(bf16[8,64,1536]{2,1,0:T(8,128)(2,1)} %split_queries.1), calls=%async_computation.1 | async-start | bytes 3145728 | tf_op jit(solution)/shard_map/all_to_all | solution.py:183
  61.0 1.0 copy-start.7
  62.1 30.4 %collective-permute-start.9 = (bf16[1,4,512,128]{3,2,1,0:T(8,128)(2,1)S(1)}, bf16[1,4,512,128]{3,2,1,0:T(8,128)(2,1)S(1)}, u32[]{:S(2)}, u32[]{:S(2)}) collective-permute-start(bf16[1,4,512,128]{3,2,1,0:T(8,128)(2,1)S(1)} %fusion), channel_id=1, source_target_pairs={{0,8},{1,9},{2,10},{3,11},{4,12},{5,13},{6,14},{7,15},{8,0},{9,1},... | collective-permute-start | bytes 1572872 | tf_op jit(solution)/shard_map/ppermute | solution.py:347
  105.8 0.7 copy-start.4
  105.8 5.2 %copy-start.5 = (bf16[24,3584]{1,0:T(8,128)(2,1)}, bf16[24,3584]{1,0:T(8,128)(2,1)S(1)}, u32[]{:S(2)}) copy-start(bf16[24,3584]{1,0:T(8,128)(2,1)S(1)} %get-tuple-element.41) | copy-start | bytes 516100
  105.8 15.9 %collective-permute-start.10 = (bf16[2,4,512,128]{3,2,1,0:T(8,128)(2,1)S(1)}, bf16[2,4,512,128]{3,2,1,0:T(8,128)(2,1)S(1)}, u32[]{:S(2)}, u32[]{:S(2)}) collective-permute-start(bf16[2,4,512,128]{3,2,1,0:T(8,128)(2,1)S(1)} %constant_dynamic-update-slice_fusion.11.weight_ref), channel_id=1, source_target_pairs={{0,1},{1,0},{2,3},{3,2},{4,5},{5,4},{6,7},{7,6},{8,9},{9,8},{10,11... | collective-permute-start | bytes 3145736 | tf_op jit(solution)/shard_map/ppermute | solution.py:347
  105.9 7.0 %collective-permute-start.11 = (bf16[24,3584]{1,0:T(8,128)(2,1)S(1)}, bf16[24,3584]{1,0:T(8,128)(2,1)S(1)}, u32[]{:S(2)}, u32[]{:S(2)}) collective-permute-start(bf16[24,3584]{1,0:T(8,128)(2,1)S(1)} %get-tuple-element.36), channel_id=1, source_target_pairs={{0,2},{1,3},{2,0},{3,1},{4,6},{5,7},{6,4},{7,5},{8,10},{9,11},{10,... | collective-permute-start | bytes 516104 | tf_op jit(solution)/shard_map/ppermute | solution.py:347
  106.5 12.7 %collective-permute-start.12 = (bf16[24,3584]{1,0:T(8,128)(2,1)S(1)}, bf16[24,3584]{1,0:T(8,128)(2,1)S(1)}, u32[]{:S(2)}, u32[]{:S(2)}) collective-permute-start(bf16[24,3584]{1,0:T(8,128)(2,1)S(1)} %get-tuple-element.37), channel_id=1, source_target_pairs={{0,4},{1,5},{2,6},{3,7},{4,0},{5,1},{6,2},{7,3},{8,12},{9,13},{10,... | collective-permute-start | bytes 516104 | tf_op jit(solution)/shard_map/ppermute | solution.py:347
  111.0 29.6 %collective-permute-start.13 = (bf16[24,3584]{1,0:T(8,128)(2,1)}, bf16[24,3584]{1,0:T(8,128)(2,1)S(1)}, u32[]{:S(2)}, u32[]{:S(2)}) collective-permute-start(bf16[24,3584]{1,0:T(8,128)(2,1)} %get-tuple-element.38), channel_id=1, source_target_pairs={{0,6},{1,7},{2,4},{3,5},{4,2},{5,3},{6,0},{7,1},{8,14},{9,15},{10,... | collective-permute-start | bytes 516104 | tf_op jit(solution)/shard_map/ppermute | solution.py:347
  111.9 28.6 %collective-permute-start.14 = (bf16[24,3584]{1,0:T(8,128)(2,1)}, bf16[24,3584]{1,0:T(8,128)(2,1)S(1)}, u32[]{:S(2)}, u32[]{:S(2)}) collective-permute-start(bf16[24,3584]{1,0:T(8,128)(2,1)} %get-tuple-element.39), channel_id=1, source_target_pairs={{0,8},{1,9},{2,10},{3,11},{4,12},{5,13},{6,14},{7,15},{8,0},{9,1},... | collective-permute-start | bytes 516104 | tf_op jit(solution)/shard_map/ppermute | solution.py:347
  112.9 27.7 %collective-permute-start.15 = (bf16[24,3584]{1,0:T(8,128)(2,1)}, bf16[24,3584]{1,0:T(8,128)(2,1)S(1)}, u32[]{:S(2)}, u32[]{:S(2)}) collective-permute-start(bf16[24,3584]{1,0:T(8,128)(2,1)} %get-tuple-element.40), channel_id=1, source_target_pairs={{0,10},{1,11},{2,8},{3,9},{4,14},{5,15},{6,12},{7,13},{8,2},{9,3},... | collective-permute-start | bytes 516104 | tf_op jit(solution)/shard_map/ppermute | solution.py:347
  119.1 21.4 %collective-permute-start.16 = (bf16[24,3584]{1,0:T(8,128)(2,1)}, bf16[24,3584]{1,0:T(8,128)(2,1)S(1)}, u32[]{:S(2)}, u32[]{:S(2)}) collective-permute-start(bf16[24,3584]{1,0:T(8,128)(2,1)} %copy-done.5), channel_id=1, source_target_pairs={{0,12},{1,13},{2,14},{3,15},{4,8},{5,9},{6,10},{7,11},{8,4},{9,5},... | collective-permute-start | bytes 516104 | tf_op jit(solution)/shard_map/ppermute | solution.py:347
  121.8 18.8 %collective-permute-start.17 = (bf16[24,3584]{1,0:T(8,128)(2,1)}, bf16[24,3584]{1,0:T(8,128)(2,1)S(1)}, u32[]{:S(2)}, u32[]{:S(2)}) collective-permute-start(bf16[24,3584]{1,0:T(8,128)(2,1)} %copy-done.4), channel_id=1, source_target_pairs={{0,14},{1,15},{2,12},{3,13},{4,10},{5,11},{6,8},{7,9},{8,6},{9,7},... | collective-permute-start | bytes 516104 | tf_op jit(solution)/shard_map/ppermute | solution.py:347
  140.6 8.8 %copy-start.9 = (f32[64,2]{0,1:T(2,128)S(1)}, f32[64,2]{0,1:T(2,128)}, u32[]{:S(2)}) copy-start(f32[64,2]{0,1:T(2,128)} %param.16) | copy-start | bytes 1540
  140.6 0.7 copy-start.2
  141.3 8.2 %copy-start.3 = (bf16[24,3584]{1,0:T(8,128)(2,1)S(1)}, bf16[24,3584]{1,0:T(8,128)(2,1)}, u32[]{:S(2)}) copy-start(bf16[24,3584]{1,0:T(8,128)(2,1)} %copy-done.2) | copy-start | bytes 516100
  141.3 22.8 %all-to-all-start.2 = ((bf16[8,64,1024]{2,1,0:T(8,128)(2,1)}), bf16[8,64,1024]{2,1,0:T(8,128)(2,1)S(1)}, u32[]{:S(2)}, u32[]{:S(2)}) async-start(bf16[8,64,1024]{2,1,0:T(8,128)(2,1)} %bitcast.12), calls=%async_computation.2 | async-start | bytes 2097152 | tf_op jit(solution)/shard_map/all_to_all | solution.py:183

commit v10 on v9

--- a/solution.py
+++ b/solution.py
@@ -231,9 +231,9 @@
 EXP_SCALE = math.log2(math.e) / math.sqrt(NOPE + ROPE)
 
 
-def attention_kernel(
-    split, rank_ref, query_ref, kv_ref, other_kv_ref, weight_ref, other_weight_ref, out_ref, keys, queries, mixed
-):
+def attention_kernel(split, rank_ref, query_ref, kv_ref, other_kv_ref, *refs):
+    weight_refs = refs[:-4]
+    out_ref, keys, queries, mixed = refs[-4:]
     tok = kv_ref.shape[1]
     part_rows = query_ref.shape[0] // split.parts
     core = rank_ref[0] & 1
@@ -248,10 +248,13 @@
                 keys[group, place, : LATENT + ROPE] = from_ref[index]
                 keys[group, place, LATENT + ROPE :] = from_ref[index, :, LATENT:]
 
-    own_core = pl.program_id(0) < split.pairs // 2
+    piece = pl.program_id(0) // split.own_pairs
 
     def weight(index):
-        return jnp.where(own_core, weight_ref[0, index], other_weight_ref[0, index])
+        value = weight_refs[0][0, index]
+        for number in range(1, len(weight_refs)):
+            value = jnp.where(piece == number, weight_refs[number][0, index], value)
+        return value
 
     contract = (((1,), (1,)), ((), ()))
     side = lax.broadcasted_iota(jnp.int32, (1, 2 * ROPE), 1) // ROPE
@@ -311,16 +314,20 @@
         ).astype(BF16)
 
 
-def attention(split, place, queries, keys, other_keys, weights, other_weights):
+def attention(split, place, queries, keys, other_keys, weights):
     count = queries.shape[0]
     length = 2 * keys.shape[0] * keys.shape[1] // split.parts
     whole = pl.BlockSpec(keys.shape, lambda p, place: (0, 0, 0))
-    each = split.pairs // 2
+    each = split.own_pairs
+
+    def pair_of(piece):
+        return lambda p, place: (jnp.clip(p - piece * each, 0, each - 1), 0, 0, 0)
+
     return call(
         functools.partial(attention_kernel, split),
         "causal_attention",
         flops=4 * count * length * split.pairs * (2 * LATENT + ROPE),
-        moved=4 * (queries.size + keys.size + weights.size),
+        moved=4 * (queries.size + keys.size + weights[0].size * len(weights)),
         grid_spec=pltpu.PrefetchScalarGridSpec(
             num_scalar_prefetch=1,
             grid=(split.pairs,),
@@ -328,9 +335,8 @@
                 pl.BlockSpec((count, 2 * (NOPE + ROPE)), lambda p, place: (0, p)),
                 whole,
                 whole,
-                pl.BlockSpec((1, 4, LATENT, VDIM), lambda p, place: (jnp.minimum(p, each - 1), 0, 0, 0)),
-                pl.BlockSpec((1, 4, LATENT, VDIM), lambda p, place: (jnp.maximum(p - each, 0), 0, 0, 0)),
-            ],
+            ]
+            + [pl.BlockSpec((1, 4, LATENT, VDIM), pair_of(piece)) for piece in range(len(weights))],
             out_specs=pl.BlockSpec((count, 2 * VDIM), lambda p, place: (0, p)),
             scratch_shapes=[
                 pltpu.VMEM((split.parts, length, LATENT + 2 * ROPE), BF16),
@@ -339,7 +345,7 @@
             ],
         ),
         out_shape=jax.ShapeDtypeStruct((count, 2 * split.pairs * VDIM), BF16),
-    )(place, queries, keys, other_keys, weights, other_weights)
+    )(place, queries, keys, other_keys, *weights)
 
 
 def send(array, mask):
@@ -405,16 +411,13 @@
     buckets = after(build_buckets(routes, moe_input, experts, rows), *keys)
     arrived = swap_chips(buckets.reshape(experts, rows, D)).reshape(experts * rows, D)
 
-    keys = jnp.stack(keys)
+    sent = split_queries(split, rank, queries)
+    keys = after(jnp.stack(keys), sent)
     for mask in later:
         keys = jnp.concatenate([keys, send(keys, mask)], axis=0)
     other_keys = send(keys, 1)
-    own_half = [expert_gate, expert_up, expert_down]
-    other_half = [send(after(part, buckets), 1) for part in own_half]
-    sent = after(split_queries(split, rank, queries), other_keys, arrived, *other_half)
-    held = split.exchange(sent).reshape(experts * tok, -1)
-
-    weights = jnp.concatenate(
+
+    near = jnp.concatenate(
         [
             key_proj.swapaxes(1, 2).reshape(-1, 2, LATENT, NOPE),
             value_proj.reshape(-1, 2, LATENT, VDIM),
@@ -422,15 +425,23 @@
         axis=1,
     )
     if split.wide:
-        weights = lax.dynamic_slice_in_dim(weights, group[0] * split.own_pairs, split.own_pairs, axis=0)
-        weights = after(weights, arrived)
-        weights = jnp.concatenate([weights, send(weights, shards // 2)], axis=0)
+        near = lax.dynamic_slice_in_dim(near, group[0] * split.own_pairs, split.own_pairs, axis=0)
+    near = after(near, buckets)
+    other_near = send(near, 1)
+
+    own_half = [expert_gate, expert_up, expert_down]
+    other_half = [send(after(part, buckets), 1) for part in own_half]
+    held = split.exchange(after(sent, other_keys, other_near, arrived, *other_half)).reshape(experts * tok, -1)
+    weights = [near, other_near]
+    if split.wide:
+        far = send(after(near, arrived), shards // 2)
 
     result = expert_rows(rank, arrived, own_half, other_half, experts)
     back = [result[0]] + [send(result[m], 2 * m) for m in range(1, experts)]
-    other_weights = send(after(weights, result[0]), 1)
-    held = after(held, result[0])
-    values = attention(split, place, held, keys, other_keys, weights, other_weights)
+    if split.wide:
+        weights = [near, far, other_near, send(after(far, back[1]), 1)]
+    held = after(held, back[1])
+    values = attention(split, place, held, keys, other_keys, weights)
     values, *back = lax.optimization_barrier((values, *back))
     values = split.exchange(values.reshape(experts, tok, values.shape[1]))
     moe_out = combine(routes ^ (rank // 2), gates, back, rows)

time: 166 us -> 158 us (0.952); the launches traced: 165 us -> 155 us
  waiting for transfers between devices: 75.7 us -> 64.3 us
    ppermute x18 -> x19, waiting for transfers between devices: 62.7 us -> 50.5 us  [send(): lax.ppermute(array, ('groups', 'ctx'), [(i, i ^ mask) for i in range(coun...]
    ppermute x18 -> x19, starting transfers between devices: 27.3 us -> 29.4 us  [send(): lax.ppermute(array, ('groups', 'ctx'), [(i, i ^ mask) for i in range(coun...]
    unnamed x27 -> x28, local copies, waits for them, and re-layouts: 6.51 us -> 8.41 us
    concatenate x2 -> x1, local copies, waits for them, and re-layouts: 2.77 us -> 0.9 us  [on_device(): keys = jnp.concatenate([keys, send(keys, mask)], axis=0)]
  transfers between devices with their start and end apart: 21 -> 22, of which waited for: 7 -> 8; matrix products, arithmetic and copies ran while one was open for 4% -> 2% of each run, Pallas kernels for 20% -> 22%
where the time goes in v10:
time: 158 us; the launch traced here: 155 us
  waiting for transfers between devices  64.3 us (41%)
  starting transfers between devices  45.7 us (29%)
  Pallas kernels  34.5 us (22%)
  local copies, waits for them, and re-layouts  9.57 us (6%)
    ppermute x19, waiting for transfers between devices, send(): lax.ppermute(array, ('groups', 'ctx'), [(i, i ^ mask) for i in range(coun...  50.5 us
    ppermute x19, starting transfers between devices, send(): lax.ppermute(array, ('groups', 'ctx'), [(i, i ^ mask) for i in range(coun...  29.4 us
    pallas_call x1, Pallas kernels, attention(): call(functools.partial(attention_kernel, split), 'causal_attention', flop...  15.2 us
    all_to_all x2, waiting for transfers between devices, exchange(): lax.all_to_all(array, ('groups', 'ctx'), split_axis=0, concat_axis=0, axi...  13.8 us
    pallas_call x1, Pallas kernels, expert_rows(): call(expert_kernel, 'expert_rows', flops=12 * count * D * HALF, moved=12...  13.1 us
    all_to_all x2, starting transfers between devices, exchange(): lax.all_to_all(array, ('groups', 'ctx'), split_axis=0, concat_axis=0, axi...  11.4 us
    unnamed x28, local copies, waits for them, and re-layouts  8.41 us
    all_to_all x1, starting transfers between devices, swap_chips(): lax.all_to_all(array, 'ctx', split_axis=0, concat_axis=0, axis_index_grou...  4.9 us
  transfers between devices with their start and end apart: 22, of which 8 were waited for; matrix products, arithmetic and copies ran while one was open for 2% of the time, Pallas kernels for 22%

profile of v10, /device:TPU:0, one launch (start us, length us, event | category | flops | bytes accessed | tf_op | source)
XLA Modules:
  0.0 155.2 jit_solution(8079135684963673529)
XLA Ops:
  0.6 4.1 %collective-permute-start = (bf16[64,576]{1,0:T(8,128)(2,1)}, bf16[64,576]{1,0:T(8,128)(2,1)S(1)}, u32[]{:S(2)}, u32[]{:S(2)}) collective-permute-start(bf16[64,576]{1,0:T(8,128)(2,1)} %param.11), channel_id=1, source_target_pairs={{0,8},{1,9},{2,10},{3,11},{4,12},{5,13},{6,14},{7,15},{8,0},{9,1},... | collective-permute-start | bytes 221192 | tf_op jit(solution)/shard_map/ppermute | solution.py:353
  4.7 1.6 %collective-permute-start.1 = (bf16[64,576]{1,0:T(8,128)(2,1)}, bf16[64,576]{1,0:T(8,128)(2,1)S(1)}, u32[]{:S(2)}, u32[]{:S(2)}) collective-permute-start(bf16[64,576]{1,0:T(8,128)(2,1)} %param.11), channel_id=1, source_target_pairs={{0,4},{1,5},{2,6},{3,7},{4,0},{5,1},{6,2},{7,3},{8,12},{9,13},{10,... | collective-permute-start | bytes 221192 | tf_op jit(solution)/shard_map/ppermute | solution.py:353
  6.3 0.0 collective-permute-start.2
  6.3 0.8 copy.17.routes_ref
  7.1 1.0 copy-done.1
  8.1 2.0 %bucket_rows.1 = bf16[192,3584]{1,0:T(8,128)(2,1)} custom-call(s32[64,2]{1,0:T(8,128)S(1)} %copy.17.routes_ref, bf16[64,3584]{1,0:T(8,128)(2,1)S(1)} %copy-done.1), custom_call_target="tpu_custom_call" | custom-call | bytes 1835008 | tf_op jit(solution)/shard_map/bucket_rows/pallas_call | solution.py:66
  10.1 0.0 collective-permute-done
  10.1 0.0 collective-permute-done.1
  10.1 2.7 %collective-permute-done.2 = bf16[64,576]{1,0:T(8,128)(2,1)S(1)} collective-permute-done((bf16[64,576]{1,0:T(8,128)(2,1)}, bf16[64,576]{1,0:T(8,128)(2,1)S(1)}, u32[]{:S(2)}, u32[]{:S(2)}) %collective-permute-start.2) | collective-permute-done | bytes 73760 | tf_op jit(solution)/shard_map/ppermute | solution.py:353
  12.8 0.0 collective-permute-start.7
  12.8 0.5 collective-permute-start.8
  13.3 0.0 collective-permute-start.9
  13.3 1.6 %split_queries.1 = bf16[8,64,1536]{2,1,0:T(8,128)(2,1)} custom-call(s32[1]{0:T(128)} %bitcast.rank_ref, bf16[64,12288]{1,0:T(8,128)(2,1)S(1)} %copy-done), custom_call_target="tpu_custom_call" | custom-call | bytes 3145728 | tf_op jit(solution)/shard_map/split_queries/pallas_call | solution.py:201
  14.8 4.9 %all-to-all-start = ((bf16[8,24,3584]{2,1,0:T(8,128)(2,1)}), bf16[8,24,3584]{2,1,0:T(8,128)(2,1)S(1)}, u32[]{:S(2)}, u32[]{:S(2)}) async-start(bf16[8,24,3584]{2,1,0:T(8,128)(2,1)} %bitcast.9), calls=%async_computation | async-start | bytes 2752512 | tf_op jit(solution)/shard_map/all_to_all | solution.py:358
  19.7 0.1 pad_maximum_fusion.1
  19.8 1.6 %collective-permute-start.3 = (bf16[4,64,576]{2,1,0:T(8,128)(2,1)S(1)}, bf16[4,64,576]{2,1,0:T(8,128)(2,1)S(1)}, u32[]{:S(2)}, u32[]{:S(2)}) collective-permute-start(bf16[4,64,576]{2,1,0:T(8,128)(2,1)S(1)} %pad_maximum_fusion.1), channel_id=1, source_target_pairs={{0,16},{1,17},{2,18},{3,19},{4,20},{5,21},{6,22},{7,23},{8,24},{9,... | collective-permute-start | bytes 884744 | tf_op jit(solution)/shard_map/ppermute | solution.py:353
  21.4 8.3 %collective-permute-done.3 = bf16[4,64,576]{2,1,0:T(8,128)(2,1)S(1)} collective-permute-done((bf16[4,64,576]{2,1,0:T(8,128)(2,1)S(1)}, bf16[4,64,576]{2,1,0:T(8,128)(2,1)S(1)}, u32[]{:S(2)}, u32[]{:S(2)}) %collective-permute-start.3) | collective-permute-done | bytes 294944 | tf_op jit(solution)/shard_map/ppermute | solution.py:353
  29.7 0.1 pad_maximum_fusion
  29.8 0.0 copy-start.8
  29.8 1.8 %collective-permute-start.4 = (bf16[8,64,576]{2,1,0:T(8,128)(2,1)S(1)}, bf16[8,64,576]{2,1,0:T(8,128)(2,1)S(1)}, u32[]{:S(2)}, u32[]{:S(2)}) collective-permute-start(bf16[8,64,576]{2,1,0:T(8,128)(2,1)S(1)} %pad_maximum_fusion), channel_id=1, source_target_pairs={{0,2},{1,3},{2,0},{3,1},{4,6},{5,7},{6,4},{7,5},{8,10},{9,11},{10,... | collective-permute-start | bytes 1769480 | tf_op jit(solution)/shard_map/ppermute | solution.py:353
  31.6 0.8 constant_dynamic-update-slice_fusion.2
  32.4 0.8 constant_dynamic-update-slice_fusion.1
  33.1 19.3 %collective-permute-done.4 = bf16[8,64,576]{2,1,0:T(8,128)(2,1)S(1)} collective-permute-done((bf16[8,64,576]{2,1,0:T(8,128)(2,1)S(1)}, bf16[8,64,576]{2,1,0:T(8,128)(2,1)S(1)}, u32[]{:S(2)}, u32[]{:S(2)}) %collective-permute-start.4) | collective-permute-done | bytes 589856 | tf_op jit(solution)/shard_map/ppermute | solution.py:353
  52.4 0.9 constant_dynamic-update-slice_fusion.kv_ref
  53.3 0.3 copy.16
  53.6 0.1 fusion.refs_0_
  53.7 0.6 collective-permute-start.6
  54.3 2.9 %collective-permute-done.6.refs_2_ = bf16[1,4,512,128]{3,2,1,0:T(8,128)(2,1)S(1)} collective-permute-done((bf16[1,4,512,128]{3,2,1,0:T(8,128)(2,1)S(1)}, bf16[1,4,512,128]{3,2,1,0:T(8,128)(2,1)S(1)}, u32[]{:S(2)}, u32[]{:S(2)}) %collective-permute-start.6) | collective-permute-done | bytes 524320 | tf_op jit(solution)/shard_map/ppermute | solution.py:353
  57.1 0.8 copy-done.2
  57.9 0.0 collective-permute-done.5.other_kv_ref
  57.9 0.0 all-to-all-done
  57.9 0.0 collective-permute-done.7.gate1
  57.9 0.0 collective-permute-done.9.down1
  58.0 4.5 %all-to-all-start.1 = ((bf16[8,64,1536]{2,1,0:T(8,128)(2,1)}), bf16[8,64,1536]{2,1,0:T(8,128)(2,1)}, u32[]{:S(2)}, u32[]{:S(2)}) async-start(bf16[8,64,1536]{2,1,0:T(8,128)(2,1)} %split_queries.1), calls=%async_computation.1 | async-start | bytes 3145728 | tf_op jit(solution)/shard_map/all_to_all | solution.py:183
  62.4 4.1 %collective-permute-start.11 = (bf16[1,4,512,128]{3,2,1,0:T(8,128)(2,1)S(1)}, bf16[1,4,512,128]{3,2,1,0:T(8,128)(2,1)S(1)}, u32[]{:S(2)}, u32[]{:S(2)}) collective-permute-start(bf16[1,4,512,128]{3,2,1,0:T(8,128)(2,1)S(1)} %fusion.refs_0_), channel_id=1, source_target_pairs={{0,8},{1,9},{2,10},{3,11},{4,12},{5,13},{6,14},{7,15},{8,0},{9,1},... | collective-permute-start | bytes 1572872 | tf_op jit(solution)/shard_map/ppermute | solution.py:353
  66.5 13.1 %expert_rows.1 = (bf16[24,3584]{1,0:T(8,128)(2,1)S(1)}, bf16[24,3584]{1,0:T(8,128)(2,1)S(1)}, bf16[24,3584]{1,0:T(8,128)(2,1)S(1)}, bf16[24,3584]{1,0:T(8,128)(2...) custom-call(s32[1]{0:T(128)} %bitcast.rank_ref, ...), custom_call_target="tpu_custom_call" | custom-call | flops 4227858432 | bytes 24772608 | tf_op jit(solution)/shard_map/expert_rows/pallas_call | solution.py:135
  79.7 0.7 copy-done.6
  80.3 0.7 copy-done.7
  81.0 2.0 %collective-permute-start.10 = (bf16[24,3584]{1,0:T(8,128)(2,1)S(1)}, bf16[24,3584]{1,0:T(8,128)(2,1)S(1)}, u32[]{:S(2)}, u32[]{:S(2)}) collective-permute-start(bf16[24,3584]{1,0:T(8,128)(2,1)S(1)} %get-tuple-element.36), channel_id=1, source_target_pairs={{0,2},{1,3},{2,0},{3,1},{4,6},{5,7},{6,4},{7,5},{8,10},{9,11},{10,... | collective-permute-start | bytes 516104 | tf_op jit(solution)/shard_map/ppermute | solution.py:353
  83.0 10.5 %collective-permute-done.11.refs_1_ = bf16[1,4,512,128]{3,2,1,0:T(8,128)(2,1)S(1)} collective-permute-done((bf16[1,4,512,128]{3,2,1,0:T(8,128)(2,1)S(1)}, bf16[1,4,512,128]{3,2,1,0:T(8,128)(2,1)S(1)}, u32[]{:S(2)}, u32[]{:S(2)}) %collective-permute-start.11) | collective-permute-done | bytes 524320 | tf_op jit(solution)/shard_map/ppermute | solution.py:353
  93.5 1.8 %collective-permute-done.10.refs_1_ = bf16[24,3584]{1,0:T(8,128)(2,1)S(1)} collective-permute-done((bf16[24,3584]{1,0:T(8,128)(2,1)S(1)}, bf16[24,3584]{1,0:T(8,128)(2,1)S(1)}, u32[]{:S(2)}, u32[]{:S(2)}) %collective-permute-start.10) | collective-permute-done | bytes 172064 | tf_op jit(solution)/shard_map/ppermute | solution.py:353
  95.3 0.0 collective-permute-start.12
  95.3 0.8 copy-done.4
  96.1 5.3 %collective-permute-start.13 = (bf16[24,3584]{1,0:T(8,128)(2,1)S(1)}, bf16[24,3584]{1,0:T(8,128)(2,1)S(1)}, u32[]{:S(2)}, u32[]{:S(2)}) collective-permute-start(bf16[24,3584]{1,0:T(8,128)(2,1)S(1)} %get-tuple-element.41), channel_id=1, source_target_pairs={{0,4},{1,5},{2,6},{3,7},{4,0},{5,1},{6,2},{7,3},{8,12},{9,13},{10,... | collective-permute-start | bytes 516104 | tf_op jit(solution)/shard_map/ppermute | solution.py:353
  101.4 0.1 pad_add_fusion.rank_ref
  101.4 0.0 collective-permute-start.14
  101.4 0.1 collective-permute-start.15
  101.5 3.7 %collective-permute-start.16 = (bf16[24,3584]{1,0:T(8,128)(2,1)}, bf16[24,3584]{1,0:T(8,128)(2,1)S(1)}, u32[]{:S(2)}, u32[]{:S(2)}) collective-permute-start(bf16[24,3584]{1,0:T(8,128)(2,1)} %get-tuple-element.44), channel_id=1, source_target_pairs={{0,10},{1,11},{2,8},{3,9},{4,14},{5,15},{6,12},{7,13},{8,2},{9,3},... | collective-permute-start | bytes 516104 | tf_op jit(solution)/shard_map/ppermute | solution.py:353
  105.3 0.0 all-to-all-done.1
  105.3 5.0 %collective-permute-done.13.refs_2_ = bf16[24,3584]{1,0:T(8,128)(2,1)S(1)} collective-permute-done((bf16[24,3584]{1,0:T(8,128)(2,1)S(1)}, bf16[24,3584]{1,0:T(8,128)(2,1)S(1)}, u32[]{:S(2)}, u32[]{:S(2)}) %collective-permute-start.13) | collective-permute-done | bytes 172064 | tf_op jit(solution)/shard_map/ppermute | solution.py:353
  110.3 4.1 %collective-permute-start.17 = (bf16[24,3584]{1,0:T(8,128)(2,1)}, bf16[24,3584]{1,0:T(8,128)(2,1)S(1)}, u32[]{:S(2)}, u32[]{:S(2)}) collective-permute-start(bf16[24,3584]{1,0:T(8,128)(2,1)} %copy-done.7), channel_id=1, source_target_pairs={{0,12},{1,13},{2,14},{3,15},{4,8},{5,9},{6,10},{7,11},{8,4},{9,5},... | collective-permute-start | bytes 516104 | tf_op jit(solution)/shard_map/ppermute | solution.py:353
  114.4 0.0 collective-permute-done.12.refs_3_
  114.4 1.0 copy-done.3
  115.4 1.0 copy-done.5
  116.5 15.2 %causal_attention.1 = bf16[512,1024]{1,0:T(8,128)(2,1)} custom-call(s32[2]{0:T(128)S(1)} %pad_add_fusion.rank_ref, bf16[512,1536]{1,0:T(8,128)(2,1)} %bitcast.11.query_ref, bf16[16,64,576]{2,1,0:T(8,128)(2,1)} %constant_dynamic-update-slice_fusion.kv_ref, bf16[16,64,576]{2,1,0:T(8,128)(2,1)} %collective-permute-done.5.other_kv_ref, ...), custom_call_target="tpu_custom_call" | custom-call | flops 9126805504 | bytes 9699328 | tf_op jit(solution)/shard_map/causal_attention/pallas_call | solution.py:326
  131.7 0.0 collective-permute-done.14.refs_3_
  131.7 0.0 collective-permute-done.15.refs_4_
  131.7 0.0 collective-permute-done.16.refs_5_
  131.7 0.0 collective-permute-done.18.refs_7_
  131.7 6.9 %all-to-all-start.2 = ((bf16[8,64,1024]{2,1,0:T(8,128)(2,1)}), bf16[8,64,1024]{2,1,0:T(8,128)(2,1)S(1)}, u32[]{:S(2)}, u32[]{:S(2)}) async-start(bf16[8,64,1024]{2,1,0:T(8,128)(2,1)} %bitcast.12), calls=%async_computation.2 | async-start | bytes 2097152 | tf_op jit(solution)/shard_map/all_to_all | solution.py:183
  138.6 0.1 copy.20.gates_ref
  138.7 1.6 %combine_routes.1 = bf16[64,3584]{1,0:T(8,128)(2,1)} custom-call(s32[64,2]{1,0:T(8,128)S(1)} %broadcast_xor_fusion.routes_ref, f32[64,2]{1,0:T(8,128)S(1)} %copy.20.gates_ref, bf16[24,3584]{1,0:T(8,128)(2,1)S(1)} %get-tuple-element.48.refs_0_, bf16[24,3584]{1,0:T(8,128)(2,1)S(1)} %collective-permute-done.10.refs_1_, ...), custom_call_target="tpu_custom_call" | custom-call | bytes 1835008 | tf_op jit(solution)/shard_map/combine_routes/pallas_call | solution.py:87
  140.3 13.8 %all-to-all-done.2.x_ref = bf16[8,64,1024]{2,1,0:T(8,128)(2,1)S(1)} async-done(((bf16[8,64,1024]{2,1,0:T(8,128)(2,1)}), bf16[8,64,1024]{2,1,0:T(8,128)(2,1)S(1)}, u32[]{:S(2)}, u32[]{:S(2)}) %all-to-all-start.2) | async-done | bytes 1048608 | tf_op jit(solution)/shard_map/all_to_all | solution.py:183
  154.1 1.1 join_values.1
  (21 shorter events, 0.0 us)
Async XLA Ops:
  0.6 12.7 %copy-start = (bf16[64,12288]{1,0:T(8,128)(2,1)S(1)}, bf16[64,12288]{1,0:T(8,128)(2,1)}, u32[]{:S(2)}) copy-start(bf16[64,12288]{1,0:T(8,128)(2,1)} %x_ref.2) | copy-start | bytes 4718596
  0.6 9.5 %collective-permute-start = (bf16[64,576]{1,0:T(8,128)(2,1)}, bf16[64,576]{1,0:T(8,128)(2,1)S(1)}, u32[]{:S(2)}, u32[]{:S(2)}) collective-permute-start(bf16[64,576]{1,0:T(8,128)(2,1)} %param.11), channel_id=1, source_target_pairs={{0,8},{1,9},{2,10},{3,11},{4,12},{5,13},{6,14},{7,15},{8,0},{9,1},... | collective-permute-start | bytes 221192 | tf_op jit(solution)/shard_map/ppermute | solution.py:353
  4.7 5.4 %collective-permute-start.1 = (bf16[64,576]{1,0:T(8,128)(2,1)}, bf16[64,576]{1,0:T(8,128)(2,1)S(1)}, u32[]{:S(2)}, u32[]{:S(2)}) collective-permute-start(bf16[64,576]{1,0:T(8,128)(2,1)} %param.11), channel_id=1, source_target_pairs={{0,4},{1,5},{2,6},{3,7},{4,0},{5,1},{6,2},{7,3},{8,12},{9,13},{10,... | collective-permute-start | bytes 221192 | tf_op jit(solution)/shard_map/ppermute | solution.py:353
  6.3 6.4 %collective-permute-start.2 = (bf16[64,576]{1,0:T(8,128)(2,1)}, bf16[64,576]{1,0:T(8,128)(2,1)S(1)}, u32[]{:S(2)}, u32[]{:S(2)}) collective-permute-start(bf16[64,576]{1,0:T(8,128)(2,1)} %param.11), channel_id=1, source_target_pairs={{0,12},{1,13},{2,14},{3,15},{4,8},{5,9},{6,10},{7,11},{8,4},{9,5},... | collective-permute-start | bytes 221192 | tf_op jit(solution)/shard_map/ppermute | solution.py:353
  7.1 1.0 copy-start.1
  12.8 45.2 %collective-permute-start.7 = (bf16[1,3584,512]{2,1,0:T(8,128)(2,1)}, bf16[1,3584,512]{2,1,0:T(8,128)(2,1)}, u32[]{:S(2)}, u32[]{:S(2)}) collective-permute-start(bf16[1,3584,512]{2,1,0:T(8,128)(2,1)} %gate0.1), channel_id=1, source_target_pairs={{0,1},{1,0},{2,3},{3,2},{4,5},{5,4},{6,7},{7,6},{8,9},{9,8},{10,11... | collective-permute-start | bytes 11010056 | tf_op jit(solution)/shard_map/ppermute | solution.py:353
  12.8 45.2 %collective-permute-start.8 = (bf16[1,3584,512]{2,1,0:T(8,128)(2,1)}, bf16[1,3584,512]{2,1,0:T(8,128)(2,1)}, u32[]{:S(2)}, u32[]{:S(2)}) collective-permute-start(bf16[1,3584,512]{2,1,0:T(8,128)(2,1)} %up0.1), channel_id=1, source_target_pairs={{0,1},{1,0},{2,3},{3,2},{4,5},{5,4},{6,7},{7,6},{8,9},{9,8},{10,11... | collective-permute-start | bytes 11010056 | tf_op jit(solution)/shard_map/ppermute | solution.py:353
  13.3 44.7 %collective-permute-start.9 = (bf16[1,512,3584]{2,1,0:T(8,128)(2,1)}, bf16[1,512,3584]{2,1,0:T(8,128)(2,1)}, u32[]{:S(2)}, u32[]{:S(2)}) collective-permute-start(bf16[1,512,3584]{2,1,0:T(8,128)(2,1)} %down0.1), channel_id=1, source_target_pairs={{0,1},{1,0},{2,3},{3,2},{4,5},{5,4},{6,7},{7,6},{8,9},{9,8},{10,11... | collective-permute-start | bytes 11010056 | tf_op jit(solution)/shard_map/ppermute | solution.py:353
  14.8 4.9 %copy-start.10 = (bf16[64,576]{1,0:T(8,128)(2,1)S(1)}, bf16[64,576]{1,0:T(8,128)(2,1)}, u32[]{:S(2)}) copy-start(bf16[64,576]{1,0:T(8,128)(2,1)} %param.11) | copy-start | bytes 221188
  14.8 43.1 %all-to-all-start = ((bf16[8,24,3584]{2,1,0:T(8,128)(2,1)}), bf16[8,24,3584]{2,1,0:T(8,128)(2,1)S(1)}, u32[]{:S(2)}, u32[]{:S(2)}) async-start(bf16[8,24,3584]{2,1,0:T(8,128)(2,1)} %bitcast.9), calls=%async_computation | async-start | bytes 2752512 | tf_op jit(solution)/shard_map/all_to_all | solution.py:358
  19.8 9.9 %collective-permute-start.3 = (bf16[4,64,576]{2,1,0:T(8,128)(2,1)S(1)}, bf16[4,64,576]{2,1,0:T(8,128)(2,1)S(1)}, u32[]{:S(2)}, u32[]{:S(2)}) collective-permute-start(bf16[4,64,576]{2,1,0:T(8,128)(2,1)S(1)} %pad_maximum_fusion.1), channel_id=1, source_target_pairs={{0,16},{1,17},{2,18},{3,19},{4,20},{5,21},{6,22},{7,23},{8,24},{9,... | collective-permute-start | bytes 884744 | tf_op jit(solution)/shard_map/ppermute | solution.py:353
  29.8 23.5 %copy-start.8 = (bf16[4,128,512]{2,1,0:T(8,128)(2,1)S(1)}, bf16[4,128,512]{2,1,0:T(8,128)(2,1)}, u32[]{:S(2)}) copy-start(bf16[4,128,512]{2,1,0:T(8,128)(2,1)} %param.12) | copy-start | bytes 1572868
  29.8 22.6 %collective-permute-start.4 = (bf16[8,64,576]{2,1,0:T(8,128)(2,1)S(1)}, bf16[8,64,576]{2,1,0:T(8,128)(2,1)S(1)}, u32[]{:S(2)}, u32[]{:S(2)}) collective-permute-start(bf16[8,64,576]{2,1,0:T(8,128)(2,1)S(1)} %pad_maximum_fusion), channel_id=1, source_target_pairs={{0,2},{1,3},{2,0},{3,1},{4,6},{5,7},{6,4},{7,5},{8,10},{9,11},{10,... | collective-permute-start | bytes 1769480 | tf_op jit(solution)/shard_map/ppermute | solution.py:353
  32.4 21.3 %copy-start.9 = (bf16[4,512,128]{2,1,0:T(8,128)(2,1)S(1)}, bf16[4,512,128]{2,1,0:T(8,128)(2,1)}, u32[]{:S(2)}) copy-start(bf16[4,512,128]{2,1,0:T(8,128)(2,1)} %param.13) | copy-start | bytes 1572868
  53.3 4.6 %collective-permute-start.5 = (bf16[16,64,576]{2,1,0:T(8,128)(2,1)}, bf16[16,64,576]{2,1,0:T(8,128)(2,1)}, u32[]{:S(2)}, u32[]{:S(2)}) collective-permute-start(bf16[16,64,576]{2,1,0:T(8,128)(2,1)} %constant_dynamic-update-slice_fusion.kv_ref), channel_id=1, source_target_pairs={{0,1},{1,0},{2,3},{3,2},{4,5},{5,4},{6,7},{7,6},{8,9},{9,8},{10,11... | collective-permute-start | bytes 3538952 | tf_op jit(solution)/shard_map/ppermute | solution.py:353
  53.7 3.4 %collective-permute-start.6 = (bf16[1,4,512,128]{3,2,1,0:T(8,128)(2,1)S(1)}, bf16[1,4,512,128]{3,2,1,0:T(8,128)(2,1)S(1)}, u32[]{:S(2)}, u32[]{:S(2)}) collective-permute-start(bf16[1,4,512,128]{3,2,1,0:T(8,128)(2,1)S(1)} %fusion.refs_0_), channel_id=1, source_target_pairs={{0,1},{1,0},{2,3},{3,2},{4,5},{5,4},{6,7},{7,6},{8,9},{9,8},{10,11... | collective-permute-start | bytes 1572872 | tf_op jit(solution)/shard_map/ppermute | solution.py:353
  57.1 0.8 copy-start.2
  58.0 47.3 %all-to-all-start.1 = ((bf16[8,64,1536]{2,1,0:T(8,128)(2,1)}), bf16[8,64,1536]{2,1,0:T(8,128)(2,1)}, u32[]{:S(2)}, u32[]{:S(2)}) async-start(bf16[8,64,1536]{2,1,0:T(8,128)(2,1)} %split_queries.1), calls=%async_computation.1 | async-start | bytes 3145728 | tf_op jit(solution)/shard_map/all_to_all | solution.py:183
  62.4 31.0 %collective-permute-start.11 = (bf16[1,4,512,128]{3,2,1,0:T(8,128)(2,1)S(1)}, bf16[1,4,512,128]{3,2,1,0:T(8,128)(2,1)S(1)}, u32[]{:S(2)}, u32[]{:S(2)}) collective-permute-start(bf16[1,4,512,128]{3,2,1,0:T(8,128)(2,1)S(1)} %fusion.refs_0_), channel_id=1, source_target_pairs={{0,8},{1,9},{2,10},{3,11},{4,12},{5,13},{6,14},{7,15},{8,0},{9,1},... | collective-permute-start | bytes 1572872 | tf_op jit(solution)/shard_map/ppermute | solution.py:353
  79.7 0.7 copy-start.6
  80.3 0.7 copy-start.7
  81.0 14.3 %collective-permute-start.10 = (bf16[24,3584]{1,0:T(8,128)(2,1)S(1)}, bf16[24,3584]{1,0:T(8,128)(2,1)S(1)}, u32[]{:S(2)}, u32[]{:S(2)}) collective-permute-start(bf16[24,3584]{1,0:T(8,128)(2,1)S(1)} %get-tuple-element.36), channel_id=1, source_target_pairs={{0,2},{1,3},{2,0},{3,1},{4,6},{5,7},{6,4},{7,5},{8,10},{9,11},{10,... | collective-permute-start | bytes 516104 | tf_op jit(solution)/shard_map/ppermute | solution.py:353
  95.3 19.1 %collective-permute-start.12 = (bf16[1,4,512,128]{3,2,1,0:T(8,128)(2,1)S(1)}, bf16[1,4,512,128]{3,2,1,0:T(8,128)(2,1)S(1)}, u32[]{:S(2)}, u32[]{:S(2)}) collective-permute-start(bf16[1,4,512,128]{3,2,1,0:T(8,128)(2,1)S(1)} %collective-permute-done.11.refs_1_), channel_id=1, source_target_pairs={{0,1},{1,0},{2,3},{3,2},{4,5},{5,4},{6,7},{7,6},{8,9},{9,8},{10,11... | collective-permute-start | bytes 1572872 | tf_op jit(solution)/shard_map/ppermute | solution.py:353
  95.3 0.8 copy-start.4
  96.1 14.2 %collective-permute-start.13 = (bf16[24,3584]{1,0:T(8,128)(2,1)S(1)}, bf16[24,3584]{1,0:T(8,128)(2,1)S(1)}, u32[]{:S(2)}, u32[]{:S(2)}) collective-permute-start(bf16[24,3584]{1,0:T(8,128)(2,1)S(1)} %get-tuple-element.41), channel_id=1, source_target_pairs={{0,4},{1,5},{2,6},{3,7},{4,0},{5,1},{6,2},{7,3},{8,12},{9,13},{10,... | collective-permute-start | bytes 516104 | tf_op jit(solution)/shard_map/ppermute | solution.py:353
  101.4 30.2 %collective-permute-start.14 = (bf16[24,3584]{1,0:T(8,128)(2,1)}, bf16[24,3584]{1,0:T(8,128)(2,1)S(1)}, u32[]{:S(2)}, u32[]{:S(2)}) collective-permute-start(bf16[24,3584]{1,0:T(8,128)(2,1)} %get-tuple-element.42), channel_id=1, source_target_pairs={{0,6},{1,7},{2,4},{3,5},{4,2},{5,3},{6,0},{7,1},{8,14},{9,15},{10,... | collective-permute-start | bytes 516104 | tf_op jit(solution)/shard_map/ppermute | solution.py:353
  101.4 30.2 %collective-permute-start.15 = (bf16[24,3584]{1,0:T(8,128)(2,1)}, bf16[24,3584]{1,0:T(8,128)(2,1)S(1)}, u32[]{:S(2)}, u32[]{:S(2)}) collective-permute-start(bf16[24,3584]{1,0:T(8,128)(2,1)} %get-tuple-element.43), channel_id=1, source_target_pairs={{0,8},{1,9},{2,10},{3,11},{4,12},{5,13},{6,14},{7,15},{8,0},{9,1},... | collective-permute-start | bytes 516104 | tf_op jit(solution)/shard_map/ppermute | solution.py:353
  101.5 30.2 %collective-permute-start.16 = (bf16[24,3584]{1,0:T(8,128)(2,1)}, bf16[24,3584]{1,0:T(8,128)(2,1)S(1)}, u32[]{:S(2)}, u32[]{:S(2)}) collective-permute-start(bf16[24,3584]{1,0:T(8,128)(2,1)} %get-tuple-element.44), channel_id=1, source_target_pairs={{0,10},{1,11},{2,8},{3,9},{4,14},{5,15},{6,12},{7,13},{8,2},{9,3},... | collective-permute-start | bytes 516104 | tf_op jit(solution)/shard_map/ppermute | solution.py:353
  110.3 21.4 %collective-permute-start.17 = (bf16[24,3584]{1,0:T(8,128)(2,1)}, bf16[24,3584]{1,0:T(8,128)(2,1)S(1)}, u32[]{:S(2)}, u32[]{:S(2)}) collective-permute-start(bf16[24,3584]{1,0:T(8,128)(2,1)} %copy-done.7), channel_id=1, source_target_pairs={{0,12},{1,13},{2,14},{3,15},{4,8},{5,9},{6,10},{7,11},{8,4},{9,5},... | collective-permute-start | bytes 516104 | tf_op jit(solution)/shard_map/ppermute | solution.py:353
  114.4 17.3 %collective-permute-start.18 = (bf16[24,3584]{1,0:T(8,128)(2,1)}, bf16[24,3584]{1,0:T(8,128)(2,1)S(1)}, u32[]{:S(2)}, u32[]{:S(2)}) collective-permute-start(bf16[24,3584]{1,0:T(8,128)(2,1)} %copy-done.6), channel_id=1, source_target_pairs={{0,14},{1,15},{2,12},{3,13},{4,10},{5,11},{6,8},{7,9},{8,6},{9,7},... | collective-permute-start | bytes 516104 | tf_op jit(solution)/shard_map/ppermute | solution.py:353
  114.4 1.0 copy-start.3
  115.4 1.0 copy-start.5
  131.7 7.0 %copy-start.11 = (f32[64,2]{0,1:T(2,128)S(1)}, f32[64,2]{0,1:T(2,128)}, u32[]{:S(2)}) copy-start(f32[64,2]{0,1:T(2,128)} %param.16) | copy-start | bytes 1540
  131.7 22.4 %all-to-all-start.2 = ((bf16[8,64,1024]{2,1,0:T(8,128)(2,1)}), bf16[8,64,1024]{2,1,0:T(8,128)(2,1)S(1)}, u32[]{:S(2)}, u32[]{:S(2)}) async-start(bf16[8,64,1024]{2,1,0:T(8,128)(2,1)} %bitcast.12), calls=%async_computation.2 | async-start | bytes 2097152 | tf_op jit(solution)/shard_map/all_to_all | solution.py:183

commit v11 on v8

--- a/solution.py
+++ b/solution.py
@@ -214,9 +214,9 @@
 EXP_SCALE = math.log2(math.e) / math.sqrt(NOPE + ROPE)
 
 
-def attention_kernel(
-    split, rank_ref, query_ref, kv_ref, other_kv_ref, weight_ref, other_weight_ref, out_ref, keys, queries, mixed
-):
+def attention_kernel(split, rank_ref, query_ref, kv_ref, other_kv_ref, *refs):
+    weight_refs = refs[:-4]
+    out_ref, keys, queries, mixed = refs[-4:]
     tok = kv_ref.shape[1]
     part_rows = query_ref.shape[0] // split.parts
     core = rank_ref[0] & 1
@@ -231,10 +231,13 @@
                 keys[group, place, : LATENT + ROPE] = from_ref[index]
                 keys[group, place, LATENT + ROPE :] = from_ref[index, :, LATENT:]
 
-    own_core = pl.program_id(0) < split.pairs // 2
+    piece = pl.program_id(0) // split.own_pairs
 
     def weight(index):
-        return jnp.where(own_core, weight_ref[0, index], other_weight_ref[0, index])
+        value = weight_refs[0][0, index]
+        for number in range(1, len(weight_refs)):
+            value = jnp.where(piece == number, weight_refs[number][0, index], value)
+        return value
 
     contract = (((1,), (1,)), ((), ()))
     side = lax.broadcasted_iota(jnp.int32, (1, 2 * ROPE), 1) // ROPE
@@ -294,16 +297,20 @@
         ).astype(BF16)
 
 
-def attention(split, place, queries, keys, other_keys, weights, other_weights):
+def attention(split, place, queries, keys, other_keys, weights):
     count = queries.shape[0]
     length = 2 * keys.shape[0] * keys.shape[1] // split.parts
     whole = pl.BlockSpec(keys.shape, lambda p, place: (0, 0, 0))
-    each = split.pairs // 2
+    each = split.own_pairs
+
+    def pair_of(piece):
+        return lambda p, place: (jnp.clip(p - piece * each, 0, each - 1), 0, 0, 0)
+
     return call(
         functools.partial(attention_kernel, split),
         "causal_attention",
         flops=4 * count * length * split.pairs * (2 * LATENT + ROPE),
-        moved=4 * (queries.size + keys.size + weights.size),
+        moved=4 * (queries.size + keys.size + weights[0].size * len(weights)),
         grid_spec=pltpu.PrefetchScalarGridSpec(
             num_scalar_prefetch=1,
             grid=(split.pairs,),
@@ -311,9 +318,8 @@
                 pl.BlockSpec((count, 2 * (NOPE + ROPE)), lambda p, place: (0, p)),
                 whole,
                 whole,
-                pl.BlockSpec((1, 4, LATENT, VDIM), lambda p, place: (jnp.minimum(p, each - 1), 0, 0, 0)),
-                pl.BlockSpec((1, 4, LATENT, VDIM), lambda p, place: (jnp.maximum(p - each, 0), 0, 0, 0)),
-            ],
+            ]
+            + [pl.BlockSpec((1, 4, LATENT, VDIM), pair_of(piece)) for piece in range(len(weights))],
             out_specs=pl.BlockSpec((count, 2 * VDIM), lambda p, place: (0, p)),
             scratch_shapes=[
                 pltpu.VMEM((split.parts, length, LATENT + 2 * ROPE), BF16),
@@ -322,7 +328,7 @@
             ],
         ),
         out_shape=jax.ShapeDtypeStruct((count, 2 * split.pairs * VDIM), BF16),
-    )(place, queries, keys, other_keys, weights, other_weights)
+    )(place, queries, keys, other_keys, *weights)
 
 
 def send(array, mask):
@@ -382,21 +388,7 @@
     group = lax.axis_index("groups").astype(jnp.int32).reshape(1)
     place = jnp.concatenate([rank, group])
 
-    direct, later = gather_masks(split)
-    keys = jnp.stack([latent_kv] + [send(latent_kv, offset) for offset in direct])
-
-    buckets = after(build_buckets(routes, moe_input, experts, rows), keys)
-    arrived = swap_chips(buckets.reshape(experts, rows, D)).reshape(experts * rows, D)
-
-    for mask in later:
-        keys = jnp.concatenate([keys, send(keys, mask)], axis=0)
-    other_keys = send(keys, 1)
-    own_half = [expert_gate, expert_up, expert_down]
-    other_half = [send(part, 1) for part in own_half]
-    sent = after(split_queries(split, rank, queries), other_keys, arrived, *other_half)
-    held = split.exchange(sent).reshape(experts * tok, -1)
-
-    weights = jnp.concatenate(
+    near = jnp.concatenate(
         [
             key_proj.swapaxes(1, 2).reshape(-1, 2, LATENT, NOPE),
             value_proj.reshape(-1, 2, LATENT, VDIM),
@@ -404,17 +396,28 @@
         axis=1,
     )
     if split.wide:
-        weights = lax.dynamic_slice_in_dim(weights, group[0] * split.own_pairs, split.own_pairs, axis=0)
-        weights = after(weights, arrived)
-        weights = jnp.concatenate([weights, send(weights, shards // 2)], axis=0)
-
-    result = expert_rows(arrived, own_half, other_half)
-    other_weights = send(after(weights, result), 1)
-    result, held = lax.optimization_barrier((result, held))
+        near = lax.dynamic_slice_in_dim(near, group[0] * split.own_pairs, split.own_pairs, axis=0)
+
+    direct, later = gather_masks(split)
+    keys = [latent_kv] + [send(latent_kv, offset) for offset in direct]
+    held = split.exchange(split_queries(split, rank, queries)).reshape(experts * tok, -1)
+    pieces = [near, send(near, shards // 2)] if split.wide else [near]
+    own_half = [expert_gate, expert_up, expert_down]
+    other_half = [send(after(part, *keys), 1) for part in own_half]
+    keys = jnp.stack(keys)
+    for mask in later:
+        keys = jnp.concatenate([keys, send(keys, mask)], axis=0)
+
+    buckets = after(build_buckets(routes, moe_input, experts, rows), held, keys, *pieces)
+    arrived = swap_chips(buckets.reshape(experts, rows, D)).reshape(experts * rows, D)
+
+    weights = pieces + [send(piece, 1) for piece in pieces]
+    values = attention(split, place, held, keys, send(keys, 1), weights)
+    values = after(values, arrived)
+    values = split.exchange(values.reshape(experts, tok, values.shape[1]))
+
+    result = after(expert_rows(arrived, own_half, other_half), values)
     back = swap_chips(result.reshape(experts, rows, D))
-    values = attention(split, place, held, keys, other_keys, weights, other_weights)
-    values, back = lax.optimization_barrier((values, back))
-    values = split.exchange(values.reshape(experts, tok, values.shape[1]))
     moe_out = combine(routes, gates, back.reshape(experts * rows, D), rows)
     return (join_values(split, rank, values), moe_out)
 

time: 153 us -> 172 us (1.12)
  waiting for transfers between devices: 77.6 us -> 90.3 us
  starting transfers between devices: 30.1 us -> 34.2 us
    all_to_all x2, waiting for transfers between devices: 29.1 us -> 1.46 us  [exchange(): lax.all_to_all(array, ('groups', 'ctx'), split_axis=0, concat_axis=0, axi...]
    all_to_all x2, waiting for transfers between devices: 14.6 us -> 36 us  [swap_chips(): lax.all_to_all(array, 'ctx', split_axis=0, concat_axis=0, axis_index_grou...]
    ppermute x11 -> x12, waiting for transfers between devices: 33.9 us -> 52.9 us  [send(): lax.ppermute(array, ('groups', 'ctx'), [(i, i ^ mask) for i in range(coun...]
    all_to_all x2, starting transfers between devices: 7.14 us -> 14.7 us  [swap_chips(): lax.all_to_all(array, 'ctx', split_axis=0, concat_axis=0, axis_index_grou...]
    ppermute x11 -> x12, starting transfers between devices: 15 us -> 9.68 us  [send(): lax.ppermute(array, ('groups', 'ctx'), [(i, i ^ mask) for i in range(coun...]
    unnamed x19 -> x28, local copies, waits for them, and re-layouts: 6.28 us -> 8.6 us
    all_to_all x2, starting transfers between devices: 7.99 us -> 9.87 us  [exchange(): lax.all_to_all(array, ('groups', 'ctx'), split_axis=0, concat_axis=0, axi...]
  transfers between devices with their start and end apart: 15 -> 16, of which waited for: 8 -> 9; matrix products, arithmetic and copies ran while one was open for 5% -> 4% of each run, Pallas kernels for 22% -> 18%
where the time goes in v11:
time: 172 us
  waiting for transfers between devices  90.3 us (52%)
  Pallas kernels  34.5 us (20%)
  starting transfers between devices  34.2 us (20%)
  local copies, waits for them, and re-layouts  10.8 us (6%)
    ppermute x12, waiting for transfers between devices, send(): lax.ppermute(array, ('groups', 'ctx'), [(i, i ^ mask) for i in range(coun...  52.9 us
    all_to_all x2, waiting for transfers between devices, swap_chips(): lax.all_to_all(array, 'ctx', split_axis=0, concat_axis=0, axis_index_grou...  36 us
    pallas_call x1, Pallas kernels, attention(): call(functools.partial(attention_kernel, split), 'causal_attention', flop...  15.1 us
    all_to_all x2, starting transfers between devices, swap_chips(): lax.all_to_all(array, 'ctx', split_axis=0, concat_axis=0, axis_index_grou...  14.7 us
    pallas_call x1, Pallas kernels, expert_rows(): call(expert_kernel, 'expert_rows', flops=12 * count * D * HALF, moved=12...  13.2 us
    all_to_all x2, starting transfers between devices, exchange(): lax.all_to_all(array, ('groups', 'ctx'), split_axis=0, concat_axis=0, axi...  9.87 us
    ppermute x12, starting transfers between devices, send(): lax.ppermute(array, ('groups', 'ctx'), [(i, i ^ mask) for i in range(coun...  9.68 us
    unnamed x28, local copies, waits for them, and re-layouts  8.6 us
  transfers between devices with their start and end apart: 16, of which 9 were waited for; matrix products, arithmetic and copies ran while one was open for 4% of the time, Pallas kernels for 18%

profile of v11, /device:TPU:0, one launch (start us, length us, event | category | flops | bytes accessed | tf_op | source)
XLA Modules:
  0.0 171.8 jit_solution(14952849951181977966)
XLA Ops:
  0.6 0.0 copy-start
  0.6 1.4 copy-done
  2.0 1.5 split_queries.1
  3.6 6.3 %all-to-all-start = ((bf16[8,64,1536]{2,1,0:T(8,128)(2,1)}), bf16[8,64,1536]{2,1,0:T(8,128)(2,1)S(1)}, u32[]{:S(2)}, u32[]{:S(2)}) async-start(bf16[8,64,1536]{2,1,0:T(8,128)(2,1)} %split_queries.1), calls=%async_computation | async-start | bytes 3145728 | tf_op jit(solution)/shard_map/all_to_all | solution.py:166
  9.9 0.0 copy-done.4
  9.9 0.0 copy-start.3
  9.9 4.1 %collective-permute-start.2 = (bf16[64,576]{1,0:T(8,128)(2,1)S(1)}, bf16[64,576]{1,0:T(8,128)(2,1)S(1)}, u32[]{:S(2)}, u32[]{:S(2)}) collective-permute-start(bf16[64,576]{1,0:T(8,128)(2,1)S(1)} %copy-done.4), channel_id=1, source_target_pairs={{0,12},{1,13},{2,14},{3,15},{4,8},{5,9},{6,10},{7,11},{8,4},{9,5},... | collective-permute-start | bytes 221192 | tf_op jit(solution)/shard_map/ppermute | solution.py:336
  14.0 0.0 collective-permute-start.1
  14.0 0.6 collective-permute-start
  14.7 0.6 constant_dynamic-update-slice_fusion.4
  15.3 21.7 %collective-permute-done.2 = bf16[64,576]{1,0:T(8,128)(2,1)S(1)} collective-permute-done((bf16[64,576]{1,0:T(8,128)(2,1)S(1)}, bf16[64,576]{1,0:T(8,128)(2,1)S(1)}, u32[]{:S(2)}, u32[]{:S(2)}) %collective-permute-start.2) | collective-permute-done | bytes 73760 | tf_op jit(solution)/shard_map/ppermute | solution.py:336
  37.0 0.0 collective-permute-done.1
  37.0 0.0 collective-permute-done
  37.0 0.1 pad_maximum_fusion
  37.1 1.2 collective-permute-start.3
  38.3 0.6 constant_dynamic-update-slice_fusion.3
  39.0 0.6 constant_dynamic-update-slice_fusion.2
  39.6 0.6 constant_dynamic-update-slice_fusion.1
  40.3 4.1 %collective-permute-done.3 = bf16[4,64,576]{2,1,0:T(8,128)(2,1)S(1)} collective-permute-done((bf16[4,64,576]{2,1,0:T(8,128)(2,1)S(1)}, bf16[4,64,576]{2,1,0:T(8,128)(2,1)S(1)}, u32[]{:S(2)}, u32[]{:S(2)}) %collective-permute-start.3) | collective-permute-done | bytes 294944 | tf_op jit(solution)/shard_map/ppermute | solution.py:336
  44.3 0.8 constant_dynamic-update-slice_fusion
  45.1 1.0 copy-done.5
  46.2 0.0 collective-permute-start.4
  46.2 0.0 copy-done.3
  46.2 0.3 copy.12
  46.5 1.0 fusion.refs_0_
  47.5 2.5 %collective-permute-start.6 = (bf16[1,4,512,128]{3,2,1,0:T(8,128)(2,1)S(1)}, bf16[1,4,512,128]{3,2,1,0:T(8,128)(2,1)S(1)}, u32[]{:S(2)}, u32[]{:S(2)}) collective-permute-start(bf16[1,4,512,128]{3,2,1,0:T(8,128)(2,1)S(1)} %fusion.refs_0_), channel_id=1, source_target_pairs={{0,8},{1,9},{2,10},{3,11},{4,12},{5,13},{6,14},{7,15},{8,0},{9,1},... | collective-permute-start | bytes 1572872 | tf_op jit(solution)/shard_map/ppermute | solution.py:336
  49.9 0.0 copy-done.8
  49.9 0.1 copy.13.routes_ref
  50.0 0.0 copy-done.1
  50.0 2.0 %bucket_rows.1 = bf16[192,3584]{1,0:T(8,128)(2,1)} custom-call(s32[64,2]{1,0:T(8,128)S(1)} %copy.13.routes_ref, bf16[64,3584]{1,0:T(8,128)(2,1)S(1)} %copy-done.1), custom_call_target="tpu_custom_call" | custom-call | bytes 1835008 | tf_op jit(solution)/shard_map/bucket_rows/pallas_call | solution.py:66
  52.0 7.7 %collective-permute-done.4 = bf16[8,64,576]{2,1,0:T(8,128)(2,1)} collective-permute-done((bf16[8,64,576]{2,1,0:T(8,128)(2,1)}, bf16[8,64,576]{2,1,0:T(8,128)(2,1)}, u32[]{:S(2)}, u32[]{:S(2)}) %collective-permute-start.4) | collective-permute-done | bytes 589856 | tf_op jit(solution)/shard_map/ppermute | solution.py:336
  59.8 0.0 copy-done.6
  59.8 1.2 constant_dynamic-update-slice_fusion.5.kv_ref
  61.0 0.0 copy-start.7
  61.0 1.1 copy-done.7
  62.0 8.3 %collective-permute-done.6.refs_1_ = bf16[1,4,512,128]{3,2,1,0:T(8,128)(2,1)S(1)} collective-permute-done((bf16[1,4,512,128]{3,2,1,0:T(8,128)(2,1)S(1)}, bf16[1,4,512,128]{3,2,1,0:T(8,128)(2,1)S(1)}, u32[]{:S(2)}, u32[]{:S(2)}) %collective-permute-start.6) | collective-permute-done | bytes 524320 | tf_op jit(solution)/shard_map/ppermute | solution.py:336
  70.3 0.0 all-to-all-done
  70.3 1.2 copy-done.2
  71.5 6.0 %all-to-all-start.1 = ((bf16[8,24,3584]{2,1,0:T(8,128)(2,1)}), bf16[8,24,3584]{2,1,0:T(8,128)(2,1)S(1)}, u32[]{:S(2)}, u32[]{:S(2)}) async-start(bf16[8,24,3584]{2,1,0:T(8,128)(2,1)} %bitcast.10), calls=%async_computation.1 | async-start | bytes 2752512 | tf_op jit(solution)/shard_map/all_to_all | solution.py:341
  77.5 0.0 collective-permute-start.9
  77.5 0.5 collective-permute-start.10
  78.0 0.1 collective-permute-start.11
  78.1 0.4 collective-permute-start.5
  78.6 0.1 collective-permute-start.7
  78.6 7.6 %collective-permute-done.7.refs_2_ = bf16[1,4,512,128]{3,2,1,0:T(8,128)(2,1)S(1)} collective-permute-done((bf16[1,4,512,128]{3,2,1,0:T(8,128)(2,1)S(1)}, bf16[1,4,512,128]{3,2,1,0:T(8,128)(2,1)S(1)}, u32[]{:S(2)}, u32[]{:S(2)}) %collective-permute-start.7) | collective-permute-done | bytes 524320 | tf_op jit(solution)/shard_map/ppermute | solution.py:336
  86.2 0.1 collective-permute-start.8
  86.3 0.1 pad_add_fusion.rank_ref
  86.4 3.5 %collective-permute-done.8.refs_3_ = bf16[1,4,512,128]{3,2,1,0:T(8,128)(2,1)S(1)} collective-permute-done((bf16[1,4,512,128]{3,2,1,0:T(8,128)(2,1)S(1)}, bf16[1,4,512,128]{3,2,1,0:T(8,128)(2,1)S(1)}, u32[]{:S(2)}, u32[]{:S(2)}) %collective-permute-start.8) | collective-permute-done | bytes 524320 | tf_op jit(solution)/shard_map/ppermute | solution.py:336
  89.9 0.0 collective-permute-done.5.other_kv_ref
  89.9 1.1 copy-done.10
  91.0 15.1 %causal_attention.1 = bf16[512,1024]{1,0:T(8,128)(2,1)} custom-call(s32[2]{0:T(128)S(1)} %pad_add_fusion.rank_ref, bf16[512,1536]{1,0:T(8,128)(2,1)} %bitcast.26, bf16[16,64,576]{2,1,0:T(8,128)(2,1)} %copy-done.7, bf16[16,64,576]{2,1,0:T(8,128)(2,1)} %copy-done.10, bf16[1,4,512,128]{3,2,1,0:T(8,128)(2,1)S(1)} %fusion.refs_0_, ...), custom_call_target="tpu_custom_call" | custom-call | flops 9126805504 | bytes 9699328 | tf_op jit(solution)/shard_map/causal_attention/pallas_call | solution.py:309
  106.1 4.4 %all-to-all-done.1 = bf16[8,24,3584]{2,1,0:T(8,128)(2,1)S(1)} async-done(((bf16[8,24,3584]{2,1,0:T(8,128)(2,1)}), bf16[8,24,3584]{2,1,0:T(8,128)(2,1)S(1)}, u32[]{:S(2)}, u32[]{:S(2)}) %all-to-all-start.1) | async-done | bytes 1376288 | tf_op jit(solution)/shard_map/all_to_all | solution.py:341
  110.5 3.6 %all-to-all-start.2 = ((bf16[8,64,1024]{2,1,0:T(8,128)(2,1)}), bf16[8,64,1024]{2,1,0:T(8,128)(2,1)S(1)}, u32[]{:S(2)}, u32[]{:S(2)}) async-start(bf16[8,64,1024]{2,1,0:T(8,128)(2,1)} %bitcast.12), calls=%async_computation.2 | async-start | bytes 2097152 | tf_op jit(solution)/shard_map/all_to_all | solution.py:166
  114.1 0.0 collective-permute-done.9.gate1
  114.1 0.0 collective-permute-done.10.up1
  114.1 0.0 collective-permute-done.11.down1
  114.1 13.2 %expert_rows.1 = bf16[192,3584]{1,0:T(8,128)(2,1)} custom-call(bf16[192,3584]{1,0:T(8,128)(2,1)S(1)} %bitcast.24, bf16[1,3584,512]{2,1,0:T(8,128)(2,1)} %gate0.1, bf16[1,3584,512]{2,1,0:T(8,128)(2,1)} %up0.1, bf16[1,3584,512]{2,1,0:T(8,128)(2,1)} %collective-permute-done.9.gate1, bf16[1,3584,512]{2,1,0:T(8,128)(2,1)} %collective-permute-done.10.up1, ...), custom_call_target="tpu_custom_call" | custom-call | flops 4227858432 | bytes 24772608 | tf_op jit(solution)/shard_map/expert_rows/pallas_call | solution.py:125
  127.3 1.5 all-to-all-done.2.x_ref
  128.8 8.7 %all-to-all-start.3 = ((bf16[8,24,3584]{2,1,0:T(8,128)(2,1)}), bf16[8,24,3584]{2,1,0:T(8,128)(2,1)S(1)}, u32[]{:S(2)}, u32[]{:S(2)}) async-start(bf16[8,24,3584]{2,1,0:T(8,128)(2,1)} %bitcast.13), calls=%async_computation.3 | async-start | bytes 2752512 | tf_op jit(solution)/shard_map/all_to_all | solution.py:341
  137.5 0.0 copy-done.9
  137.5 0.1 copy.15.gates_ref
  137.6 1.1 join_values.1
  138.7 31.6 %all-to-all-done.3 = bf16[8,24,3584]{2,1,0:T(8,128)(2,1)S(1)} async-done(((bf16[8,24,3584]{2,1,0:T(8,128)(2,1)}), bf16[8,24,3584]{2,1,0:T(8,128)(2,1)S(1)}, u32[]{:S(2)}, u32[]{:S(2)}) %all-to-all-start.3) | async-done | bytes 1376288 | tf_op jit(solution)/shard_map/all_to_all | solution.py:341
  170.3 1.6 combine_routes.1
  (8 shorter events, 0.0 us)
Async XLA Ops:
  0.6 1.4 copy-start
  3.6 6.3 %copy-start.4 = (bf16[64,576]{1,0:T(8,128)(2,1)S(1)}, bf16[64,576]{1,0:T(8,128)(2,1)}, u32[]{:S(2)}) copy-start(bf16[64,576]{1,0:T(8,128)(2,1)} %param.11) | copy-start | bytes 221188
  3.6 66.8 %all-to-all-start = ((bf16[8,64,1536]{2,1,0:T(8,128)(2,1)}), bf16[8,64,1536]{2,1,0:T(8,128)(2,1)S(1)}, u32[]{:S(2)}, u32[]{:S(2)}) async-start(bf16[8,64,1536]{2,1,0:T(8,128)(2,1)} %split_queries.1), calls=%async_computation | async-start | bytes 3145728 | tf_op jit(solution)/shard_map/all_to_all | solution.py:166
  9.9 36.3 %copy-start.3 = (bf16[4,128,512]{2,1,0:T(8,128)(2,1)S(1)}, bf16[4,128,512]{2,1,0:T(8,128)(2,1)}, u32[]{:S(2)}) copy-start(bf16[4,128,512]{2,1,0:T(8,128)(2,1)} %param.12) | copy-start | bytes 1572868
  9.9 27.1 %collective-permute-start.2 = (bf16[64,576]{1,0:T(8,128)(2,1)S(1)}, bf16[64,576]{1,0:T(8,128)(2,1)S(1)}, u32[]{:S(2)}, u32[]{:S(2)}) collective-permute-start(bf16[64,576]{1,0:T(8,128)(2,1)S(1)} %copy-done.4), channel_id=1, source_target_pairs={{0,12},{1,13},{2,14},{3,15},{4,8},{5,9},{6,10},{7,11},{8,4},{9,5},... | collective-permute-start | bytes 221192 | tf_op jit(solution)/shard_map/ppermute | solution.py:336
  14.0 23.0 %collective-permute-start.1 = (bf16[64,576]{1,0:T(8,128)(2,1)S(1)}, bf16[64,576]{1,0:T(8,128)(2,1)S(1)}, u32[]{:S(2)}, u32[]{:S(2)}) collective-permute-start(bf16[64,576]{1,0:T(8,128)(2,1)S(1)} %copy-done.4), channel_id=1, source_target_pairs={{0,4},{1,5},{2,6},{3,7},{4,0},{5,1},{6,2},{7,3},{8,12},{9,13},{10,... | collective-permute-start | bytes 221192 | tf_op jit(solution)/shard_map/ppermute | solution.py:336
  14.0 23.0 %collective-permute-start = (bf16[64,576]{1,0:T(8,128)(2,1)S(1)}, bf16[64,576]{1,0:T(8,128)(2,1)S(1)}, u32[]{:S(2)}, u32[]{:S(2)}) collective-permute-start(bf16[64,576]{1,0:T(8,128)(2,1)S(1)} %copy-done.4), channel_id=1, source_target_pairs={{0,8},{1,9},{2,10},{3,11},{4,12},{5,13},{6,14},{7,15},{8,0},{9,1},... | collective-permute-start | bytes 221192 | tf_op jit(solution)/shard_map/ppermute | solution.py:336
  37.1 7.3 %collective-permute-start.3 = (bf16[4,64,576]{2,1,0:T(8,128)(2,1)S(1)}, bf16[4,64,576]{2,1,0:T(8,128)(2,1)S(1)}, u32[]{:S(2)}, u32[]{:S(2)}) collective-permute-start(bf16[4,64,576]{2,1,0:T(8,128)(2,1)S(1)} %pad_maximum_fusion), channel_id=1, source_target_pairs={{0,16},{1,17},{2,18},{3,19},{4,20},{5,21},{6,22},{7,23},{8,24},{9,... | collective-permute-start | bytes 884744 | tf_op jit(solution)/shard_map/ppermute | solution.py:336
  45.1 1.1 copy-start.5
  46.2 13.6 %collective-permute-start.4 = (bf16[8,64,576]{2,1,0:T(8,128)(2,1)}, bf16[8,64,576]{2,1,0:T(8,128)(2,1)}, u32[]{:S(2)}, u32[]{:S(2)}) collective-permute-start(bf16[8,64,576]{2,1,0:T(8,128)(2,1)} %get-tuple-element.14), channel_id=1, source_target_pairs={{0,2},{1,3},{2,0},{3,1},{4,6},{5,7},{6,4},{7,5},{8,10},{9,11},{10,... | collective-permute-start | bytes 1769480 | tf_op jit(solution)/shard_map/ppermute | solution.py:336
  46.2 3.8 %copy-start.8 = (s32[64,2]{0,1:T(2,128)S(1)}, s32[64,2]{0,1:T(2,128)}, u32[]{:S(2)}) copy-start(s32[64,2]{0,1:T(2,128)} %param.15) | copy-start | bytes 1540
  46.2 3.9 %copy-start.1 = (bf16[64,3584]{1,0:T(8,128)(2,1)S(1)}, bf16[64,3584]{1,0:T(8,128)(2,1)}, u32[]{:S(2)}) copy-start(bf16[64,3584]{1,0:T(8,128)(2,1)} %x_ref.3) | copy-start | bytes 1376260
  47.5 22.9 %collective-permute-start.6 = (bf16[1,4,512,128]{3,2,1,0:T(8,128)(2,1)S(1)}, bf16[1,4,512,128]{3,2,1,0:T(8,128)(2,1)S(1)}, u32[]{:S(2)}, u32[]{:S(2)}) collective-permute-start(bf16[1,4,512,128]{3,2,1,0:T(8,128)(2,1)S(1)} %fusion.refs_0_), channel_id=1, source_target_pairs={{0,8},{1,9},{2,10},{3,11},{4,12},{5,13},{6,14},{7,15},{8,0},{9,1},... | collective-permute-start | bytes 1572872 | tf_op jit(solution)/shard_map/ppermute | solution.py:336
  50.0 9.8 %copy-start.6 = (bf16[16,64,576]{2,1,0:T(8,128)(2,1)S(1)}, bf16[16,64,576]{2,1,0:T(8,128)(2,1)}, u32[]{:S(2)}) copy-start(bf16[16,64,576]{2,1,0:T(8,128)(2,1)} %copy-done.5) | copy-start | bytes 3538948
  61.0 1.1 copy-start.7
  70.3 1.2 copy-start.2
  71.5 39.0 %all-to-all-start.1 = ((bf16[8,24,3584]{2,1,0:T(8,128)(2,1)}), bf16[8,24,3584]{2,1,0:T(8,128)(2,1)S(1)}, u32[]{:S(2)}, u32[]{:S(2)}) async-start(bf16[8,24,3584]{2,1,0:T(8,128)(2,1)} %bitcast.10), calls=%async_computation.1 | async-start | bytes 2752512 | tf_op jit(solution)/shard_map/all_to_all | solution.py:341
  77.5 36.5 %collective-permute-start.9 = (bf16[1,3584,512]{2,1,0:T(8,128)(2,1)}, bf16[1,3584,512]{2,1,0:T(8,128)(2,1)}, u32[]{:S(2)}, u32[]{:S(2)}) collective-permute-start(bf16[1,3584,512]{2,1,0:T(8,128)(2,1)} %gate0.1), channel_id=1, source_target_pairs={{0,1},{1,0},{2,3},{3,2},{4,5},{5,4},{6,7},{7,6},{8,9},{9,8},{10,11... | collective-permute-start | bytes 11010056 | tf_op jit(solution)/shard_map/ppermute | solution.py:336
  77.5 36.5 %collective-permute-start.10 = (bf16[1,3584,512]{2,1,0:T(8,128)(2,1)}, bf16[1,3584,512]{2,1,0:T(8,128)(2,1)}, u32[]{:S(2)}, u32[]{:S(2)}) collective-permute-start(bf16[1,3584,512]{2,1,0:T(8,128)(2,1)} %up0.1), channel_id=1, source_target_pairs={{0,1},{1,0},{2,3},{3,2},{4,5},{5,4},{6,7},{7,6},{8,9},{9,8},{10,11... | collective-permute-start | bytes 11010056 | tf_op jit(solution)/shard_map/ppermute | solution.py:336
  78.0 36.1 %collective-permute-start.11 = (bf16[1,512,3584]{2,1,0:T(8,128)(2,1)}, bf16[1,512,3584]{2,1,0:T(8,128)(2,1)}, u32[]{:S(2)}, u32[]{:S(2)}) collective-permute-start(bf16[1,512,3584]{2,1,0:T(8,128)(2,1)} %down0.1), channel_id=1, source_target_pairs={{0,1},{1,0},{2,3},{3,2},{4,5},{5,4},{6,7},{7,6},{8,9},{9,8},{10,11... | collective-permute-start | bytes 11010056 | tf_op jit(solution)/shard_map/ppermute | solution.py:336
  78.1 11.8 %collective-permute-start.5 = (bf16[16,64,576]{2,1,0:T(8,128)(2,1)}, bf16[16,64,576]{2,1,0:T(8,128)(2,1)S(1)}, u32[]{:S(2)}, u32[]{:S(2)}) collective-permute-start(bf16[16,64,576]{2,1,0:T(8,128)(2,1)} %copy-done.7), channel_id=1, source_target_pairs={{0,1},{1,0},{2,3},{3,2},{4,5},{5,4},{6,7},{7,6},{8,9},{9,8},{10,11... | collective-permute-start | bytes 3538952 | tf_op jit(solution)/shard_map/ppermute | solution.py:336
  78.6 7.6 %collective-permute-start.7 = (bf16[1,4,512,128]{3,2,1,0:T(8,128)(2,1)S(1)}, bf16[1,4,512,128]{3,2,1,0:T(8,128)(2,1)S(1)}, u32[]{:S(2)}, u32[]{:S(2)}) collective-permute-start(bf16[1,4,512,128]{3,2,1,0:T(8,128)(2,1)S(1)} %fusion.refs_0_), channel_id=1, source_target_pairs={{0,1},{1,0},{2,3},{3,2},{4,5},{5,4},{6,7},{7,6},{8,9},{9,8},{10,11... | collective-permute-start | bytes 1572872 | tf_op jit(solution)/shard_map/ppermute | solution.py:336
  86.2 3.7 %collective-permute-start.8 = (bf16[1,4,512,128]{3,2,1,0:T(8,128)(2,1)S(1)}, bf16[1,4,512,128]{3,2,1,0:T(8,128)(2,1)S(1)}, u32[]{:S(2)}, u32[]{:S(2)}) collective-permute-start(bf16[1,4,512,128]{3,2,1,0:T(8,128)(2,1)S(1)} %collective-permute-done.6.refs_1_), channel_id=1, source_target_pairs={{0,1},{1,0},{2,3},{3,2},{4,5},{5,4},{6,7},{7,6},{8,9},{9,8},{10,11... | collective-permute-start | bytes 1572872 | tf_op jit(solution)/shard_map/ppermute | solution.py:336
  89.9 1.1 copy-start.10
  110.5 18.3 %all-to-all-start.2 = ((bf16[8,64,1024]{2,1,0:T(8,128)(2,1)}), bf16[8,64,1024]{2,1,0:T(8,128)(2,1)S(1)}, u32[]{:S(2)}, u32[]{:S(2)}) async-start(bf16[8,64,1024]{2,1,0:T(8,128)(2,1)} %bitcast.12), calls=%async_computation.2 | async-start | bytes 2097152 | tf_op jit(solution)/shard_map/all_to_all | solution.py:166
  128.8 8.7 %copy-start.9 = (f32[64,2]{0,1:T(2,128)S(1)}, f32[64,2]{0,1:T(2,128)}, u32[]{:S(2)}) copy-start(f32[64,2]{0,1:T(2,128)} %param.16) | copy-start | bytes 1540
  128.8 41.5 %all-to-all-start.3 = ((bf16[8,24,3584]{2,1,0:T(8,128)(2,1)}), bf16[8,24,3584]{2,1,0:T(8,128)(2,1)S(1)}, u32[]{:S(2)}, u32[]{:S(2)}) async-start(bf16[8,24,3584]{2,1,0:T(8,128)(2,1)} %bitcast.13), calls=%async_computation.3 | async-start | bytes 2752512 | tf_op jit(solution)/shard_map/all_to_all | solution.py:341

commit v12 on v11

--- a/solution.py
+++ b/solution.py
@@ -388,6 +388,18 @@
     group = lax.axis_index("groups").astype(jnp.int32).reshape(1)
     place = jnp.concatenate([rank, group])
 
+    direct, later = gather_masks(split)
+    keys = [latent_kv] + [send(latent_kv, offset) for offset in direct]
+
+    buckets = after(build_buckets(routes, moe_input, experts, rows), *keys)
+    arrived = swap_chips(buckets.reshape(experts, rows, D)).reshape(experts * rows, D)
+
+    sent = split_queries(split, rank, queries)
+    keys = after(jnp.stack(keys), sent)
+    for mask in later:
+        keys = jnp.concatenate([keys, send(keys, mask)], axis=0)
+    other_keys = send(keys, 1)
+
     near = jnp.concatenate(
         [
             key_proj.swapaxes(1, 2).reshape(-1, 2, LATENT, NOPE),
@@ -397,27 +409,20 @@
     )
     if split.wide:
         near = lax.dynamic_slice_in_dim(near, group[0] * split.own_pairs, split.own_pairs, axis=0)
-
-    direct, later = gather_masks(split)
-    keys = [latent_kv] + [send(latent_kv, offset) for offset in direct]
-    held = split.exchange(split_queries(split, rank, queries)).reshape(experts * tok, -1)
-    pieces = [near, send(near, shards // 2)] if split.wide else [near]
+    near = after(near, buckets)
+
     own_half = [expert_gate, expert_up, expert_down]
-    other_half = [send(after(part, *keys), 1) for part in own_half]
-    keys = jnp.stack(keys)
-    for mask in later:
-        keys = jnp.concatenate([keys, send(keys, mask)], axis=0)
-
-    buckets = after(build_buckets(routes, moe_input, experts, rows), held, keys, *pieces)
-    arrived = swap_chips(buckets.reshape(experts, rows, D)).reshape(experts * rows, D)
-
-    weights = pieces + [send(piece, 1) for piece in pieces]
-    values = attention(split, place, held, keys, send(keys, 1), weights)
-    values = after(values, arrived)
+    other_half = [send(after(part, buckets), 1) for part in own_half]
+    held = split.exchange(after(sent, near, arrived, *other_half)).reshape(experts * tok, -1)
+    pieces = [near, send(after(near, arrived), shards // 2)] if split.wide else [near]
+
+    result = expert_rows(arrived, own_half, other_half)
+    weights = pieces + [send(after(piece, result), 1) for piece in pieces]
+    result, held, keys, other_keys = lax.optimization_barrier((result, held, keys, other_keys))
+    back = swap_chips(result.reshape(experts, rows, D))
+    values = attention(split, place, held, keys, other_keys, weights)
+    values, back = lax.optimization_barrier((values, back))
     values = split.exchange(values.reshape(experts, tok, values.shape[1]))
-
-    result = after(expert_rows(arrived, own_half, other_half), values)
-    back = swap_chips(result.reshape(experts, rows, D))
     moe_out = combine(routes, gates, back.reshape(experts * rows, D), rows)
     return (join_values(split, rank, values), moe_out)
 

time: 172 us -> 216 us (1.26); the launches traced: 172 us -> 213 us
  waiting for transfers between devices: 90.3 us -> 144 us
  local copies, waits for them, and re-layouts: 10.8 us -> 3.51 us
  starting transfers between devices: 34.2 us -> 28 us
    ppermute x12, waiting for transfers between devices: 52.9 us -> 100 us  [send(): lax.ppermute(array, ('groups', 'ctx'), [(i, i ^ mask) for i in range(coun...]
    all_to_all x2, waiting for transfers between devices: 1.46 us -> 14.8 us  [exchange(): lax.all_to_all(array, ('groups', 'ctx'), split_axis=0, concat_axis=0, axi...]
    unnamed x28 -> x26, local copies, waits for them, and re-layouts: 8.6 us -> 2.11 us
    all_to_all x2, waiting for transfers between devices: 36 us -> 29.5 us  [swap_chips(): lax.all_to_all(array, 'ctx', split_axis=0, concat_axis=0, axis_index_grou...]
    all_to_all x2, starting transfers between devices: 14.7 us -> 8.64 us  [swap_chips(): lax.all_to_all(array, 'ctx', split_axis=0, concat_axis=0, axis_index_grou...]
  transfers between devices with their start and end apart: 16 -> 16, of which waited for: 9 -> 7; matrix products, arithmetic and copies ran while one was open for 4% -> 2% of each run, Pallas kernels for 18% -> 16%
where the time goes in v12:
time: 216 us; the launch traced here: 213 us
  waiting for transfers between devices  144 us (67%)
  Pallas kernels  34.9 us (16%)
  starting transfers between devices  28 us (13%)
  local copies, waits for them, and re-layouts  3.51 us (2%)
    ppermute x12, waiting for transfers between devices, send(): lax.ppermute(array, ('groups', 'ctx'), [(i, i ^ mask) for i in range(coun...  100 us
    all_to_all x2, waiting for transfers between devices, swap_chips(): lax.all_to_all(array, 'ctx', split_axis=0, concat_axis=0, axis_index_grou...  29.5 us
    pallas_call x1, Pallas kernels, attention(): call(functools.partial(attention_kernel, split), 'causal_attention', flop...  15.1 us
    all_to_all x2, waiting for transfers between devices, exchange(): lax.all_to_all(array, ('groups', 'ctx'), split_axis=0, concat_axis=0, axi...  14.8 us
    pallas_call x1, Pallas kernels, expert_rows(): call(expert_kernel, 'expert_rows', flops=12 * count * D * HALF, moved=12...  13.6 us
    ppermute x12, starting transfers between devices, send(): lax.ppermute(array, ('groups', 'ctx'), [(i, i ^ mask) for i in range(coun...  11.2 us
    all_to_all x2, starting transfers between devices, swap_chips(): lax.all_to_all(array, 'ctx', split_axis=0, concat_axis=0, axis_index_grou...  8.64 us
    all_to_all x2, starting transfers between devices, exchange(): lax.all_to_all(array, ('groups', 'ctx'), split_axis=0, concat_axis=0, axi...  8.13 us
  transfers between devices with their start and end apart: 16, of which 7 were waited for; matrix products, arithmetic and copies ran while one was open for 2% of the time, Pallas kernels for 16%

profile of v12, /device:TPU:0, one launch (start us, length us, event | category | flops | bytes accessed | tf_op | source)
XLA Modules:
  0.0 212.7 jit_solution(12238591477394311997)
XLA Ops:
  0.6 4.1 %collective-permute-start = (bf16[64,576]{1,0:T(8,128)(2,1)}, bf16[64,576]{1,0:T(8,128)(2,1)S(1)}, u32[]{:S(2)}, u32[]{:S(2)}) collective-permute-start(bf16[64,576]{1,0:T(8,128)(2,1)} %param.11), channel_id=1, source_target_pairs={{0,8},{1,9},{2,10},{3,11},{4,12},{5,13},{6,14},{7,15},{8,0},{9,1},... | collective-permute-start | bytes 221192 | tf_op jit(solution)/shard_map/ppermute | solution.py:336
  4.7 1.6 collective-permute-start.1
  6.3 0.0 collective-permute-start.2
  6.3 0.8 copy.12.routes_ref
  7.1 0.0 copy-start.1
  7.1 1.0 copy-done.1
  8.1 2.0 bucket_rows.1
  10.1 0.0 collective-permute-done
  10.1 0.0 collective-permute-done.1
  10.1 0.0 copy-start.5
  10.1 2.6 %collective-permute-done.2 = bf16[64,576]{1,0:T(8,128)(2,1)S(1)} collective-permute-done((bf16[64,576]{1,0:T(8,128)(2,1)}, bf16[64,576]{1,0:T(8,128)(2,1)S(1)}, u32[]{:S(2)}, u32[]{:S(2)}) %collective-permute-start.2) | collective-permute-done | bytes 73760 | tf_op jit(solution)/shard_map/ppermute | solution.py:336
  12.8 0.0 collective-permute-start.3
  12.8 0.5 collective-permute-start.4
  13.3 0.0 collective-permute-start.5
  13.3 0.0 copy-done.3
  13.3 0.0 copy-done.5
  13.3 0.1 copy-done.7
  13.4 4.9 %all-to-all-start = ((bf16[8,24,3584]{2,1,0:T(8,128)(2,1)}), bf16[8,24,3584]{2,1,0:T(8,128)(2,1)S(1)}, u32[]{:S(2)}, u32[]{:S(2)}) async-start(bf16[8,24,3584]{2,1,0:T(8,128)(2,1)} %bitcast.2), calls=%async_computation | async-start | bytes 2752512 | tf_op jit(solution)/shard_map/all_to_all | solution.py:341
  18.3 1.3 copy.13
  19.6 0.0 copy-done
  19.6 1.5 split_queries.1
  21.1 1.0 fusion.refs_0_
  22.1 29.5 %all-to-all-done = bf16[8,24,3584]{2,1,0:T(8,128)(2,1)S(1)} async-done(((bf16[8,24,3584]{2,1,0:T(8,128)(2,1)}), bf16[8,24,3584]{2,1,0:T(8,128)(2,1)S(1)}, u32[]{:S(2)}, u32[]{:S(2)}) %all-to-all-start) | async-done | bytes 1376288 | tf_op jit(solution)/shard_map/all_to_all | solution.py:341
  51.7 0.0 collective-permute-done.3.gate1
  51.7 0.0 collective-permute-done.4.up1
  51.7 0.0 collective-permute-done.5.down1
  51.7 0.0 copy-start.2
  51.7 0.0 copy-start.4
  51.7 0.0 copy-start.6
  51.7 0.0 copy-start.8
  51.7 4.4 %all-to-all-start.1 = ((bf16[8,64,1536]{2,1,0:T(8,128)(2,1)}), bf16[8,64,1536]{2,1,0:T(8,128)(2,1)}, u32[]{:S(2)}, u32[]{:S(2)}) async-start(bf16[8,64,1536]{2,1,0:T(8,128)(2,1)} %split_queries.1), calls=%async_computation.1 | async-start | bytes 3145728 | tf_op jit(solution)/shard_map/all_to_all | solution.py:166
  56.2 0.0 copy-done.2
  56.2 0.0 copy-done.4
  56.2 0.0 copy-done.6
  56.2 0.0 copy-done.8
  56.2 0.1 pad_maximum_fusion.1
  56.3 2.0 collective-permute-start.6
  58.3 27.5 %collective-permute-done.6 = bf16[4,64,576]{2,1,0:T(8,128)(2,1)S(1)} collective-permute-done((bf16[4,64,576]{2,1,0:T(8,128)(2,1)S(1)}, bf16[4,64,576]{2,1,0:T(8,128)(2,1)S(1)}, u32[]{:S(2)}, u32[]{:S(2)}) %collective-permute-start.6) | collective-permute-done | bytes 294944 | tf_op jit(solution)/shard_map/ppermute | solution.py:336
  85.8 0.1 pad_maximum_fusion
  85.9 0.1 collective-permute-start.7
  86.1 15.3 %collective-permute-done.7 = bf16[8,64,576]{2,1,0:T(8,128)(2,1)S(1)} collective-permute-done((bf16[8,64,576]{2,1,0:T(8,128)(2,1)S(1)}, bf16[8,64,576]{2,1,0:T(8,128)(2,1)S(1)}, u32[]{:S(2)}, u32[]{:S(2)}) %collective-permute-start.7) | collective-permute-done | bytes 589856 | tf_op jit(solution)/shard_map/ppermute | solution.py:336
  101.4 0.1 constant_dynamic-update-slice_fusion.kv_ref
  101.5 0.0 copy-start.9
  101.5 0.1 collective-permute-start.8
  101.6 13.6 %expert_rows.1 = bf16[192,3584]{1,0:T(8,128)(2,1)} custom-call(bf16[192,3584]{1,0:T(8,128)(2,1)S(1)} %bitcast.16, bf16[1,3584,512]{2,1,0:T(8,128)(2,1)} %gate0.1, bf16[1,3584,512]{2,1,0:T(8,128)(2,1)} %up0.1, bf16[1,3584,512]{2,1,0:T(8,128)(2,1)} %collective-permute-done.3.gate1, bf16[1,3584,512]{2,1,0:T(8,128)(2,1)} %collective-permute-done.4.up1, ...), custom_call_target="tpu_custom_call" | custom-call | flops 4227858432 | bytes 24772608 | tf_op jit(solution)/shard_map/expert_rows/pallas_call | solution.py:125
  115.1 0.0 copy-done.9
  115.1 0.0 collective-permute-done.8.other_kv_ref
  115.1 0.0 all-to-all-done.1
  115.2 3.7 %all-to-all-start.2 = ((bf16[8,24,3584]{2,1,0:T(8,128)(2,1)}), bf16[8,24,3584]{2,1,0:T(8,128)(2,1)S(1)}, u32[]{:S(2)}, u32[]{:S(2)}) async-start(bf16[8,24,3584]{2,1,0:T(8,128)(2,1)} %bitcast.12), calls=%async_computation.2 | async-start | bytes 2752512 | tf_op jit(solution)/shard_map/all_to_all | solution.py:341
  118.9 2.9 %collective-permute-start.9 = (bf16[1,4,512,128]{3,2,1,0:T(8,128)(2,1)S(1)}, bf16[1,4,512,128]{3,2,1,0:T(8,128)(2,1)S(1)}, u32[]{:S(2)}, u32[]{:S(2)}) collective-permute-start(bf16[1,4,512,128]{3,2,1,0:T(8,128)(2,1)S(1)} %fusion.refs_0_), channel_id=1, source_target_pairs={{0,8},{1,9},{2,10},{3,11},{4,12},{5,13},{6,14},{7,15},{8,0},{9,1},... | collective-permute-start | bytes 1572872 | tf_op jit(solution)/shard_map/ppermute | solution.py:336
  121.8 0.0 collective-permute-start.10
  121.8 52.7 %collective-permute-done.9.refs_1_ = bf16[1,4,512,128]{3,2,1,0:T(8,128)(2,1)S(1)} collective-permute-done((bf16[1,4,512,128]{3,2,1,0:T(8,128)(2,1)S(1)}, bf16[1,4,512,128]{3,2,1,0:T(8,128)(2,1)S(1)}, u32[]{:S(2)}, u32[]{:S(2)}) %collective-permute-start.9) | collective-permute-done | bytes 524320 | tf_op jit(solution)/shard_map/ppermute | solution.py:336
  174.5 0.0 collective-permute-start.11
  174.5 0.1 pad_add_fusion.rank_ref
  174.6 0.0 collective-permute-done.10.refs_2_
  174.6 1.8 collective-permute-done.11.refs_3_
  176.4 15.1 %causal_attention.1 = bf16[512,1024]{1,0:T(8,128)(2,1)} custom-call(s32[2]{0:T(128)S(1)} %pad_add_fusion.rank_ref, bf16[512,1536]{1,0:T(8,128)(2,1)} %bitcast.7.query_ref, bf16[16,64,576]{2,1,0:T(8,128)(2,1)} %copy-done.9, bf16[16,64,576]{2,1,0:T(8,128)(2,1)} %collective-permute-done.8.other_kv_ref, bf16[1,4,512,128]{3,2,1,0:T(8,128)(2,1)S(1)} %fusion.refs_0_, ...), custom_call_target="tpu_custom_call" | custom-call | flops 9126805504 | bytes 9699328 | tf_op jit(solution)/shard_map/causal_attention/pallas_call | solution.py:309
  191.5 0.0 all-to-all-done.2
  191.5 3.7 %all-to-all-start.3 = ((bf16[8,64,1024]{2,1,0:T(8,128)(2,1)}), bf16[8,64,1024]{2,1,0:T(8,128)(2,1)S(1)}, u32[]{:S(2)}, u32[]{:S(2)}) async-start(bf16[8,64,1024]{2,1,0:T(8,128)(2,1)} %bitcast.13), calls=%async_computation.3 | async-start | bytes 2097152 | tf_op jit(solution)/shard_map/all_to_all | solution.py:166
  195.2 0.0 copy-done.10
  195.3 0.1 copy.15.gates_ref
  195.4 1.6 combine_routes.1
  196.9 14.7 %all-to-all-done.3.x_ref = bf16[8,64,1024]{2,1,0:T(8,128)(2,1)S(1)} async-done(((bf16[8,64,1024]{2,1,0:T(8,128)(2,1)}), bf16[8,64,1024]{2,1,0:T(8,128)(2,1)S(1)}, u32[]{:S(2)}, u32[]{:S(2)}) %all-to-all-start.3) | async-done | bytes 1048608 | tf_op jit(solution)/shard_map/all_to_all | solution.py:166
  211.7 1.1 join_values.1
  (6 shorter events, 0.1 us)
Async XLA Ops:
  0.6 9.5 %collective-permute-start = (bf16[64,576]{1,0:T(8,128)(2,1)}, bf16[64,576]{1,0:T(8,128)(2,1)S(1)}, u32[]{:S(2)}, u32[]{:S(2)}) collective-permute-start(bf16[64,576]{1,0:T(8,128)(2,1)} %param.11), channel_id=1, source_target_pairs={{0,8},{1,9},{2,10},{3,11},{4,12},{5,13},{6,14},{7,15},{8,0},{9,1},... | collective-permute-start | bytes 221192 | tf_op jit(solution)/shard_map/ppermute | solution.py:336
  4.7 5.4 %collective-permute-start.1 = (bf16[64,576]{1,0:T(8,128)(2,1)}, bf16[64,576]{1,0:T(8,128)(2,1)S(1)}, u32[]{:S(2)}, u32[]{:S(2)}) collective-permute-start(bf16[64,576]{1,0:T(8,128)(2,1)} %param.11), channel_id=1, source_target_pairs={{0,4},{1,5},{2,6},{3,7},{4,0},{5,1},{6,2},{7,3},{8,12},{9,13},{10,... | collective-permute-start | bytes 221192 | tf_op jit(solution)/shard_map/ppermute | solution.py:336
  6.3 6.4 %collective-permute-start.2 = (bf16[64,576]{1,0:T(8,128)(2,1)}, bf16[64,576]{1,0:T(8,128)(2,1)S(1)}, u32[]{:S(2)}, u32[]{:S(2)}) collective-permute-start(bf16[64,576]{1,0:T(8,128)(2,1)} %param.11), channel_id=1, source_target_pairs={{0,12},{1,13},{2,14},{3,15},{4,8},{5,9},{6,10},{7,11},{8,4},{9,5},... | collective-permute-start | bytes 221192 | tf_op jit(solution)/shard_map/ppermute | solution.py:336
  7.1 1.0 copy-start.1
  10.1 3.2 %copy-start.3 = (bf16[64,576]{1,0:T(8,128)(2,1)}, bf16[64,576]{1,0:T(8,128)(2,1)S(1)}, u32[]{:S(2)}) copy-start(bf16[64,576]{1,0:T(8,128)(2,1)S(1)} %collective-permute-done) | copy-start | bytes 221188
  10.1 3.2 %copy-start.5 = (bf16[64,576]{1,0:T(8,128)(2,1)}, bf16[64,576]{1,0:T(8,128)(2,1)S(1)}, u32[]{:S(2)}) copy-start(bf16[64,576]{1,0:T(8,128)(2,1)S(1)} %collective-permute-done.1) | copy-start | bytes 221188
  12.8 0.6 copy-start.7
  12.8 38.9 %collective-permute-start.3 = (bf16[1,3584,512]{2,1,0:T(8,128)(2,1)}, bf16[1,3584,512]{2,1,0:T(8,128)(2,1)}, u32[]{:S(2)}, u32[]{:S(2)}) collective-permute-start(bf16[1,3584,512]{2,1,0:T(8,128)(2,1)} %gate0.1), channel_id=1, source_target_pairs={{0,1},{1,0},{2,3},{3,2},{4,5},{5,4},{6,7},{7,6},{8,9},{9,8},{10,11... | collective-permute-start | bytes 11010056 | tf_op jit(solution)/shard_map/ppermute | solution.py:336
  12.8 38.9 %collective-permute-start.4 = (bf16[1,3584,512]{2,1,0:T(8,128)(2,1)}, bf16[1,3584,512]{2,1,0:T(8,128)(2,1)}, u32[]{:S(2)}, u32[]{:S(2)}) collective-permute-start(bf16[1,3584,512]{2,1,0:T(8,128)(2,1)} %up0.1), channel_id=1, source_target_pairs={{0,1},{1,0},{2,3},{3,2},{4,5},{5,4},{6,7},{7,6},{8,9},{9,8},{10,11... | collective-permute-start | bytes 11010056 | tf_op jit(solution)/shard_map/ppermute | solution.py:336
  13.3 38.4 %collective-permute-start.5 = (bf16[1,512,3584]{2,1,0:T(8,128)(2,1)}, bf16[1,512,3584]{2,1,0:T(8,128)(2,1)}, u32[]{:S(2)}, u32[]{:S(2)}) collective-permute-start(bf16[1,512,3584]{2,1,0:T(8,128)(2,1)} %down0.1), channel_id=1, source_target_pairs={{0,1},{1,0},{2,3},{3,2},{4,5},{5,4},{6,7},{7,6},{8,9},{9,8},{10,11... | collective-permute-start | bytes 11010056 | tf_op jit(solution)/shard_map/ppermute | solution.py:336
  13.3 6.3 %copy-start = (bf16[64,12288]{1,0:T(8,128)(2,1)S(1)}, bf16[64,12288]{1,0:T(8,128)(2,1)}, u32[]{:S(2)}) copy-start(bf16[64,12288]{1,0:T(8,128)(2,1)} %x_ref.3) | copy-start | bytes 4718596
  13.4 38.3 %all-to-all-start = ((bf16[8,24,3584]{2,1,0:T(8,128)(2,1)}), bf16[8,24,3584]{2,1,0:T(8,128)(2,1)S(1)}, u32[]{:S(2)}, u32[]{:S(2)}) async-start(bf16[8,24,3584]{2,1,0:T(8,128)(2,1)} %bitcast.2), calls=%async_computation | async-start | bytes 2752512 | tf_op jit(solution)/shard_map/all_to_all | solution.py:341
  51.7 4.5 %copy-start.2 = (bf16[64,576]{1,0:T(8,128)(2,1)S(1)}, bf16[64,576]{1,0:T(8,128)(2,1)}, u32[]{:S(2)}) copy-start(bf16[64,576]{1,0:T(8,128)(2,1)} %param.11) | copy-start | bytes 221188
  51.7 4.5 %copy-start.4 = (bf16[64,576]{1,0:T(8,128)(2,1)S(1)}, bf16[64,576]{1,0:T(8,128)(2,1)}, u32[]{:S(2)}) copy-start(bf16[64,576]{1,0:T(8,128)(2,1)} %copy-done.3) | copy-start | bytes 221188
  51.7 4.5 %copy-start.6 = (bf16[64,576]{1,0:T(8,128)(2,1)S(1)}, bf16[64,576]{1,0:T(8,128)(2,1)}, u32[]{:S(2)}) copy-start(bf16[64,576]{1,0:T(8,128)(2,1)} %copy-done.5) | copy-start | bytes 221188
  51.7 4.5 %copy-start.8 = (bf16[64,576]{1,0:T(8,128)(2,1)S(1)}, bf16[64,576]{1,0:T(8,128)(2,1)}, u32[]{:S(2)}) copy-start(bf16[64,576]{1,0:T(8,128)(2,1)} %copy-done.7) | copy-start | bytes 221188
  51.7 63.4 %all-to-all-start.1 = ((bf16[8,64,1536]{2,1,0:T(8,128)(2,1)}), bf16[8,64,1536]{2,1,0:T(8,128)(2,1)}, u32[]{:S(2)}, u32[]{:S(2)}) async-start(bf16[8,64,1536]{2,1,0:T(8,128)(2,1)} %split_queries.1), calls=%async_computation.1 | async-start | bytes 3145728 | tf_op jit(solution)/shard_map/all_to_all | solution.py:166
  56.3 29.5 %collective-permute-start.6 = (bf16[4,64,576]{2,1,0:T(8,128)(2,1)S(1)}, bf16[4,64,576]{2,1,0:T(8,128)(2,1)S(1)}, u32[]{:S(2)}, u32[]{:S(2)}) collective-permute-start(bf16[4,64,576]{2,1,0:T(8,128)(2,1)S(1)} %pad_maximum_fusion.1), channel_id=1, source_target_pairs={{0,16},{1,17},{2,18},{3,19},{4,20},{5,21},{6,22},{7,23},{8,24},{9,... | collective-permute-start | bytes 884744 | tf_op jit(solution)/shard_map/ppermute | solution.py:336
  85.9 15.5 %collective-permute-start.7 = (bf16[8,64,576]{2,1,0:T(8,128)(2,1)S(1)}, bf16[8,64,576]{2,1,0:T(8,128)(2,1)S(1)}, u32[]{:S(2)}, u32[]{:S(2)}) collective-permute-start(bf16[8,64,576]{2,1,0:T(8,128)(2,1)S(1)} %pad_maximum_fusion), channel_id=1, source_target_pairs={{0,2},{1,3},{2,0},{3,1},{4,6},{5,7},{6,4},{7,5},{8,10},{9,11},{10,... | collective-permute-start | bytes 1769480 | tf_op jit(solution)/shard_map/ppermute | solution.py:336
  101.5 13.7 %copy-start.9 = (bf16[16,64,576]{2,1,0:T(8,128)(2,1)}, bf16[16,64,576]{2,1,0:T(8,128)(2,1)S(1)}, u32[]{:S(2)}) copy-start(bf16[16,64,576]{2,1,0:T(8,128)(2,1)S(1)} %constant_dynamic-update-slice_fusion.kv_ref) | copy-start | bytes 3538948
  101.5 13.7 %collective-permute-start.8 = (bf16[16,64,576]{2,1,0:T(8,128)(2,1)S(1)}, bf16[16,64,576]{2,1,0:T(8,128)(2,1)}, u32[]{:S(2)}, u32[]{:S(2)}) collective-permute-start(bf16[16,64,576]{2,1,0:T(8,128)(2,1)S(1)} %constant_dynamic-update-slice_fusion.kv_ref), channel_id=1, source_target_pairs={{0,1},{1,0},{2,3},{3,2},{4,5},{5,4},{6,7},{7,6},{8,9},{9,8},{10,11... | collective-permute-start | bytes 3538952 | tf_op jit(solution)/shard_map/ppermute | solution.py:336
  115.2 76.4 %all-to-all-start.2 = ((bf16[8,24,3584]{2,1,0:T(8,128)(2,1)}), bf16[8,24,3584]{2,1,0:T(8,128)(2,1)S(1)}, u32[]{:S(2)}, u32[]{:S(2)}) async-start(bf16[8,24,3584]{2,1,0:T(8,128)(2,1)} %bitcast.12), calls=%async_computation.2 | async-start | bytes 2752512 | tf_op jit(solution)/shard_map/all_to_all | solution.py:341
  118.9 55.6 %collective-permute-start.9 = (bf16[1,4,512,128]{3,2,1,0:T(8,128)(2,1)S(1)}, bf16[1,4,512,128]{3,2,1,0:T(8,128)(2,1)S(1)}, u32[]{:S(2)}, u32[]{:S(2)}) collective-permute-start(bf16[1,4,512,128]{3,2,1,0:T(8,128)(2,1)S(1)} %fusion.refs_0_), channel_id=1, source_target_pairs={{0,8},{1,9},{2,10},{3,11},{4,12},{5,13},{6,14},{7,15},{8,0},{9,1},... | collective-permute-start | bytes 1572872 | tf_op jit(solution)/shard_map/ppermute | solution.py:336
  121.8 52.8 %collective-permute-start.10 = (bf16[1,4,512,128]{3,2,1,0:T(8,128)(2,1)S(1)}, bf16[1,4,512,128]{3,2,1,0:T(8,128)(2,1)S(1)}, u32[]{:S(2)}, u32[]{:S(2)}) collective-permute-start(bf16[1,4,512,128]{3,2,1,0:T(8,128)(2,1)S(1)} %fusion.refs_0_), channel_id=1, source_target_pairs={{0,1},{1,0},{2,3},{3,2},{4,5},{5,4},{6,7},{7,6},{8,9},{9,8},{10,11... | collective-permute-start | bytes 1572872 | tf_op jit(solution)/shard_map/ppermute | solution.py:336
  174.5 1.9 collective-permute-start.11
  191.5 3.7 %copy-start.10 = (f32[64,2]{0,1:T(2,128)S(1)}, f32[64,2]{0,1:T(2,128)}, u32[]{:S(2)}) copy-start(f32[64,2]{0,1:T(2,128)} %param.16) | copy-start | bytes 1540
  191.5 20.1 %all-to-all-start.3 = ((bf16[8,64,1024]{2,1,0:T(8,128)(2,1)}), bf16[8,64,1024]{2,1,0:T(8,128)(2,1)S(1)}, u32[]{:S(2)}, u32[]{:S(2)}) async-start(bf16[8,64,1024]{2,1,0:T(8,128)(2,1)} %bitcast.13), calls=%async_computation.3 | async-start | bytes 2097152 | tf_op jit(solution)/shard_map/all_to_all | solution.py:166

commit v13 on v12

--- a/solution.py
+++ b/solution.py
@@ -398,7 +398,6 @@
     keys = after(jnp.stack(keys), sent)
     for mask in later:
         keys = jnp.concatenate([keys, send(keys, mask)], axis=0)
-    other_keys = send(keys, 1)
 
     near = jnp.concatenate(
         [
@@ -413,12 +412,17 @@
 
     own_half = [expert_gate, expert_up, expert_down]
     other_half = [send(after(part, buckets), 1) for part in own_half]
-    held = split.exchange(after(sent, near, arrived, *other_half)).reshape(experts * tok, -1)
-    pieces = [near, send(after(near, arrived), shards // 2)] if split.wide else [near]
+    held = split.exchange(after(sent, keys, near, arrived, *other_half)).reshape(experts * tok, -1)
 
     result = expert_rows(arrived, own_half, other_half)
-    weights = pieces + [send(after(piece, result), 1) for piece in pieces]
-    result, held, keys, other_keys = lax.optimization_barrier((result, held, keys, other_keys))
+    other_keys = send(after(keys, result), 1)
+    other_near = send(after(near, result), 1)
+    weights = [near, other_near]
+    if split.wide:
+        far = after(send(after(near, arrived), shards // 2), other_near)
+        result = after(result, far)
+        weights = [near, far, other_near, send(far, 1)]
+    result, held, other_keys = lax.optimization_barrier((result, held, other_keys))
     back = swap_chips(result.reshape(experts, rows, D))
     values = attention(split, place, held, keys, other_keys, weights)
     values, back = lax.optimization_barrier((values, back))

time: 216 us -> 159 us (0.74); the launches traced: 213 us -> 159 us
  waiting for transfers between devices: 144 us -> 82.1 us
  starting transfers between devices: 28 us -> 33.7 us
  local copies, waits for them, and re-layouts: 3.51 us -> 5.68 us
    ppermute x12, waiting for transfers between devices: 100 us -> 53.1 us  [send(): lax.ppermute(array, ('groups', 'ctx'), [(i, i ^ mask) for i in range(coun...]
    all_to_all x2, waiting for transfers between devices: 29.5 us -> 16 us  [swap_chips(): lax.all_to_all(array, 'ctx', split_axis=0, concat_axis=0, axis_index_grou...]
    all_to_all x2, starting transfers between devices: 8.64 us -> 11.8 us  [swap_chips(): lax.all_to_all(array, 'ctx', split_axis=0, concat_axis=0, axis_index_grou...]
  transfers between devices with their start and end apart: 16 -> 16, of which waited for: 7 -> 7; matrix products, arithmetic and copies ran while one was open for 2% -> 4% of each run, Pallas kernels for 16% -> 21%
where the time goes in v13:
time: 159 us
  waiting for transfers between devices  82.1 us (52%)
  Pallas kernels  34.6 us (22%)
  starting transfers between devices  33.7 us (21%)
  local copies, waits for them, and re-layouts  5.68 us (4%)
  other arithmetic  2.08 us (1%)
    ppermute x12, waiting for transfers between devices, send(): lax.ppermute(array, ('groups', 'ctx'), [(i, i ^ mask) for i in range(coun...  53.1 us
    all_to_all x2, waiting for transfers between devices, swap_chips(): lax.all_to_all(array, 'ctx', split_axis=0, concat_axis=0, axis_index_grou...  16 us
    pallas_call x1, Pallas kernels, attention(): call(functools.partial(attention_kernel, split), 'causal_attention', flop...  15.1 us
    pallas_call x1, Pallas kernels, expert_rows(): call(expert_kernel, 'expert_rows', flops=12 * count * D * HALF, moved=12...  13.3 us
    all_to_all x2, waiting for transfers between devices, exchange(): lax.all_to_all(array, ('groups', 'ctx'), split_axis=0, concat_axis=0, axi...  13.1 us
    ppermute x12, starting transfers between devices, send(): lax.ppermute(array, ('groups', 'ctx'), [(i, i ^ mask) for i in range(coun...  12.7 us
    all_to_all x2, starting transfers between devices, swap_chips(): lax.all_to_all(array, 'ctx', split_axis=0, concat_axis=0, axis_index_grou...  11.8 us
    all_to_all x2, starting transfers between devices, exchange(): lax.all_to_all(array, ('groups', 'ctx'), split_axis=0, concat_axis=0, axi...  9.2 us
  transfers between devices with their start and end apart: 16, of which 7 were waited for; matrix products, arithmetic and copies ran while one was open for 4% of the time, Pallas kernels for 21%

profile of v13, /device:TPU:0, one launch (start us, length us, event | category | flops | bytes accessed | tf_op | source)
XLA Modules:
  0.0 158.9 jit_solution(10327031563097801894)
XLA Ops:
  0.6 5.1 %collective-permute-start.2 = (bf16[64,576]{1,0:T(8,128)(2,1)}, bf16[64,576]{1,0:T(8,128)(2,1)S(1)}, u32[]{:S(2)}, u32[]{:S(2)}) collective-permute-start(bf16[64,576]{1,0:T(8,128)(2,1)} %param.11), channel_id=1, source_target_pairs={{0,12},{1,13},{2,14},{3,15},{4,8},{5,9},{6,10},{7,11},{8,4},{9,5},... | collective-permute-start | bytes 221192 | tf_op jit(solution)/shard_map/ppermute | solution.py:336
  5.7 0.0 collective-permute-start.1
  5.7 0.6 collective-permute-start
  6.4 0.8 copy.12.routes_ref
  7.2 0.0 copy-start.1
  7.2 1.0 copy-done.1
  8.2 2.0 %bucket_rows.1 = bf16[192,3584]{1,0:T(8,128)(2,1)} custom-call(s32[64,2]{1,0:T(8,128)S(1)} %copy.12.routes_ref, bf16[64,3584]{1,0:T(8,128)(2,1)S(1)} %copy-done.1), custom_call_target="tpu_custom_call" | custom-call | bytes 1835008 | tf_op jit(solution)/shard_map/bucket_rows/pallas_call | solution.py:66
  10.2 0.0 collective-permute-done.2
  10.2 2.0 %collective-permute-done.1 = bf16[64,576]{1,0:T(8,128)(2,1)S(1)} collective-permute-done((bf16[64,576]{1,0:T(8,128)(2,1)}, bf16[64,576]{1,0:T(8,128)(2,1)S(1)}, u32[]{:S(2)}, u32[]{:S(2)}) %collective-permute-start.1) | collective-permute-done | bytes 73760 | tf_op jit(solution)/shard_map/ppermute | solution.py:336
  12.2 0.0 collective-permute-done
  12.2 0.0 collective-permute-start.3
  12.2 0.5 collective-permute-start.4
  12.7 0.0 collective-permute-start.5
  12.7 0.0 copy-start
  12.7 5.7 %all-to-all-start = ((bf16[8,24,3584]{2,1,0:T(8,128)(2,1)}), bf16[8,24,3584]{2,1,0:T(8,128)(2,1)S(1)}, u32[]{:S(2)}, u32[]{:S(2)}) async-start(bf16[8,24,3584]{2,1,0:T(8,128)(2,1)} %bitcast.2), calls=%async_computation | async-start | bytes 2752512 | tf_op jit(solution)/shard_map/all_to_all | solution.py:341
  18.4 0.0 copy-done
  18.4 0.0 copy-start.3
  18.4 1.6 split_queries.1
  20.0 0.0 copy-start.2
  20.0 0.0 copy-done.3
  20.0 0.1 pad_maximum_fusion.1
  20.1 1.6 collective-permute-start.8
  21.6 8.3 %collective-permute-done.8 = bf16[4,64,576]{2,1,0:T(8,128)(2,1)S(1)} collective-permute-done((bf16[4,64,576]{2,1,0:T(8,128)(2,1)S(1)}, bf16[4,64,576]{2,1,0:T(8,128)(2,1)S(1)}, u32[]{:S(2)}, u32[]{:S(2)}) %collective-permute-start.8) | collective-permute-done | bytes 294944 | tf_op jit(solution)/shard_map/ppermute | solution.py:336
  30.0 0.9 pad_maximum_fusion
  30.9 1.7 %collective-permute-start.9 = (bf16[8,64,576]{2,1,0:T(8,128)(2,1)}, bf16[8,64,576]{2,1,0:T(8,128)(2,1)}, u32[]{:S(2)}, u32[]{:S(2)}) collective-permute-start(bf16[8,64,576]{2,1,0:T(8,128)(2,1)} %pad_maximum_fusion), channel_id=1, source_target_pairs={{0,2},{1,3},{2,0},{3,1},{4,6},{5,7},{6,4},{7,5},{8,10},{9,11},{10,... | collective-permute-start | bytes 1769480 | tf_op jit(solution)/shard_map/ppermute | solution.py:336
  32.6 0.0 copy-done.2
  32.6 0.3 copy.13
  32.9 1.0 fusion.refs_0_
  33.9 0.8 constant_dynamic-update-slice_fusion.2
  34.7 0.8 constant_dynamic-update-slice_fusion.1
  35.4 17.3 %collective-permute-done.9 = bf16[8,64,576]{2,1,0:T(8,128)(2,1)} collective-permute-done((bf16[8,64,576]{2,1,0:T(8,128)(2,1)}, bf16[8,64,576]{2,1,0:T(8,128)(2,1)}, u32[]{:S(2)}, u32[]{:S(2)}) %collective-permute-start.9) | collective-permute-done | bytes 589856 | tf_op jit(solution)/shard_map/ppermute | solution.py:336
  52.7 2.0 %constant_dynamic-update-slice_fusion.kv_ref = bf16[16,64,576]{2,1,0:T(8,128)(2,1)} fusion(bf16[16,64,576]{2,1,0:T(8,128)(2,1)} %constant_dynamic-update-slice_fusion.1, bf16[8,64,576]{2,1,0:T(8,128)(2,1)} %collective-permute-done.9), kind=kLoop, calls=%fused_computation.5 | loop fusion | bytes 1310720 | tf_op jit(solution)/shard_map/concatenate | solution.py:400
  54.7 0.0 all-to-all-done
  54.7 0.0 collective-permute-done.3.gate1
  54.7 0.0 collective-permute-done.4.up1
  54.7 0.0 collective-permute-done.5.down1
  54.7 5.6 %all-to-all-start.1 = ((bf16[8,64,1536]{2,1,0:T(8,128)(2,1)}), bf16[8,64,1536]{2,1,0:T(8,128)(2,1)}, u32[]{:S(2)}, u32[]{:S(2)}) async-start(bf16[8,64,1536]{2,1,0:T(8,128)(2,1)} %split_queries.1), calls=%async_computation.1 | async-start | bytes 3145728 | tf_op jit(solution)/shard_map/all_to_all | solution.py:166
  60.3 13.3 %expert_rows.1 = bf16[192,3584]{1,0:T(8,128)(2,1)} custom-call(bf16[192,3584]{1,0:T(8,128)(2,1)S(1)} %bitcast.16, bf16[1,3584,512]{2,1,0:T(8,128)(2,1)} %gate0.1, bf16[1,3584,512]{2,1,0:T(8,128)(2,1)} %up0.1, bf16[1,3584,512]{2,1,0:T(8,128)(2,1)} %collective-permute-done.3.gate1, bf16[1,3584,512]{2,1,0:T(8,128)(2,1)} %collective-permute-done.4.up1, ...), custom_call_target="tpu_custom_call" | custom-call | flops 4227858432 | bytes 24772608 | tf_op jit(solution)/shard_map/expert_rows/pallas_call | solution.py:125
  73.5 0.0 collective-permute-start.10
  73.5 3.0 %collective-permute-start.6 = (bf16[1,4,512,128]{3,2,1,0:T(8,128)(2,1)S(1)}, bf16[1,4,512,128]{3,2,1,0:T(8,128)(2,1)S(1)}, u32[]{:S(2)}, u32[]{:S(2)}) collective-permute-start(bf16[1,4,512,128]{3,2,1,0:T(8,128)(2,1)S(1)} %fusion.refs_0_), channel_id=1, source_target_pairs={{0,8},{1,9},{2,10},{3,11},{4,12},{5,13},{6,14},{7,15},{8,0},{9,1},... | collective-permute-start | bytes 1572872 | tf_op jit(solution)/shard_map/ppermute | solution.py:336
  76.5 0.2 collective-permute-start.7
  76.7 23.6 %collective-permute-done.6.refs_1_ = bf16[1,4,512,128]{3,2,1,0:T(8,128)(2,1)S(1)} collective-permute-done((bf16[1,4,512,128]{3,2,1,0:T(8,128)(2,1)S(1)}, bf16[1,4,512,128]{3,2,1,0:T(8,128)(2,1)S(1)}, u32[]{:S(2)}, u32[]{:S(2)}) %collective-permute-start.6) | collective-permute-done | bytes 524320 | tf_op jit(solution)/shard_map/ppermute | solution.py:336
  100.3 0.0 collective-permute-done.7.refs_2_
  100.3 0.0 collective-permute-done.10.other_kv_ref
  100.3 0.0 all-to-all-done.1
  100.3 6.1 %all-to-all-start.2 = ((bf16[8,24,3584]{2,1,0:T(8,128)(2,1)}), bf16[8,24,3584]{2,1,0:T(8,128)(2,1)S(1)}, u32[]{:S(2)}, u32[]{:S(2)}) async-start(bf16[8,24,3584]{2,1,0:T(8,128)(2,1)} %bitcast.12), calls=%async_computation.2 | async-start | bytes 2752512 | tf_op jit(solution)/shard_map/all_to_all | solution.py:341
  106.4 0.0 collective-permute-start.11
  106.4 0.1 pad_add_fusion.rank_ref
  106.5 1.8 %collective-permute-done.11.refs_3_ = bf16[1,4,512,128]{3,2,1,0:T(8,128)(2,1)S(1)} collective-permute-done((bf16[1,4,512,128]{3,2,1,0:T(8,128)(2,1)S(1)}, bf16[1,4,512,128]{3,2,1,0:T(8,128)(2,1)S(1)}, u32[]{:S(2)}, u32[]{:S(2)}) %collective-permute-start.11) | collective-permute-done | bytes 524320 | tf_op jit(solution)/shard_map/ppermute | solution.py:336
  108.3 15.1 %causal_attention.1 = bf16[512,1024]{1,0:T(8,128)(2,1)} custom-call(s32[2]{0:T(128)S(1)} %pad_add_fusion.rank_ref, bf16[512,1536]{1,0:T(8,128)(2,1)} %bitcast.11.query_ref, bf16[16,64,576]{2,1,0:T(8,128)(2,1)} %constant_dynamic-update-slice_fusion.kv_ref, bf16[16,64,576]{2,1,0:T(8,128)(2,1)} %collective-permute-done.10.other_kv_ref, ...), custom_call_target="tpu_custom_call" | custom-call | flops 9126805504 | bytes 9699328 | tf_op jit(solution)/shard_map/causal_attention/pallas_call | solution.py:309
  123.5 0.0 copy-start.4
  123.5 16.0 %all-to-all-done.2 = bf16[8,24,3584]{2,1,0:T(8,128)(2,1)S(1)} async-done(((bf16[8,24,3584]{2,1,0:T(8,128)(2,1)}), bf16[8,24,3584]{2,1,0:T(8,128)(2,1)S(1)}, u32[]{:S(2)}, u32[]{:S(2)}) %all-to-all-start.2) | async-done | bytes 1376288 | tf_op jit(solution)/shard_map/all_to_all | solution.py:341
  139.5 3.6 %all-to-all-start.3 = ((bf16[8,64,1024]{2,1,0:T(8,128)(2,1)}), bf16[8,64,1024]{2,1,0:T(8,128)(2,1)S(1)}, u32[]{:S(2)}, u32[]{:S(2)}) async-start(bf16[8,64,1024]{2,1,0:T(8,128)(2,1)} %bitcast.13), calls=%async_computation.3 | async-start | bytes 2097152 | tf_op jit(solution)/shard_map/all_to_all | solution.py:166
  143.1 0.0 copy-done.4
  143.1 0.1 copy.15.gates_ref
  143.2 1.6 combine_routes.1
  144.7 13.0 %all-to-all-done.3.x_ref = bf16[8,64,1024]{2,1,0:T(8,128)(2,1)S(1)} async-done(((bf16[8,64,1024]{2,1,0:T(8,128)(2,1)}), bf16[8,64,1024]{2,1,0:T(8,128)(2,1)S(1)}, u32[]{:S(2)}, u32[]{:S(2)}) %all-to-all-start.3) | async-done | bytes 1048608 | tf_op jit(solution)/shard_map/all_to_all | solution.py:166
  157.8 1.1 join_values.1
Async XLA Ops:
  0.6 9.6 %collective-permute-start.2 = (bf16[64,576]{1,0:T(8,128)(2,1)}, bf16[64,576]{1,0:T(8,128)(2,1)S(1)}, u32[]{:S(2)}, u32[]{:S(2)}) collective-permute-start(bf16[64,576]{1,0:T(8,128)(2,1)} %param.11), channel_id=1, source_target_pairs={{0,12},{1,13},{2,14},{3,15},{4,8},{5,9},{6,10},{7,11},{8,4},{9,5},... | collective-permute-start | bytes 221192 | tf_op jit(solution)/shard_map/ppermute | solution.py:336
  5.7 6.4 %collective-permute-start.1 = (bf16[64,576]{1,0:T(8,128)(2,1)}, bf16[64,576]{1,0:T(8,128)(2,1)S(1)}, u32[]{:S(2)}, u32[]{:S(2)}) collective-permute-start(bf16[64,576]{1,0:T(8,128)(2,1)} %param.11), channel_id=1, source_target_pairs={{0,4},{1,5},{2,6},{3,7},{4,0},{5,1},{6,2},{7,3},{8,12},{9,13},{10,... | collective-permute-start | bytes 221192 | tf_op jit(solution)/shard_map/ppermute | solution.py:336
  5.7 6.4 %collective-permute-start = (bf16[64,576]{1,0:T(8,128)(2,1)}, bf16[64,576]{1,0:T(8,128)(2,1)S(1)}, u32[]{:S(2)}, u32[]{:S(2)}) collective-permute-start(bf16[64,576]{1,0:T(8,128)(2,1)} %param.11), channel_id=1, source_target_pairs={{0,8},{1,9},{2,10},{3,11},{4,12},{5,13},{6,14},{7,15},{8,0},{9,1},... | collective-permute-start | bytes 221192 | tf_op jit(solution)/shard_map/ppermute | solution.py:336
  7.2 1.0 copy-start.1
  12.2 42.5 %collective-permute-start.3 = (bf16[1,3584,512]{2,1,0:T(8,128)(2,1)}, bf16[1,3584,512]{2,1,0:T(8,128)(2,1)}, u32[]{:S(2)}, u32[]{:S(2)}) collective-permute-start(bf16[1,3584,512]{2,1,0:T(8,128)(2,1)} %gate0.1), channel_id=1, source_target_pairs={{0,1},{1,0},{2,3},{3,2},{4,5},{5,4},{6,7},{7,6},{8,9},{9,8},{10,11... | collective-permute-start | bytes 11010056 | tf_op jit(solution)/shard_map/ppermute | solution.py:336
  12.2 42.5 %collective-permute-start.4 = (bf16[1,3584,512]{2,1,0:T(8,128)(2,1)}, bf16[1,3584,512]{2,1,0:T(8,128)(2,1)}, u32[]{:S(2)}, u32[]{:S(2)}) collective-permute-start(bf16[1,3584,512]{2,1,0:T(8,128)(2,1)} %up0.1), channel_id=1, source_target_pairs={{0,1},{1,0},{2,3},{3,2},{4,5},{5,4},{6,7},{7,6},{8,9},{9,8},{10,11... | collective-permute-start | bytes 11010056 | tf_op jit(solution)/shard_map/ppermute | solution.py:336
  12.7 42.0 %collective-permute-start.5 = (bf16[1,512,3584]{2,1,0:T(8,128)(2,1)}, bf16[1,512,3584]{2,1,0:T(8,128)(2,1)}, u32[]{:S(2)}, u32[]{:S(2)}) collective-permute-start(bf16[1,512,3584]{2,1,0:T(8,128)(2,1)} %down0.1), channel_id=1, source_target_pairs={{0,1},{1,0},{2,3},{3,2},{4,5},{5,4},{6,7},{7,6},{8,9},{9,8},{10,11... | collective-permute-start | bytes 11010056 | tf_op jit(solution)/shard_map/ppermute | solution.py:336
  12.7 5.7 %copy-start = (bf16[64,12288]{1,0:T(8,128)(2,1)S(1)}, bf16[64,12288]{1,0:T(8,128)(2,1)}, u32[]{:S(2)}) copy-start(bf16[64,12288]{1,0:T(8,128)(2,1)} %x_ref.3) | copy-start | bytes 4718596
  12.7 42.0 %all-to-all-start = ((bf16[8,24,3584]{2,1,0:T(8,128)(2,1)}), bf16[8,24,3584]{2,1,0:T(8,128)(2,1)S(1)}, u32[]{:S(2)}, u32[]{:S(2)}) async-start(bf16[8,24,3584]{2,1,0:T(8,128)(2,1)} %bitcast.2), calls=%async_computation | async-start | bytes 2752512 | tf_op jit(solution)/shard_map/all_to_all | solution.py:341
  18.4 1.6 copy-start.3
  20.0 12.6 %copy-start.2 = (bf16[4,128,512]{2,1,0:T(8,128)(2,1)S(1)}, bf16[4,128,512]{2,1,0:T(8,128)(2,1)}, u32[]{:S(2)}) copy-start(bf16[4,128,512]{2,1,0:T(8,128)(2,1)} %param.12) | copy-start | bytes 1572868
  20.1 9.9 %collective-permute-start.8 = (bf16[4,64,576]{2,1,0:T(8,128)(2,1)S(1)}, bf16[4,64,576]{2,1,0:T(8,128)(2,1)S(1)}, u32[]{:S(2)}, u32[]{:S(2)}) collective-permute-start(bf16[4,64,576]{2,1,0:T(8,128)(2,1)S(1)} %pad_maximum_fusion.1), channel_id=1, source_target_pairs={{0,16},{1,17},{2,18},{3,19},{4,20},{5,21},{6,22},{7,23},{8,24},{9,... | collective-permute-start | bytes 884744 | tf_op jit(solution)/shard_map/ppermute | solution.py:336
  30.9 21.8 %collective-permute-start.9 = (bf16[8,64,576]{2,1,0:T(8,128)(2,1)}, bf16[8,64,576]{2,1,0:T(8,128)(2,1)}, u32[]{:S(2)}, u32[]{:S(2)}) collective-permute-start(bf16[8,64,576]{2,1,0:T(8,128)(2,1)} %pad_maximum_fusion), channel_id=1, source_target_pairs={{0,2},{1,3},{2,0},{3,1},{4,6},{5,7},{6,4},{7,5},{8,10},{9,11},{10,... | collective-permute-start | bytes 1769480 | tf_op jit(solution)/shard_map/ppermute | solution.py:336
  54.7 45.6 %all-to-all-start.1 = ((bf16[8,64,1536]{2,1,0:T(8,128)(2,1)}), bf16[8,64,1536]{2,1,0:T(8,128)(2,1)}, u32[]{:S(2)}, u32[]{:S(2)}) async-start(bf16[8,64,1536]{2,1,0:T(8,128)(2,1)} %split_queries.1), calls=%async_computation.1 | async-start | bytes 3145728 | tf_op jit(solution)/shard_map/all_to_all | solution.py:166
  73.5 26.8 %collective-permute-start.10 = (bf16[16,64,576]{2,1,0:T(8,128)(2,1)}, bf16[16,64,576]{2,1,0:T(8,128)(2,1)}, u32[]{:S(2)}, u32[]{:S(2)}) collective-permute-start(bf16[16,64,576]{2,1,0:T(8,128)(2,1)} %constant_dynamic-update-slice_fusion.kv_ref), channel_id=1, source_target_pairs={{0,1},{1,0},{2,3},{3,2},{4,5},{5,4},{6,7},{7,6},{8,9},{9,8},{10,11... | collective-permute-start | bytes 3538952 | tf_op jit(solution)/shard_map/ppermute | solution.py:336
  73.5 26.8 %collective-permute-start.6 = (bf16[1,4,512,128]{3,2,1,0:T(8,128)(2,1)S(1)}, bf16[1,4,512,128]{3,2,1,0:T(8,128)(2,1)S(1)}, u32[]{:S(2)}, u32[]{:S(2)}) collective-permute-start(bf16[1,4,512,128]{3,2,1,0:T(8,128)(2,1)S(1)} %fusion.refs_0_), channel_id=1, source_target_pairs={{0,8},{1,9},{2,10},{3,11},{4,12},{5,13},{6,14},{7,15},{8,0},{9,1},... | collective-permute-start | bytes 1572872 | tf_op jit(solution)/shard_map/ppermute | solution.py:336
  76.5 23.8 %collective-permute-start.7 = (bf16[1,4,512,128]{3,2,1,0:T(8,128)(2,1)S(1)}, bf16[1,4,512,128]{3,2,1,0:T(8,128)(2,1)S(1)}, u32[]{:S(2)}, u32[]{:S(2)}) collective-permute-start(bf16[1,4,512,128]{3,2,1,0:T(8,128)(2,1)S(1)} %fusion.refs_0_), channel_id=1, source_target_pairs={{0,1},{1,0},{2,3},{3,2},{4,5},{5,4},{6,7},{7,6},{8,9},{9,8},{10,11... | collective-permute-start | bytes 1572872 | tf_op jit(solution)/shard_map/ppermute | solution.py:336
  100.3 39.1 %all-to-all-start.2 = ((bf16[8,24,3584]{2,1,0:T(8,128)(2,1)}), bf16[8,24,3584]{2,1,0:T(8,128)(2,1)S(1)}, u32[]{:S(2)}, u32[]{:S(2)}) async-start(bf16[8,24,3584]{2,1,0:T(8,128)(2,1)} %bitcast.12), calls=%async_computation.2 | async-start | bytes 2752512 | tf_op jit(solution)/shard_map/all_to_all | solution.py:341
  106.4 1.9 %collective-permute-start.11 = (bf16[1,4,512,128]{3,2,1,0:T(8,128)(2,1)S(1)}, bf16[1,4,512,128]{3,2,1,0:T(8,128)(2,1)S(1)}, u32[]{:S(2)}, u32[]{:S(2)}) collective-permute-start(bf16[1,4,512,128]{3,2,1,0:T(8,128)(2,1)S(1)} %collective-permute-done.6.refs_1_), channel_id=1, source_target_pairs={{0,1},{1,0},{2,3},{3,2},{4,5},{5,4},{6,7},{7,6},{8,9},{9,8},{10,11... | collective-permute-start | bytes 1572872 | tf_op jit(solution)/shard_map/ppermute | solution.py:336
  123.5 19.6 %copy-start.4 = (f32[64,2]{0,1:T(2,128)S(1)}, f32[64,2]{0,1:T(2,128)}, u32[]{:S(2)}) copy-start(f32[64,2]{0,1:T(2,128)} %param.16) | copy-start | bytes 1540
  139.5 18.3 %all-to-all-start.3 = ((bf16[8,64,1024]{2,1,0:T(8,128)(2,1)}), bf16[8,64,1024]{2,1,0:T(8,128)(2,1)S(1)}, u32[]{:S(2)}, u32[]{:S(2)}) async-start(bf16[8,64,1024]{2,1,0:T(8,128)(2,1)} %bitcast.13), calls=%async_computation.3 | async-start | bytes 2097152 | tf_op jit(solution)/shard_map/all_to_all | solution.py:166

commit v14 on v8

--- a/solution.py
+++ b/solution.py
@@ -383,17 +383,19 @@
     place = jnp.concatenate([rank, group])
 
     direct, later = gather_masks(split)
-    keys = jnp.stack([latent_kv] + [send(latent_kv, offset) for offset in direct])
-
-    buckets = after(build_buckets(routes, moe_input, experts, rows), keys)
+    keys = [latent_kv] + [send(latent_kv, offset) for offset in direct]
+
+    buckets = after(build_buckets(routes, moe_input, experts, rows), *keys)
     arrived = swap_chips(buckets.reshape(experts, rows, D)).reshape(experts * rows, D)
 
+    sent = split_queries(split, rank, queries)
+    keys = after(jnp.stack(keys), sent)
     for mask in later:
         keys = jnp.concatenate([keys, send(keys, mask)], axis=0)
     other_keys = send(keys, 1)
     own_half = [expert_gate, expert_up, expert_down]
-    other_half = [send(part, 1) for part in own_half]
-    sent = after(split_queries(split, rank, queries), other_keys, arrived, *other_half)
+    other_half = [send(after(part, buckets), 1) for part in own_half]
+    sent = after(sent, other_keys, arrived, *other_half)
     held = split.exchange(sent).reshape(experts * tok, -1)
 
     weights = jnp.concatenate(

time: 153 us -> 149 us (0.974)
  local copies, waits for them, and re-layouts: 9.41 us -> 3.42 us
  starting transfers between devices: 30.1 us -> 32 us
    unnamed x19, local copies, waits for them, and re-layouts: 6.28 us -> 2.99 us
    all_to_all x2, starting transfers between devices: 7.14 us -> 9.99 us  [swap_chips(): lax.all_to_all(array, 'ctx', split_axis=0, concat_axis=0, axis_index_grou...]
    concatenate x2 -> x1, local copies, waits for them, and re-layouts: 2.78 us -> 0.09 us  [on_device(): keys = jnp.concatenate([keys, send(keys, mask)], axis=0)]
    ppermute x11, waiting for transfers between devices: 33.9 us -> 36.5 us  [send(): lax.ppermute(array, ('groups', 'ctx'), [(i, i ^ mask) for i in range(coun...]
    all_to_all x2, waiting for transfers between devices: 29.1 us -> 27.3 us  [exchange(): lax.all_to_all(array, ('groups', 'ctx'), split_axis=0, concat_axis=0, axi...]
  transfers between devices with their start and end apart: 15 -> 15, of which waited for: 8 -> 8; matrix products, arithmetic and copies ran while one was open for 5% -> 1% of each run, Pallas kernels for 22% -> 22%
where the time goes in v14:
time: 149 us
  waiting for transfers between devices  78 us (52%)
  Pallas kernels  34.4 us (23%)
  starting transfers between devices  32 us (21%)
  local copies, waits for them, and re-layouts  3.42 us (2%)
    ppermute x11, waiting for transfers between devices, send(): lax.ppermute(array, ('groups', 'ctx'), [(i, i ^ mask) for i in range(coun...  36.5 us
    all_to_all x2, waiting for transfers between devices, exchange(): lax.all_to_all(array, ('groups', 'ctx'), split_axis=0, concat_axis=0, axi...  27.3 us
    pallas_call x1, Pallas kernels, attention(): call(functools.partial(attention_kernel, split), 'causal_attention', flop...  15 us
    all_to_all x2, waiting for transfers between devices, swap_chips(): lax.all_to_all(array, 'ctx', split_axis=0, concat_axis=0, axis_index_grou...  14.3 us
    ppermute x11, starting transfers between devices, send(): lax.ppermute(array, ('groups', 'ctx'), [(i, i ^ mask) for i in range(coun...  13.8 us
    pallas_call x1, Pallas kernels, expert_rows(): call(expert_kernel, 'expert_rows', flops=12 * count * D * HALF, moved=12...  13.2 us
    all_to_all x2, starting transfers between devices, swap_chips(): lax.all_to_all(array, 'ctx', split_axis=0, concat_axis=0, axis_index_grou...  9.99 us
    all_to_all x2, starting transfers between devices, exchange(): lax.all_to_all(array, ('groups', 'ctx'), split_axis=0, concat_axis=0, axi...  8.16 us
  transfers between devices with their start and end apart: 15, of which 8 were waited for; matrix products, arithmetic and copies ran while one was open for 1% of the time, Pallas kernels for 22%

profile of v14, /device:TPU:0, one launch (start us, length us, event | category | flops | bytes accessed | tf_op | source)
XLA Modules:
  0.0 148.9 jit_solution(6290493196812148348)
XLA Ops:
  0.6 0.0 copy-start
  0.6 4.1 %collective-permute-start = (bf16[64,576]{1,0:T(8,128)(2,1)}, bf16[64,576]{1,0:T(8,128)(2,1)S(1)}, u32[]{:S(2)}, u32[]{:S(2)}) collective-permute-start(bf16[64,576]{1,0:T(8,128)(2,1)} %param.11), channel_id=1, source_target_pairs={{0,8},{1,9},{2,10},{3,11},{4,12},{5,13},{6,14},{7,15},{8,0},{9,1},... | collective-permute-start | bytes 221192 | tf_op jit(solution)/shard_map/ppermute | solution.py:330
  4.7 1.6 %collective-permute-start.1 = (bf16[64,576]{1,0:T(8,128)(2,1)}, bf16[64,576]{1,0:T(8,128)(2,1)S(1)}, u32[]{:S(2)}, u32[]{:S(2)}) collective-permute-start(bf16[64,576]{1,0:T(8,128)(2,1)} %param.11), channel_id=1, source_target_pairs={{0,4},{1,5},{2,6},{3,7},{4,0},{5,1},{6,2},{7,3},{8,12},{9,13},{10,... | collective-permute-start | bytes 221192 | tf_op jit(solution)/shard_map/ppermute | solution.py:330
  6.3 0.0 collective-permute-start.2
  6.3 0.8 copy.12.routes_ref
  7.1 0.0 copy-start.1
  7.1 1.0 copy-done.1
  8.1 2.0 %bucket_rows.1 = bf16[192,3584]{1,0:T(8,128)(2,1)} custom-call(s32[64,2]{1,0:T(8,128)S(1)} %copy.12.routes_ref, bf16[64,3584]{1,0:T(8,128)(2,1)S(1)} %copy-done.1), custom_call_target="tpu_custom_call" | custom-call | bytes 1835008 | tf_op jit(solution)/shard_map/bucket_rows/pallas_call | solution.py:66
  10.1 0.0 collective-permute-done
  10.1 0.0 collective-permute-done.1
  10.1 2.6 %collective-permute-done.2 = bf16[64,576]{1,0:T(8,128)(2,1)S(1)} collective-permute-done((bf16[64,576]{1,0:T(8,128)(2,1)}, bf16[64,576]{1,0:T(8,128)(2,1)S(1)}, u32[]{:S(2)}, u32[]{:S(2)}) %collective-permute-start.2) | collective-permute-done | bytes 73760 | tf_op jit(solution)/shard_map/ppermute | solution.py:330
  12.8 0.0 collective-permute-start.3
  12.8 0.5 collective-permute-start.4
  13.3 0.0 collective-permute-start.5
  13.3 0.0 copy-done
  13.3 1.5 %split_queries.1 = bf16[8,64,1536]{2,1,0:T(8,128)(2,1)} custom-call(s32[1]{0:T(128)} %bitcast.rank_ref, bf16[64,12288]{1,0:T(8,128)(2,1)S(1)} %copy-done), custom_call_target="tpu_custom_call" | custom-call | bytes 3145728 | tf_op jit(solution)/shard_map/split_queries/pallas_call | solution.py:184
  14.8 0.0 copy-start.4
  14.8 4.9 %all-to-all-start = ((bf16[8,24,3584]{2,1,0:T(8,128)(2,1)}), bf16[8,24,3584]{2,1,0:T(8,128)(2,1)S(1)}, u32[]{:S(2)}, u32[]{:S(2)}) async-start(bf16[8,24,3584]{2,1,0:T(8,128)(2,1)} %bitcast.2), calls=%async_computation | async-start | bytes 2752512 | tf_op jit(solution)/shard_map/all_to_all | solution.py:335
  19.7 0.0 copy-done.4
  19.7 0.1 pad_maximum_fusion.1
  19.8 1.6 %collective-permute-start.6 = (bf16[4,64,576]{2,1,0:T(8,128)(2,1)S(1)}, bf16[4,64,576]{2,1,0:T(8,128)(2,1)S(1)}, u32[]{:S(2)}, u32[]{:S(2)}) collective-permute-start(bf16[4,64,576]{2,1,0:T(8,128)(2,1)S(1)} %pad_maximum_fusion.1), channel_id=1, source_target_pairs={{0,16},{1,17},{2,18},{3,19},{4,20},{5,21},{6,22},{7,23},{8,24},{9,... | collective-permute-start | bytes 884744 | tf_op jit(solution)/shard_map/ppermute | solution.py:330
  21.4 8.3 %collective-permute-done.6 = bf16[4,64,576]{2,1,0:T(8,128)(2,1)S(1)} collective-permute-done((bf16[4,64,576]{2,1,0:T(8,128)(2,1)S(1)}, bf16[4,64,576]{2,1,0:T(8,128)(2,1)S(1)}, u32[]{:S(2)}, u32[]{:S(2)}) %collective-permute-start.6) | collective-permute-done | bytes 294944 | tf_op jit(solution)/shard_map/ppermute | solution.py:330
  29.7 0.1 pad_maximum_fusion
  29.8 1.8 %collective-permute-start.7 = (bf16[8,64,576]{2,1,0:T(8,128)(2,1)S(1)}, bf16[8,64,576]{2,1,0:T(8,128)(2,1)S(1)}, u32[]{:S(2)}, u32[]{:S(2)}) collective-permute-start(bf16[8,64,576]{2,1,0:T(8,128)(2,1)S(1)} %pad_maximum_fusion), channel_id=1, source_target_pairs={{0,2},{1,3},{2,0},{3,1},{4,6},{5,7},{6,4},{7,5},{8,10},{9,11},{10,... | collective-permute-start | bytes 1769480 | tf_op jit(solution)/shard_map/ppermute | solution.py:330
  31.7 20.8 %collective-permute-done.7 = bf16[8,64,576]{2,1,0:T(8,128)(2,1)S(1)} collective-permute-done((bf16[8,64,576]{2,1,0:T(8,128)(2,1)S(1)}, bf16[8,64,576]{2,1,0:T(8,128)(2,1)S(1)}, u32[]{:S(2)}, u32[]{:S(2)}) %collective-permute-start.7) | collective-permute-done | bytes 589856 | tf_op jit(solution)/shard_map/ppermute | solution.py:330
  52.4 0.1 constant_dynamic-update-slice_fusion.kv_ref
  52.5 0.0 copy-start.5
  52.5 0.1 collective-permute-start.8
  52.6 1.0 copy-done.5
  53.6 2.2 %collective-permute-done.8.other_kv_ref = bf16[16,64,576]{2,1,0:T(8,128)(2,1)} collective-permute-done((bf16[16,64,576]{2,1,0:T(8,128)(2,1)S(1)}, bf16[16,64,576]{2,1,0:T(8,128)(2,1)}, u32[]{:S(2)}, u32[]{:S(2)}) %collective-permute-start.8) | collective-permute-done | bytes 1179680 | tf_op jit(solution)/shard_map/ppermute | solution.py:330
  55.8 0.0 all-to-all-done
  55.8 0.0 collective-permute-done.3.gate1
  55.8 0.0 collective-permute-done.4.up1
  55.8 0.0 collective-permute-done.5.down1
  55.8 0.0 copy-start.2
  55.8 0.0 copy-start.3
  55.8 4.6 %all-to-all-start.1 = ((bf16[8,64,1536]{2,1,0:T(8,128)(2,1)}), bf16[8,64,1536]{2,1,0:T(8,128)(2,1)}, u32[]{:S(2)}, u32[]{:S(2)}) async-start(bf16[8,64,1536]{2,1,0:T(8,128)(2,1)} %split_queries.1), calls=%async_computation.1 | async-start | bytes 3145728 | tf_op jit(solution)/shard_map/all_to_all | solution.py:166
  60.4 0.0 copy-done.2
  60.4 0.3 copy.13
  60.7 0.0 copy-done.3
  60.7 0.1 fusion
  60.8 4.1 %collective-permute-start.9 = (bf16[1,4,512,128]{3,2,1,0:T(8,128)(2,1)S(1)}, bf16[1,4,512,128]{3,2,1,0:T(8,128)(2,1)S(1)}, u32[]{:S(2)}, u32[]{:S(2)}) collective-permute-start(bf16[1,4,512,128]{3,2,1,0:T(8,128)(2,1)S(1)} %fusion), channel_id=1, source_target_pairs={{0,8},{1,9},{2,10},{3,11},{4,12},{5,13},{6,14},{7,15},{8,0},{9,1},... | collective-permute-start | bytes 1572872 | tf_op jit(solution)/shard_map/ppermute | solution.py:330
  64.9 13.2 %expert_rows.1 = bf16[192,3584]{1,0:T(8,128)(2,1)} custom-call(bf16[192,3584]{1,0:T(8,128)(2,1)S(1)} %bitcast.16, bf16[1,3584,512]{2,1,0:T(8,128)(2,1)} %gate0.1, bf16[1,3584,512]{2,1,0:T(8,128)(2,1)} %up0.1, bf16[1,3584,512]{2,1,0:T(8,128)(2,1)} %collective-permute-done.3.gate1, bf16[1,3584,512]{2,1,0:T(8,128)(2,1)} %collective-permute-done.4.up1, ...), custom_call_target="tpu_custom_call" | custom-call | flops 4227858432 | bytes 24772608 | tf_op jit(solution)/shard_map/expert_rows/pallas_call | solution.py:125
  78.1 15.3 %all-to-all-done.1 = bf16[8,64,1536]{2,1,0:T(8,128)(2,1)} async-done(((bf16[8,64,1536]{2,1,0:T(8,128)(2,1)}), bf16[8,64,1536]{2,1,0:T(8,128)(2,1)}, u32[]{:S(2)}, u32[]{:S(2)}) %all-to-all-start.1) | async-done | bytes 1572896 | tf_op jit(solution)/shard_map/all_to_all | solution.py:166
  93.4 5.1 %all-to-all-start.2 = ((bf16[8,24,3584]{2,1,0:T(8,128)(2,1)}), bf16[8,24,3584]{2,1,0:T(8,128)(2,1)S(1)}, u32[]{:S(2)}, u32[]{:S(2)}) async-start(bf16[8,24,3584]{2,1,0:T(8,128)(2,1)} %bitcast.12), calls=%async_computation.2 | async-start | bytes 2752512 | tf_op jit(solution)/shard_map/all_to_all | solution.py:335
  98.5 0.0 collective-permute-done.9
  98.5 0.1 constant_dynamic-update-slice_fusion.3.weight_ref
  98.6 0.1 collective-permute-start.10
  98.7 0.1 pad_add_fusion.rank_ref
  98.8 2.6 %collective-permute-done.10.other_weight_ref = bf16[2,4,512,128]{3,2,1,0:T(8,128)(2,1)S(1)} collective-permute-done((bf16[2,4,512,128]{3,2,1,0:T(8,128)(2,1)S(1)}, bf16[2,4,512,128]{3,2,1,0:T(8,128)(2,1)S(1)}, u32[]{:S(2)}, u32[]{:S(2)}) %collective-permute-start.10) | collective-permute-done | bytes 1048608 | tf_op jit(solution)/shard_map/ppermute | solution.py:330
  101.3 15.0 %causal_attention.1 = bf16[512,1024]{1,0:T(8,128)(2,1)} custom-call(s32[2]{0:T(128)S(1)} %pad_add_fusion.rank_ref, bf16[512,1536]{1,0:T(8,128)(2,1)} %bitcast.8.query_ref, bf16[16,64,576]{2,1,0:T(8,128)(2,1)} %copy-done.5, bf16[16,64,576]{2,1,0:T(8,128)(2,1)} %collective-permute-done.8.other_kv_ref, ...), custom_call_target="tpu_custom_call" | custom-call | flops 9126805504 | bytes 7602176 | tf_op jit(solution)/shard_map/causal_attention/pallas_call | solution.py:302
  116.3 0.0 copy-start.6
  116.3 14.3 %all-to-all-done.2 = bf16[8,24,3584]{2,1,0:T(8,128)(2,1)S(1)} async-done(((bf16[8,24,3584]{2,1,0:T(8,128)(2,1)}), bf16[8,24,3584]{2,1,0:T(8,128)(2,1)S(1)}, u32[]{:S(2)}, u32[]{:S(2)}) %all-to-all-start.2) | async-done | bytes 1376288 | tf_op jit(solution)/shard_map/all_to_all | solution.py:335
  130.6 3.6 %all-to-all-start.3 = ((bf16[8,64,1024]{2,1,0:T(8,128)(2,1)}), bf16[8,64,1024]{2,1,0:T(8,128)(2,1)S(1)}, u32[]{:S(2)}, u32[]{:S(2)}) async-start(bf16[8,64,1024]{2,1,0:T(8,128)(2,1)} %bitcast.13), calls=%async_computation.3 | async-start | bytes 2097152 | tf_op jit(solution)/shard_map/all_to_all | solution.py:166
  134.1 0.0 copy-done.6
  134.2 0.1 copy.15.gates_ref
  134.3 1.5 %combine_routes.1 = bf16[64,3584]{1,0:T(8,128)(2,1)} custom-call(s32[64,2]{1,0:T(8,128)S(1)} %copy.12.routes_ref, f32[64,2]{1,0:T(8,128)S(1)} %copy.15.gates_ref, bf16[192,3584]{1,0:T(8,128)(2,1)S(1)} %bitcast.15), custom_call_target="tpu_custom_call" | custom-call | bytes 1835008 | tf_op jit(solution)/shard_map/combine_routes/pallas_call | solution.py:86
  135.8 12.0 %all-to-all-done.3.x_ref = bf16[8,64,1024]{2,1,0:T(8,128)(2,1)S(1)} async-done(((bf16[8,64,1024]{2,1,0:T(8,128)(2,1)}), bf16[8,64,1024]{2,1,0:T(8,128)(2,1)S(1)}, u32[]{:S(2)}, u32[]{:S(2)}) %all-to-all-start.3) | async-done | bytes 1048608 | tf_op jit(solution)/shard_map/all_to_all | solution.py:166
  147.8 1.1 join_values.1
  (3 shorter events, 0.1 us)
Async XLA Ops:
  0.6 12.7 %copy-start = (bf16[64,12288]{1,0:T(8,128)(2,1)S(1)}, bf16[64,12288]{1,0:T(8,128)(2,1)}, u32[]{:S(2)}) copy-start(bf16[64,12288]{1,0:T(8,128)(2,1)} %x_ref.3) | copy-start | bytes 4718596
  0.6 9.5 %collective-permute-start = (bf16[64,576]{1,0:T(8,128)(2,1)}, bf16[64,576]{1,0:T(8,128)(2,1)S(1)}, u32[]{:S(2)}, u32[]{:S(2)}) collective-permute-start(bf16[64,576]{1,0:T(8,128)(2,1)} %param.11), channel_id=1, source_target_pairs={{0,8},{1,9},{2,10},{3,11},{4,12},{5,13},{6,14},{7,15},{8,0},{9,1},... | collective-permute-start | bytes 221192 | tf_op jit(solution)/shard_map/ppermute | solution.py:330
  4.7 5.4 %collective-permute-start.1 = (bf16[64,576]{1,0:T(8,128)(2,1)}, bf16[64,576]{1,0:T(8,128)(2,1)S(1)}, u32[]{:S(2)}, u32[]{:S(2)}) collective-permute-start(bf16[64,576]{1,0:T(8,128)(2,1)} %param.11), channel_id=1, source_target_pairs={{0,4},{1,5},{2,6},{3,7},{4,0},{5,1},{6,2},{7,3},{8,12},{9,13},{10,... | collective-permute-start | bytes 221192 | tf_op jit(solution)/shard_map/ppermute | solution.py:330
  6.3 6.4 %collective-permute-start.2 = (bf16[64,576]{1,0:T(8,128)(2,1)}, bf16[64,576]{1,0:T(8,128)(2,1)S(1)}, u32[]{:S(2)}, u32[]{:S(2)}) collective-permute-start(bf16[64,576]{1,0:T(8,128)(2,1)} %param.11), channel_id=1, source_target_pairs={{0,12},{1,13},{2,14},{3,15},{4,8},{5,9},{6,10},{7,11},{8,4},{9,5},... | collective-permute-start | bytes 221192 | tf_op jit(solution)/shard_map/ppermute | solution.py:330
  7.1 1.0 copy-start.1
  12.8 43.0 %collective-permute-start.3 = (bf16[1,3584,512]{2,1,0:T(8,128)(2,1)}, bf16[1,3584,512]{2,1,0:T(8,128)(2,1)}, u32[]{:S(2)}, u32[]{:S(2)}) collective-permute-start(bf16[1,3584,512]{2,1,0:T(8,128)(2,1)} %gate0.1), channel_id=1, source_target_pairs={{0,1},{1,0},{2,3},{3,2},{4,5},{5,4},{6,7},{7,6},{8,9},{9,8},{10,11... | collective-permute-start | bytes 11010056 | tf_op jit(solution)/shard_map/ppermute | solution.py:330
  12.8 43.0 %collective-permute-start.4 = (bf16[1,3584,512]{2,1,0:T(8,128)(2,1)}, bf16[1,3584,512]{2,1,0:T(8,128)(2,1)}, u32[]{:S(2)}, u32[]{:S(2)}) collective-permute-start(bf16[1,3584,512]{2,1,0:T(8,128)(2,1)} %up0.1), channel_id=1, source_target_pairs={{0,1},{1,0},{2,3},{3,2},{4,5},{5,4},{6,7},{7,6},{8,9},{9,8},{10,11... | collective-permute-start | bytes 11010056 | tf_op jit(solution)/shard_map/ppermute | solution.py:330
  13.3 42.5 %collective-permute-start.5 = (bf16[1,512,3584]{2,1,0:T(8,128)(2,1)}, bf16[1,512,3584]{2,1,0:T(8,128)(2,1)}, u32[]{:S(2)}, u32[]{:S(2)}) collective-permute-start(bf16[1,512,3584]{2,1,0:T(8,128)(2,1)} %down0.1), channel_id=1, source_target_pairs={{0,1},{1,0},{2,3},{3,2},{4,5},{5,4},{6,7},{7,6},{8,9},{9,8},{10,11... | collective-permute-start | bytes 11010056 | tf_op jit(solution)/shard_map/ppermute | solution.py:330
  14.8 4.9 %copy-start.4 = (bf16[64,576]{1,0:T(8,128)(2,1)S(1)}, bf16[64,576]{1,0:T(8,128)(2,1)}, u32[]{:S(2)}) copy-start(bf16[64,576]{1,0:T(8,128)(2,1)} %param.11) | copy-start | bytes 221188
  14.8 40.9 %all-to-all-start = ((bf16[8,24,3584]{2,1,0:T(8,128)(2,1)}), bf16[8,24,3584]{2,1,0:T(8,128)(2,1)S(1)}, u32[]{:S(2)}, u32[]{:S(2)}) async-start(bf16[8,24,3584]{2,1,0:T(8,128)(2,1)} %bitcast.2), calls=%async_computation | async-start | bytes 2752512 | tf_op jit(solution)/shard_map/all_to_all | solution.py:335
  19.8 9.9 %collective-permute-start.6 = (bf16[4,64,576]{2,1,0:T(8,128)(2,1)S(1)}, bf16[4,64,576]{2,1,0:T(8,128)(2,1)S(1)}, u32[]{:S(2)}, u32[]{:S(2)}) collective-permute-start(bf16[4,64,576]{2,1,0:T(8,128)(2,1)S(1)} %pad_maximum_fusion.1), channel_id=1, source_target_pairs={{0,16},{1,17},{2,18},{3,19},{4,20},{5,21},{6,22},{7,23},{8,24},{9,... | collective-permute-start | bytes 884744 | tf_op jit(solution)/shard_map/ppermute | solution.py:330
  29.8 22.6 %collective-permute-start.7 = (bf16[8,64,576]{2,1,0:T(8,128)(2,1)S(1)}, bf16[8,64,576]{2,1,0:T(8,128)(2,1)S(1)}, u32[]{:S(2)}, u32[]{:S(2)}) collective-permute-start(bf16[8,64,576]{2,1,0:T(8,128)(2,1)S(1)} %pad_maximum_fusion), channel_id=1, source_target_pairs={{0,2},{1,3},{2,0},{3,1},{4,6},{5,7},{6,4},{7,5},{8,10},{9,11},{10,... | collective-permute-start | bytes 1769480 | tf_op jit(solution)/shard_map/ppermute | solution.py:330
  52.5 1.1 copy-start.5
  52.5 3.2 %collective-permute-start.8 = (bf16[16,64,576]{2,1,0:T(8,128)(2,1)S(1)}, bf16[16,64,576]{2,1,0:T(8,128)(2,1)}, u32[]{:S(2)}, u32[]{:S(2)}) collective-permute-start(bf16[16,64,576]{2,1,0:T(8,128)(2,1)S(1)} %constant_dynamic-update-slice_fusion.kv_ref), channel_id=1, source_target_pairs={{0,1},{1,0},{2,3},{3,2},{4,5},{5,4},{6,7},{7,6},{8,9},{9,8},{10,11... | collective-permute-start | bytes 3538952 | tf_op jit(solution)/shard_map/ppermute | solution.py:330
  55.8 4.6 %copy-start.2 = (bf16[4,128,512]{2,1,0:T(8,128)(2,1)S(1)}, bf16[4,128,512]{2,1,0:T(8,128)(2,1)}, u32[]{:S(2)}) copy-start(bf16[4,128,512]{2,1,0:T(8,128)(2,1)} %param.12) | copy-start | bytes 1572868
  55.8 4.9 %copy-start.3 = (bf16[4,512,128]{2,1,0:T(8,128)(2,1)S(1)}, bf16[4,512,128]{2,1,0:T(8,128)(2,1)}, u32[]{:S(2)}) copy-start(bf16[4,512,128]{2,1,0:T(8,128)(2,1)} %param.13) | copy-start | bytes 1572868
  55.8 37.6 %all-to-all-start.1 = ((bf16[8,64,1536]{2,1,0:T(8,128)(2,1)}), bf16[8,64,1536]{2,1,0:T(8,128)(2,1)}, u32[]{:S(2)}, u32[]{:S(2)}) async-start(bf16[8,64,1536]{2,1,0:T(8,128)(2,1)} %split_queries.1), calls=%async_computation.1 | async-start | bytes 3145728 | tf_op jit(solution)/shard_map/all_to_all | solution.py:166
  60.8 37.7 %collective-permute-start.9 = (bf16[1,4,512,128]{3,2,1,0:T(8,128)(2,1)S(1)}, bf16[1,4,512,128]{3,2,1,0:T(8,128)(2,1)S(1)}, u32[]{:S(2)}, u32[]{:S(2)}) collective-permute-start(bf16[1,4,512,128]{3,2,1,0:T(8,128)(2,1)S(1)} %fusion), channel_id=1, source_target_pairs={{0,8},{1,9},{2,10},{3,11},{4,12},{5,13},{6,14},{7,15},{8,0},{9,1},... | collective-permute-start | bytes 1572872 | tf_op jit(solution)/shard_map/ppermute | solution.py:330
  93.4 37.2 %all-to-all-start.2 = ((bf16[8,24,3584]{2,1,0:T(8,128)(2,1)}), bf16[8,24,3584]{2,1,0:T(8,128)(2,1)S(1)}, u32[]{:S(2)}, u32[]{:S(2)}) async-start(bf16[8,24,3584]{2,1,0:T(8,128)(2,1)} %bitcast.12), calls=%async_computation.2 | async-start | bytes 2752512 | tf_op jit(solution)/shard_map/all_to_all | solution.py:335
  98.6 2.7 %collective-permute-start.10 = (bf16[2,4,512,128]{3,2,1,0:T(8,128)(2,1)S(1)}, bf16[2,4,512,128]{3,2,1,0:T(8,128)(2,1)S(1)}, u32[]{:S(2)}, u32[]{:S(2)}) collective-permute-start(bf16[2,4,512,128]{3,2,1,0:T(8,128)(2,1)S(1)} %constant_dynamic-update-slice_fusion.3.weight_ref), channel_id=1, source_target_pairs={{0,1},{1,0},{2,3},{3,2},{4,5},{5,4},{6,7},{7,6},{8,9},{9,8},{10,11... | collective-permute-start | bytes 3145736 | tf_op jit(solution)/shard_map/ppermute | solution.py:330
  116.3 17.8 %copy-start.6 = (f32[64,2]{0,1:T(2,128)S(1)}, f32[64,2]{0,1:T(2,128)}, u32[]{:S(2)}) copy-start(f32[64,2]{0,1:T(2,128)} %param.16) | copy-start | bytes 1540
  130.6 17.2 %all-to-all-start.3 = ((bf16[8,64,1024]{2,1,0:T(8,128)(2,1)}), bf16[8,64,1024]{2,1,0:T(8,128)(2,1)S(1)}, u32[]{:S(2)}, u32[]{:S(2)}) async-start(bf16[8,64,1024]{2,1,0:T(8,128)(2,1)} %bitcast.13), calls=%async_computation.3 | async-start | bytes 2097152 | tf_op jit(solution)/shard_map/all_to_all | solution.py:166

commit v15 on v14

--- a/solution.py
+++ b/solution.py
@@ -395,7 +395,7 @@
     other_keys = send(keys, 1)
     own_half = [expert_gate, expert_up, expert_down]
     other_half = [send(after(part, buckets), 1) for part in own_half]
-    sent = after(sent, other_keys, arrived, *other_half)
+    sent = after(sent, keys, arrived, *other_half)
     held = split.exchange(sent).reshape(experts * tok, -1)
 
     weights = jnp.concatenate(

time: 149 us -> 145 us (0.973)
  waiting for transfers between devices: 78 us -> 71.4 us
    ppermute x11, waiting for transfers between devices: 36.5 us -> 33.2 us  [send(): lax.ppermute(array, ('groups', 'ctx'), [(i, i ^ mask) for i in range(coun...]
    all_to_all x2, waiting for transfers between devices: 14.3 us -> 11.8 us  [swap_chips(): lax.all_to_all(array, 'ctx', split_axis=0, concat_axis=0, axis_index_grou...]
  transfers between devices with their start and end apart: 15 -> 15, of which waited for: 8 -> 8; matrix products, arithmetic and copies ran while one was open for 1% -> 3% of each run, Pallas kernels for 22% -> 23%
where the time goes in v15:
time: 145 us; the launch traced here: 144 us
  waiting for transfers between devices  71.4 us (49%)
  Pallas kernels  34.4 us (24%)
  starting transfers between devices  32.7 us (23%)
  local copies, waits for them, and re-layouts  4.69 us (3%)
    ppermute x11, waiting for transfers between devices, send(): lax.ppermute(array, ('groups', 'ctx'), [(i, i ^ mask) for i in range(coun...  33.2 us
    all_to_all x2, waiting for transfers between devices, exchange(): lax.all_to_all(array, ('groups', 'ctx'), split_axis=0, concat_axis=0, axi...  26.4 us
    pallas_call x1, Pallas kernels, attention(): call(functools.partial(attention_kernel, split), 'causal_attention', flop...  15 us
    pallas_call x1, Pallas kernels, expert_rows(): call(expert_kernel, 'expert_rows', flops=12 * count * D * HALF, moved=12...  13.2 us
    ppermute x11, starting transfers between devices, send(): lax.ppermute(array, ('groups', 'ctx'), [(i, i ^ mask) for i in range(coun...  13.2 us
    all_to_all x2, waiting for transfers between devices, swap_chips(): lax.all_to_all(array, 'ctx', split_axis=0, concat_axis=0, axis_index_grou...  11.8 us
    all_to_all x2, starting transfers between devices, swap_chips(): lax.all_to_all(array, 'ctx', split_axis=0, concat_axis=0, axis_index_grou...  10.5 us
    all_to_all x2, starting transfers between devices, exchange(): lax.all_to_all(array, ('groups', 'ctx'), split_axis=0, concat_axis=0, axi...  9.08 us
  transfers between devices with their start and end apart: 15, of which 8 were waited for; matrix products, arithmetic and copies ran while one was open for 3% of the time, Pallas kernels for 23%

profile of v15, /device:TPU:0, one launch (start us, length us, event | category | flops | bytes accessed | tf_op | source)
XLA Modules:
  0.0 144.3 jit_solution(7065312321026877098)
XLA Ops:
  0.6 4.1 %collective-permute-start = (bf16[64,576]{1,0:T(8,128)(2,1)}, bf16[64,576]{1,0:T(8,128)(2,1)S(1)}, u32[]{:S(2)}, u32[]{:S(2)}) collective-permute-start(bf16[64,576]{1,0:T(8,128)(2,1)} %param.11), channel_id=1, source_target_pairs={{0,8},{1,9},{2,10},{3,11},{4,12},{5,13},{6,14},{7,15},{8,0},{9,1},... | collective-permute-start | bytes 221192 | tf_op jit(solution)/shard_map/ppermute | solution.py:330
  4.7 1.6 %collective-permute-start.1 = (bf16[64,576]{1,0:T(8,128)(2,1)}, bf16[64,576]{1,0:T(8,128)(2,1)S(1)}, u32[]{:S(2)}, u32[]{:S(2)}) collective-permute-start(bf16[64,576]{1,0:T(8,128)(2,1)} %param.11), channel_id=1, source_target_pairs={{0,4},{1,5},{2,6},{3,7},{4,0},{5,1},{6,2},{7,3},{8,12},{9,13},{10,... | collective-permute-start | bytes 221192 | tf_op jit(solution)/shard_map/ppermute | solution.py:330
  6.3 0.0 collective-permute-start.2
  6.3 0.8 copy.12.routes_ref
  7.1 0.0 copy-start.1
  7.1 1.0 copy-done.1
  8.1 2.0 %bucket_rows.1 = bf16[192,3584]{1,0:T(8,128)(2,1)} custom-call(s32[64,2]{1,0:T(8,128)S(1)} %copy.12.routes_ref, bf16[64,3584]{1,0:T(8,128)(2,1)S(1)} %copy-done.1), custom_call_target="tpu_custom_call" | custom-call | bytes 1835008 | tf_op jit(solution)/shard_map/bucket_rows/pallas_call | solution.py:66
  10.1 0.0 collective-permute-done
  10.1 0.0 collective-permute-done.1
  10.1 2.6 %collective-permute-done.2 = bf16[64,576]{1,0:T(8,128)(2,1)S(1)} collective-permute-done((bf16[64,576]{1,0:T(8,128)(2,1)}, bf16[64,576]{1,0:T(8,128)(2,1)S(1)}, u32[]{:S(2)}, u32[]{:S(2)}) %collective-permute-start.2) | collective-permute-done | bytes 73760 | tf_op jit(solution)/shard_map/ppermute | solution.py:330
  12.8 0.0 collective-permute-start.3
  12.8 0.5 collective-permute-start.4
  13.3 0.0 collective-permute-start.5
  13.3 0.0 copy-start
  13.3 4.9 %all-to-all-start = ((bf16[8,24,3584]{2,1,0:T(8,128)(2,1)}), bf16[8,24,3584]{2,1,0:T(8,128)(2,1)S(1)}, u32[]{:S(2)}, u32[]{:S(2)}) async-start(bf16[8,24,3584]{2,1,0:T(8,128)(2,1)} %bitcast.2), calls=%async_computation | async-start | bytes 2752512 | tf_op jit(solution)/shard_map/all_to_all | solution.py:335
  18.2 0.0 copy-done
  18.2 0.0 copy-start.4
  18.2 1.6 %split_queries.1 = bf16[8,64,1536]{2,1,0:T(8,128)(2,1)} custom-call(s32[1]{0:T(128)} %bitcast.rank_ref, bf16[64,12288]{1,0:T(8,128)(2,1)S(1)} %copy-done), custom_call_target="tpu_custom_call" | custom-call | bytes 3145728 | tf_op jit(solution)/shard_map/split_queries/pallas_call | solution.py:184
  19.7 0.0 copy-done.4
  19.7 0.1 pad_maximum_fusion.1
  19.8 1.6 %collective-permute-start.6 = (bf16[4,64,576]{2,1,0:T(8,128)(2,1)S(1)}, bf16[4,64,576]{2,1,0:T(8,128)(2,1)S(1)}, u32[]{:S(2)}, u32[]{:S(2)}) collective-permute-start(bf16[4,64,576]{2,1,0:T(8,128)(2,1)S(1)} %pad_maximum_fusion.1), channel_id=1, source_target_pairs={{0,16},{1,17},{2,18},{3,19},{4,20},{5,21},{6,22},{7,23},{8,24},{9,... | collective-permute-start | bytes 884744 | tf_op jit(solution)/shard_map/ppermute | solution.py:330
  21.4 8.3 %collective-permute-done.6 = bf16[4,64,576]{2,1,0:T(8,128)(2,1)S(1)} collective-permute-done((bf16[4,64,576]{2,1,0:T(8,128)(2,1)S(1)}, bf16[4,64,576]{2,1,0:T(8,128)(2,1)S(1)}, u32[]{:S(2)}, u32[]{:S(2)}) %collective-permute-start.6) | collective-permute-done | bytes 294944 | tf_op jit(solution)/shard_map/ppermute | solution.py:330
  29.7 0.1 pad_maximum_fusion
  29.8 1.8 %collective-permute-start.7 = (bf16[8,64,576]{2,1,0:T(8,128)(2,1)S(1)}, bf16[8,64,576]{2,1,0:T(8,128)(2,1)S(1)}, u32[]{:S(2)}, u32[]{:S(2)}) collective-permute-start(bf16[8,64,576]{2,1,0:T(8,128)(2,1)S(1)} %pad_maximum_fusion), channel_id=1, source_target_pairs={{0,2},{1,3},{2,0},{3,1},{4,6},{5,7},{6,4},{7,5},{8,10},{9,11},{10,... | collective-permute-start | bytes 1769480 | tf_op jit(solution)/shard_map/ppermute | solution.py:330
  31.6 0.8 constant_dynamic-update-slice_fusion.2
  32.4 0.7 constant_dynamic-update-slice_fusion.1
  33.1 18.4 %collective-permute-done.7 = bf16[8,64,576]{2,1,0:T(8,128)(2,1)S(1)} collective-permute-done((bf16[8,64,576]{2,1,0:T(8,128)(2,1)S(1)}, bf16[8,64,576]{2,1,0:T(8,128)(2,1)S(1)}, u32[]{:S(2)}, u32[]{:S(2)}) %collective-permute-start.7) | collective-permute-done | bytes 589856 | tf_op jit(solution)/shard_map/ppermute | solution.py:330
  51.5 0.9 constant_dynamic-update-slice_fusion.kv_ref
  52.4 0.0 all-to-all-done
  52.4 0.0 collective-permute-done.3.gate1
  52.4 0.0 collective-permute-done.4.up1
  52.4 0.0 collective-permute-done.5.down1
  52.4 0.0 copy-start.2
  52.5 0.0 copy-start.3
  52.5 5.5 %all-to-all-start.1 = ((bf16[8,64,1536]{2,1,0:T(8,128)(2,1)}), bf16[8,64,1536]{2,1,0:T(8,128)(2,1)}, u32[]{:S(2)}, u32[]{:S(2)}) async-start(bf16[8,64,1536]{2,1,0:T(8,128)(2,1)} %split_queries.1), calls=%async_computation.1 | async-start | bytes 3145728 | tf_op jit(solution)/shard_map/all_to_all | solution.py:166
  58.0 0.0 copy-done.2
  58.0 0.3 copy.13
  58.3 0.0 copy-done.3
  58.3 0.1 fusion
  58.3 3.1 %collective-permute-start.9 = (bf16[1,4,512,128]{3,2,1,0:T(8,128)(2,1)S(1)}, bf16[1,4,512,128]{3,2,1,0:T(8,128)(2,1)S(1)}, u32[]{:S(2)}, u32[]{:S(2)}) collective-permute-start(bf16[1,4,512,128]{3,2,1,0:T(8,128)(2,1)S(1)} %fusion), channel_id=1, source_target_pairs={{0,8},{1,9},{2,10},{3,11},{4,12},{5,13},{6,14},{7,15},{8,0},{9,1},... | collective-permute-start | bytes 1572872 | tf_op jit(solution)/shard_map/ppermute | solution.py:330
  61.4 13.2 %expert_rows.1 = bf16[192,3584]{1,0:T(8,128)(2,1)} custom-call(bf16[192,3584]{1,0:T(8,128)(2,1)S(1)} %bitcast.16, bf16[1,3584,512]{2,1,0:T(8,128)(2,1)} %gate0.1, bf16[1,3584,512]{2,1,0:T(8,128)(2,1)} %up0.1, bf16[1,3584,512]{2,1,0:T(8,128)(2,1)} %collective-permute-done.3.gate1, bf16[1,3584,512]{2,1,0:T(8,128)(2,1)} %collective-permute-done.4.up1, ...), custom_call_target="tpu_custom_call" | custom-call | flops 4227858432 | bytes 24772608 | tf_op jit(solution)/shard_map/expert_rows/pallas_call | solution.py:125
  74.6 14.2 %all-to-all-done.1 = bf16[8,64,1536]{2,1,0:T(8,128)(2,1)} async-done(((bf16[8,64,1536]{2,1,0:T(8,128)(2,1)}), bf16[8,64,1536]{2,1,0:T(8,128)(2,1)}, u32[]{:S(2)}, u32[]{:S(2)}) %all-to-all-start.1) | async-done | bytes 1572896 | tf_op jit(solution)/shard_map/all_to_all | solution.py:166
  88.8 5.6 %all-to-all-start.2 = ((bf16[8,24,3584]{2,1,0:T(8,128)(2,1)}), bf16[8,24,3584]{2,1,0:T(8,128)(2,1)S(1)}, u32[]{:S(2)}, u32[]{:S(2)}) async-start(bf16[8,24,3584]{2,1,0:T(8,128)(2,1)} %bitcast.12), calls=%async_computation.2 | async-start | bytes 2752512 | tf_op jit(solution)/shard_map/all_to_all | solution.py:335
  94.4 0.0 collective-permute-start.8
  94.4 0.0 collective-permute-done.9
  94.4 0.1 constant_dynamic-update-slice_fusion.3.weight_ref
  94.5 0.6 collective-permute-start.10
  95.1 0.1 pad_add_fusion.rank_ref
  95.2 2.5 %collective-permute-done.8.other_kv_ref = bf16[16,64,576]{2,1,0:T(8,128)(2,1)S(1)} collective-permute-done((bf16[16,64,576]{2,1,0:T(8,128)(2,1)}, bf16[16,64,576]{2,1,0:T(8,128)(2,1)S(1)}, u32[]{:S(2)}, u32[]{:S(2)}) %collective-permute-start.8) | collective-permute-done | bytes 1179680 | tf_op jit(solution)/shard_map/ppermute | solution.py:330
  97.6 0.0 copy-start.6
  97.6 1.3 collective-permute-done.10.other_weight_ref
  98.9 0.0 copy-done.6
  98.9 15.0 %causal_attention.1 = bf16[512,1024]{1,0:T(8,128)(2,1)} custom-call(s32[2]{0:T(128)S(1)} %pad_add_fusion.rank_ref, bf16[512,1536]{1,0:T(8,128)(2,1)} %bitcast.8.query_ref, bf16[16,64,576]{2,1,0:T(8,128)(2,1)} %constant_dynamic-update-slice_fusion.kv_ref, bf16[16,64,576]{2,1,0:T(8,128)(2,1)} %copy-done.6, ...), custom_call_target="tpu_custom_call" | custom-call | flops 9126805504 | bytes 7602176 | tf_op jit(solution)/shard_map/causal_attention/pallas_call | solution.py:302
  113.9 0.0 copy-start.5
  113.9 11.8 %all-to-all-done.2 = bf16[8,24,3584]{2,1,0:T(8,128)(2,1)S(1)} async-done(((bf16[8,24,3584]{2,1,0:T(8,128)(2,1)}), bf16[8,24,3584]{2,1,0:T(8,128)(2,1)S(1)}, u32[]{:S(2)}, u32[]{:S(2)}) %all-to-all-start.2) | async-done | bytes 1376288 | tf_op jit(solution)/shard_map/all_to_all | solution.py:335
  125.7 3.6 %all-to-all-start.3 = ((bf16[8,64,1024]{2,1,0:T(8,128)(2,1)}), bf16[8,64,1024]{2,1,0:T(8,128)(2,1)S(1)}, u32[]{:S(2)}, u32[]{:S(2)}) async-start(bf16[8,64,1024]{2,1,0:T(8,128)(2,1)} %bitcast.13), calls=%async_computation.3 | async-start | bytes 2097152 | tf_op jit(solution)/shard_map/all_to_all | solution.py:166
  129.3 0.0 copy-done.5
  129.3 0.1 copy.15.gates_ref
  129.4 1.6 %combine_routes.1 = bf16[64,3584]{1,0:T(8,128)(2,1)} custom-call(s32[64,2]{1,0:T(8,128)S(1)} %copy.12.routes_ref, f32[64,2]{1,0:T(8,128)S(1)} %copy.15.gates_ref, bf16[192,3584]{1,0:T(8,128)(2,1)S(1)} %bitcast.15), custom_call_target="tpu_custom_call" | custom-call | bytes 1835008 | tf_op jit(solution)/shard_map/combine_routes/pallas_call | solution.py:86
  131.0 12.2 %all-to-all-done.3.x_ref = bf16[8,64,1024]{2,1,0:T(8,128)(2,1)S(1)} async-done(((bf16[8,64,1024]{2,1,0:T(8,128)(2,1)}), bf16[8,64,1024]{2,1,0:T(8,128)(2,1)S(1)}, u32[]{:S(2)}, u32[]{:S(2)}) %all-to-all-start.3) | async-done | bytes 1048608 | tf_op jit(solution)/shard_map/all_to_all | solution.py:166
  143.2 1.1 join_values.1
  (1 shorter events, 0.0 us)
Async XLA Ops:
  0.6 9.5 %collective-permute-start = (bf16[64,576]{1,0:T(8,128)(2,1)}, bf16[64,576]{1,0:T(8,128)(2,1)S(1)}, u32[]{:S(2)}, u32[]{:S(2)}) collective-permute-start(bf16[64,576]{1,0:T(8,128)(2,1)} %param.11), channel_id=1, source_target_pairs={{0,8},{1,9},{2,10},{3,11},{4,12},{5,13},{6,14},{7,15},{8,0},{9,1},... | collective-permute-start | bytes 221192 | tf_op jit(solution)/shard_map/ppermute | solution.py:330
  4.7 5.4 %collective-permute-start.1 = (bf16[64,576]{1,0:T(8,128)(2,1)}, bf16[64,576]{1,0:T(8,128)(2,1)S(1)}, u32[]{:S(2)}, u32[]{:S(2)}) collective-permute-start(bf16[64,576]{1,0:T(8,128)(2,1)} %param.11), channel_id=1, source_target_pairs={{0,4},{1,5},{2,6},{3,7},{4,0},{5,1},{6,2},{7,3},{8,12},{9,13},{10,... | collective-permute-start | bytes 221192 | tf_op jit(solution)/shard_map/ppermute | solution.py:330
  6.3 6.4 %collective-permute-start.2 = (bf16[64,576]{1,0:T(8,128)(2,1)}, bf16[64,576]{1,0:T(8,128)(2,1)S(1)}, u32[]{:S(2)}, u32[]{:S(2)}) collective-permute-start(bf16[64,576]{1,0:T(8,128)(2,1)} %param.11), channel_id=1, source_target_pairs={{0,12},{1,13},{2,14},{3,15},{4,8},{5,9},{6,10},{7,11},{8,4},{9,5},... | collective-permute-start | bytes 221192 | tf_op jit(solution)/shard_map/ppermute | solution.py:330
  7.1 1.0 copy-start.1
  12.8 39.7 %collective-permute-start.3 = (bf16[1,3584,512]{2,1,0:T(8,128)(2,1)}, bf16[1,3584,512]{2,1,0:T(8,128)(2,1)}, u32[]{:S(2)}, u32[]{:S(2)}) collective-permute-start(bf16[1,3584,512]{2,1,0:T(8,128)(2,1)} %gate0.1), channel_id=1, source_target_pairs={{0,1},{1,0},{2,3},{3,2},{4,5},{5,4},{6,7},{7,6},{8,9},{9,8},{10,11... | collective-permute-start | bytes 11010056 | tf_op jit(solution)/shard_map/ppermute | solution.py:330
  12.8 39.7 %collective-permute-start.4 = (bf16[1,3584,512]{2,1,0:T(8,128)(2,1)}, bf16[1,3584,512]{2,1,0:T(8,128)(2,1)}, u32[]{:S(2)}, u32[]{:S(2)}) collective-permute-start(bf16[1,3584,512]{2,1,0:T(8,128)(2,1)} %up0.1), channel_id=1, source_target_pairs={{0,1},{1,0},{2,3},{3,2},{4,5},{5,4},{6,7},{7,6},{8,9},{9,8},{10,11... | collective-permute-start | bytes 11010056 | tf_op jit(solution)/shard_map/ppermute | solution.py:330
  13.3 39.2 %collective-permute-start.5 = (bf16[1,512,3584]{2,1,0:T(8,128)(2,1)}, bf16[1,512,3584]{2,1,0:T(8,128)(2,1)}, u32[]{:S(2)}, u32[]{:S(2)}) collective-permute-start(bf16[1,512,3584]{2,1,0:T(8,128)(2,1)} %down0.1), channel_id=1, source_target_pairs={{0,1},{1,0},{2,3},{3,2},{4,5},{5,4},{6,7},{7,6},{8,9},{9,8},{10,11... | collective-permute-start | bytes 11010056 | tf_op jit(solution)/shard_map/ppermute | solution.py:330
  13.3 4.9 %copy-start = (bf16[64,12288]{1,0:T(8,128)(2,1)S(1)}, bf16[64,12288]{1,0:T(8,128)(2,1)}, u32[]{:S(2)}) copy-start(bf16[64,12288]{1,0:T(8,128)(2,1)} %x_ref.3) | copy-start | bytes 4718596
  13.3 39.2 %all-to-all-start = ((bf16[8,24,3584]{2,1,0:T(8,128)(2,1)}), bf16[8,24,3584]{2,1,0:T(8,128)(2,1)S(1)}, u32[]{:S(2)}, u32[]{:S(2)}) async-start(bf16[8,24,3584]{2,1,0:T(8,128)(2,1)} %bitcast.2), calls=%async_computation | async-start | bytes 2752512 | tf_op jit(solution)/shard_map/all_to_all | solution.py:335
  18.2 1.6 %copy-start.4 = (bf16[64,576]{1,0:T(8,128)(2,1)S(1)}, bf16[64,576]{1,0:T(8,128)(2,1)}, u32[]{:S(2)}) copy-start(bf16[64,576]{1,0:T(8,128)(2,1)} %param.11) | copy-start | bytes 221188
  19.8 9.9 %collective-permute-start.6 = (bf16[4,64,576]{2,1,0:T(8,128)(2,1)S(1)}, bf16[4,64,576]{2,1,0:T(8,128)(2,1)S(1)}, u32[]{:S(2)}, u32[]{:S(2)}) collective-permute-start(bf16[4,64,576]{2,1,0:T(8,128)(2,1)S(1)} %pad_maximum_fusion.1), channel_id=1, source_target_pairs={{0,16},{1,17},{2,18},{3,19},{4,20},{5,21},{6,22},{7,23},{8,24},{9,... | collective-permute-start | bytes 884744 | tf_op jit(solution)/shard_map/ppermute | solution.py:330
  29.8 21.7 %collective-permute-start.7 = (bf16[8,64,576]{2,1,0:T(8,128)(2,1)S(1)}, bf16[8,64,576]{2,1,0:T(8,128)(2,1)S(1)}, u32[]{:S(2)}, u32[]{:S(2)}) collective-permute-start(bf16[8,64,576]{2,1,0:T(8,128)(2,1)S(1)} %pad_maximum_fusion), channel_id=1, source_target_pairs={{0,2},{1,3},{2,0},{3,1},{4,6},{5,7},{6,4},{7,5},{8,10},{9,11},{10,... | collective-permute-start | bytes 1769480 | tf_op jit(solution)/shard_map/ppermute | solution.py:330
  52.4 5.5 %copy-start.2 = (bf16[4,128,512]{2,1,0:T(8,128)(2,1)S(1)}, bf16[4,128,512]{2,1,0:T(8,128)(2,1)}, u32[]{:S(2)}) copy-start(bf16[4,128,512]{2,1,0:T(8,128)(2,1)} %param.12) | copy-start | bytes 1572868
  52.5 5.8 %copy-start.3 = (bf16[4,512,128]{2,1,0:T(8,128)(2,1)S(1)}, bf16[4,512,128]{2,1,0:T(8,128)(2,1)}, u32[]{:S(2)}) copy-start(bf16[4,512,128]{2,1,0:T(8,128)(2,1)} %param.13) | copy-start | bytes 1572868
  52.5 36.4 %all-to-all-start.1 = ((bf16[8,64,1536]{2,1,0:T(8,128)(2,1)}), bf16[8,64,1536]{2,1,0:T(8,128)(2,1)}, u32[]{:S(2)}, u32[]{:S(2)}) async-start(bf16[8,64,1536]{2,1,0:T(8,128)(2,1)} %split_queries.1), calls=%async_computation.1 | async-start | bytes 3145728 | tf_op jit(solution)/shard_map/all_to_all | solution.py:166
  58.3 36.1 %collective-permute-start.9 = (bf16[1,4,512,128]{3,2,1,0:T(8,128)(2,1)S(1)}, bf16[1,4,512,128]{3,2,1,0:T(8,128)(2,1)S(1)}, u32[]{:S(2)}, u32[]{:S(2)}) collective-permute-start(bf16[1,4,512,128]{3,2,1,0:T(8,128)(2,1)S(1)} %fusion), channel_id=1, source_target_pairs={{0,8},{1,9},{2,10},{3,11},{4,12},{5,13},{6,14},{7,15},{8,0},{9,1},... | collective-permute-start | bytes 1572872 | tf_op jit(solution)/shard_map/ppermute | solution.py:330
  88.8 36.9 %all-to-all-start.2 = ((bf16[8,24,3584]{2,1,0:T(8,128)(2,1)}), bf16[8,24,3584]{2,1,0:T(8,128)(2,1)S(1)}, u32[]{:S(2)}, u32[]{:S(2)}) async-start(bf16[8,24,3584]{2,1,0:T(8,128)(2,1)} %bitcast.12), calls=%async_computation.2 | async-start | bytes 2752512 | tf_op jit(solution)/shard_map/all_to_all | solution.py:335
  94.4 3.2 %collective-permute-start.8 = (bf16[16,64,576]{2,1,0:T(8,128)(2,1)}, bf16[16,64,576]{2,1,0:T(8,128)(2,1)S(1)}, u32[]{:S(2)}, u32[]{:S(2)}) collective-permute-start(bf16[16,64,576]{2,1,0:T(8,128)(2,1)} %constant_dynamic-update-slice_fusion.kv_ref), channel_id=1, source_target_pairs={{0,1},{1,0},{2,3},{3,2},{4,5},{5,4},{6,7},{7,6},{8,9},{9,8},{10,11... | collective-permute-start | bytes 3538952 | tf_op jit(solution)/shard_map/ppermute | solution.py:330
  94.5 4.4 %collective-permute-start.10 = (bf16[2,4,512,128]{3,2,1,0:T(8,128)(2,1)S(1)}, bf16[2,4,512,128]{3,2,1,0:T(8,128)(2,1)S(1)}, u32[]{:S(2)}, u32[]{:S(2)}) collective-permute-start(bf16[2,4,512,128]{3,2,1,0:T(8,128)(2,1)S(1)} %constant_dynamic-update-slice_fusion.3.weight_ref), channel_id=1, source_target_pairs={{0,1},{1,0},{2,3},{3,2},{4,5},{5,4},{6,7},{7,6},{8,9},{9,8},{10,11... | collective-permute-start | bytes 3145736 | tf_op jit(solution)/shard_map/ppermute | solution.py:330
  97.6 1.3 copy-start.6
  113.9 15.4 %copy-start.5 = (f32[64,2]{0,1:T(2,128)S(1)}, f32[64,2]{0,1:T(2,128)}, u32[]{:S(2)}) copy-start(f32[64,2]{0,1:T(2,128)} %param.16) | copy-start | bytes 1540
  125.7 17.4 %all-to-all-start.3 = ((bf16[8,64,1024]{2,1,0:T(8,128)(2,1)}), bf16[8,64,1024]{2,1,0:T(8,128)(2,1)S(1)}, u32[]{:S(2)}, u32[]{:S(2)}) async-start(bf16[8,64,1024]{2,1,0:T(8,128)(2,1)} %bitcast.13), calls=%async_computation.3 | async-start | bytes 2097152 | tf_op jit(solution)/shard_map/all_to_all | solution.py:166

commit v16 on v15

--- a/solution.py
+++ b/solution.py
@@ -53,12 +53,23 @@
     return first * rows + slot0, second * rows + slot1
 
 
+STEP = 896
+STEPS = D // STEP
+
+
 def bucket_kernel(rows, routes_ref, x_ref, out_ref):
-    target0, target1 = slot_targets(routes_ref[...], rows)
+    target0, target1 = slot_targets(routes_ref[...], STEPS * rows)
     column = lax.broadcasted_iota(jnp.int32, (x_ref.shape[0], out_ref.shape[0]), 1)
-    chosen = jnp.where((column == target0) | (column == target1), 1.0, 0.0).astype(BF16)
+    chosen = []
+    for part in range(STEPS):
+        hit = (column == target0 + part * rows) | (column == target1 + part * rows)
+        chosen.append(jnp.where(hit, 1.0, 0.0).astype(BF16))
+    parts = [x_ref[:, part * STEP : (part + 1) * STEP] for part in range(STEPS)]
     out_ref[...] = lax.dot_general(
-        chosen, x_ref[...], (((0,), (0,)), ((), ())), preferred_element_type=F32
+        jnp.concatenate(chosen, axis=0),
+        jnp.concatenate(parts, axis=0),
+        (((0,), (0,)), ((), ())),
+        preferred_element_type=F32,
     ).astype(BF16)
 
 
@@ -67,19 +78,21 @@
         functools.partial(bucket_kernel, rows),
         "bucket_rows",
         moved=2 * D * (moe_input.shape[0] + experts * rows),
-        out_shape=jax.ShapeDtypeStruct((experts * rows, D), BF16),
+        out_shape=jax.ShapeDtypeStruct((experts * STEPS * rows, STEP), BF16),
     )(routes, moe_input)
 
 
 def combine_kernel(rows, routes_ref, gates_ref, back_ref, out_ref):
-    back = back_ref[...]
     tok = routes_ref.shape[0]
-    target0, target1 = slot_targets(routes_ref[...], rows)
+    target0, target1 = slot_targets(routes_ref[...], STEPS * rows)
     targets = jnp.concatenate([target0, target1], axis=0)
-    column = lax.broadcasted_iota(jnp.int32, (2 * tok, back.shape[0]), 1)
-    chosen = jnp.where(column == targets, 1.0, 0.0).astype(BF16)
-    picked = jnp.dot(chosen, back, preferred_element_type=F32)
-    out_ref[...] = (picked[:tok] * gates_ref[:, 0:1] + picked[tok:] * gates_ref[:, 1:2]).astype(BF16)
+    column = lax.broadcasted_iota(jnp.int32, (2 * tok, back_ref.shape[0]), 1)
+    for part in range(STEPS):
+        chosen = jnp.where(column == targets + part * rows, 1.0, 0.0).astype(BF16)
+        picked = jnp.dot(chosen, back_ref[...], preferred_element_type=F32)
+        out_ref[:, part * STEP : (part + 1) * STEP] = (
+            picked[:tok] * gates_ref[:, 0:1] + picked[tok:] * gates_ref[:, 1:2]
+        ).astype(BF16)
 
 
 def combine(routes, gates, back, rows):
@@ -91,19 +104,30 @@
     )(routes, gates, back)
 
 
-STEP = 896
-STEPS = D // STEP
-
-
-def expert_kernel(x_ref, gate0, up0, gate1, up1, down0, down1, out_ref, sums, hidden):
+def rows_of_part(experts, rows, part):
+    shape = (experts * rows, experts * STEPS * rows)
+    row = lax.broadcasted_iota(jnp.int32, shape, 0)
+    source = row + part * rows
+    for chip in range(1, experts):
+        source = source + jnp.where(row >= chip * rows, (STEPS - 1) * rows, 0)
+    return jnp.where(lax.broadcasted_iota(jnp.int32, shape, 1) == source, 1.0, 0.0).astype(BF16)
+
+
+def expert_kernel(experts, x_ref, gate0, up0, gate1, up1, down0, down1, out_ref, x, sums, hidden, result):
     step = pl.program_id(0)
+    rows = x.shape[1] // experts
+
+    @pl.when(step == 0)
+    def _():
+        for part in range(STEPS):
+            chosen = rows_of_part(experts, rows, part)
+            x[part] = jnp.dot(chosen, x_ref[...], preferred_element_type=F32).astype(BF16)
 
     @pl.when(step < STEPS)
     def _():
-        x = x_ref[...]
         for index, weight_ref in enumerate((gate0, up0, gate1, up1)):
-            part = jnp.dot(x, weight_ref[0], preferred_element_type=F32)
-            sums[index] = jnp.where(step == 0, part, sums[index] + part)
+            product = jnp.dot(x[step], weight_ref[0], preferred_element_type=F32)
+            sums[index] = jnp.where(step == 0, product, sums[index] + product)
 
     @pl.when(step == STEPS)
     def _():
@@ -115,23 +139,41 @@
     def _():
         first = jnp.dot(hidden[0], down0[0], preferred_element_type=F32).astype(BF16)
         second = jnp.dot(hidden[1], down1[0], preferred_element_type=F32).astype(BF16)
-        out_ref[...] = (first.astype(F32) + second.astype(F32)).astype(BF16)
-
-
-def expert_rows(x, own, other):
-    count = x.shape[0]
+        result[step - STEPS] = (first.astype(F32) + second.astype(F32)).astype(BF16)
+
+    @pl.when(step == 2 * STEPS - 1)
+    def _():
+        total = jnp.zeros(out_ref.shape, F32)
+        for part in range(STEPS):
+            total = total + lax.dot_general(
+                rows_of_part(experts, rows, part),
+                result[part],
+                (((0,), (0,)), ((), ())),
+                preferred_element_type=F32,
+            )
+        out_ref[...] = total.astype(BF16)
+
+
+def expert_rows(x, own, other, experts):
+    count = x.shape[0] // STEPS
     weights = pl.BlockSpec((1, STEP, HALF), lambda k: (0, jnp.minimum(k, STEPS - 1), 0))
     down = pl.BlockSpec((1, HALF, STEP), lambda k: (0, 0, jnp.maximum(k - STEPS, 0)))
-    return call(
-        expert_kernel,
+    whole = pl.BlockSpec(x.shape, lambda k: (0, 0))
+    return call(
+        functools.partial(expert_kernel, experts),
         "expert_rows",
         flops=12 * count * D * HALF,
         moved=12 * D * HALF + 4 * count * D,
         grid=(2 * STEPS,),
-        in_specs=[pl.BlockSpec((count, STEP), lambda k: (0, jnp.minimum(k, STEPS - 1)))] + [weights] * 4 + [down] * 2,
-        out_specs=pl.BlockSpec((count, STEP), lambda k: (0, jnp.maximum(k - STEPS, 0))),
-        scratch_shapes=[pltpu.VMEM((4, count, HALF), F32), pltpu.VMEM((2, count, HALF), BF16)],
-        out_shape=jax.ShapeDtypeStruct((count, D), BF16),
+        in_specs=[whole] + [weights] * 4 + [down] * 2,
+        out_specs=whole,
+        scratch_shapes=[
+            pltpu.VMEM((STEPS, count, STEP), BF16),
+            pltpu.VMEM((4, count, HALF), F32),
+            pltpu.VMEM((2, count, HALF), BF16),
+            pltpu.VMEM((STEPS, count, STEP), BF16),
+        ],
+        out_shape=jax.ShapeDtypeStruct(x.shape, BF16),
     )(x, own[0], own[1], other[0], other[1], own[2], other[2])
 
 
@@ -377,7 +419,7 @@
     tok = queries.shape[0]
     experts = shards // 2
     capacity = 2 * ((4 * tok * TOP + 6 * experts - 1) // (6 * experts))
-    rows = -(-capacity // 8) * 8
+    rows = capacity
     rank = lax.axis_index("ctx").astype(jnp.int32).reshape(1)
     group = lax.axis_index("groups").astype(jnp.int32).reshape(1)
     place = jnp.concatenate([rank, group])
@@ -386,7 +428,7 @@
     keys = [latent_kv] + [send(latent_kv, offset) for offset in direct]
 
     buckets = after(build_buckets(routes, moe_input, experts, rows), *keys)
-    arrived = swap_chips(buckets.reshape(experts, rows, D)).reshape(experts * rows, D)
+    arrived = swap_chips(buckets.reshape(experts, STEPS * rows, STEP)).reshape(-1, STEP)
 
     sent = split_queries(split, rank, queries)
     keys = after(jnp.stack(keys), sent)
@@ -410,14 +452,14 @@
         weights = after(weights, arrived)
         weights = jnp.concatenate([weights, send(weights, shards // 2)], axis=0)
 
-    result = expert_rows(arrived, own_half, other_half)
+    result = expert_rows(arrived, own_half, other_half, experts)
     other_weights = send(after(weights, result), 1)
     result, held = lax.optimization_barrier((result, held))
-    back = swap_chips(result.reshape(experts, rows, D))
+    back = swap_chips(result.reshape(experts, STEPS * rows, STEP))
     values = attention(split, place, held, keys, other_keys, weights, other_weights)
     values, back = lax.optimization_barrier((values, back))
     values = split.exchange(values.reshape(experts, tok, values.shape[1]))
-    moe_out = combine(routes, gates, back.reshape(experts * rows, D), rows)
+    moe_out = combine(routes, gates, back.reshape(-1, STEP), rows)
     return (join_values(split, rank, values), moe_out)
 
 

time: 145 us -> 141 us (0.972)
  waiting for transfers between devices: 71.4 us -> 63.8 us
  Pallas kernels: 34.4 us -> 38 us
    all_to_all x2, waiting for transfers between devices: 26.4 us -> 22.2 us  [exchange(): lax.all_to_all(array, ('groups', 'ctx'), split_axis=0, concat_axis=0, axi...]
    pallas_call x1, Pallas kernels: 13.2 us -> 16.1 us  [expert_rows(): call(functools.partial(expert_kernel, experts), 'expert_rows', flops=12 *...]
    all_to_all x2, waiting for transfers between devices: 11.8 us -> 9.33 us  [swap_chips(): lax.all_to_all(array, 'ctx', split_axis=0, concat_axis=0, axis_index_grou...]
  transfers between devices with their start and end apart: 15 -> 15, of which waited for: 8 -> 8; matrix products, arithmetic and copies ran while one was open for 3% -> 3% of each run, Pallas kernels for 23% -> 26%
where the time goes in v16:
time: 141 us
  waiting for transfers between devices  63.8 us (45%)
  Pallas kernels  38 us (27%)
  starting transfers between devices  32.5 us (23%)
  local copies, waits for them, and re-layouts  5.48 us (4%)
    ppermute x11, waiting for transfers between devices, send(): lax.ppermute(array, ('groups', 'ctx'), [(i, i ^ mask) for i in range(coun...  32.2 us
    all_to_all x2, waiting for transfers between devices, exchange(): lax.all_to_all(array, ('groups', 'ctx'), split_axis=0, concat_axis=0, axi...  22.2 us
    pallas_call x1, Pallas kernels, expert_rows(): call(functools.partial(expert_kernel, experts), 'expert_rows', flops=12 *...  16.1 us
    pallas_call x1, Pallas kernels, attention(): call(functools.partial(attention_kernel, split), 'causal_attention', flop...  15 us
    ppermute x11, starting transfers between devices, send(): lax.ppermute(array, ('groups', 'ctx'), [(i, i ^ mask) for i in range(coun...  13.1 us
    all_to_all x2, starting transfers between devices, swap_chips(): lax.all_to_all(array, 'ctx', split_axis=0, concat_axis=0, axis_index_grou...  10.1 us
    all_to_all x2, waiting for transfers between devices, swap_chips(): lax.all_to_all(array, 'ctx', split_axis=0, concat_axis=0, axis_index_grou...  9.33 us
    all_to_all x2, starting transfers between devices, exchange(): lax.all_to_all(array, ('groups', 'ctx'), split_axis=0, concat_axis=0, axi...  9.26 us
  transfers between devices with their start and end apart: 15, of which 8 were waited for; matrix products, arithmetic and copies ran while one was open for 3% of the time, Pallas kernels for 26%

profile of v16, /device:TPU:0, one launch (start us, length us, event | category | flops | bytes accessed | tf_op | source)
XLA Modules:
  0.0 140.8 jit_solution(9509210399757064265)
XLA Ops:
  0.6 4.1 %collective-permute-start = (bf16[64,576]{1,0:T(8,128)(2,1)}, bf16[64,576]{1,0:T(8,128)(2,1)S(1)}, u32[]{:S(2)}, u32[]{:S(2)}) collective-permute-start(bf16[64,576]{1,0:T(8,128)(2,1)} %param.11), channel_id=1, source_target_pairs={{0,8},{1,9},{2,10},{3,11},{4,12},{5,13},{6,14},{7,15},{8,0},{9,1},... | collective-permute-start | bytes 221192 | tf_op jit(solution)/shard_map/ppermute | solution.py:372
  4.7 1.6 %collective-permute-start.1 = (bf16[64,576]{1,0:T(8,128)(2,1)}, bf16[64,576]{1,0:T(8,128)(2,1)S(1)}, u32[]{:S(2)}, u32[]{:S(2)}) collective-permute-start(bf16[64,576]{1,0:T(8,128)(2,1)} %param.11), channel_id=1, source_target_pairs={{0,4},{1,5},{2,6},{3,7},{4,0},{5,1},{6,2},{7,3},{8,12},{9,13},{10,... | collective-permute-start | bytes 221192 | tf_op jit(solution)/shard_map/ppermute | solution.py:372
  6.3 0.0 collective-permute-start.2
  6.3 0.8 copy.12.routes_ref
  7.1 0.0 copy-start.1
  7.1 1.0 copy-done.1
  8.1 2.1 %bucket_rows.1 = bf16[704,896]{1,0:T(8,128)(2,1)} custom-call(s32[64,2]{1,0:T(8,128)S(1)} %copy.12.routes_ref, bf16[64,3584]{1,0:T(8,128)(2,1)S(1)} %copy-done.1), custom_call_target="tpu_custom_call" | custom-call | bytes 1720320 | tf_op jit(solution)/shard_map/bucket_rows/pallas_call | solution.py:77
  10.2 0.0 copy-start
  10.2 0.0 collective-permute-done
  10.2 0.0 collective-permute-done.1
  10.2 2.5 %collective-permute-done.2 = bf16[64,576]{1,0:T(8,128)(2,1)S(1)} collective-permute-done((bf16[64,576]{1,0:T(8,128)(2,1)}, bf16[64,576]{1,0:T(8,128)(2,1)S(1)}, u32[]{:S(2)}, u32[]{:S(2)}) %collective-permute-start.2) | collective-permute-done | bytes 73760 | tf_op jit(solution)/shard_map/ppermute | solution.py:372
  12.8 0.0 collective-permute-start.3
  12.8 0.5 collective-permute-start.4
  13.3 0.0 collective-permute-start.5
  13.3 4.8 %all-to-all-start = ((bf16[8,88,896]{2,1,0:T(8,128)(2,1)}), bf16[8,88,896]{2,1,0:T(8,128)(2,1)S(1)}, u32[]{:S(2)}, u32[]{:S(2)}) async-start(bf16[8,88,896]{2,1,0:T(8,128)(2,1)} %bitcast.2), calls=%async_computation | async-start | bytes 2523136 | tf_op jit(solution)/shard_map/all_to_all | solution.py:377
  18.0 0.0 copy-done
  18.0 0.0 copy-start.4
  18.1 1.6 %split_queries.1 = bf16[8,64,1536]{2,1,0:T(8,128)(2,1)} custom-call(s32[1]{0:T(128)} %bitcast.rank_ref, bf16[64,12288]{1,0:T(8,128)(2,1)S(1)} %copy-done), custom_call_target="tpu_custom_call" | custom-call | bytes 3145728 | tf_op jit(solution)/shard_map/split_queries/pallas_call | solution.py:226
  19.6 0.0 copy-done.4
  19.6 0.1 pad_maximum_fusion.1
  19.7 1.6 %collective-permute-start.6 = (bf16[4,64,576]{2,1,0:T(8,128)(2,1)S(1)}, bf16[4,64,576]{2,1,0:T(8,128)(2,1)S(1)}, u32[]{:S(2)}, u32[]{:S(2)}) collective-permute-start(bf16[4,64,576]{2,1,0:T(8,128)(2,1)S(1)} %pad_maximum_fusion.1), channel_id=1, source_target_pairs={{0,16},{1,17},{2,18},{3,19},{4,20},{5,21},{6,22},{7,23},{8,24},{9,... | collective-permute-start | bytes 884744 | tf_op jit(solution)/shard_map/ppermute | solution.py:372
  21.2 8.3 %collective-permute-done.6 = bf16[4,64,576]{2,1,0:T(8,128)(2,1)S(1)} collective-permute-done((bf16[4,64,576]{2,1,0:T(8,128)(2,1)S(1)}, bf16[4,64,576]{2,1,0:T(8,128)(2,1)S(1)}, u32[]{:S(2)}, u32[]{:S(2)}) %collective-permute-start.6) | collective-permute-done | bytes 294944 | tf_op jit(solution)/shard_map/ppermute | solution.py:372
  29.6 0.1 pad_maximum_fusion
  29.7 1.8 %collective-permute-start.7 = (bf16[8,64,576]{2,1,0:T(8,128)(2,1)S(1)}, bf16[8,64,576]{2,1,0:T(8,128)(2,1)S(1)}, u32[]{:S(2)}, u32[]{:S(2)}) collective-permute-start(bf16[8,64,576]{2,1,0:T(8,128)(2,1)S(1)} %pad_maximum_fusion), channel_id=1, source_target_pairs={{0,2},{1,3},{2,0},{3,1},{4,6},{5,7},{6,4},{7,5},{8,10},{9,11},{10,... | collective-permute-start | bytes 1769480 | tf_op jit(solution)/shard_map/ppermute | solution.py:372
  31.5 0.8 constant_dynamic-update-slice_fusion.2
  32.2 0.8 constant_dynamic-update-slice_fusion.1
  33.0 17.6 %collective-permute-done.7 = bf16[8,64,576]{2,1,0:T(8,128)(2,1)S(1)} collective-permute-done((bf16[8,64,576]{2,1,0:T(8,128)(2,1)S(1)}, bf16[8,64,576]{2,1,0:T(8,128)(2,1)S(1)}, u32[]{:S(2)}, u32[]{:S(2)}) %collective-permute-start.7) | collective-permute-done | bytes 589856 | tf_op jit(solution)/shard_map/ppermute | solution.py:372
  50.6 0.9 constant_dynamic-update-slice_fusion.kv_ref
  51.5 0.0 all-to-all-done
  51.5 0.0 collective-permute-done.3.gate1
  51.5 0.0 collective-permute-done.4.up1
  51.5 0.0 collective-permute-done.5.down1
  51.5 0.0 copy-start.2
  51.5 5.7 %all-to-all-start.1 = ((bf16[8,64,1536]{2,1,0:T(8,128)(2,1)}), bf16[8,64,1536]{2,1,0:T(8,128)(2,1)}, u32[]{:S(2)}, u32[]{:S(2)}) async-start(bf16[8,64,1536]{2,1,0:T(8,128)(2,1)} %split_queries.1), calls=%async_computation.1 | async-start | bytes 3145728 | tf_op jit(solution)/shard_map/all_to_all | solution.py:208
  57.2 0.0 copy-start.3
  57.2 0.0 copy-done.2
  57.3 0.3 copy.13
  57.5 0.7 copy-done.3
  58.3 3.0 %collective-permute-start.9 = (bf16[1,4,512,128]{3,2,1,0:T(8,128)(2,1)S(1)}, bf16[1,4,512,128]{3,2,1,0:T(8,128)(2,1)S(1)}, u32[]{:S(2)}, u32[]{:S(2)}) collective-permute-start(bf16[1,4,512,128]{3,2,1,0:T(8,128)(2,1)S(1)} %fusion), channel_id=1, source_target_pairs={{0,8},{1,9},{2,10},{3,11},{4,12},{5,13},{6,14},{7,15},{8,0},{9,1},... | collective-permute-start | bytes 1572872 | tf_op jit(solution)/shard_map/ppermute | solution.py:372
  61.3 16.1 %expert_rows.1 = bf16[704,896]{1,0:T(8,128)(2,1)} custom-call(bf16[704,896]{1,0:T(8,128)(2,1)S(1)} %bitcast.16, bf16[1,3584,512]{2,1,0:T(8,128)(2,1)} %gate0.1, bf16[1,3584,512]{2,1,0:T(8,128)(2,1)} %up0.1, bf16[1,3584,512]{2,1,0:T(8,128)(2,1)} %collective-permute-done.3.gate1, bf16[1,3584,512]{2,1,0:T(8,128)(2,1)} %collective-permute-done.4.up1, ...), custom_call_target="tpu_custom_call" | custom-call | flops 3875536896 | bytes 24543232 | tf_op jit(solution)/shard_map/expert_rows/pallas_call | solution.py:162
  77.4 10.7 %all-to-all-done.1 = bf16[8,64,1536]{2,1,0:T(8,128)(2,1)} async-done(((bf16[8,64,1536]{2,1,0:T(8,128)(2,1)}), bf16[8,64,1536]{2,1,0:T(8,128)(2,1)}, u32[]{:S(2)}, u32[]{:S(2)}) %all-to-all-start.1) | async-done | bytes 1572896 | tf_op jit(solution)/shard_map/all_to_all | solution.py:208
  88.1 5.4 %all-to-all-start.2 = ((bf16[8,88,896]{2,1,0:T(8,128)(2,1)}), bf16[8,88,896]{2,1,0:T(8,128)(2,1)S(1)}, u32[]{:S(2)}, u32[]{:S(2)}) async-start(bf16[8,88,896]{2,1,0:T(8,128)(2,1)} %bitcast.12), calls=%async_computation.2 | async-start | bytes 2523136 | tf_op jit(solution)/shard_map/all_to_all | solution.py:377
  93.5 0.0 collective-permute-start.8
  93.5 0.0 collective-permute-done.9
  93.5 0.1 constant_dynamic-update-slice_fusion.3.weight_ref
  93.6 0.6 collective-permute-start.10
  94.2 0.1 pad_add_fusion.rank_ref
  94.2 2.5 %collective-permute-done.8.other_kv_ref = bf16[16,64,576]{2,1,0:T(8,128)(2,1)S(1)} collective-permute-done((bf16[16,64,576]{2,1,0:T(8,128)(2,1)}, bf16[16,64,576]{2,1,0:T(8,128)(2,1)S(1)}, u32[]{:S(2)}, u32[]{:S(2)}) %collective-permute-start.8) | collective-permute-done | bytes 1179680 | tf_op jit(solution)/shard_map/ppermute | solution.py:372
  96.7 0.0 copy-start.6
  96.7 1.3 collective-permute-done.10.other_weight_ref
  98.0 0.0 copy-done.6
  98.0 15.0 %causal_attention.1 = bf16[512,1024]{1,0:T(8,128)(2,1)} custom-call(s32[2]{0:T(128)S(1)} %pad_add_fusion.rank_ref, bf16[512,1536]{1,0:T(8,128)(2,1)} %bitcast.8.query_ref, bf16[16,64,576]{2,1,0:T(8,128)(2,1)} %constant_dynamic-update-slice_fusion.kv_ref, bf16[16,64,576]{2,1,0:T(8,128)(2,1)} %copy-done.6, ...), custom_call_target="tpu_custom_call" | custom-call | flops 9126805504 | bytes 7602176 | tf_op jit(solution)/shard_map/causal_attention/pallas_call | solution.py:344
  113.0 0.0 copy-start.5
  113.0 9.3 %all-to-all-done.2 = bf16[8,88,896]{2,1,0:T(8,128)(2,1)S(1)} async-done(((bf16[8,88,896]{2,1,0:T(8,128)(2,1)}), bf16[8,88,896]{2,1,0:T(8,128)(2,1)S(1)}, u32[]{:S(2)}, u32[]{:S(2)}) %all-to-all-start.2) | async-done | bytes 1261600 | tf_op jit(solution)/shard_map/all_to_all | solution.py:377
  122.3 3.6 %all-to-all-start.3 = ((bf16[8,64,1024]{2,1,0:T(8,128)(2,1)}), bf16[8,64,1024]{2,1,0:T(8,128)(2,1)S(1)}, u32[]{:S(2)}, u32[]{:S(2)}) async-start(bf16[8,64,1024]{2,1,0:T(8,128)(2,1)} %bitcast.13), calls=%async_computation.3 | async-start | bytes 2097152 | tf_op jit(solution)/shard_map/all_to_all | solution.py:208
  125.9 0.0 copy-done.5
  125.9 0.1 copy.15.gates_ref
  126.0 2.2 %combine_routes.1 = bf16[64,3584]{1,0:T(8,128)(2,1)} custom-call(s32[64,2]{1,0:T(8,128)S(1)} %copy.12.routes_ref, f32[64,2]{1,0:T(8,128)S(1)} %copy.15.gates_ref, bf16[704,896]{1,0:T(8,128)(2,1)S(1)} %bitcast.15), custom_call_target="tpu_custom_call" | custom-call | bytes 5505024 | tf_op jit(solution)/shard_map/combine_routes/pallas_call | solution.py:99
  128.2 11.6 %all-to-all-done.3.x_ref = bf16[8,64,1024]{2,1,0:T(8,128)(2,1)S(1)} async-done(((bf16[8,64,1024]{2,1,0:T(8,128)(2,1)}), bf16[8,64,1024]{2,1,0:T(8,128)(2,1)S(1)}, u32[]{:S(2)}, u32[]{:S(2)}) %all-to-all-start.3) | async-done | bytes 1048608 | tf_op jit(solution)/shard_map/all_to_all | solution.py:208
  139.7 1.1 join_values.1
  (2 shorter events, 0.1 us)
Async XLA Ops:
  0.6 9.6 %collective-permute-start = (bf16[64,576]{1,0:T(8,128)(2,1)}, bf16[64,576]{1,0:T(8,128)(2,1)S(1)}, u32[]{:S(2)}, u32[]{:S(2)}) collective-permute-start(bf16[64,576]{1,0:T(8,128)(2,1)} %param.11), channel_id=1, source_target_pairs={{0,8},{1,9},{2,10},{3,11},{4,12},{5,13},{6,14},{7,15},{8,0},{9,1},... | collective-permute-start | bytes 221192 | tf_op jit(solution)/shard_map/ppermute | solution.py:372
  4.7 5.5 %collective-permute-start.1 = (bf16[64,576]{1,0:T(8,128)(2,1)}, bf16[64,576]{1,0:T(8,128)(2,1)S(1)}, u32[]{:S(2)}, u32[]{:S(2)}) collective-permute-start(bf16[64,576]{1,0:T(8,128)(2,1)} %param.11), channel_id=1, source_target_pairs={{0,4},{1,5},{2,6},{3,7},{4,0},{5,1},{6,2},{7,3},{8,12},{9,13},{10,... | collective-permute-start | bytes 221192 | tf_op jit(solution)/shard_map/ppermute | solution.py:372
  6.3 6.4 %collective-permute-start.2 = (bf16[64,576]{1,0:T(8,128)(2,1)}, bf16[64,576]{1,0:T(8,128)(2,1)S(1)}, u32[]{:S(2)}, u32[]{:S(2)}) collective-permute-start(bf16[64,576]{1,0:T(8,128)(2,1)} %param.11), channel_id=1, source_target_pairs={{0,12},{1,13},{2,14},{3,15},{4,8},{5,9},{6,10},{7,11},{8,4},{9,5},... | collective-permute-start | bytes 221192 | tf_op jit(solution)/shard_map/ppermute | solution.py:372
  7.1 1.0 copy-start.1
  10.2 7.8 %copy-start = (bf16[64,12288]{1,0:T(8,128)(2,1)S(1)}, bf16[64,12288]{1,0:T(8,128)(2,1)}, u32[]{:S(2)}) copy-start(bf16[64,12288]{1,0:T(8,128)(2,1)} %x_ref.3) | copy-start | bytes 4718596
  12.8 38.8 %collective-permute-start.3 = (bf16[1,3584,512]{2,1,0:T(8,128)(2,1)}, bf16[1,3584,512]{2,1,0:T(8,128)(2,1)}, u32[]{:S(2)}, u32[]{:S(2)}) collective-permute-start(bf16[1,3584,512]{2,1,0:T(8,128)(2,1)} %gate0.1), channel_id=1, source_target_pairs={{0,1},{1,0},{2,3},{3,2},{4,5},{5,4},{6,7},{7,6},{8,9},{9,8},{10,11... | collective-permute-start | bytes 11010056 | tf_op jit(solution)/shard_map/ppermute | solution.py:372
  12.8 38.8 %collective-permute-start.4 = (bf16[1,3584,512]{2,1,0:T(8,128)(2,1)}, bf16[1,3584,512]{2,1,0:T(8,128)(2,1)}, u32[]{:S(2)}, u32[]{:S(2)}) collective-permute-start(bf16[1,3584,512]{2,1,0:T(8,128)(2,1)} %up0.1), channel_id=1, source_target_pairs={{0,1},{1,0},{2,3},{3,2},{4,5},{5,4},{6,7},{7,6},{8,9},{9,8},{10,11... | collective-permute-start | bytes 11010056 | tf_op jit(solution)/shard_map/ppermute | solution.py:372
  13.3 38.2 %collective-permute-start.5 = (bf16[1,512,3584]{2,1,0:T(8,128)(2,1)}, bf16[1,512,3584]{2,1,0:T(8,128)(2,1)}, u32[]{:S(2)}, u32[]{:S(2)}) collective-permute-start(bf16[1,512,3584]{2,1,0:T(8,128)(2,1)} %down0.1), channel_id=1, source_target_pairs={{0,1},{1,0},{2,3},{3,2},{4,5},{5,4},{6,7},{7,6},{8,9},{9,8},{10,11... | collective-permute-start | bytes 11010056 | tf_op jit(solution)/shard_map/ppermute | solution.py:372
  13.3 38.2 %all-to-all-start = ((bf16[8,88,896]{2,1,0:T(8,128)(2,1)}), bf16[8,88,896]{2,1,0:T(8,128)(2,1)S(1)}, u32[]{:S(2)}, u32[]{:S(2)}) async-start(bf16[8,88,896]{2,1,0:T(8,128)(2,1)} %bitcast.2), calls=%async_computation | async-start | bytes 2523136 | tf_op jit(solution)/shard_map/all_to_all | solution.py:377
  18.0 1.6 %copy-start.4 = (bf16[64,576]{1,0:T(8,128)(2,1)S(1)}, bf16[64,576]{1,0:T(8,128)(2,1)}, u32[]{:S(2)}) copy-start(bf16[64,576]{1,0:T(8,128)(2,1)} %param.11) | copy-start | bytes 221188
  19.7 9.9 %collective-permute-start.6 = (bf16[4,64,576]{2,1,0:T(8,128)(2,1)S(1)}, bf16[4,64,576]{2,1,0:T(8,128)(2,1)S(1)}, u32[]{:S(2)}, u32[]{:S(2)}) collective-permute-start(bf16[4,64,576]{2,1,0:T(8,128)(2,1)S(1)} %pad_maximum_fusion.1), channel_id=1, source_target_pairs={{0,16},{1,17},{2,18},{3,19},{4,20},{5,21},{6,22},{7,23},{8,24},{9,... | collective-permute-start | bytes 884744 | tf_op jit(solution)/shard_map/ppermute | solution.py:372
  29.7 20.9 %collective-permute-start.7 = (bf16[8,64,576]{2,1,0:T(8,128)(2,1)S(1)}, bf16[8,64,576]{2,1,0:T(8,128)(2,1)S(1)}, u32[]{:S(2)}, u32[]{:S(2)}) collective-permute-start(bf16[8,64,576]{2,1,0:T(8,128)(2,1)S(1)} %pad_maximum_fusion), channel_id=1, source_target_pairs={{0,2},{1,3},{2,0},{3,1},{4,6},{5,7},{6,4},{7,5},{8,10},{9,11},{10,... | collective-permute-start | bytes 1769480 | tf_op jit(solution)/shard_map/ppermute | solution.py:372
  51.5 5.7 %copy-start.2 = (bf16[4,128,512]{2,1,0:T(8,128)(2,1)S(1)}, bf16[4,128,512]{2,1,0:T(8,128)(2,1)}, u32[]{:S(2)}) copy-start(bf16[4,128,512]{2,1,0:T(8,128)(2,1)} %param.12) | copy-start | bytes 1572868
  51.5 36.6 %all-to-all-start.1 = ((bf16[8,64,1536]{2,1,0:T(8,128)(2,1)}), bf16[8,64,1536]{2,1,0:T(8,128)(2,1)}, u32[]{:S(2)}, u32[]{:S(2)}) async-start(bf16[8,64,1536]{2,1,0:T(8,128)(2,1)} %split_queries.1), calls=%async_computation.1 | async-start | bytes 3145728 | tf_op jit(solution)/shard_map/all_to_all | solution.py:208
  57.2 1.0 copy-start.3
  58.3 35.2 %collective-permute-start.9 = (bf16[1,4,512,128]{3,2,1,0:T(8,128)(2,1)S(1)}, bf16[1,4,512,128]{3,2,1,0:T(8,128)(2,1)S(1)}, u32[]{:S(2)}, u32[]{:S(2)}) collective-permute-start(bf16[1,4,512,128]{3,2,1,0:T(8,128)(2,1)S(1)} %fusion), channel_id=1, source_target_pairs={{0,8},{1,9},{2,10},{3,11},{4,12},{5,13},{6,14},{7,15},{8,0},{9,1},... | collective-permute-start | bytes 1572872 | tf_op jit(solution)/shard_map/ppermute | solution.py:372
  88.1 34.2 %all-to-all-start.2 = ((bf16[8,88,896]{2,1,0:T(8,128)(2,1)}), bf16[8,88,896]{2,1,0:T(8,128)(2,1)S(1)}, u32[]{:S(2)}, u32[]{:S(2)}) async-start(bf16[8,88,896]{2,1,0:T(8,128)(2,1)} %bitcast.12), calls=%async_computation.2 | async-start | bytes 2523136 | tf_op jit(solution)/shard_map/all_to_all | solution.py:377
  93.5 3.2 %collective-permute-start.8 = (bf16[16,64,576]{2,1,0:T(8,128)(2,1)}, bf16[16,64,576]{2,1,0:T(8,128)(2,1)S(1)}, u32[]{:S(2)}, u32[]{:S(2)}) collective-permute-start(bf16[16,64,576]{2,1,0:T(8,128)(2,1)} %constant_dynamic-update-slice_fusion.kv_ref), channel_id=1, source_target_pairs={{0,1},{1,0},{2,3},{3,2},{4,5},{5,4},{6,7},{7,6},{8,9},{9,8},{10,11... | collective-permute-start | bytes 3538952 | tf_op jit(solution)/shard_map/ppermute | solution.py:372
  93.6 4.4 %collective-permute-start.10 = (bf16[2,4,512,128]{3,2,1,0:T(8,128)(2,1)S(1)}, bf16[2,4,512,128]{3,2,1,0:T(8,128)(2,1)S(1)}, u32[]{:S(2)}, u32[]{:S(2)}) collective-permute-start(bf16[2,4,512,128]{3,2,1,0:T(8,128)(2,1)S(1)} %constant_dynamic-update-slice_fusion.3.weight_ref), channel_id=1, source_target_pairs={{0,1},{1,0},{2,3},{3,2},{4,5},{5,4},{6,7},{7,6},{8,9},{9,8},{10,11... | collective-permute-start | bytes 3145736 | tf_op jit(solution)/shard_map/ppermute | solution.py:372
  96.7 1.3 copy-start.6
  113.0 12.9 %copy-start.5 = (f32[64,2]{0,1:T(2,128)S(1)}, f32[64,2]{0,1:T(2,128)}, u32[]{:S(2)}) copy-start(f32[64,2]{0,1:T(2,128)} %param.16) | copy-start | bytes 1540
  122.3 17.4 %all-to-all-start.3 = ((bf16[8,64,1024]{2,1,0:T(8,128)(2,1)}), bf16[8,64,1024]{2,1,0:T(8,128)(2,1)S(1)}, u32[]{:S(2)}, u32[]{:S(2)}) async-start(bf16[8,64,1024]{2,1,0:T(8,128)(2,1)} %bitcast.13), calls=%async_computation.3 | async-start | bytes 2097152 | tf_op jit(solution)/shard_map/all_to_all | solution.py:208
